TPU v7x, 32 devices: a whole 2x2x4 slice. The times are simulated.
32 devices in a mesh: row: 8 (over z, x), col: 4 (over y, core).
Axes of the slice: x: 2, y: 2, z: 4, core: 2. Of those that a mesh axis runs over, the one named last changes fastest.
Arguments:
- charges: bfloat16 [262144], P(('row', 'col')), may hold values from -6 to 6
- panel_order: int32 [262144], P(('row', 'col')), may hold values from 0 to 8191, as said below
- patch_anchor: int32 [3, 4096], P(None, ('row', 'col')), may hold values from 0 to 252, as said below
- project: bfloat16 [4096, 4096], P(('row', 'col')), may hold values from -0.75 to 0.75
- interpolate: bfloat16 [4096, 4096], P(('row', 'col')), may hold values from -0.75 to 0.75
- kernel_spectrum: float32 [512, 512, 512], P('row', 'col'), may hold values from 0.5 to 8
- near_pairs: int32 [2, 16384], P(None, ('row', 'col')), may hold values from 0 to 4095, as said below
- near_blocks: bfloat16 [16384, 4096], P(('row', 'col')), may hold values from -0.75 to 0.75
Outputs:
- potential: float32 [262144], P(('row', 'col'))
Inputs may be any that keep to these rules, and one draw needn't show every extreme that they name: `panel_order`: the entries of each aligned run of 8192 slots (one device's slots) are a permutation of 0 to 8191. `patch_anchor`: block b lies on device d = b // 128 at row index r = d // 4 and col index c = d % 4; its first coordinate lies in r * 32 to (r + 1) * 32 - 1, its second in c * 64 to (c + 1) * 64 - 1, and all three coordinates are at most 252. `near_pairs`: the pairs on a device have that device's blocks as targets, each block exactly 4 times; each source block lies on the same device or on one whose row and col indices each differ by at most one.
All inputs are finite; a program needn't handle non-finite values.
Results may differ from a plain program's by a relative error of at most 0.0025.
Values may be sent and summed in bfloat16 or wider, within the bound.
No kernel may reach another device: no remote copies, remote signals or barrier semaphores. Data moves between devices by JAX's collectives and lax.ppermute only.
A program may use at most 128 MiB of HBM per device.

v0:
```python
import math

import jax
import jax.numpy as jnp
from jax import lax
from jax.sharding import PartitionSpec as P

G = 256
P_SIZE = 512
BLK = 64
PTS = 64


def extended_2(array, sides, width):
    for axis, dim in sides:
        count, length = (lax.axis_size(axis), array.shape[dim])
        up = [(i, (i + 1) % count) for i in range(count - 1)]
        down = [(j, i) for i, j in up]
        last = lax.slice_in_dim(array, length - width, length, axis=dim)
        first = lax.slice_in_dim(array, 0, width, axis=dim)
        before = lax.ppermute(last, axis, up)
        after = lax.ppermute(first, axis, down)
        array = jnp.concatenate([before, array, after], axis=dim)
    return array


def from_behind(block, axis, distance):
    devices = range(lax.axis_size(axis))
    route = [(i - distance, i) for i in devices if i - distance in devices]
    return lax.ppermute(block, axis, route)


def for_sending(array):

    def short(part):
        return part.astype(jnp.bfloat16) if part.dtype == jnp.float32 else part

    return jax.tree.map(short, array)


def cas_table(rows, cols):
    first = jnp.arange(rows, dtype=jnp.int32)[:, None]
    second = jnp.arange(cols, dtype=jnp.int32)[None, :]
    phase = (first * second % P_SIZE).astype(jnp.float32) * (2.0 * math.pi / P_SIZE)
    return (jnp.cos(phase) + jnp.sin(phase)) / math.sqrt(P_SIZE)


def forward_transform(grid):
    highest = lax.Precision.HIGHEST
    forward = cas_table(G, P_SIZE)
    spec = jnp.einsum("xyz,zf->xyf", grid, forward, precision=highest)
    moved = lax.all_to_all(spec, "col", split_axis=2, concat_axis=1, tiled=True)
    whole = moved
    spec = jnp.einsum("xyf,yg->xgf", whole, forward, precision=highest)
    moved = lax.all_to_all(spec, "row", split_axis=1, concat_axis=0, tiled=True)
    whole = moved
    return jnp.einsum("xgf,xh->gfh", whole, forward, precision=highest)


def backward_transform(spec, margin):
    highest = lax.Precision.HIGHEST
    backward = cas_table(P_SIZE, G + margin)
    field = jnp.einsum("gfh,hx->xgf", spec, backward, precision=highest)
    pieces = field
    moved = lax.all_to_all(pieces, "row", split_axis=0, concat_axis=1, tiled=True)
    field = jnp.einsum("xgf,gy->xyf", moved, backward, precision=highest)
    pieces = field
    moved = lax.all_to_all(pieces, "col", split_axis=1, concat_axis=2, tiled=True)
    return jnp.einsum("xyf,fz->xyz", moved, cas_table(P_SIZE, G), precision=highest)


def selector(starts, length):
    offsets = jnp.arange(4, dtype=jnp.int32)
    cells = jnp.arange(length, dtype=jnp.int32)
    return (cells[None, None, :] == (starts[:, None] + offsets[None, :])[:, :, None]).astype(
        jnp.float32
    )


def body(
    charges,
    panel_order,
    patch_anchor,
    project,
    interpolate,
    kernel_spectrum,
    near_pairs,
    near_blocks,
):
    highest = lax.Precision.HIGHEST
    rows_count = lax.axis_size("row")
    cols_count = lax.axis_size("col")
    row_at = lax.axis_index("row")
    col_at = lax.axis_index("col")
    blocks_here = project.shape[0]
    panels_here = charges.shape[0]
    cells_x = G // rows_count
    cells_y = G // cols_count
    device = row_at * cols_count + col_at
    upper_part = panel_order // 128
    lower_part = panel_order % 128
    row_select = (
        upper_part[:, None] == jnp.arange(panels_here // 128, dtype=jnp.int32)[None, :]
    ).astype(jnp.bfloat16)
    lane_select = lower_part[:, None] == jnp.arange(128, dtype=jnp.int32)[None, :]
    charge_rows = jnp.dot(
        row_select, charges.reshape(panels_here // 128, 128), preferred_element_type=jnp.float32
    )
    block_q = (
        jnp.sum(jnp.where(lane_select, charge_rows, 0.0), axis=1)
        .astype(jnp.bfloat16)
        .reshape(blocks_here, BLK)
    )
    project_mats = project.reshape(blocks_here, PTS, BLK)
    patch = jnp.einsum("bgp,bp->bg", project_mats, block_q, preferred_element_type=jnp.float32)
    local_x = patch_anchor[0] - row_at * cells_x
    local_y = patch_anchor[1] - col_at * cells_y
    select_x = selector(local_x, cells_x + 3)
    select_y = selector(local_y, cells_y + 3)
    select_z = selector(patch_anchor[2], G)
    cube = patch.reshape(blocks_here, 4, 4, 4)
    placed = jnp.einsum("bijl,blz->bijz", cube, select_z, precision=highest)
    placed = jnp.einsum("bijz,bjy->biyz", placed, select_y, precision=highest)
    extended = jnp.einsum("bix,biyz->xyz", select_x, placed, precision=highest)
    neighbours = extended_2(block_q[None, None], (("row", 0), ("col", 1)), 1)
    neighbours = neighbours.reshape(9 * blocks_here, BLK)
    source = near_pairs[1]
    source_device = source // blocks_here
    code = (source_device // cols_count - row_at + 1) * 3 + (
        source_device % cols_count - col_at + 1
    )
    wanted = code * blocks_here + source % blocks_here
    pick_table = (wanted[:, None] == jnp.arange(9 * blocks_here, dtype=jnp.int32)[None, :]).astype(
        jnp.bfloat16
    )
    picked = jnp.dot(pick_table, neighbours, preferred_element_type=jnp.float32).astype(
        jnp.bfloat16
    )
    near_mats = near_blocks.reshape(near_blocks.shape[0], BLK, BLK)
    near_terms = jnp.einsum("pij,pj->pi", near_mats, picked, preferred_element_type=jnp.float32)
    target_table = (
        (near_pairs[0] - device * blocks_here)[:, None]
        == jnp.arange(blocks_here, dtype=jnp.int32)[None, :]
    ).astype(jnp.float32)
    near = jnp.einsum("pb,pi->bi", target_table, near_terms, precision=highest)
    spilled = from_behind(extended[:, cells_y:], "col", 1)
    folded = extended[:, :cells_y].at[:, :3].add(spilled)
    spilled = from_behind(folded[cells_x:], "row", 1)
    owned = folded[:cells_x].at[:3].add(spilled)
    spec = forward_transform(owned)
    own_field = backward_transform(spec * kernel_spectrum, 0)
    below = from_behind(own_field[:3].astype(jnp.bfloat16), "row", -1).astype(jnp.float32)
    taller = jnp.concatenate([own_field, below], axis=0)
    beside = from_behind(for_sending(taller[:, :3]), "col", -1)
    field = jnp.concatenate([taller, beside], axis=1)
    sampled = jnp.einsum("bix,xyz->biyz", select_x, field, precision=highest)
    sampled = jnp.einsum("bjy,biyz->bijz", select_y, sampled, precision=highest)
    sampled = jnp.einsum("blz,bijz->bijl", select_z, sampled, precision=highest)
    values = sampled.reshape(blocks_here, PTS).astype(jnp.bfloat16)
    interp_mats = interpolate.reshape(blocks_here, BLK, PTS)
    far = jnp.einsum("bpg,bg->bp", interp_mats, values, preferred_element_type=jnp.float32)
    total = (far + near).reshape(panels_here)
    spread = jnp.where(lane_select, total[:, None], 0.0)
    placed_back = jnp.einsum("kh,kl->hl", row_select.astype(jnp.float32), spread, precision=highest)
    return placed_back.reshape(panels_here)


def solution(mesh):
    placed = (
        P(("row", "col")),
        P(("row", "col")),
        P(None, ("row", "col")),
        P(("row", "col"), None),
        P(("row", "col"), None),
        P("row", "col", None),
        P(None, ("row", "col")),
        P(("row", "col"), None),
    )
    return jax.shard_map(
        body, mesh=mesh, in_specs=placed, out_specs=P(("row", "col")), check_vma=False
    )
```

profile of v0, /device:TPU:0, one launch (start us, length us, event | category | flops | bytes accessed | tf_op | source)
XLA Modules:
  0.0 825.1 jit_solution(7685910628455148872)
XLA Ops:
  5.7 21.6 %convolution_bitcast_fusion = f32[128,4,67,256]{3,2,1,0:T(8,128)} fusion(f32[128,4,4,256]{3,2,1,0:T(4,128)S(1)} %fusion.56, s32[128,4]{1,0:T(8,128)S(1)} %get-tuple-element.37), kind=kOutput, calls=%fused_computation.6 | convolution fusion | flops 421561856 | bytes 37226496 | tf_op jit(solution)/shard_map/bijz,bjy->biyz/dot_general | solution.py:123
  27.3 30.0 %fusion.19 = f32[35,67,256]{2,0,1:T(8,128)S(1)} fusion(f32[128,4,67,256]{3,2,1,0:T(8,128)} %convolution_bitcast_fusion, s32[128,4]{0,1:T(4,128)S(1)} %iota_add_fusion.2), kind=kOutput, calls=%fused_computation.31 | convolution fusion | flops 3688384000 | bytes 37530624 | tf_op jit(solution)/shard_map/bix,biyz->xyz/dot_general | solution.py:124
  72.0 7.1 fusion.41
  79.1 9.2 %copy.77 = f32[32,64,512]{1,0,2:T(8,128)} copy(f32[32,64,512]{2,0,1:T(8,128)} %fusion.41) | data formatting | bytes 8388608 | tf_op jit(solution)/shard_map/xyz,zf->xyf/dot_general | solution.py:51
  88.3 8.6 %reshape.291 = f32[4,1,262144]{2,1,0:T(1,128)} reshape(f32[512,32,64]{2,1,0:T(8,128)} %bitcast.111) | data formatting | bytes 8388608
  96.9 54.3 %all_to_all.72 = f32[4,1,262144]{2,1,0:T(1,128)} all-to-all(f32[4,1,262144]{2,1,0:T(1,128)} %reshape.291), channel_id=1, replica_groups=mesh['row'=8,'col'=4] {'col'}, dimensions={0} | all-to-all | bytes 8388608 | tf_op jit(solution)/shard_map/all_to_all | solution.py:52
  151.8 15.3 %reduce.10 = f32[4,262144]{1,0:T(4,128)} reduce(f32[4,1,262144]{2,1,0:T(1,128)} %all_to_all.72, f32[]{:T(128)} %broadcast.331), dimensions={1}, to_apply=%all_to_all.52.reduce_sub_computation | reduce | bytes 8388612 | tf_op jit(solution)/shard_map/all_to_all | solution.py:52
  167.0 9.3 %reshape.292 = f32[512,32,64]{2,1,0:T(8,128)} reshape(f32[4,262144]{1,0:T(4,128)} %reduce.10) | data formatting | bytes 8388608
  176.3 7.0 copy.78
  183.3 12.1 %convolution_bitcast_fusion.1 = f32[32,512,128]{2,1,0:T(8,128)S(1)} fusion(f32[32,256,128]{2,1,0:T(8,128)} %bitcast.116), kind=kOutput, calls=%fused_computation.15 | convolution fusion | flops 6444548096 | bytes 12582912 | tf_op jit(solution)/shard_map/xyf,yg->xgf/dot_general | solution.py:54
  195.4 5.1 copy.80
  200.4 189.8 %all_to_all.73 = f32[32,512,128]{2,0,1:T(8,128)S(1)} all-to-all(f32[32,512,128]{2,0,1:T(8,128)S(1)} %copy.80), channel_id=1, replica_groups=mesh['row'=8,'col'=4] {'row'}, dimensions={1} | all-to-all | bytes 16777216 | tf_op jit(solution)/shard_map/all_to_all | solution.py:55
  394.9 24.6 %fusion.6 = f32[64,128,512]{2,1,0:T(8,128)S(1)} fusion(f32[256,64,128]{2,1,0:T(8,128)S(1)} %bitcast.110), kind=kOutput, calls=%fused_computation.9 | convolution fusion | flops 12886999040 | bytes 25165824 | tf_op jit(solution)/shard_map/xgf,xh->gfh/dot_general | solution.py:57
  419.6 35.6 %fusion.4 = f32[256,64,128]{2,0,1:T(8,128)S(1)} fusion(f32[64,128,512]{2,1,0:T(8,128)S(1)} %fusion.6, f32[64,128,512]{2,1,0:T(8,128)} %param.17), kind=kOutput, calls=%fused_computation.4 | convolution fusion | flops 12891193344 | bytes 41943040 | tf_op jit(solution)/shard_map/gfh,hx->xgf/dot_general | solution.py:63
  460.1 186.0 %all_to_all.74 = f32[256,64,128]{2,1,0:T(8,128)S(1)} all-to-all(f32[256,64,128]{2,1,0:T(8,128)S(1)} %copy.85), channel_id=1, replica_groups=mesh['row'=8,'col'=4] {'row'}, dimensions={0} | all-to-all | bytes 16777216 | tf_op jit(solution)/shard_map/all_to_all | solution.py:65
  647.7 10.5 %convolution_bitcast_fusion.2 = f32[32,256,128]{2,1,0:T(8,128)S(1)} fusion(f32[32,512,128]{2,1,0:T(8,128)S(1)} %bitcast.115), kind=kOutput, calls=%fused_computation.22 | convolution fusion | flops 6444548096 | bytes 12582912 | tf_op jit(solution)/shard_map/xgf,gy->xyf/dot_general | solution.py:66
  680.1 6.5 copy.130
  686.7 29.3 %all-to-all-done.3 = f32[32,256,128]{2,0,1:T(8,128)} async-done(((f32[32,256,128]{2,0,1:T(8,128)}), f32[32,256,128]{2,0,1:T(8,128)}, u32[]{:S(2)}, u32[]{:S(2)}) %all-to-all-start.3) | async-done | bytes 4194336 | tf_op jit(solution)/shard_map/all_to_all | solution.py:68
  716.0 6.8 copy.150
  722.9 5.5 all_to_all.67
  728.4 7.9 fusion.44
  738.2 5.5 collective-permute-done.2
  747.2 18.2 %fusion.10 = f32[128,4,67,256]{3,0,2,1:T(8,128)} fusion(f32[35,67,256]{2,1,0:T(8,128)S(1)} %pad_maximum_fusion, s32[128,4]{0,1:T(4,128)S(1)} %iota_add_fusion.2), kind=kOutput, calls=%fused_computation.16 | convolution fusion | flops 3688384000 | bytes 37530624 | tf_op jit(solution)/shard_map/bix,xyz->biyz/dot_general | solution.py:156
  765.4 50.9 %fusion = f32[128,4,256,4]{2,3,1,0:T(4,128)S(1)} fusion(f32[128,4,67,256]{3,0,2,1:T(8,128)} %fusion.10, s32[128,4]{1,0:T(8,128)S(1)} %get-tuple-element.37), kind=kOutput, calls=%fused_computation | convolution fusion | flops 421561856 | bytes 37226496 | tf_op jit(solution)/shard_map/bjy,biyz->bijz/dot_general | solution.py:157
  (88 shorter events, 67.6 us)
Async XLA Ops:
  0.0 0.9 copy-start
  0.0 2.3 copy-start.3
  0.9 1.2 copy-start.7
  0.9 3.1 copy-start.9
  0.9 3.1 copy-start.12
  4.1 23.2 %copy-start.5 = (s32[128,4]{1,0:T(8,128)}, s32[128,4]{1,0:T(8,128)S(1)}, u32[]{:S(2)}) copy-start(s32[128,4]{1,0:T(8,128)S(1)} %get-tuple-element.36) | copy-start | bytes 6148
  57.4 3.3 collective-permute-start
  60.8 9.1 %collective-permute-start.1 = (f32[3,64,256]{2,0,1:T(4,128)S(1)}, f32[3,64,256]{2,0,1:T(4,128)S(1)}, u32[]{:S(2)}, u32[]{:S(2)}) collective-permute-start(f32[3,64,256]{2,0,1:T(4,128)S(1)} %slice.103), channel_id=1, source_target_pairs={{0,4},{4,8},{8,12},{12,16},{16,20},{20,24},{24,28},{1,5},{5,9},{9,... | collective-permute-start | bytes 589832 | tf_op jit(solution)/shard_map/ppermute | solution.py:30
  662.8 9.4 %copy-start.11 = (s32[2,512]{1,0:T(2,128)S(1)}, s32[2,512]{1,0:T(2,128)}, u32[]{:S(2)}) copy-start(s32[2,512]{1,0:T(2,128)} %param.18) | copy-start | bytes 12292
  662.8 16.6 %copy-start.4 = (bf16[128,4096]{1,0:T(8,128)(2,1)S(1)}, bf16[128,4096]{1,0:T(8,128)(2,1)}, u32[]{:S(2)}) copy-start(bf16[128,4096]{1,0:T(8,128)(2,1)} %param.16) | copy-start | bytes 3145732
  662.8 53.2 %all-to-all-start.3 = ((f32[32,256,128]{2,0,1:T(8,128)}), f32[32,256,128]{2,0,1:T(8,128)}, u32[]{:S(2)}, u32[]{:S(2)}) async-start(f32[32,256,128]{2,0,1:T(8,128)} %copy.88), calls=%async_computation.3 | async-start | bytes 8388608 | tf_op jit(solution)/shard_map/all_to_all | solution.py:68
  667.9 4.6 collective-permute-start.4
  671.0 5.8 collective-permute-start.5
  676.8 9.8 %collective-permute-start.6 = (bf16[3,1,128,64]{3,2,1,0:T(8,128)(2,1)S(1)}, bf16[3,1,128,64]{3,2,1,0:T(8,128)(2,1)S(1)}, u32[]{:S(2)}, u32[]{:S(2)}) collective-permute-start(bf16[3,1,128,64]{3,2,1,0:T(8,128)(2,1)S(1)} %constant_dynamic-update-slice_fusion), channel_id=1, source_target_pairs={{0,1},{1,2},{2,3},{4,5},{5,6},{6,7},{8,9},{9,10},{10,11},{12,13},{... | collective-permute-start | bytes 147464 | tf_op jit(solution)/shard_map/ppermute | solution.py:21
  678.1 8.5 %collective-permute-start.7 = (bf16[3,1,128,64]{3,2,1,0:T(8,128)(2,1)S(1)}, bf16[3,1,128,64]{3,2,1,0:T(8,128)(2,1)S(1)}, u32[]{:S(2)}, u32[]{:S(2)}) collective-permute-start(bf16[3,1,128,64]{3,2,1,0:T(8,128)(2,1)S(1)} %constant_dynamic-update-slice_fusion), channel_id=1, source_target_pairs={{1,0},{2,1},{3,2},{5,4},{6,5},{7,6},{9,8},{10,9},{11,10},{13,12},{... | collective-permute-start | bytes 147464 | tf_op jit(solution)/shard_map/ppermute | solution.py:22
  728.4 17.1 %copy-start.2 = (bf16[512,4096]{0,1:T(8,128)(2,1)S(1)}, bf16[512,4096]{0,1:T(8,128)(2,1)}, u32[]{:S(2)}) copy-start(bf16[512,4096]{0,1:T(8,128)(2,1)} %copy.130) | copy-start | bytes 12582916
  736.3 7.4 collective-permute-start.2
  743.8 3.2 collective-permute-start.3
  765.4 50.9 %copy-start.6 = (s32[128,4]{1,0:T(8,128)S(1)}, s32[128,4]{1,0:T(8,128)}, u32[]{:S(2)}) copy-start(s32[128,4]{1,0:T(8,128)} %copy-done.5) | copy-start | bytes 6148
  765.4 59.3 %copy-start.1 = (bf16[8192]{0:T(1024)(128)(2,1)S(1)}, bf16[8192]{0:T(1024)(128)(2,1)}, u32[]{:S(2)}) copy-start(bf16[8192]{0:T(1024)(128)(2,1)} %param.12) | copy-start | bytes 49156
  816.3 4.7 copy-start.8
  816.3 4.7 copy-start.10
where the time goes:
time: 834 us; the launch traced here: 825 us
  blocking collectives  430 us (52%)
  matrix products  228 us (27%)
  local copies, waits for them, and re-layouts  80.8 us (10%)
  waiting for transfers between devices  44.7 us (5%)
  starting transfers between devices  21.5 us (3%)
  other arithmetic  18.8 us (2%)
    all_to_all x1, blocking collectives, forward_transform(): moved = lax.all_to_all(spec, 'row', split_axis=1, concat_axis=0, tiled=True)  190 us
    all_to_all x1, blocking collectives, backward_transform(): lax.all_to_all(pieces, 'row', split_axis=0, concat_axis=1, tiled=True)  186 us
    all_to_all x1, blocking collectives, forward_transform(): moved = lax.all_to_all(spec, 'col', split_axis=2, concat_axis=1, tiled=True)  54.3 us
    dot_general x1, matrix products, body(): sampled = jnp.einsum('bjy,biyz->bijz', select_y, sampled, precision=highest)  50.9 us
    dot_general x1, matrix products, backward_transform(): field = jnp.einsum('gfh,hx->xgf', spec, backward, precision=highest)  35.6 us
    dot_general x1, matrix products, body(): extended = jnp.einsum('bix,biyz->xyz', select_x, placed, precision=highest)  30 us
    all_to_all x1, waiting for transfers between devices, backward_transform(): lax.all_to_all(pieces, 'col', split_axis=1, concat_axis=2, tiled=True)  29.3 us
    unnamed x34, local copies, waits for them, and re-layouts  25.8 us
  transfers between devices with their start and end apart: 9, of which 7 were waited for; matrix products, arithmetic and copies ran while one was open for 1% of the time, Pallas kernels for 0%

commit v1 on v0

v1 whole, which is shorter than its diff:
```python
import functools

import jax
import jax.numpy as jnp
import ml_dtypes
import numpy as np
from jax import lax
from jax.experimental import pallas as pl
from jax.experimental.pallas import tpu as pltpu
from jax.sharding import PartitionSpec as P

G = 256
P_SIZE = 512
BLK = 64
PTS = 64
LANES = 128
GROUP = LANES // 4
HALVES = G // LANES
SLABS = 4
PIECE = G // SLABS
SLAB = PIECE + 8
ZC = 16
MB = 1 << 20
NT = (((1,), (1,)), ((), ()))


def cas_table():
    index = np.arange(P_SIZE, dtype=np.int64)
    phase = (index[:, None] * index[None, :] % P_SIZE).astype(np.float64) * (2.0 * np.pi / P_SIZE)
    return ((np.cos(phase) + np.sin(phase)) / np.sqrt(P_SIZE)).astype(ml_dtypes.bfloat16)


CAS = cas_table()


def dot(a, b):
    return jnp.dot(a, b, preferred_element_type=jnp.float32)


def dot_nt(a, b):
    return lax.dot_general(a, b, NT, preferred_element_type=jnp.float32)


def iota(shape, dim):
    return lax.broadcasted_iota(jnp.int32, shape, dim)


def split(value):
    high = value.astype(jnp.bfloat16)
    return high, (value - high.astype(jnp.float32)).astype(jnp.bfloat16)


def lane_gather(table, index):
    return jnp.take_along_axis(table, index, axis=1, mode="promise_in_bounds")


def block_sums(mats, vecs):
    rows = vecs.shape[0]
    pair = jnp.concatenate([vecs, vecs], axis=1)
    total = jnp.zeros((2 * rows, LANES), jnp.float32)
    for t in range(mats.shape[1] // 256):
        high, low = split(mats[:, 256 * t : 256 * t + 256].astype(jnp.float32) * pair)
        owner = iota((256, LANES), 0) // BLK + 4 * t
        table = (owner == iota((256, LANES), 1) % BLK).astype(jnp.bfloat16)
        total = total + dot(jnp.concatenate([high, low], axis=0), table)
    return total[:rows] + total[rows:]


def patch_places(blocks):
    lanes = [
        (iota((blocks, 4 * blocks), 1) == 4 * iota((blocks, 4 * blocks), 0) + i).astype(
            jnp.bfloat16
        )
        for i in range(4)
    ]
    row = iota((16, LANES), 0)
    rows = [
        (iota((16, LANES), 1) % PTS == 16 * i + 4 * (row % 4) + row // 4).astype(jnp.bfloat16)
        for i in range(4)
    ]
    return rows, lanes


def project_kernel(charges, order, project, out, table):
    blocks = order.shape[0]
    table[...] = charges[...].astype(jnp.float32)
    upper = order[...] // LANES
    lower = order[...] % LANES

    def step(u, acc):
        row = jnp.broadcast_to(table[pl.ds(u, 1), :], lower.shape)
        return jnp.where(upper == u, lane_gather(row, lower), acc)

    twice = lax.fori_loop(0, table.shape[0], step, jnp.zeros(lower.shape, jnp.float32), unroll=4)
    out[:blocks] = twice.astype(jnp.bfloat16)
    patch = block_sums(project, twice)
    patch = jnp.where(iota(patch.shape, 1) < PTS, patch, 0.0)
    rows, lanes = patch_places(blocks)
    start = blocks
    for part in split(patch):
        spread = jnp.zeros((16, 4 * blocks), jnp.float32)
        for i in range(4):
            turned = dot_nt(rows[i], part).astype(jnp.bfloat16)
            spread = spread + dot(turned, lanes[i])
        for t in range(blocks // GROUP):
            out[start : start + 16] = spread[:, LANES * t : LANES * t + LANES].astype(jnp.bfloat16)
            start += 16


def inverse_kernel(order, out):
    rows = order.shape[0]

    def step(r, acc):
        here = order[pl.ds(r, 1), :]
        upper = iota((rows, LANES), 0) == here // LANES
        lower = iota((LANES, LANES), 0) == here % LANES
        values = jnp.concatenate(
            [
                jnp.where(upper, r.astype(jnp.float32), 0.0),
                jnp.where(upper, iota((rows, LANES), 1).astype(jnp.float32), 0.0),
            ],
            axis=0,
        )
        return acc + dot_nt(
            values.astype(jnp.bfloat16), lower.astype(jnp.float32).astype(jnp.bfloat16)
        )

    out[...] = lax.fori_loop(
        0, rows, step, jnp.zeros((2 * rows, LANES), jnp.float32), unroll=4
    ).astype(jnp.int32)


def near_kernel(source, near_blocks, target, charges, out, table, picked):
    step = pl.program_id(0)
    pairs = picked.shape[0]
    blocks = out.shape[0]

    @pl.when(step == 0)
    def _():
        for d in range(charges.shape[0]):
            table[d * blocks : (d + 1) * blocks] = charges[d].astype(jnp.float32)
        out[...] = jnp.zeros_like(out)

    def pick(p, carry):
        picked[pl.ds(p, 1), :] = table[pl.ds(source[step * pairs + p], 1), :]
        return carry

    lax.fori_loop(0, pairs, pick, 0, unroll=8)
    terms = block_sums(near_blocks, picked[...])
    owner = (iota((blocks, pairs), 0) == target[...]).astype(jnp.float32).astype(jnp.bfloat16)
    high, low = split(terms)
    out[...] += dot(owner, high) + dot(owner, low)


def lane_spot(first, half, lane):
    return ((lane - (first - half * LANES)) & -4) == 0


def tile_loop(half, rows, cols, groups, body):
    per_slab = cols // SLABS
    low = jnp.maximum(half * (rows // HALVES) - 1, 0)
    high = (half + 1) * (rows // HALVES)
    per_row = per_slab * groups

    def step(n, carry):
        row = low + n // per_row
        left = n % per_row
        devices = [row * cols + s * per_slab + left // groups for s in range(SLABS)]
        body(devices, left % groups)
        return carry

    lax.fori_loop(0, (high - low) * per_row, step, 0)


def scatter_kernel(cols, first, place, patches, table, out, columns, *slabs):
    half = pl.program_id(0)
    chunk = pl.program_id(1)
    devices, held, _ = patches.shape
    groups = held // (GROUP + 32)
    blocks = groups * GROUP
    freqs = table.shape[0]
    lane = iota((8, LANES), 1)
    sub = iota((8, LANES), 0)

    @pl.when((half == 0) & (chunk == 0))
    def _():
        def clear(n, carry):
            for slab in slabs:
                slab[pl.ds(pl.multiple_of(n * SLAB, 8), SLAB), :] = jnp.zeros(
                    (SLAB, LANES), jnp.float32
                )
            return carry

        lax.fori_loop(0, G, clear, 0)

    @pl.when(chunk == 0)
    def _():
        def tile(numbers, t):
            values = []
            for d in numbers:
                at = pl.multiple_of(blocks + 16 * t, 16)
                high = patches[d, pl.ds(at, 16), :].astype(jnp.float32)
                at = pl.multiple_of(blocks + 16 * groups + 16 * t, 16)
                both = high + patches[d, pl.ds(at, 16), :].astype(jnp.float32)
                values.append((both[:8], both[8:]))

            def one(k, carry):
                sums = []
                for s in range(SLABS):
                    b = numbers[s] * blocks + t * GROUP + k
                    spot = lane_spot(first[b], half, lane)
                    spots = (spot & (sub < 4), spot & (sub >= 4))
                    shift = (first[b] - 4 * k) & (LANES - 1)
                    for l in range(4):
                        if l % 2 == 0:
                            moved = pltpu.roll(values[s][l // 2], shift, 1)
                        at = place[b] + (l * SLAB - 4 * (l % 2))
                        new = jnp.where(spots[l % 2], moved, 0.0)
                        sums.append((s, at, slabs[s][pl.ds(at, 8), :] + new))
                for s, at, new in sums:
                    slabs[s][pl.ds(at, 8), :] = new
                return carry

            lax.fori_loop(0, GROUP, one, 0, unroll=4)

        tile_loop(half, devices // cols, cols, groups, tile)

    for z in range(0, ZC, 2):
        pair = []
        for plane in (z, z + 1):
            at = pl.multiple_of((chunk * ZC + plane) * SLAB, 8)
            parts = []
            for s in range(SLABS):
                part = slabs[s][pl.ds(at, PIECE), :]
                if s > 0:
                    over = slabs[s - 1][pl.ds(at + PIECE, 8), :]
                    part = jnp.concatenate([part[:8] + over, part[8:]], axis=0)
                parts.append(part.astype(jnp.bfloat16))
            for slab in slabs:
                slab[pl.ds(at, SLAB), :] = jnp.zeros((SLAB, LANES), jnp.float32)
            pair.append(jnp.concatenate(parts, axis=0))
        lines = dot(table[...], jnp.concatenate(pair, axis=1))
        columns[pl.ds(z, freqs, stride=ZC), :] = lines[:, :LANES]
        columns[pl.ds(z + 1, freqs, stride=ZC), :] = lines[:, LANES:]
    out[...] = columns[...].reshape(freqs, ZC, LANES).astype(jnp.bfloat16)


def spectrum_kernel(lines, weights, third, third_back, first, first_back, out):
    for g in range(lines.shape[0]):
        v = dot(third[...], lines[g]).astype(jnp.bfloat16)
        s = (dot(v, first[...]) * weights[g]).astype(jnp.bfloat16)
        v = dot(s, first_back[...]).astype(jnp.bfloat16)
        out[g] = dot(third_back[...], v).astype(jnp.bfloat16)


def sample_kernel(cols, first, place, lines, table, out, columns, cells):
    half = pl.program_id(0)
    chunk = pl.program_id(1)
    devices, held, _ = out.shape
    groups = held // 16
    blocks = groups * GROUP
    freqs = table.shape[1]
    lane = iota((8, LANES), 1)
    sub = iota((8, LANES), 0)
    columns[...] = lines[...].astype(jnp.float32).reshape(freqs * ZC, LANES)
    for z in range(0, ZC, 2):
        pair = [
            columns[pl.ds(plane, freqs, stride=ZC), :].astype(jnp.bfloat16) for plane in (z, z + 1)
        ]
        field = dot(table[...], jnp.concatenate(pair, axis=1))
        at = pl.multiple_of((chunk * ZC + z) * G, 8)
        cells[pl.ds(at, G), :] = field[:, :LANES]
        cells[pl.ds(at + G, G), :] = field[:, LANES:]

    @pl.when((half == 0) & (chunk == 0))
    def _():
        out[...] = jnp.zeros_like(out)

    @pl.when(chunk == pl.num_programs(1) - 1)
    def _():
        def tile(numbers, t):
            def one(k, sums):
                sums = list(sums)
                for s in range(SLABS):
                    b = numbers[s] * blocks + t * GROUP + k
                    spot = lane_spot(first[b], half, lane)
                    spots = (spot & (sub < 4), spot & (sub >= 4))
                    shift = (4 * k - first[b]) & (LANES - 1)
                    for v in range(2):
                        even = cells[pl.ds(place[b] + 2 * v * G, 8), :]
                        odd = cells[pl.ds(place[b] + ((2 * v + 1) * G - 4), 8), :]
                        here = jnp.where(spots[0], even, jnp.where(spots[1], odd, 0.0))
                        sums[2 * s + v] = sums[2 * s + v] + pltpu.roll(here, shift, 1)
                return tuple(sums)

            zero = jnp.zeros((8, LANES), jnp.float32)
            sums = lax.fori_loop(0, GROUP, one, (zero,) * (2 * SLABS), unroll=4)
            at = pl.multiple_of(16 * t, 16)
            for s in range(SLABS):
                out[numbers[s], pl.ds(at, 16), :] += jnp.concatenate(
                    [sums[2 * s], sums[2 * s + 1]], axis=0
                )

        tile_loop(half, devices // cols, cols, groups, tile)


def finish_kernel(values, interpolate, near, inverse, out, total):
    blocks = near.shape[0]
    groups = values.shape[0] // 16
    rows, lanes = patch_places(blocks)
    spread = jnp.concatenate([values[16 * t : 16 * t + 16] for t in range(groups)], axis=1)
    patch = jnp.zeros((blocks, LANES), jnp.float32)
    for part in split(spread):
        for i in range(4):
            turned = dot_nt(lanes[i], part).astype(jnp.bfloat16)
            patch = patch + dot(turned, rows[i])
    total[...] = block_sums(interpolate, patch) + near[...]
    count = out.shape[0]
    even = total[pl.ds(0, count, stride=2), :]
    odd = total[pl.ds(1, count, stride=2), :]
    total[:count] = jnp.where(iota(even.shape, 1) < BLK, even, odd)
    upper = inverse[:count]
    lower = inverse[count:]

    def step(u, acc):
        row = jnp.broadcast_to(total[pl.ds(u, 1), :], lower.shape)
        return jnp.where(upper == u, lane_gather(row, lower), acc)

    out[...] = lax.fori_loop(0, count, step, jnp.zeros(out.shape, jnp.float32), unroll=4)


def struct(shape, dtype):
    return jax.ShapeDtypeStruct(shape, dtype)


def whole(shape):
    return pl.BlockSpec(shape, lambda *_: (0,) * len(shape))


def params(mib):
    return pltpu.CompilerParams(vmem_limit_bytes=mib * MB)


def body(
    charges,
    panel_order,
    patch_anchor,
    project,
    interpolate,
    kernel_spectrum,
    near_pairs,
    near_blocks,
):
    axes = ("row", "col")
    rows = lax.axis_size("row")
    cols = lax.axis_size("col")
    devices = rows * cols
    row_at = lax.axis_index("row")
    col_at = lax.axis_index("col")
    blocks = project.shape[0]
    groups = blocks // GROUP
    panels = charges.shape[0]
    strips = panels // LANES
    gs, fs, _ = kernel_spectrum.shape

    anchors = lax.all_gather(patch_anchor, axes)
    order = panel_order.reshape(blocks, BLK)
    sent = pl.pallas_call(
        project_kernel,
        out_shape=struct((blocks + 32 * groups, LANES), jnp.bfloat16),
        scratch_shapes=[pltpu.VMEM((strips, LANES), jnp.float32)],
        compiler_params=params(32),
        name="project",
    )(charges.reshape(strips, LANES), jnp.concatenate([order, order], axis=1), project)
    gathered = lax.all_gather(sent, axes)
    inverse = pl.pallas_call(
        inverse_kernel,
        out_shape=struct((2 * strips, LANES), jnp.int32),
        compiler_params=params(32),
        name="inverse",
    )(panel_order.reshape(strips, LANES))

    first = anchors[:, 0].reshape(devices * blocks)
    piece = (jnp.arange(devices, dtype=jnp.int32) % cols * SLABS // cols * PIECE)[:, None]
    slab_place = (anchors[:, 2] * SLAB + anchors[:, 1] - piece).reshape(devices * blocks)
    cell_place = (anchors[:, 2] * G + anchors[:, 1]).reshape(devices * blocks)

    table = jnp.asarray(CAS)
    second = lax.dynamic_slice_in_dim(table[:, :G], row_at * gs, gs, axis=0)
    third = lax.dynamic_slice_in_dim(table[:, :G], col_at * fs, fs, axis=0)
    chunks = G // ZC
    smem = pl.BlockSpec(memory_space=pltpu.SMEM)
    line_block = pl.BlockSpec((gs, ZC, LANES), lambda h, z: (0, z, h))
    lines = pl.pallas_call(
        functools.partial(scatter_kernel, cols),
        grid=(HALVES, chunks),
        in_specs=[smem, smem, whole(gathered.shape), whole(second.shape)],
        out_specs=line_block,
        out_shape=struct((gs, G, G), jnp.bfloat16),
        scratch_shapes=[pltpu.VMEM((gs * ZC, LANES), jnp.float32)]
        + [pltpu.VMEM((G * SLAB, LANES), jnp.float32)] * SLABS,
        compiler_params=params(56),
        name="scatter",
    )(first, slab_place, gathered, second)

    batch = 4
    part = lambda shape: pl.BlockSpec((batch,) + shape, lambda n: (n, 0, 0))
    lines = pl.pallas_call(
        spectrum_kernel,
        grid=(gs // batch,),
        in_specs=[
            part((G, G)),
            part((fs, P_SIZE)),
            whole((fs, G)),
            whole((G, fs)),
            whole((G, P_SIZE)),
            whole((P_SIZE, G)),
        ],
        out_specs=part((G, G)),
        out_shape=struct((gs, G, G), jnp.bfloat16),
        compiler_params=params(48),
        name="spectrum",
    )(lines, kernel_spectrum, third, third.T, table[:G], table[:, :G])

    values = pl.pallas_call(
        functools.partial(sample_kernel, cols),
        grid=(HALVES, chunks),
        in_specs=[smem, smem, line_block, whole((G, gs))],
        out_specs=whole((devices, 16 * groups, LANES)),
        out_shape=struct((devices, 16 * groups, LANES), jnp.float32),
        scratch_shapes=[
            pltpu.VMEM((gs * ZC, LANES), jnp.float32),
            pltpu.VMEM((G * G + 8, LANES), jnp.float32),
        ],
        compiler_params=params(56),
        name="sample",
    )(first, cell_place, lines, second.T)
    values = lax.psum_scatter(
        values.reshape(devices * 16 * groups, LANES), axes, scatter_dimension=0, tiled=True
    )

    pairs = near_blocks.shape[0]
    target = near_pairs[0] - (row_at * cols + col_at) * blocks
    near = pl.pallas_call(
        near_kernel,
        grid=(pairs // blocks,),
        in_specs=[
            smem,
            pl.BlockSpec((blocks, BLK * BLK), lambda n: (n, 0)),
            pl.BlockSpec((1, blocks), lambda n: (0, n)),
            whole((devices, blocks, LANES)),
        ],
        out_specs=whole((blocks, LANES)),
        out_shape=struct((blocks, LANES), jnp.float32),
        scratch_shapes=[
            pltpu.VMEM((devices * blocks, LANES), jnp.float32),
            pltpu.VMEM((blocks, LANES), jnp.float32),
        ],
        compiler_params=params(48),
        name="near",
    )(near_pairs[1], near_blocks, target.reshape(1, pairs), gathered)

    result = pl.pallas_call(
        finish_kernel,
        out_shape=struct((strips, LANES), jnp.float32),
        scratch_shapes=[pltpu.VMEM((blocks, LANES), jnp.float32)],
        compiler_params=params(32),
        name="finish",
    )(values, interpolate, near, inverse)
    return result.reshape(panels)


def solution(mesh):
    placed = (
        P(("row", "col")),
        P(("row", "col")),
        P(None, ("row", "col")),
        P(("row", "col"), None),
        P(("row", "col"), None),
        P("row", "col", None),
        P(None, ("row", "col")),
        P(("row", "col"), None),
    )
    return jax.shard_map(
        body, mesh=mesh, in_specs=placed, out_specs=P(("row", "col")), check_vma=False
    )
```

time: 834 us -> 368 us (0.44)
  blocking collectives: 430 us -> 43.7 us
  matrix products: 228 us -> 0 us
  Pallas kernels: 0 us -> 166 us
  waiting for transfers between devices: 44.7 us -> 135 us
  local copies, waits for them, and re-layouts: 80.8 us -> 6.79 us
  starting transfers between devices: 21.5 us -> 0.04 us
  other arithmetic: 18.8 us -> 1.42 us
  between operations: 0.88 us -> 13.5 us
    all_to_all x3 -> x0, blocking collectives: 430 us -> none  [the longest x1 190 us: forward_transform(): moved = lax.all_to_all(spec, 'row', split_axis=1, concat_axis=0, tiled=True)]
    dot_general x16 -> x0, matrix products: 228 us -> none  [the longest x1 50.9 us: body(): sampled = jnp.einsum('bjy,biyz->bijz', select_y, sampled, precision=highest)]
    pallas_call x0 -> x7, Pallas kernels: none -> 166 us  [the longest x1 58 us: body(): pl.pallas_call(functools.partial(sample_kernel, cols), grid=(HALVES, chun...]
    reduce_scatter x0 -> x1, waiting for transfers between devices: none -> 124 us  [body(): lax.psum_scatter(values.reshape(devices * 16 * groups, LANES), axes, scat...]
    all_gather x0 -> x1, blocking collectives: none -> 43.7 us  [body(): anchors = lax.all_gather(patch_anchor, axes)]
    all_to_all x1 -> x0, waiting for transfers between devices: 29.3 us -> none  [backward_transform(): lax.all_to_all(pieces, 'col', split_axis=1, concat_axis=2, tiled=True)]
    all_to_all x6 -> x0, local copies, waits for them, and re-layouts: 26.3 us -> none  [the longest x2 12.3 us: backward_transform(): lax.all_to_all(pieces, 'col', split_axis=1, concat_axis=2, tiled=True)]
    unnamed x34 -> x18, local copies, waits for them, and re-layouts: 25.8 us -> 2.72 us
  transfers between devices with their start and end apart: 9 -> 2, of which waited for: 7 -> 2; matrix products, arithmetic and copies ran while one was open for 1% -> 1% of each run, Pallas kernels for 0% -> 3%
where the time goes in v1:
time: 368 us; the launch traced here: 367 us
  Pallas kernels  166 us (45%)
  waiting for transfers between devices  135 us (37%)
  blocking collectives  43.7 us (12%)
  between operations  13.5 us (4%)
  local copies, waits for them, and re-layouts  6.79 us (2%)
    reduce_scatter x1, waiting for transfers between devices, body(): lax.psum_scatter(values.reshape(devices * 16 * groups, LANES), axes, scat...  124 us
    pallas_call x1, Pallas kernels, body(): pl.pallas_call(functools.partial(sample_kernel, cols), grid=(HALVES, chun...  58 us
    pallas_call x1, Pallas kernels, body(): pl.pallas_call(functools.partial(scatter_kernel, cols), grid=(HALVES, chu...  55.8 us
    all_gather x1, blocking collectives, body(): anchors = lax.all_gather(patch_anchor, axes)  43.7 us
    pallas_call x1, Pallas kernels, body(): pl.pallas_call(spectrum_kernel, grid=(gs // batch,), in_specs=[part((G, G...  31.3 us
    all_gather x1, waiting for transfers between devices, body(): gathered = lax.all_gather(sent, axes)  11 us
  transfers between devices with their start and end apart: 2, of which 2 were waited for; matrix products, arithmetic and copies ran while one was open for 1% of the time, Pallas kernels for 3%

profile of v1, /device:TPU:0, one launch (start us, length us, event | category | flops | bytes accessed | tf_op | source)
XLA Modules:
  0.0 366.7 jit_solution(15892588755737766700)
XLA Ops:
  6.5 0.8 reshape.56
  7.4 0.1 pad_add_fusion.order
  7.5 1.2 copy-done.1
  8.7 0.7 copy-done.7
  9.4 6.4 %project.2 = bf16[256,128]{1,0:T(8,128)(2,1)} custom-call(bf16[64,128]{1,0:T(8,128)(2,1)S(1)} %bitcast.19, s32[128,128]{1,0:T(8,128)S(1)} %pad_add_fusion.order, bf16[128,4096]{1,0:T(8,128)(2,1)S(1)} %copy-done.1), custom_call_target="tpu_custom_call" | custom-call | tf_op jit(solution)/shard_map/project/pallas_call | solution.py:368
  15.8 0.0 all-gather.5.cloned.1.call-update
  15.9 0.0 reduce-scatter.2.cloned.1.call-start
  15.9 0.9 dynamic-slice_bitcast_fusion
  16.8 0.1 copy.17.third
  16.9 1.6 dynamic-slice_bitcast_fusion.1
  18.5 0.7 copy.16.table
  19.2 43.7 %all-gather.2 = s32[32,3,128]{2,1,0:T(4,128)S(1)} all-gather(s32[1,3,128]{2,1,0:T(4,128)} %bitcast.26), channel_id=2, replica_groups=mesh['row'=8,'col'=4] {'row','col'}, dimensions={0}, use_global_device_ids=true | all-gather | bytes 50688 | tf_op jit(solution)/shard_map/all_gather | solution.py:366
  62.9 0.6 multiply_add_fusion
  63.6 0.7 bitcast_subtract_fusion.place
  64.2 11.0 %all-gather.5.cloned.1.call-done = bf16[8192,128]{1,0:T(8,128)(2,1)} async-done(((bf16[256,128]{1,0:T(8,128)(2,1)}), bf16[8192,128]{1,0:T(8,128)(2,1)}) %all-gather.5.cloned.1.call-update) | async-done | bytes 2097168 | tf_op jit(solution)/shard_map/all_gather | solution.py:375
  75.2 55.8 %scatter.1.lines = bf16[64,256,256]{2,1,0:T(8,128)(2,1)} custom-call(s32[4096]{0:T(1024)} %bitcast.22, s32[4096]{0:T(1024)} %bitcast_subtract_fusion.place, bf16[32,256,128]{2,1,0:T(8,128)(2,1)} %bitcast.16, bf16[64,256]{1,0:T(8,128)(2,1)} %copy.16.table), custom_call_target="tpu_custom_call" | custom-call | tf_op jit(solution)/shard_map/scatter/pallas_call | solution.py:394
  131.0 31.3 %spectrum.1.lines = bf16[64,256,256]{2,1,0:T(8,128)(2,1)} custom-call(bf16[64,256,256]{2,1,0:T(8,128)(2,1)} %scatter.1.lines, f32[64,128,512]{2,1,0:T(8,128)} %weights.1, bf16[128,256]{1,0:T(8,128)(2,1)S(1)} %copy.17.third, bf16[256,128]{1,0:T(8,128)(2,1)S(1)} %get-tuple-element.7.third_back, bf16[256,512]{1,0:T(8,128)(2,1)S(1)} %copy-done.4, ...), custom_call_target="tpu_custom_call" | custom-call | tf_op jit(solution)/shard_map/spectrum/pallas_call | solution.py:408
  162.4 58.0 %sample.1 = f32[32,64,128]{2,1,0:T(8,128)} custom-call(s32[4096]{0:T(1024)} %bitcast.23, s32[4096]{0:T(1024)} %bitcast.24, bf16[64,256,256]{2,1,0:T(8,128)(2,1)} %spectrum.1.lines, bf16[256,64]{1,0:T(8,128)(2,1)} %get-tuple-element.5.table), custom_call_target="tpu_custom_call" | custom-call | tf_op jit(solution)/shard_map/sample/pallas_call | solution.py:425
  220.4 0.0 reduce-scatter.2.cloned.1.call-update
  220.4 3.8 %inverse.1 = s32[128,128]{1,0:T(8,128)S(1)} custom-call(s32[64,128]{1,0:T(8,128)S(1)} %bitcast.18), custom_call_target="tpu_custom_call" | custom-call | tf_op jit(solution)/shard_map/inverse/pallas_call | solution.py:376
  224.2 6.2 %near.1 = f32[128,128]{1,0:T(8,128)S(1)} custom-call(s32[512]{0:T(512)S(1)} %bitcast.20, bf16[512,4096]{1,0:T(8,128)(2,1)} %near_blocks.1, s32[1,512]{1,0:T(1,128)S(1)} %get-tuple-element.12.target, bf16[32,256,128]{2,1,0:T(8,128)(2,1)S(1)} %bitcast.17), custom_call_target="tpu_custom_call" | custom-call | tf_op jit(solution)/shard_map/near/pallas_call | solution.py:444
  230.4 123.9 %reduce-scatter.2.cloned.1.call-done.values = f32[64,128]{1,0:T(8,128)} async-done(((f32[2048,128]{1,0:T(8,128)}), f32[64,128]{1,0:T(8,128)}) %reduce-scatter.2.cloned.1.call-update) | async-done | bytes 32784 | tf_op jit(solution)/shard_map/reduce_scatter | solution.py:438
  354.3 0.8 copy-done.6
  355.1 4.8 %finish.1 = f32[64,128]{1,0:T(8,128)} custom-call(f32[64,128]{1,0:T(8,128)S(1)} %copy-done.6, bf16[128,4096]{1,0:T(8,128)(2,1)S(1)} %copy-done.2, f32[128,128]{1,0:T(8,128)S(1)} %near.1, s32[128,128]{1,0:T(8,128)S(1)} %inverse.1), custom_call_target="tpu_custom_call" | custom-call | tf_op jit(solution)/shard_map/finish/pallas_call | solution.py:463
  (18 shorter events, 0.1 us)
Async XLA Ops:
  6.5 68.7 %all-gather.5.cloned.1.call-start = ((), (), s32[]{:S(2)}) async-start(), calls=%async_computation.2 | async-start | bytes 2162688 | tf_op jit(solution)/shard_map/all_gather | solution.py:375
  7.5 1.2 copy-start.1
  8.7 0.7 copy-start.7
  9.4 121.6 %copy-start.3 = (bf16[512,256]{1,0:T(8,128)(2,1)S(1)}, bf16[512,256]{1,0:T(8,128)(2,1)}, u32[]{:S(2)}) copy-start(bf16[512,256]{1,0:T(8,128)(2,1)} %constant.56.first_back) | copy-start | bytes 786436
  9.4 121.6 %copy-start.4 = (bf16[256,512]{1,0:T(8,128)(2,1)S(1)}, bf16[256,512]{1,0:T(8,128)(2,1)}, u32[]{:S(2)}) copy-start(bf16[256,512]{1,0:T(8,128)(2,1)} %constant.55.first) | copy-start | bytes 786436
  15.9 338.4 %reduce-scatter.2.cloned.1.call-start = ((), (), s32[]{:S(2)}) async-start(), calls=%async_computation.1 | async-start | bytes 1081344 | tf_op jit(solution)/shard_map/reduce_scatter | solution.py:438
  162.4 58.0 %copy-start.5 = (s32[8192]{0:T(1024)S(1)}, s32[8192]{0:T(1024)}, u32[]{:S(2)}) copy-start(s32[8192]{0:T(1024)} %param.10) | copy-start | bytes 98308
  162.4 61.8 %copy-start.8 = (s32[2,512]{1,0:T(2,128)S(1)}, s32[2,512]{1,0:T(2,128)}, u32[]{:S(2)}) copy-start(s32[2,512]{1,0:T(2,128)} %param.15) | copy-start | bytes 12292
  162.4 61.9 %copy-start = (bf16[8192,128]{1,0:T(8,128)(2,1)S(1)}, bf16[8192,128]{1,0:T(8,128)(2,1)}, u32[]{:S(2)}) copy-start(bf16[8192,128]{1,0:T(8,128)(2,1)} %all-gather.5.cloned.1.call-done) | copy-start | bytes 6291460
  162.4 191.9 %copy-start.2 = (bf16[128,4096]{1,0:T(8,128)(2,1)S(1)}, bf16[128,4096]{1,0:T(8,128)(2,1)}, u32[]{:S(2)}) copy-start(bf16[128,4096]{1,0:T(8,128)(2,1)} %interpolate.1) | copy-start | bytes 3145732
  354.3 0.8 copy-start.6
Sparse Core Ops, SparseCore 0:
  16.0 59.1 all-gather.4
  220.5 133.7 reduce-scatter.1

commit v2 on v1

v2 whole, which is shorter than its diff:
```python
import functools

import jax
import jax.numpy as jnp
import ml_dtypes
import numpy as np
from jax import lax
from jax.experimental import pallas as pl
from jax.experimental.pallas import tpu as pltpu
from jax.sharding import PartitionSpec as P

G = 256
P_SIZE = 512
BLK = 64
PTS = 64
LANES = 128
GROUP = LANES // 4
HALVES = G // LANES
SLABS = 4
PIECE = G // SLABS
SLAB = PIECE + 8
ZC = 16
MB = 1 << 20
NT = (((1,), (1,)), ((), ()))


def cas_table():
    index = np.arange(P_SIZE, dtype=np.int64)
    phase = (index[:, None] * index[None, :] % P_SIZE).astype(np.float64) * (2.0 * np.pi / P_SIZE)
    return ((np.cos(phase) + np.sin(phase)) / np.sqrt(P_SIZE)).astype(ml_dtypes.bfloat16)


CAS = cas_table()


def dot(a, b):
    return jnp.dot(a, b, preferred_element_type=jnp.float32)


def dot_nt(a, b):
    return lax.dot_general(a, b, NT, preferred_element_type=jnp.float32)


def iota(shape, dim):
    return lax.broadcasted_iota(jnp.int32, shape, dim)


def split(value):
    high = value.astype(jnp.bfloat16)
    return high, (value - high.astype(jnp.float32)).astype(jnp.bfloat16)


def lane_gather(table, index):
    return jnp.take_along_axis(table, index, axis=1, mode="promise_in_bounds")


def block_sums(mats, vecs):
    rows = vecs.shape[0]
    pair = jnp.concatenate([vecs, vecs], axis=1)
    total = jnp.zeros((2 * rows, LANES), jnp.float32)
    for t in range(mats.shape[1] // 256):
        high, low = split(mats[:, 256 * t : 256 * t + 256].astype(jnp.float32) * pair)
        owner = iota((256, LANES), 0) // BLK + 4 * t
        table = (owner == iota((256, LANES), 1) % BLK).astype(jnp.bfloat16)
        total = total + dot(jnp.concatenate([high, low], axis=0), table)
    return total[:rows] + total[rows:]


def patch_places(blocks):
    lanes = [
        (iota((blocks, 4 * blocks), 1) == 4 * iota((blocks, 4 * blocks), 0) + i).astype(
            jnp.bfloat16
        )
        for i in range(4)
    ]
    row = iota((16, LANES), 0)
    rows = [
        (iota((16, LANES), 1) % PTS == 16 * i + 4 * (row % 4) + row // 4).astype(jnp.bfloat16)
        for i in range(4)
    ]
    return rows, lanes


def project_kernel(charges, order, project, anchors, charge_out, patch_out, table):
    blocks = order.shape[0]
    groups = blocks // GROUP
    table[...] = charges[...].astype(jnp.float32)
    upper = order[...] // LANES
    lower = order[...] % LANES

    def step(u, acc):
        row = jnp.broadcast_to(table[pl.ds(u, 1), :], lower.shape)
        return jnp.where(upper == u, lane_gather(row, lower), acc)

    twice = lax.fori_loop(0, table.shape[0], step, jnp.zeros(lower.shape, jnp.float32), unroll=4)
    charge_out[...] = twice.astype(jnp.bfloat16)
    patch = block_sums(project, twice)
    patch = jnp.where(iota(patch.shape, 1) < PTS, patch, 0.0).astype(jnp.bfloat16)
    rows, lanes = patch_places(blocks)
    corner = anchors[...].astype(jnp.float32)
    spread = jnp.zeros((16, 4 * blocks), jnp.float32)
    cells = (iota((8, 4 * blocks), 1) % 4).astype(jnp.float32)
    start = jnp.broadcast_to(corner[:1], (8, blocks)).astype(jnp.bfloat16)
    for i in range(4):
        spread = spread + dot(dot_nt(rows[i], patch).astype(jnp.bfloat16), lanes[i])
        cells = cells + dot(start, lanes[i])
    tiles = [slice(LANES * t, LANES * t + LANES) for t in range(groups)]
    for t in range(groups):
        patch_out[16 * t : 16 * t + 16] = spread[:, tiles[t]].astype(jnp.bfloat16)
    extra = [cells[:1, tile] for tile in tiles] + [corner]
    extra.append(jnp.zeros((16 - groups - corner.shape[0], LANES), jnp.float32))
    patch_out[16 * groups :] = jnp.concatenate(extra, axis=0).astype(jnp.bfloat16)


def inverse_kernel(order, out):
    rows = order.shape[0]

    def step(r, acc):
        here = order[pl.ds(r, 1), :]
        upper = iota((rows, LANES), 0) == here // LANES
        lower = iota((LANES, LANES), 0) == here % LANES
        values = jnp.concatenate(
            [
                jnp.where(upper, r.astype(jnp.float32), 0.0),
                jnp.where(upper, iota((rows, LANES), 1).astype(jnp.float32), 0.0),
            ],
            axis=0,
        )
        return acc + dot_nt(
            values.astype(jnp.bfloat16), lower.astype(jnp.float32).astype(jnp.bfloat16)
        )

    out[...] = lax.fori_loop(
        0, rows, step, jnp.zeros((2 * rows, LANES), jnp.float32), unroll=4
    ).astype(jnp.int32)


def near_kernel(source, near_blocks, target, charges, out, table, picked):
    step = pl.program_id(0)
    pairs = picked.shape[0]
    blocks = out.shape[0]

    @pl.when(step == 0)
    def _():
        for d in range(charges.shape[0]):
            table[d * blocks : (d + 1) * blocks] = charges[d].astype(jnp.float32)
        out[...] = jnp.zeros_like(out)

    def pick(p, carry):
        picked[pl.ds(p, 1), :] = table[pl.ds(source[step * pairs + p], 1), :]
        return carry

    lax.fori_loop(0, pairs, pick, 0, unroll=8)
    terms = block_sums(near_blocks, picked[...])
    owner = (iota((blocks, pairs), 0) == target[...]).astype(jnp.float32).astype(jnp.bfloat16)
    high, low = split(terms)
    out[...] += dot(owner, high) + dot(owner, low)


def tile_loop(half, rows, cols, groups, body):
    per_slab = cols // SLABS
    low = jnp.maximum(half * (rows // HALVES) - 1, 0)
    high = (half + 1) * (rows // HALVES)
    per_row = per_slab * groups

    def step(n, carry):
        row = low + n // per_row
        left = n % per_row
        devices = [row * cols + s * per_slab + left // groups for s in range(SLABS)]
        body(devices, left % groups)
        return carry

    lax.fori_loop(0, (high - low) * per_row, step, 0)


def tile_cells(patches, d, t, groups):
    extra = patches[d, 16 * groups :, :].astype(jnp.float32)
    picked = jnp.where(iota(extra.shape, 0) == t, extra, 0.0)
    return jnp.broadcast_to(jnp.sum(picked, axis=0, keepdims=True), (8, LANES))


def scatter_kernel(cols, place, shift, second, third, patches, table, out, columns, *slabs):
    half = place[0]
    chunk = pl.program_id(0)
    devices, held, _ = patches.shape
    groups = (held - 16) // 16
    blocks = groups * GROUP
    freqs = table.shape[0]
    quad = iota((8, LANES), 1) // 4

    @pl.when(chunk == 0)
    def _():
        def clear(n, carry):
            for slab in slabs:
                slab[n] = jnp.zeros((SLAB, LANES), jnp.float32)
            return carry

        lax.fori_loop(0, G, clear, 0)

        def tile(numbers, t):
            values = []
            for d in numbers:
                both = patches[d, pl.ds(pl.multiple_of(16 * t, 16), 16), :].astype(jnp.float32)
                cells = tile_cells(patches, d, t, groups) - (half * LANES).astype(jnp.float32)
                inside = (cells >= 0.0) & (cells < LANES) & (iota((8, LANES), 0) < 4)
                planes = [jnp.concatenate([both[4 * l : 4 * l + 4]] * 2, axis=0) for l in range(4)]
                values.append([jnp.where(inside, plane, 0.0) for plane in planes])

            def one(k, carry):
                spot = quad == k
                sums = []
                for s in range(SLABS):
                    b = numbers[s] * blocks + t * GROUP + k
                    amount = shift[b]
                    at = (pl.ds(third[b], 4), pl.ds(second[b], 8))
                    new = [
                        pltpu.roll(jnp.where(spot, plane, 0.0), amount, 1) for plane in values[s]
                    ]
                    sums.append((at, slabs[s][at[0], at[1], :] + jnp.stack(new)))
                for s, (at, new) in enumerate(sums):
                    slabs[s][at[0], at[1], :] = new
                return carry

            lax.fori_loop(0, GROUP, one, 0, unroll=4)

        tile_loop(half, devices // cols, cols, groups, tile)

    for z in range(0, ZC, 2):
        pair = []
        for plane in (z, z + 1):
            at = chunk * ZC + plane
            parts = []
            for s in range(SLABS):
                part = slabs[s][at, :PIECE, :]
                if s > 0:
                    over = slabs[s - 1][at, PIECE:, :]
                    part = jnp.concatenate([part[:8] + over, part[8:]], axis=0)
                parts.append(part.astype(jnp.bfloat16))
            pair.append(jnp.concatenate(parts, axis=0))
        lines = dot(table[...], jnp.concatenate(pair, axis=1))
        columns[pl.ds(z, freqs, stride=ZC), :] = lines[:, :LANES]
        columns[pl.ds(z + 1, freqs, stride=ZC), :] = lines[:, LANES:]
    out[...] = columns[...].reshape(freqs, ZC, LANES).astype(jnp.bfloat16)


def spectrum_kernel(
    own, other, weights, third, third_back, first, first_back, own_out, other_out, held
):
    count, freqs, _ = weights.shape
    for g in range(count):
        line = jnp.concatenate([own[g], other[g]], axis=1)
        held[g * freqs : (g + 1) * freqs] = dot(third[...], line).astype(jnp.bfloat16)
    s = dot(held[...], first[...]) * weights[...].reshape(count * freqs, P_SIZE)
    held[...] = dot(s.astype(jnp.bfloat16), first_back[...]).astype(jnp.bfloat16)
    for g in range(count):
        line = dot(third_back[...], held[g * freqs : (g + 1) * freqs]).astype(jnp.bfloat16)
        own_out[g] = line[:, :LANES]
        other_out[g] = line[:, LANES:]


def sample_kernel(
    cols, place, shift, second, third, patches, own, other, table, out, columns, cells
):
    half = place[0]
    chunk = pl.program_id(0)
    devices, held, _ = out.shape
    groups = held // 16
    blocks = groups * GROUP
    freqs = table.shape[1]
    quad = iota((8, LANES), 1) // 4
    both = own[...].astype(jnp.float32) + other[...].astype(jnp.float32)
    columns[...] = both.reshape(freqs * ZC, LANES)
    for z in range(0, ZC, 2):
        pair = [
            columns[pl.ds(plane, freqs, stride=ZC), :].astype(jnp.bfloat16) for plane in (z, z + 1)
        ]
        field = dot(table[...], jnp.concatenate(pair, axis=1))
        cells[chunk * ZC + z, :G, :] = field[:, :LANES]
        cells[chunk * ZC + z + 1, :G, :] = field[:, LANES:]

    @pl.when(chunk == pl.num_programs(0) - 1)
    def _():
        out[...] = jnp.zeros_like(out)

        def tile(numbers, t):
            def one(k, sums):
                spot = quad == k
                sums = list(sums)
                for s in range(SLABS):
                    b = numbers[s] * blocks + t * GROUP + k
                    amount = shift[b]
                    here = cells[pl.ds(third[b], 4), pl.ds(second[b], 8), :]
                    for l in range(4):
                        moved = pltpu.roll(here[l], amount, 1)
                        sums[4 * s + l] = jnp.where(spot, moved, sums[4 * s + l])
                return tuple(sums)

            zero = jnp.zeros((8, LANES), jnp.float32)
            sums = lax.fori_loop(0, GROUP, one, (zero,) * (4 * SLABS), unroll=4)
            at = pl.multiple_of(16 * t, 16)
            for s in range(SLABS):
                first = tile_cells(patches, numbers[s], t, groups)
                first = first - (half * LANES).astype(jnp.float32)
                inside = (first >= 0.0) & (first < LANES)
                planes = [jnp.where(inside, sums[4 * s + l], 0.0)[:4] for l in range(4)]
                out[numbers[s], pl.ds(at, 16), :] = jnp.concatenate(planes, axis=0).astype(
                    jnp.bfloat16
                )

        tile_loop(half, devices // cols, cols, groups, tile)


def finish_kernel(values, interpolate, near, inverse, out, total):
    blocks = near.shape[0]
    groups = values.shape[1] // 16
    rows, lanes = patch_places(blocks)
    summed = values[0].astype(jnp.float32)
    for d in range(1, values.shape[0]):
        summed = summed + values[d].astype(jnp.float32)
    spread = jnp.concatenate([summed[16 * t : 16 * t + 16] for t in range(groups)], axis=1)
    patch = jnp.zeros((blocks, LANES), jnp.float32)
    for part in split(spread):
        for i in range(4):
            turned = dot_nt(lanes[i], part).astype(jnp.bfloat16)
            patch = patch + dot(turned, rows[i])
    total[...] = block_sums(interpolate, patch) + near[...]
    count = out.shape[0]
    even = total[pl.ds(0, count, stride=2), :]
    odd = total[pl.ds(1, count, stride=2), :]
    total[:count] = jnp.where(iota(even.shape, 1) < BLK, even, odd)
    upper = inverse[:count]
    lower = inverse[count:]

    def step(u, acc):
        row = jnp.broadcast_to(total[pl.ds(u, 1), :], lower.shape)
        return jnp.where(upper == u, lane_gather(row, lower), acc)

    out[...] = lax.fori_loop(0, count, step, jnp.zeros(out.shape, jnp.float32), unroll=4)


def struct(shape, dtype):
    return jax.ShapeDtypeStruct(shape, dtype)


def whole(shape):
    return pl.BlockSpec(shape, lambda *_: (0,) * len(shape))


def params(mib):
    return pltpu.CompilerParams(vmem_limit_bytes=mib * MB)


def neighbourhood(array):
    array = array[None, None]
    for axis, dim in (("row", 0), ("col", 1)):
        count = lax.axis_size(axis)
        up = [(i, i + 1) for i in range(count - 1)]
        down = [(j, i) for i, j in up]
        before = lax.ppermute(array, axis, up)
        after = lax.ppermute(array, axis, down)
        array = jnp.concatenate([before, array, after], axis=dim)
    return array


def body(
    charges,
    panel_order,
    patch_anchor,
    project,
    interpolate,
    kernel_spectrum,
    near_pairs,
    near_blocks,
):
    axes = ("row", "col")
    rows = lax.axis_size("row")
    cols = lax.axis_size("col")
    devices = rows * cols
    row_at = lax.axis_index("row")
    col_at = lax.axis_index("col")
    half = col_at % HALVES
    mates = [(c, c ^ 1) for c in range(cols)]
    blocks = project.shape[0]
    groups = blocks // GROUP
    panels = charges.shape[0]
    strips = panels // LANES
    gs, fs, _ = kernel_spectrum.shape
    held = 16 * groups + 16

    order = panel_order.reshape(blocks, BLK)
    block_charges, sent = pl.pallas_call(
        project_kernel,
        out_shape=(
            struct((blocks, LANES), jnp.bfloat16),
            struct((held, LANES), jnp.bfloat16),
        ),
        scratch_shapes=[pltpu.VMEM((strips, LANES), jnp.float32)],
        compiler_params=params(32),
        name="project",
    )(
        charges.reshape(strips, LANES),
        jnp.concatenate([order, order], axis=1),
        project,
        patch_anchor,
    )
    copies = jnp.broadcast_to(sent[None], (devices, held, LANES))
    gathered = lax.all_to_all(copies, axes, split_axis=0, concat_axis=0, tiled=True)
    inverse = pl.pallas_call(
        inverse_kernel,
        out_shape=struct((2 * strips, LANES), jnp.int32),
        compiler_params=params(32),
        name="inverse",
    )(panel_order.reshape(strips, LANES))

    anchors = gathered[:, 17 * groups : 17 * groups + 3].astype(jnp.int32)
    lane = 4 * (jnp.arange(blocks, dtype=jnp.int32) % GROUP)
    forth = ((anchors[:, 0] - lane) & (LANES - 1)).reshape(devices * blocks)
    back = ((lane - anchors[:, 0]) & (LANES - 1)).reshape(devices * blocks)
    second_at = anchors[:, 1].reshape(devices * blocks)
    piece = (jnp.arange(devices, dtype=jnp.int32) % cols * SLABS // cols * PIECE)[:, None]
    slab_at = (anchors[:, 1] - piece).reshape(devices * blocks)
    third_at = anchors[:, 2].reshape(devices * blocks)
    place = half.astype(jnp.int32).reshape(1)

    table = jnp.asarray(CAS)
    second = lax.dynamic_slice_in_dim(table[:, :G], row_at * gs, gs, axis=0)
    third = lax.dynamic_slice_in_dim(table[:, :G], col_at * fs, fs, axis=0)
    mine = lax.dynamic_slice_in_dim(table, half * LANES, LANES, axis=0)
    yours = lax.dynamic_slice_in_dim(table, (1 - half) * LANES, LANES, axis=0)
    first = jnp.concatenate([mine, yours], axis=0)
    chunks = G // ZC
    smem = pl.BlockSpec(memory_space=pltpu.SMEM)
    line_block = pl.BlockSpec((gs, ZC, LANES), lambda z: (0, z, 0))
    lines_type = struct((gs, G, LANES), jnp.bfloat16)
    own = pl.pallas_call(
        functools.partial(scatter_kernel, cols),
        grid=(chunks,),
        in_specs=[smem] * 4 + [whole(gathered.shape), whole(second.shape)],
        out_specs=line_block,
        out_shape=lines_type,
        scratch_shapes=[pltpu.VMEM((gs * ZC, LANES), jnp.float32)]
        + [pltpu.VMEM((G, SLAB, LANES), jnp.float32)] * SLABS,
        compiler_params=params(56),
        name="scatter",
    )(place, forth, slab_at, third_at, gathered, second)
    other = lax.ppermute(own, "col", mates)

    batch = 8
    part = lambda shape: pl.BlockSpec((batch,) + shape, lambda n: (n, 0, 0))
    own, other = pl.pallas_call(
        spectrum_kernel,
        grid=(gs // batch,),
        in_specs=[
            part((G, LANES)),
            part((G, LANES)),
            part((fs, P_SIZE)),
            whole((fs, G)),
            whole((G, fs)),
            whole((G, P_SIZE)),
            whole((P_SIZE, G)),
        ],
        out_specs=(part((G, LANES)), part((G, LANES))),
        out_shape=(lines_type, lines_type),
        scratch_shapes=[pltpu.VMEM((batch * fs, G), jnp.bfloat16)],
        compiler_params=params(56),
        name="spectrum",
    )(own, other, kernel_spectrum, third, third.T, first, first.T)
    other = lax.ppermute(other, "col", mates)

    source = near_pairs[1]
    source_device = source // blocks
    code = (source_device // cols - row_at + 1) * 3 + (source_device % cols - col_at + 1)
    wanted = code * blocks + source % blocks
    target = near_pairs[0] - (row_at * cols + col_at) * blocks
    around = neighbourhood(block_charges).reshape(9, blocks, LANES)
    pairs = near_blocks.shape[0]
    near = pl.pallas_call(
        near_kernel,
        grid=(pairs // blocks,),
        in_specs=[
            smem,
            pl.BlockSpec((blocks, BLK * BLK), lambda n: (n, 0)),
            pl.BlockSpec((1, blocks), lambda n: (0, n)),
            whole((9, blocks, LANES)),
        ],
        out_specs=whole((blocks, LANES)),
        out_shape=struct((blocks, LANES), jnp.float32),
        scratch_shapes=[
            pltpu.VMEM((9 * blocks, LANES), jnp.float32),
            pltpu.VMEM((blocks, LANES), jnp.float32),
        ],
        compiler_params=params(48),
        name="near",
    )(wanted, near_blocks, target.reshape(1, pairs), around)

    values = pl.pallas_call(
        functools.partial(sample_kernel, cols),
        grid=(chunks,),
        in_specs=[smem] * 4 + [whole(gathered.shape), line_block, line_block, whole((G, gs))],
        out_specs=whole((devices, 16 * groups, LANES)),
        out_shape=struct((devices, 16 * groups, LANES), jnp.bfloat16),
        scratch_shapes=[
            pltpu.VMEM((gs * ZC, LANES), jnp.float32),
            pltpu.VMEM((G, G + 8, LANES), jnp.float32),
        ],
        compiler_params=params(56),
        name="sample",
    )(place, back, second_at, third_at, gathered, own, other, second.T)
    values = lax.all_to_all(values, axes, split_axis=0, concat_axis=0, tiled=True)

    result = pl.pallas_call(
        finish_kernel,
        out_shape=struct((strips, LANES), jnp.float32),
        scratch_shapes=[pltpu.VMEM((blocks, LANES), jnp.float32)],
        compiler_params=params(32),
        name="finish",
    )(values, interpolate, near, inverse)
    return result.reshape(panels)


def solution(mesh):
    placed = (
        P(("row", "col")),
        P(("row", "col")),
        P(None, ("row", "col")),
        P(("row", "col"), None),
        P(("row", "col"), None),
        P("row", "col", None),
        P(None, ("row", "col")),
        P(("row", "col"), None),
    )
    return jax.shard_map(
        body, mesh=mesh, in_specs=placed, out_specs=P(("row", "col")), check_vma=False
    )
```

time: 368 us -> 186 us (0.51)
  the two profiles are of different devices: /device:TPU:0 before, /device:TPU:11 now
where the time goes in v2:
time: 186 us; the launch traced here: 185 us
  Pallas kernels  112 us (60%)
  waiting for transfers between devices  32.5 us (17%)
  starting transfers between devices  23.4 us (13%)
  local copies, waits for them, and re-layouts  14.7 us (8%)
    pallas_call x1, Pallas kernels, body(): pl.pallas_call(functools.partial(sample_kernel, cols), grid=(chunks,), in...  38 us
    pallas_call x1, Pallas kernels, body(): pl.pallas_call(functools.partial(scatter_kernel, cols), grid=(chunks,), i...  36.9 us
    pallas_call x1, Pallas kernels, body(): pl.pallas_call(spectrum_kernel, grid=(gs // batch,), in_specs=[part((G, L...  18.2 us
    all_to_all x1, waiting for transfers between devices, body(): lax.all_to_all(copies, axes, split_axis=0, concat_axis=0, tiled=True)  13.9 us
    ppermute x2, waiting for transfers between devices, neighbourhood(): after = lax.ppermute(array, axis, down)  7.63 us
    ppermute x1, waiting for transfers between devices, body(): other = lax.ppermute(other, 'col', mates)  7.24 us
    ppermute x2, starting transfers between devices, neighbourhood(): before = lax.ppermute(array, axis, up)  6.99 us
    unnamed x22, local copies, waits for them, and re-layouts  6.85 us
  transfers between devices with their start and end apart: 8, of which 4 were waited for; matrix products, arithmetic and copies ran while one was open for 3% of the time, Pallas kernels for 5%

profile of v2, /device:TPU:11, one launch (start us, length us, event | category | flops | bytes accessed | tf_op | source)
XLA Modules:
  0.0 184.7 jit_solution(6634331885766439424)
XLA Ops:
  0.9 1.2 copy-done.1
  3.6 5.2 %project.2 = (bf16[128,128]{1,0:T(8,128)(2,1)S(1)}, bf16[80,128]{1,0:T(8,128)(2,1)S(1)}) custom-call(bf16[64,128]{1,0:T(8,128)(2,1)S(1)} %bitcast.31, s32[128,128]{1,0:T(8,128)S(1)} %pad_add_fusion.order, bf16[128,4096]{1,0:T(8,128)(2,1)S(1)} %copy-done.1, s32[3,128]{1,0:T(4,128)S(1)} %copy-done.5), custom_call_target="tpu_custom_call" | custom-call | tf_op jit(solution)/shard_map/project/pallas_call | solution.py:391
  8.8 0.9 broadcast_in_dim.4
  9.7 6.3 %all-to-all-start = ((bf16[32,80,128]{2,1,0:T(8,128)(2,1)}), bf16[32,80,128]{2,1,0:T(8,128)(2,1)S(1)}, u32[]{:S(2)}, u32[]{:S(2)}) async-start(bf16[32,80,128]{2,1,0:T(8,128)(2,1)} %broadcast_in_dim.4), calls=%async_computation | async-start | bytes 1310720 | tf_op jit(solution)/shard_map/all_to_all | solution.py:407
  16.0 1.6 dynamic-slice_bitcast_fusion.1
  18.3 13.9 %all-to-all-done.patches = bf16[32,80,128]{2,1,0:T(8,128)(2,1)S(1)} async-done(((bf16[32,80,128]{2,1,0:T(8,128)(2,1)}), bf16[32,80,128]{2,1,0:T(8,128)(2,1)S(1)}, u32[]{:S(2)}, u32[]{:S(2)}) %all-to-all-start) | async-done | bytes 655392 | tf_op jit(solution)/shard_map/all_to_all | solution.py:407
  33.7 36.9 %scatter.1.own = bf16[64,256,128]{2,1,0:T(8,128)(2,1)} custom-call(s32[1]{0:T(128)} %bitcast.place, s32[4096]{0:T(1024)} %get-tuple-element.24.shift, s32[4096]{0:T(1024)} %get-tuple-element.28.second, s32[4096]{0:T(1024)} %bitcast.32, bf16[32,80,128]{2,1,0:T(8,128)(2,1)} %copy-done.6, bf16[64,256]{1,0:T(8,128)(2,1)} %copy.13.table), custom_call_target="tpu_custom_call" | custom-call | tf_op jit(solution)/shard_map/scatter/pallas_call | solution.py:435
  70.6 1.5 dynamic-slice_bitcast_fusion
  73.5 0.8 copy.15.first
  74.4 3.7 %collective-permute-done.other = bf16[64,256,128]{2,1,0:T(8,128)(2,1)} collective-permute-done((bf16[64,256,128]{2,1,0:T(8,128)(2,1)}, bf16[64,256,128]{2,1,0:T(8,128)(2,1)}, u32[]{:S(2)}, u32[]{:S(2)}) %collective-permute-start) | collective-permute-done | bytes 4194336 | tf_op jit(solution)/shard_map/ppermute | solution.py:446
  78.1 18.2 %spectrum.1 = (bf16[64,256,128]{2,1,0:T(8,128)(2,1)}, bf16[64,256,128]{2,1,0:T(8,128)(2,1)}) custom-call(bf16[64,256,128]{2,1,0:T(8,128)(2,1)} %scatter.1.own, bf16[64,256,128]{2,1,0:T(8,128)(2,1)} %collective-permute-done.other, f32[64,128,512]{2,1,0:T(8,128)} %weights.1, bf16[128,256]{1,0:T(8,128)(2,1)} %copy.14.third, ...), custom_call_target="tpu_custom_call" | custom-call | tf_op jit(solution)/shard_map/spectrum/pallas_call | solution.py:450
  96.5 7.2 %collective-permute-done.1.other = bf16[64,256,128]{2,1,0:T(8,128)(2,1)S(1)} collective-permute-done((bf16[64,256,128]{2,1,0:T(8,128)(2,1)}, bf16[64,256,128]{2,1,0:T(8,128)(2,1)S(1)}, u32[]{:S(2)}, u32[]{:S(2)}) %collective-permute-start.1) | collective-permute-done | bytes 4194336 | tf_op jit(solution)/shard_map/ppermute | solution.py:468
  103.8 2.0 %copy-done.7 = bf16[64,256,128]{2,1,0:T(8,128)(2,1)} copy-done((bf16[64,256,128]{2,1,0:T(8,128)(2,1)}, bf16[64,256,128]{2,1,0:T(8,128)(2,1)S(1)}, u32[]{:S(2)}) %copy-start.7) | copy-done | bytes 4194328
  105.8 38.0 %sample.1 = bf16[32,64,128]{2,1,0:T(8,128)(2,1)} custom-call(s32[1]{0:T(128)} %bitcast.place, s32[4096]{0:T(1024)} %get-tuple-element.25.shift, s32[4096]{0:T(1024)} %bitcast.35, s32[4096]{0:T(1024)} %bitcast.33, bf16[32,80,128]{2,1,0:T(8,128)(2,1)} %copy-done.6, bf16[64,256,128]{2,1,0:T(8,128)(2,1)} %get-tuple-element.10.own, ...), custom_call_target="tpu_custom_call" | custom-call | tf_op jit(solution)/shard_map/sample/pallas_call | solution.py:496
  143.8 4.8 %all-to-all-start.1 = ((bf16[32,64,128]{2,1,0:T(8,128)(2,1)}), bf16[32,64,128]{2,1,0:T(8,128)(2,1)S(1)}, u32[]{:S(2)}, u32[]{:S(2)}) async-start(bf16[32,64,128]{2,1,0:T(8,128)(2,1)} %sample.1), calls=%async_computation.1 | async-start | bytes 1048576 | tf_op jit(solution)/shard_map/all_to_all | solution.py:509
  148.6 2.2 %collective-permute-start.3 = (bf16[1,1,128,128]{3,2,1,0:T(8,128)(2,1)S(1)}, bf16[1,1,128,128]{3,2,1,0:T(8,128)(2,1)S(1)}, u32[]{:S(2)}, u32[]{:S(2)}) collective-permute-start(bf16[1,1,128,128]{3,2,1,0:T(8,128)(2,1)S(1)} %bitcast.27), channel_id=1, source_target_pairs={{4,0},{8,4},{12,8},{16,12},{20,16},{24,20},{28,24},{5,1},{9,5},{13... | collective-permute-start | bytes 98312 | tf_op jit(solution)/shard_map/ppermute | solution.py:360
  150.8 4.0 %collective-permute-start.2 = (bf16[1,1,128,128]{3,2,1,0:T(8,128)(2,1)S(1)}, bf16[1,1,128,128]{3,2,1,0:T(8,128)(2,1)S(1)}, u32[]{:S(2)}, u32[]{:S(2)}) collective-permute-start(bf16[1,1,128,128]{3,2,1,0:T(8,128)(2,1)S(1)} %bitcast.28), channel_id=1, source_target_pairs={{0,4},{4,8},{8,12},{12,16},{16,20},{20,24},{24,28},{1,5},{5,9},{9,... | collective-permute-start | bytes 98312 | tf_op jit(solution)/shard_map/ppermute | solution.py:359
  154.8 7.6 %collective-permute-done.3 = bf16[1,1,128,128]{3,2,1,0:T(8,128)(2,1)S(1)} collective-permute-done((bf16[1,1,128,128]{3,2,1,0:T(8,128)(2,1)S(1)}, bf16[1,1,128,128]{3,2,1,0:T(8,128)(2,1)S(1)}, u32[]{:S(2)}, u32[]{:S(2)}) %collective-permute-start.3) | collective-permute-done | bytes 32800 | tf_op jit(solution)/shard_map/ppermute | solution.py:360
  162.5 2.9 %collective-permute-start.5 = (bf16[3,1,128,128]{3,2,1,0:T(8,128)(2,1)S(1)}, bf16[3,1,128,128]{3,2,1,0:T(8,128)(2,1)S(1)}, u32[]{:S(2)}, u32[]{:S(2)}) collective-permute-start(bf16[3,1,128,128]{3,2,1,0:T(8,128)(2,1)S(1)} %pad_maximum_fusion.2), channel_id=1, source_target_pairs={{1,0},{2,1},{3,2},{5,4},{6,5},{7,6},{9,8},{10,9},{11,10},{13,12},{... | collective-permute-start | bytes 294920 | tf_op jit(solution)/shard_map/ppermute | solution.py:360
  165.4 3.0 %collective-permute-start.4 = (bf16[3,1,128,128]{3,2,1,0:T(8,128)(2,1)S(1)}, bf16[3,1,128,128]{3,2,1,0:T(8,128)(2,1)S(1)}, u32[]{:S(2)}, u32[]{:S(2)}) collective-permute-start(bf16[3,1,128,128]{3,2,1,0:T(8,128)(2,1)S(1)} %pad_maximum_fusion.2), channel_id=1, source_target_pairs={{0,1},{1,2},{2,3},{4,5},{5,6},{6,7},{8,9},{9,10},{10,11},{12,13},{... | collective-permute-start | bytes 294920 | tf_op jit(solution)/shard_map/ppermute | solution.py:359
  168.5 3.8 %inverse.1 = s32[128,128]{1,0:T(8,128)S(1)} custom-call(s32[64,128]{1,0:T(8,128)S(1)} %bitcast.26), custom_call_target="tpu_custom_call" | custom-call | tf_op jit(solution)/shard_map/inverse/pallas_call | solution.py:408
  172.3 2.2 %copy-done = bf16[512,4096]{1,0:T(8,128)(2,1)S(1)} copy-done((bf16[512,4096]{1,0:T(8,128)(2,1)S(1)}, bf16[512,4096]{1,0:T(8,128)(2,1)}, u32[]{:S(2)}) %copy-start) | copy-done | bytes 4194328
  174.5 5.4 %near.1 = f32[128,128]{1,0:T(8,128)S(1)} custom-call(s32[512]{0:T(512)S(1)} %fusion.7.source, bf16[512,4096]{1,0:T(8,128)(2,1)S(1)} %copy-done, s32[1,512]{1,0:T(1,128)S(1)} %get-tuple-element.26.target, bf16[9,128,128]{2,1,0:T(8,128)(2,1)S(1)} %bitcast.25), custom_call_target="tpu_custom_call" | custom-call | tf_op jit(solution)/shard_map/near/pallas_call | solution.py:477
  179.9 4.8 %finish.1 = f32[64,128]{1,0:T(8,128)} custom-call(bf16[32,64,128]{2,1,0:T(8,128)(2,1)S(1)} %all-to-all-done.1.values, bf16[128,4096]{1,0:T(8,128)(2,1)S(1)} %copy-done.2, f32[128,128]{1,0:T(8,128)S(1)} %near.1, s32[128,128]{1,0:T(8,128)S(1)} %inverse.1), custom_call_target="tpu_custom_call" | custom-call | tf_op jit(solution)/shard_map/finish/pallas_call | solution.py:511
  (40 shorter events, 6.3 us)
Async XLA Ops:
  0.9 1.2 copy-start.1
  2.2 0.7 copy-start.4
  2.9 0.7 copy-start.5
  8.8 64.0 %copy-start.9 = (bf16[512,512]{0,1:T(8,128)(2,1)S(1)}, bf16[512,512]{0,1:T(8,128)(2,1)}, u32[]{:S(2)}) copy-start(bf16[512,512]{0,1:T(8,128)(2,1)} %constant.115.clone) | copy-start | bytes 1572868
  9.7 22.6 %all-to-all-start = ((bf16[32,80,128]{2,1,0:T(8,128)(2,1)}), bf16[32,80,128]{2,1,0:T(8,128)(2,1)S(1)}, u32[]{:S(2)}, u32[]{:S(2)}) async-start(bf16[32,80,128]{2,1,0:T(8,128)(2,1)} %broadcast_in_dim.4), calls=%async_computation | async-start | bytes 1310720 | tf_op jit(solution)/shard_map/all_to_all | solution.py:407
  32.2 1.4 copy-start.6
  33.0 63.3 %copy-start.8 = (s32[32,1,128]{2,1,0:T(1,128)}, s32[32,1,128]{2,1,0:T(1,128)S(1)}, u32[]{:S(2)}) copy-start(s32[32,1,128]{2,1,0:T(1,128)S(1)} %get-tuple-element.22) | copy-start | bytes 49156
  70.6 7.5 %collective-permute-start = (bf16[64,256,128]{2,1,0:T(8,128)(2,1)}, bf16[64,256,128]{2,1,0:T(8,128)(2,1)}, u32[]{:S(2)}, u32[]{:S(2)}) collective-permute-start(bf16[64,256,128]{2,1,0:T(8,128)(2,1)} %scatter.1.own), channel_id=1, source_target_pairs={{0,1},{1,0},{2,3},{3,2},{4,5},{5,4},{6,7},{7,6},{8,9},{9,8},{10,11... | collective-permute-start | bytes 12582920 | tf_op jit(solution)/shard_map/ppermute | solution.py:446
  96.3 7.4 %collective-permute-start.1 = (bf16[64,256,128]{2,1,0:T(8,128)(2,1)}, bf16[64,256,128]{2,1,0:T(8,128)(2,1)S(1)}, u32[]{:S(2)}, u32[]{:S(2)}) collective-permute-start(bf16[64,256,128]{2,1,0:T(8,128)(2,1)} %get-tuple-element.11), channel_id=1, source_target_pairs={{0,1},{1,0},{2,3},{3,2},{4,5},{5,4},{6,7},{7,6},{8,9},{9,8},{10,11... | collective-permute-start | bytes 12582920 | tf_op jit(solution)/shard_map/ppermute | solution.py:468
  103.7 2.0 %copy-start.7 = (bf16[64,256,128]{2,1,0:T(8,128)(2,1)}, bf16[64,256,128]{2,1,0:T(8,128)(2,1)S(1)}, u32[]{:S(2)}) copy-start(bf16[64,256,128]{2,1,0:T(8,128)(2,1)S(1)} %collective-permute-done.1.other) | copy-start | bytes 12582916
  105.8 49.0 %copy-start.10 = (s32[2,512]{1,0:T(2,128)S(1)}, s32[2,512]{1,0:T(2,128)}, u32[]{:S(2)}) copy-start(s32[2,512]{1,0:T(2,128)} %param.15) | copy-start | bytes 12292
  105.8 62.7 %copy-start.3 = (s32[8192]{0:T(1024)S(1)}, s32[8192]{0:T(1024)}, u32[]{:S(2)}) copy-start(s32[8192]{0:T(1024)} %param.10) | copy-start | bytes 98308
  143.8 36.1 %copy-start.2 = (bf16[128,4096]{1,0:T(8,128)(2,1)S(1)}, bf16[128,4096]{1,0:T(8,128)(2,1)}, u32[]{:S(2)}) copy-start(bf16[128,4096]{1,0:T(8,128)(2,1)} %interpolate.1) | copy-start | bytes 3145732
  143.8 36.1 %all-to-all-start.1 = ((bf16[32,64,128]{2,1,0:T(8,128)(2,1)}), bf16[32,64,128]{2,1,0:T(8,128)(2,1)S(1)}, u32[]{:S(2)}, u32[]{:S(2)}) async-start(bf16[32,64,128]{2,1,0:T(8,128)(2,1)} %sample.1), calls=%async_computation.1 | async-start | bytes 1048576 | tf_op jit(solution)/shard_map/all_to_all | solution.py:509
  148.6 13.9 %collective-permute-start.3 = (bf16[1,1,128,128]{3,2,1,0:T(8,128)(2,1)S(1)}, bf16[1,1,128,128]{3,2,1,0:T(8,128)(2,1)S(1)}, u32[]{:S(2)}, u32[]{:S(2)}) collective-permute-start(bf16[1,1,128,128]{3,2,1,0:T(8,128)(2,1)S(1)} %bitcast.27), channel_id=1, source_target_pairs={{4,0},{8,4},{12,8},{16,12},{20,16},{24,20},{28,24},{5,1},{9,5},{13... | collective-permute-start | bytes 98312 | tf_op jit(solution)/shard_map/ppermute | solution.py:360
  150.8 11.7 %collective-permute-start.2 = (bf16[1,1,128,128]{3,2,1,0:T(8,128)(2,1)S(1)}, bf16[1,1,128,128]{3,2,1,0:T(8,128)(2,1)S(1)}, u32[]{:S(2)}, u32[]{:S(2)}) collective-permute-start(bf16[1,1,128,128]{3,2,1,0:T(8,128)(2,1)S(1)} %bitcast.28), channel_id=1, source_target_pairs={{0,4},{4,8},{8,12},{12,16},{16,20},{20,24},{24,28},{1,5},{5,9},{9,... | collective-permute-start | bytes 98312 | tf_op jit(solution)/shard_map/ppermute | solution.py:359
  162.5 9.7 %collective-permute-start.5 = (bf16[3,1,128,128]{3,2,1,0:T(8,128)(2,1)S(1)}, bf16[3,1,128,128]{3,2,1,0:T(8,128)(2,1)S(1)}, u32[]{:S(2)}, u32[]{:S(2)}) collective-permute-start(bf16[3,1,128,128]{3,2,1,0:T(8,128)(2,1)S(1)} %pad_maximum_fusion.2), channel_id=1, source_target_pairs={{1,0},{2,1},{3,2},{5,4},{6,5},{7,6},{9,8},{10,9},{11,10},{13,12},{... | collective-permute-start | bytes 294920 | tf_op jit(solution)/shard_map/ppermute | solution.py:360
  165.4 6.8 %collective-permute-start.4 = (bf16[3,1,128,128]{3,2,1,0:T(8,128)(2,1)S(1)}, bf16[3,1,128,128]{3,2,1,0:T(8,128)(2,1)S(1)}, u32[]{:S(2)}, u32[]{:S(2)}) collective-permute-start(bf16[3,1,128,128]{3,2,1,0:T(8,128)(2,1)S(1)} %pad_maximum_fusion.2), channel_id=1, source_target_pairs={{0,1},{1,2},{2,3},{4,5},{5,6},{6,7},{8,9},{9,10},{10,11},{12,13},{... | collective-permute-start | bytes 294920 | tf_op jit(solution)/shard_map/ppermute | solution.py:359
  172.3 2.2 %copy-start = (bf16[512,4096]{1,0:T(8,128)(2,1)S(1)}, bf16[512,4096]{1,0:T(8,128)(2,1)}, u32[]{:S(2)}) copy-start(bf16[512,4096]{1,0:T(8,128)(2,1)} %near_blocks.1) | copy-start | bytes 12582916

commit v3 on v2

--- a/solution.py
+++ b/solution.py
@@ -18,8 +18,9 @@
 HALVES = G // LANES
 SLABS = 4
 PIECE = G // SLABS
-SLAB = PIECE + 8
-ZC = 16
+PAD = 8
+SLAB = PIECE + 2 * PAD
+ZC = 32
 MB = 1 << 20
 NT = (((1,), (1,)), ((), ()))
 
@@ -81,10 +82,11 @@
     return rows, lanes
 
 
-def project_kernel(charges, order, project, anchors, charge_out, patch_out, table):
-    blocks = order.shape[0]
+def project_kernel(charges, order, project, anchors, charge_out, patch_out, table, doubled):
+    blocks = charge_out.shape[0]
     groups = blocks // GROUP
     table[...] = charges[...].astype(jnp.float32)
+    strips = table.shape[0]
     upper = order[...] // LANES
     lower = order[...] % LANES
 
@@ -92,7 +94,12 @@
         row = jnp.broadcast_to(table[pl.ds(u, 1), :], lower.shape)
         return jnp.where(upper == u, lane_gather(row, lower), acc)
 
-    twice = lax.fori_loop(0, table.shape[0], step, jnp.zeros(lower.shape, jnp.float32), unroll=4)
+    slots = lax.fori_loop(0, strips, step, jnp.zeros(lower.shape, jnp.float32), unroll=4)
+    turned = pltpu.roll(slots, BLK, 1)
+    left = iota(slots.shape, 1) < BLK
+    doubled[pl.ds(0, strips, stride=2), :] = jnp.where(left, slots, turned)
+    doubled[pl.ds(1, strips, stride=2), :] = jnp.where(left, turned, slots)
+    twice = doubled[...]
     charge_out[...] = twice.astype(jnp.bfloat16)
     patch = block_sums(project, twice)
     patch = jnp.where(iota(patch.shape, 1) < PTS, patch, 0.0).astype(jnp.bfloat16)
@@ -167,7 +174,7 @@
         row = low + n // per_row
         left = n % per_row
         devices = [row * cols + s * per_slab + left // groups for s in range(SLABS)]
-        body(devices, left % groups)
+        body(devices, left % groups, row < half * (rows // HALVES))
         return carry
 
     lax.fori_loop(0, (high - low) * per_row, step, 0)
@@ -177,6 +184,11 @@
     extra = patches[d, 16 * groups :, :].astype(jnp.float32)
     picked = jnp.where(iota(extra.shape, 0) == t, extra, 0.0)
     return jnp.broadcast_to(jnp.sum(picked, axis=0, keepdims=True), (8, LANES))
+
+
+def crosses(shift, numbers, k):
+    found = [((shift[b] + 4 * k) & (LANES - 1)) > LANES - 4 for b in numbers]
+    return functools.reduce(jnp.logical_or, found)
 
 
 def scatter_kernel(cols, place, shift, second, third, patches, table, out, columns, *slabs):
@@ -187,6 +199,7 @@
     blocks = groups * GROUP
     freqs = table.shape[0]
     quad = iota((8, LANES), 1) // 4
+    upper = iota((8, LANES), 0) < 4
 
     @pl.when(chunk == 0)
     def _():
@@ -197,31 +210,48 @@
 
         lax.fori_loop(0, G, clear, 0)
 
-        def tile(numbers, t):
+        def tile(numbers, t, crossing):
             values = []
             for d in numbers:
                 both = patches[d, pl.ds(pl.multiple_of(16 * t, 16), 16), :].astype(jnp.float32)
                 cells = tile_cells(patches, d, t, groups) - (half * LANES).astype(jnp.float32)
-                inside = (cells >= 0.0) & (cells < LANES) & (iota((8, LANES), 0) < 4)
-                planes = [jnp.concatenate([both[4 * l : 4 * l + 4]] * 2, axis=0) for l in range(4)]
-                values.append([jnp.where(inside, plane, 0.0) for plane in planes])
-
-            def one(k, carry):
+                inside = (cells >= 0.0) & (cells < LANES)
+                values.append([jnp.where(inside, part, 0.0) for part in (both[:8], both[8:])])
+
+            def add(k):
                 spot = quad == k
                 sums = []
                 for s in range(SLABS):
                     b = numbers[s] * blocks + t * GROUP + k
                     amount = shift[b]
-                    at = (pl.ds(third[b], 4), pl.ds(second[b], 8))
-                    new = [
-                        pltpu.roll(jnp.where(spot, plane, 0.0), amount, 1) for plane in values[s]
-                    ]
-                    sums.append((at, slabs[s][at[0], at[1], :] + jnp.stack(new)))
-                for s, (at, new) in enumerate(sums):
-                    slabs[s][at[0], at[1], :] = new
+                    planes = slabs[s].at[pl.ds(third[b], 4)]
+                    rows = (pl.ds(second[b] + PAD, 8), pl.ds(second[b] + (PAD - 4), 8))
+                    for v in range(2):
+                        moved = pltpu.roll(jnp.where(spot, values[s][v], 0.0), amount, 1)
+                        parts = (jnp.where(upper, moved, 0.0), jnp.where(upper, 0.0, moved))
+                        for odd in range(2):
+                            l = 2 * v + odd
+                            sums.append((planes, l, rows[odd], planes[l, rows[odd], :] + parts[odd]))
+                for planes, l, at, new in sums:
+                    planes[l, at, :] = new
+
+            def one(k, carry):
+                add(k)
                 return carry
 
-            lax.fori_loop(0, GROUP, one, 0, unroll=4)
+            def one_crossing(k, carry):
+                pl.when(crosses(shift, [d * blocks + t * GROUP + k for d in numbers], k))(
+                    lambda: add(k)
+                )
+                return carry
+
+            @pl.when(crossing)
+            def _():
+                lax.fori_loop(0, GROUP, one_crossing, 0)
+
+            @pl.when(jnp.logical_not(crossing))
+            def _():
+                lax.fori_loop(0, GROUP, one, 0, unroll=4)
 
         tile_loop(half, devices // cols, cols, groups, tile)
 
@@ -231,9 +261,9 @@
             at = chunk * ZC + plane
             parts = []
             for s in range(SLABS):
-                part = slabs[s][at, :PIECE, :]
+                part = slabs[s][at, PAD : PAD + PIECE, :]
                 if s > 0:
-                    over = slabs[s - 1][at, PIECE:, :]
+                    over = slabs[s - 1][at, PAD + PIECE :, :]
                     part = jnp.concatenate([part[:8] + over, part[8:]], axis=0)
                 parts.append(part.astype(jnp.bfloat16))
             pair.append(jnp.concatenate(parts, axis=0))
@@ -250,8 +280,11 @@
     for g in range(count):
         line = jnp.concatenate([own[g], other[g]], axis=1)
         held[g * freqs : (g + 1) * freqs] = dot(third[...], line).astype(jnp.bfloat16)
-    s = dot(held[...], first[...]) * weights[...].reshape(count * freqs, P_SIZE)
-    held[...] = dot(s.astype(jnp.bfloat16), first_back[...]).astype(jnp.bfloat16)
+    step = max(1, G // freqs)
+    for g in range(0, count, step):
+        rows = slice(g * freqs, (g + step) * freqs)
+        s = dot(held[rows], first[...]) * weights[g : g + step].reshape(step * freqs, P_SIZE)
+        held[rows] = dot(s.astype(jnp.bfloat16), first_back[...]).astype(jnp.bfloat16)
     for g in range(count):
         line = dot(third_back[...], held[g * freqs : (g + 1) * freqs]).astype(jnp.bfloat16)
         own_out[g] = line[:, :LANES]
@@ -259,7 +292,7 @@
 
 
 def sample_kernel(
-    cols, place, shift, second, third, patches, own, other, table, out, columns, cells
+    cols, place, shift, back, second, third, patches, own, other, table, out, columns, cells
 ):
     half = place[0]
     chunk = pl.program_id(0)
@@ -268,6 +301,7 @@
     blocks = groups * GROUP
     freqs = table.shape[1]
     quad = iota((8, LANES), 1) // 4
+    upper = iota((8, LANES), 0) < 4
     both = own[...].astype(jnp.float32) + other[...].astype(jnp.float32)
     columns[...] = both.reshape(freqs * ZC, LANES)
     for z in range(0, ZC, 2):
@@ -275,37 +309,51 @@
             columns[pl.ds(plane, freqs, stride=ZC), :].astype(jnp.bfloat16) for plane in (z, z + 1)
         ]
         field = dot(table[...], jnp.concatenate(pair, axis=1))
-        cells[chunk * ZC + z, :G, :] = field[:, :LANES]
-        cells[chunk * ZC + z + 1, :G, :] = field[:, LANES:]
+        cells[chunk * ZC + z, PAD : PAD + G, :] = field[:, :LANES]
+        cells[chunk * ZC + z + 1, PAD : PAD + G, :] = field[:, LANES:]
 
     @pl.when(chunk == pl.num_programs(0) - 1)
     def _():
         out[...] = jnp.zeros_like(out)
 
-        def tile(numbers, t):
+        def tile(numbers, t, crossing):
             def one(k, sums):
                 spot = quad == k
                 sums = list(sums)
                 for s in range(SLABS):
                     b = numbers[s] * blocks + t * GROUP + k
                     amount = shift[b]
-                    here = cells[pl.ds(third[b], 4), pl.ds(second[b], 8), :]
-                    for l in range(4):
-                        moved = pltpu.roll(here[l], amount, 1)
-                        sums[4 * s + l] = jnp.where(spot, moved, sums[4 * s + l])
+                    planes = cells.at[pl.ds(third[b], 4)]
+                    for v in range(2):
+                        even = planes[2 * v, pl.ds(second[b] + PAD, 8), :]
+                        odd = planes[2 * v + 1, pl.ds(second[b] + (PAD - 4), 8), :]
+                        moved = pltpu.roll(jnp.where(upper, even, odd), amount, 1)
+                        sums[2 * s + v] = jnp.where(spot, moved, sums[2 * s + v])
                 return tuple(sums)
 
-            zero = jnp.zeros((8, LANES), jnp.float32)
-            sums = lax.fori_loop(0, GROUP, one, (zero,) * (4 * SLABS), unroll=4)
-            at = pl.multiple_of(16 * t, 16)
-            for s in range(SLABS):
-                first = tile_cells(patches, numbers[s], t, groups)
-                first = first - (half * LANES).astype(jnp.float32)
-                inside = (first >= 0.0) & (first < LANES)
-                planes = [jnp.where(inside, sums[4 * s + l], 0.0)[:4] for l in range(4)]
-                out[numbers[s], pl.ds(at, 16), :] = jnp.concatenate(planes, axis=0).astype(
-                    jnp.bfloat16
-                )
+            def one_crossing(k, sums):
+                found = crosses(back, [d * blocks + t * GROUP + k for d in numbers], k)
+                return lax.cond(found, lambda old: one(k, old), lambda old: old, sums)
+
+            zero = (jnp.zeros((8, LANES), jnp.float32),) * (2 * SLABS)
+
+            def store(sums):
+                for s in range(SLABS):
+                    first = tile_cells(patches, numbers[s], t, groups)
+                    first = first - (half * LANES).astype(jnp.float32)
+                    inside = (first >= 0.0) & (first < LANES)
+                    parts = [jnp.where(inside, part, 0.0) for part in sums[2 * s : 2 * s + 2]]
+                    out[numbers[s], pl.ds(pl.multiple_of(16 * t, 16), 16), :] = jnp.concatenate(
+                        parts, axis=0
+                    ).astype(jnp.bfloat16)
+
+            @pl.when(crossing)
+            def _():
+                store(lax.fori_loop(0, GROUP, one_crossing, zero))
+
+            @pl.when(jnp.logical_not(crossing))
+            def _():
+                store(lax.fori_loop(0, GROUP, one, zero, unroll=4))
 
         tile_loop(half, devices // cols, cols, groups, tile)
 
@@ -387,19 +435,22 @@
     gs, fs, _ = kernel_spectrum.shape
     held = 16 * groups + 16
 
-    order = panel_order.reshape(blocks, BLK)
+    order = panel_order.reshape(strips, LANES)
     block_charges, sent = pl.pallas_call(
         project_kernel,
         out_shape=(
             struct((blocks, LANES), jnp.bfloat16),
             struct((held, LANES), jnp.bfloat16),
         ),
-        scratch_shapes=[pltpu.VMEM((strips, LANES), jnp.float32)],
+        scratch_shapes=[
+            pltpu.VMEM((strips, LANES), jnp.float32),
+            pltpu.VMEM((blocks, LANES), jnp.float32),
+        ],
         compiler_params=params(32),
         name="project",
     )(
         charges.reshape(strips, LANES),
-        jnp.concatenate([order, order], axis=1),
+        order,
         project,
         patch_anchor,
     )
@@ -410,8 +461,10 @@
         out_shape=struct((2 * strips, LANES), jnp.int32),
         compiler_params=params(32),
         name="inverse",
-    )(panel_order.reshape(strips, LANES))
-
+    )(order)
+
+    around = neighbourhood(block_charges).reshape(9, blocks, LANES)
+    gathered, around = lax.optimization_barrier((gathered, around))
     anchors = gathered[:, 17 * groups : 17 * groups + 3].astype(jnp.int32)
     lane = 4 * (jnp.arange(blocks, dtype=jnp.int32) % GROUP)
     forth = ((anchors[:, 0] - lane) & (LANES - 1)).reshape(devices * blocks)
@@ -445,6 +498,32 @@
     )(place, forth, slab_at, third_at, gathered, second)
     other = lax.ppermute(own, "col", mates)
 
+    source = near_pairs[1]
+    source_device = source // blocks
+    code = (source_device // cols - row_at + 1) * 3 + (source_device % cols - col_at + 1)
+    wanted = code * blocks + source % blocks
+    target = near_pairs[0] - (row_at * cols + col_at) * blocks
+    pairs = near_blocks.shape[0]
+    near = pl.pallas_call(
+        near_kernel,
+        grid=(pairs // blocks,),
+        in_specs=[
+            smem,
+            pl.BlockSpec((blocks, BLK * BLK), lambda n: (n, 0)),
+            pl.BlockSpec((1, blocks), lambda n: (0, n)),
+            whole((9, blocks, LANES)),
+        ],
+        out_specs=whole((blocks, LANES)),
+        out_shape=struct((blocks, LANES), jnp.float32),
+        scratch_shapes=[
+            pltpu.VMEM((9 * blocks, LANES), jnp.float32),
+            pltpu.VMEM((blocks, LANES), jnp.float32),
+        ],
+        compiler_params=params(48),
+        name="near",
+    )(wanted, near_blocks, target.reshape(1, pairs), around)
+    other, near = lax.optimization_barrier((other, near))
+
     batch = 8
     part = lambda shape: pl.BlockSpec((batch,) + shape, lambda n: (n, 0, 0))
     own, other = pl.pallas_call(
@@ -467,45 +546,20 @@
     )(own, other, kernel_spectrum, third, third.T, first, first.T)
     other = lax.ppermute(other, "col", mates)
 
-    source = near_pairs[1]
-    source_device = source // blocks
-    code = (source_device // cols - row_at + 1) * 3 + (source_device % cols - col_at + 1)
-    wanted = code * blocks + source % blocks
-    target = near_pairs[0] - (row_at * cols + col_at) * blocks
-    around = neighbourhood(block_charges).reshape(9, blocks, LANES)
-    pairs = near_blocks.shape[0]
-    near = pl.pallas_call(
-        near_kernel,
-        grid=(pairs // blocks,),
-        in_specs=[
-            smem,
-            pl.BlockSpec((blocks, BLK * BLK), lambda n: (n, 0)),
-            pl.BlockSpec((1, blocks), lambda n: (0, n)),
-            whole((9, blocks, LANES)),
-        ],
-        out_specs=whole((blocks, LANES)),
-        out_shape=struct((blocks, LANES), jnp.float32),
-        scratch_shapes=[
-            pltpu.VMEM((9 * blocks, LANES), jnp.float32),
-            pltpu.VMEM((blocks, LANES), jnp.float32),
-        ],
-        compiler_params=params(48),
-        name="near",
-    )(wanted, near_blocks, target.reshape(1, pairs), around)
-
+    other, inverse = lax.optimization_barrier((other, inverse))
     values = pl.pallas_call(
         functools.partial(sample_kernel, cols),
         grid=(chunks,),
-        in_specs=[smem] * 4 + [whole(gathered.shape), line_block, line_block, whole((G, gs))],
+        in_specs=[smem] * 5 + [whole(gathered.shape), line_block, line_block, whole((G, gs))],
         out_specs=whole((devices, 16 * groups, LANES)),
         out_shape=struct((devices, 16 * groups, LANES), jnp.bfloat16),
         scratch_shapes=[
             pltpu.VMEM((gs * ZC, LANES), jnp.float32),
-            pltpu.VMEM((G, G + 8, LANES), jnp.float32),
+            pltpu.VMEM((G, G + 2 * PAD, LANES), jnp.float32),
         ],
         compiler_params=params(56),
         name="sample",
-    )(place, back, second_at, third_at, gathered, own, other, second.T)
+    )(place, back, forth, second_at, third_at, gathered, own, other, second.T)
     values = lax.all_to_all(values, axes, split_axis=0, concat_axis=0, tiled=True)
 
     result = pl.pallas_call(

time: 186 us -> 167 us (0.90)
  the two profiles are of different devices: /device:TPU:11 before, /device:TPU:0 now
where the time goes in v3:
time: 167 us; the launch traced here: 166 us
  Pallas kernels  88.2 us (53%)
  blocking collectives  31.1 us (19%)
  starting transfers between devices  21.5 us (13%)
  local copies, waits for them, and re-layouts  14.7 us (9%)
  waiting for transfers between devices  9.17 us (5%)
    all_to_all x1, blocking collectives, body(): lax.all_to_all(values, axes, split_axis=0, concat_axis=0, tiled=True)  31.1 us
    pallas_call x1, Pallas kernels, body(): pl.pallas_call(functools.partial(sample_kernel, cols), grid=(chunks,), in...  26.9 us
    pallas_call x1, Pallas kernels, body(): pl.pallas_call(functools.partial(scatter_kernel, cols), grid=(chunks,), i...  26.7 us
    pallas_call x1, Pallas kernels, body(): pl.pallas_call(spectrum_kernel, grid=(gs // batch,), in_specs=[part((G, L...  16.8 us
    unnamed x24, local copies, waits for them, and re-layouts  7.62 us
    ppermute x2, starting transfers between devices, neighbourhood(): before = lax.ppermute(array, axis, up)  7.58 us
    all_to_all x1, starting transfers between devices, body(): lax.all_to_all(copies, axes, split_axis=0, concat_axis=0, tiled=True)  7.3 us
    pallas_call x1, Pallas kernels, body(): pl.pallas_call(near_kernel, grid=(pairs // blocks,), in_specs=[smem, pl.B...  5.35 us
  transfers between devices with their start and end apart: 7, of which 3 were waited for; matrix products, arithmetic and copies ran while one was open for 4% of the time, Pallas kernels for 5%

profile of v3, /device:TPU:0, one launch (start us, length us, event | category | flops | bytes accessed | tf_op | source)
XLA Modules:
  0.0 166.3 jit_solution(2523754724904568183)
XLA Ops:
  0.0 1.2 copy-done.1
  3.4 3.8 %project.2 = (bf16[128,128]{1,0:T(8,128)(2,1)S(1)}, bf16[80,128]{1,0:T(8,128)(2,1)S(1)}) custom-call(bf16[64,128]{1,0:T(8,128)(2,1)S(1)} %bitcast.32, s32[64,128]{1,0:T(8,128)S(1)} %bitcast.26, bf16[128,4096]{1,0:T(8,128)(2,1)S(1)} %copy-done.1, s32[3,128]{1,0:T(4,128)S(1)} %copy-done.6), custom_call_target="tpu_custom_call" | custom-call | tf_op jit(solution)/shard_map/project/pallas_call | solution.py:439
  7.2 0.9 broadcast_in_dim.4
  8.1 7.3 %all-to-all-start = ((bf16[32,80,128]{2,1,0:T(8,128)(2,1)}), bf16[32,80,128]{2,1,0:T(8,128)(2,1)S(1)}, u32[]{:S(2)}, u32[]{:S(2)}) async-start(bf16[32,80,128]{2,1,0:T(8,128)(2,1)} %broadcast_in_dim.4), calls=%async_computation | async-start | bytes 1310720 | tf_op jit(solution)/shard_map/all_to_all | solution.py:458
  15.4 1.3 collective-permute-start.1
  16.7 4.5 %collective-permute-start = (bf16[1,1,128,128]{3,2,1,0:T(8,128)(2,1)S(1)}, bf16[1,1,128,128]{3,2,1,0:T(8,128)(2,1)S(1)}, u32[]{:S(2)}, u32[]{:S(2)}) collective-permute-start(bf16[1,1,128,128]{3,2,1,0:T(8,128)(2,1)S(1)} %bitcast.29), channel_id=1, source_target_pairs={{0,4},{4,8},{8,12},{12,16},{16,20},{20,24},{24,28},{1,5},{5,9},{9,... | collective-permute-start | bytes 98312 | tf_op jit(solution)/shard_map/ppermute | solution.py:407
  21.3 1.6 dynamic-slice_bitcast_fusion.1
  23.6 1.3 collective-permute-start.3
  24.9 3.0 %collective-permute-start.2 = (bf16[3,1,128,128]{3,2,1,0:T(8,128)(2,1)S(1)}, bf16[3,1,128,128]{3,2,1,0:T(8,128)(2,1)S(1)}, u32[]{:S(2)}, u32[]{:S(2)}) collective-permute-start(bf16[3,1,128,128]{3,2,1,0:T(8,128)(2,1)S(1)} %pad_maximum_fusion.2), channel_id=1, source_target_pairs={{0,1},{1,2},{2,3},{4,5},{5,6},{6,7},{8,9},{9,10},{10,11},{12,13},{... | collective-permute-start | bytes 294920 | tf_op jit(solution)/shard_map/ppermute | solution.py:407
  28.0 0.9 collective-permute-done.2
  28.9 4.7 %all-to-all-done.patches = bf16[32,80,128]{2,1,0:T(8,128)(2,1)S(1)} async-done(((bf16[32,80,128]{2,1,0:T(8,128)(2,1)}), bf16[32,80,128]{2,1,0:T(8,128)(2,1)S(1)}, u32[]{:S(2)}, u32[]{:S(2)}) %all-to-all-start) | async-done | bytes 655392 | tf_op jit(solution)/shard_map/all_to_all | solution.py:458
  35.1 26.7 %scatter.1.own = bf16[64,256,128]{2,1,0:T(8,128)(2,1)} custom-call(s32[1]{0:T(128)} %bitcast.place, s32[4096]{0:T(1024)} %get-tuple-element.36.shift.back, s32[4096]{0:T(1024)} %get-tuple-element.40.second, s32[4096]{0:T(1024)} %bitcast.33, bf16[32,80,128]{2,1,0:T(8,128)(2,1)} %copy-done.7, bf16[64,256]{1,0:T(8,128)(2,1)} %copy.10.table), custom_call_target="tpu_custom_call" | custom-call | tf_op jit(solution)/shard_map/scatter/pallas_call | solution.py:488
  61.8 4.1 %collective-permute-start.4 = (bf16[64,256,128]{2,1,0:T(8,128)(2,1)}, bf16[64,256,128]{2,1,0:T(8,128)(2,1)}, u32[]{:S(2)}, u32[]{:S(2)}) collective-permute-start(bf16[64,256,128]{2,1,0:T(8,128)(2,1)} %scatter.1.own), channel_id=1, source_target_pairs={{0,1},{1,0},{2,3},{3,2},{4,5},{5,4},{6,7},{7,6},{8,9},{9,8},{10,11... | collective-permute-start | bytes 12582920 | tf_op jit(solution)/shard_map/ppermute | solution.py:499
  65.9 1.5 dynamic-slice_bitcast_fusion
  68.9 0.9 copy.12.first
  69.8 2.2 %copy-done = bf16[512,4096]{1,0:T(8,128)(2,1)S(1)} copy-done((bf16[512,4096]{1,0:T(8,128)(2,1)S(1)}, bf16[512,4096]{1,0:T(8,128)(2,1)}, u32[]{:S(2)}) %copy-start) | copy-done | bytes 4194328
  72.0 5.4 %near.1 = f32[128,128]{1,0:T(8,128)S(1)} custom-call(s32[512]{0:T(512)S(1)} %fusion.7.source, bf16[512,4096]{1,0:T(8,128)(2,1)S(1)} %copy-done, s32[1,512]{1,0:T(1,128)S(1)} %get-tuple-element.38.target, bf16[9,128,128]{2,1,0:T(8,128)(2,1)S(1)} %bitcast.25), custom_call_target="tpu_custom_call" | custom-call | tf_op jit(solution)/shard_map/near/pallas_call | solution.py:507
  77.4 16.8 %spectrum.1 = (bf16[64,256,128]{2,1,0:T(8,128)(2,1)}, bf16[64,256,128]{2,1,0:T(8,128)(2,1)}) custom-call(bf16[64,256,128]{2,1,0:T(8,128)(2,1)} %scatter.1.own, bf16[64,256,128]{2,1,0:T(8,128)(2,1)} %collective-permute-done.4.other, f32[64,128,512]{2,1,0:T(8,128)} %weights.1, bf16[128,256]{1,0:T(8,128)(2,1)} %copy.11.third, ...), custom_call_target="tpu_custom_call" | custom-call | tf_op jit(solution)/shard_map/spectrum/pallas_call | solution.py:529
  94.2 3.8 %inverse.1 = s32[128,128]{1,0:T(8,128)S(1)} custom-call(s32[64,128]{1,0:T(8,128)S(1)} %bitcast.27), custom_call_target="tpu_custom_call" | custom-call | tf_op jit(solution)/shard_map/inverse/pallas_call | solution.py:459
  98.0 3.6 %collective-permute-done.5.other = bf16[64,256,128]{2,1,0:T(8,128)(2,1)S(1)} collective-permute-done((bf16[64,256,128]{2,1,0:T(8,128)(2,1)}, bf16[64,256,128]{2,1,0:T(8,128)(2,1)S(1)}, u32[]{:S(2)}, u32[]{:S(2)}) %collective-permute-start.5) | collective-permute-done | bytes 4194336 | tf_op jit(solution)/shard_map/ppermute | solution.py:547
  101.5 2.0 %copy-done.8 = bf16[64,256,128]{2,1,0:T(8,128)(2,1)} copy-done((bf16[64,256,128]{2,1,0:T(8,128)(2,1)}, bf16[64,256,128]{2,1,0:T(8,128)(2,1)S(1)}, u32[]{:S(2)}) %copy-start.8) | copy-done | bytes 4194328
  103.6 26.9 %sample.1 = bf16[32,64,128]{2,1,0:T(8,128)(2,1)} custom-call(s32[1]{0:T(128)} %bitcast.place, s32[4096]{0:T(1024)} %get-tuple-element.37.shift, s32[4096]{0:T(1024)} %get-tuple-element.36.shift.back, s32[4096]{0:T(1024)} %bitcast.36, s32[4096]{0:T(1024)} %bitcast.34, bf16[32,80,128]{2,1,0:T(8,128)(2,1)} %copy-done.7, ...), custom_call_target="tpu_custom_call" | custom-call | tf_op jit(solution)/shard_map/sample/pallas_call | solution.py:550
  130.4 31.1 %all_to_all.10.values = bf16[32,64,128]{2,1,0:T(8,128)(2,1)S(1)} all-to-all(bf16[32,64,128]{2,1,0:T(8,128)(2,1)} %sample.1), channel_id=1, replica_groups=mesh['row'=8,'col'=4] {'row','col'}, dimensions={0} | all-to-all | bytes 1048576 | tf_op jit(solution)/shard_map/all_to_all | solution.py:563
  161.5 4.8 %finish.1 = f32[64,128]{1,0:T(8,128)} custom-call(bf16[32,64,128]{2,1,0:T(8,128)(2,1)S(1)} %all_to_all.10.values, bf16[128,4096]{1,0:T(8,128)(2,1)S(1)} %copy-done.2, f32[128,128]{1,0:T(8,128)S(1)} %near.1, s32[128,128]{1,0:T(8,128)S(1)} %inverse.1), custom_call_target="tpu_custom_call" | custom-call | tf_op jit(solution)/shard_map/finish/pallas_call | solution.py:565
  (39 shorter events, 6.0 us)
Async XLA Ops:
  0.0 1.2 copy-start.1
  1.2 0.8 copy-start.3
  2.0 0.7 copy-start.5
  2.7 0.7 copy-start.6
  7.2 60.9 %copy-start.10 = (bf16[512,512]{0,1:T(8,128)(2,1)S(1)}, bf16[512,512]{0,1:T(8,128)(2,1)}, u32[]{:S(2)}) copy-start(bf16[512,512]{0,1:T(8,128)(2,1)} %constant.115.clone) | copy-start | bytes 1572868
  8.1 25.5 %all-to-all-start = ((bf16[32,80,128]{2,1,0:T(8,128)(2,1)}), bf16[32,80,128]{2,1,0:T(8,128)(2,1)S(1)}, u32[]{:S(2)}, u32[]{:S(2)}) async-start(bf16[32,80,128]{2,1,0:T(8,128)(2,1)} %broadcast_in_dim.4), calls=%async_computation | async-start | bytes 1310720 | tf_op jit(solution)/shard_map/all_to_all | solution.py:458
  15.4 8.1 %collective-permute-start.1 = (bf16[1,1,128,128]{3,2,1,0:T(8,128)(2,1)S(1)}, bf16[1,1,128,128]{3,2,1,0:T(8,128)(2,1)S(1)}, u32[]{:S(2)}, u32[]{:S(2)}) collective-permute-start(bf16[1,1,128,128]{3,2,1,0:T(8,128)(2,1)S(1)} %bitcast.28), channel_id=1, source_target_pairs={{4,0},{8,4},{12,8},{16,12},{20,16},{24,20},{28,24},{5,1},{9,5},{13... | collective-permute-start | bytes 98312 | tf_op jit(solution)/shard_map/ppermute | solution.py:408
  16.7 6.8 %collective-permute-start = (bf16[1,1,128,128]{3,2,1,0:T(8,128)(2,1)S(1)}, bf16[1,1,128,128]{3,2,1,0:T(8,128)(2,1)S(1)}, u32[]{:S(2)}, u32[]{:S(2)}) collective-permute-start(bf16[1,1,128,128]{3,2,1,0:T(8,128)(2,1)S(1)} %bitcast.29), channel_id=1, source_target_pairs={{0,4},{4,8},{8,12},{12,16},{16,20},{20,24},{24,28},{1,5},{5,9},{9,... | collective-permute-start | bytes 98312 | tf_op jit(solution)/shard_map/ppermute | solution.py:407
  22.9 46.9 %copy-start.11 = (s32[2,512]{1,0:T(2,128)S(1)}, s32[2,512]{1,0:T(2,128)}, u32[]{:S(2)}) copy-start(s32[2,512]{1,0:T(2,128)} %param.15) | copy-start | bytes 12292
  23.6 4.4 %collective-permute-start.3 = (bf16[3,1,128,128]{3,2,1,0:T(8,128)(2,1)S(1)}, bf16[3,1,128,128]{3,2,1,0:T(8,128)(2,1)S(1)}, u32[]{:S(2)}, u32[]{:S(2)}) collective-permute-start(bf16[3,1,128,128]{3,2,1,0:T(8,128)(2,1)S(1)} %pad_maximum_fusion.2), channel_id=1, source_target_pairs={{1,0},{2,1},{3,2},{5,4},{6,5},{7,6},{9,8},{10,9},{11,10},{13,12},{... | collective-permute-start | bytes 294920 | tf_op jit(solution)/shard_map/ppermute | solution.py:408
  24.9 4.0 %collective-permute-start.2 = (bf16[3,1,128,128]{3,2,1,0:T(8,128)(2,1)S(1)}, bf16[3,1,128,128]{3,2,1,0:T(8,128)(2,1)S(1)}, u32[]{:S(2)}, u32[]{:S(2)}) collective-permute-start(bf16[3,1,128,128]{3,2,1,0:T(8,128)(2,1)S(1)} %pad_maximum_fusion.2), channel_id=1, source_target_pairs={{0,1},{1,2},{2,3},{4,5},{5,6},{6,7},{8,9},{9,10},{10,11},{12,13},{... | collective-permute-start | bytes 294920 | tf_op jit(solution)/shard_map/ppermute | solution.py:407
  33.6 1.5 copy-start.7
  34.4 42.9 %copy-start.9 = (s32[32,1,128]{2,1,0:T(1,128)}, s32[32,1,128]{2,1,0:T(1,128)S(1)}, u32[]{:S(2)}) copy-start(s32[32,1,128]{2,1,0:T(1,128)S(1)} %get-tuple-element.34) | copy-start | bytes 49156
  61.8 15.5 %collective-permute-start.4 = (bf16[64,256,128]{2,1,0:T(8,128)(2,1)}, bf16[64,256,128]{2,1,0:T(8,128)(2,1)}, u32[]{:S(2)}, u32[]{:S(2)}) collective-permute-start(bf16[64,256,128]{2,1,0:T(8,128)(2,1)} %scatter.1.own), channel_id=1, source_target_pairs={{0,1},{1,0},{2,3},{3,2},{4,5},{5,4},{6,7},{7,6},{8,9},{9,8},{10,11... | collective-permute-start | bytes 12582920 | tf_op jit(solution)/shard_map/ppermute | solution.py:499
  69.8 2.2 %copy-start = (bf16[512,4096]{1,0:T(8,128)(2,1)S(1)}, bf16[512,4096]{1,0:T(8,128)(2,1)}, u32[]{:S(2)}) copy-start(bf16[512,4096]{1,0:T(8,128)(2,1)} %near_blocks.1) | copy-start | bytes 12582916
  77.4 16.8 %copy-start.4 = (s32[8192]{0:T(1024)S(1)}, s32[8192]{0:T(1024)}, u32[]{:S(2)}) copy-start(s32[8192]{0:T(1024)} %param.10) | copy-start | bytes 98308
  94.2 7.4 %collective-permute-start.5 = (bf16[64,256,128]{2,1,0:T(8,128)(2,1)}, bf16[64,256,128]{2,1,0:T(8,128)(2,1)S(1)}, u32[]{:S(2)}, u32[]{:S(2)}) collective-permute-start(bf16[64,256,128]{2,1,0:T(8,128)(2,1)} %get-tuple-element.21), channel_id=1, source_target_pairs={{0,1},{1,0},{2,3},{3,2},{4,5},{5,4},{6,7},{7,6},{8,9},{9,8},{10,11... | collective-permute-start | bytes 12582920 | tf_op jit(solution)/shard_map/ppermute | solution.py:547
  101.5 2.0 %copy-start.8 = (bf16[64,256,128]{2,1,0:T(8,128)(2,1)}, bf16[64,256,128]{2,1,0:T(8,128)(2,1)S(1)}, u32[]{:S(2)}) copy-start(bf16[64,256,128]{2,1,0:T(8,128)(2,1)S(1)} %collective-permute-done.5.other) | copy-start | bytes 12582916
  103.6 57.9 %copy-start.2 = (bf16[128,4096]{1,0:T(8,128)(2,1)S(1)}, bf16[128,4096]{1,0:T(8,128)(2,1)}, u32[]{:S(2)}) copy-start(bf16[128,4096]{1,0:T(8,128)(2,1)} %interpolate.1) | copy-start | bytes 3145732

commit v4 on v2

--- a/solution.py
+++ b/solution.py
@@ -18,8 +18,11 @@
 HALVES = G // LANES
 SLABS = 4
 PIECE = G // SLABS
-SLAB = PIECE + 8
-ZC = 16
+QUAD = 4
+PAD = 8
+SLAB = PAD + QUAD * PIECE + 32
+CELLS = PAD + QUAD * G + 16
+ZC = 32
 MB = 1 << 20
 NT = (((1,), (1,)), ((), ()))
 
@@ -75,16 +78,17 @@
     ]
     row = iota((16, LANES), 0)
     rows = [
-        (iota((16, LANES), 1) % PTS == 16 * i + 4 * (row % 4) + row // 4).astype(jnp.bfloat16)
+        (iota((16, LANES), 1) % PTS == 16 * i + row).astype(jnp.bfloat16)
         for i in range(4)
     ]
     return rows, lanes
 
 
-def project_kernel(charges, order, project, anchors, charge_out, patch_out, table):
-    blocks = order.shape[0]
+def project_kernel(charges, order, project, anchors, charge_out, patch_out, table, doubled):
+    blocks = charge_out.shape[0]
     groups = blocks // GROUP
     table[...] = charges[...].astype(jnp.float32)
+    strips = table.shape[0]
     upper = order[...] // LANES
     lower = order[...] % LANES
 
@@ -92,7 +96,12 @@
         row = jnp.broadcast_to(table[pl.ds(u, 1), :], lower.shape)
         return jnp.where(upper == u, lane_gather(row, lower), acc)
 
-    twice = lax.fori_loop(0, table.shape[0], step, jnp.zeros(lower.shape, jnp.float32), unroll=4)
+    slots = lax.fori_loop(0, strips, step, jnp.zeros(lower.shape, jnp.float32), unroll=4)
+    turned = pltpu.roll(slots, BLK, 1)
+    left = iota(slots.shape, 1) < BLK
+    doubled[pl.ds(0, strips, stride=2), :] = jnp.where(left, slots, turned)
+    doubled[pl.ds(1, strips, stride=2), :] = jnp.where(left, turned, slots)
+    twice = doubled[...]
     charge_out[...] = twice.astype(jnp.bfloat16)
     patch = block_sums(project, twice)
     patch = jnp.where(iota(patch.shape, 1) < PTS, patch, 0.0).astype(jnp.bfloat16)
@@ -166,80 +175,83 @@
     def step(n, carry):
         row = low + n // per_row
         left = n % per_row
-        devices = [row * cols + s * per_slab + left // groups for s in range(SLABS)]
-        body(devices, left % groups)
+        body([row * cols + s * per_slab + left // groups for s in range(SLABS)], left % groups)
         return carry
 
     lax.fori_loop(0, (high - low) * per_row, step, 0)
 
 
-def tile_cells(patches, d, t, groups):
+def lanes_inside(patches, d, t, groups, half):
     extra = patches[d, 16 * groups :, :].astype(jnp.float32)
     picked = jnp.where(iota(extra.shape, 0) == t, extra, 0.0)
-    return jnp.broadcast_to(jnp.sum(picked, axis=0, keepdims=True), (8, LANES))
-
-
-def scatter_kernel(cols, place, shift, second, third, patches, table, out, columns, *slabs):
+    cells = jnp.sum(picked, axis=0, keepdims=True) - (half * LANES).astype(jnp.float32)
+    return jnp.broadcast_to((cells >= 0.0) & (cells < LANES), (16, LANES))
+
+
+def scatter_kernel(cols, place, shift, start, patches, table, out, columns, *slabs):
     half = place[0]
     chunk = pl.program_id(0)
     devices, held, _ = patches.shape
     groups = (held - 16) // 16
     blocks = groups * GROUP
     freqs = table.shape[0]
-    quad = iota((8, LANES), 1) // 4
+    owner = iota((16, LANES), 1) // 4
+    plane = iota((16, LANES), 0) % QUAD
 
     @pl.when(chunk == 0)
     def _():
         def clear(n, carry):
             for slab in slabs:
-                slab[n] = jnp.zeros((SLAB, LANES), jnp.float32)
+                slab[pl.ds(pl.multiple_of(n * SLAB, 8), SLAB), :] = jnp.zeros(
+                    (SLAB, LANES), jnp.float32
+                )
             return carry
 
-        lax.fori_loop(0, G, clear, 0)
+        lax.fori_loop(0, slabs[0].shape[0] // SLAB, clear, 0)
 
         def tile(numbers, t):
             values = []
             for d in numbers:
-                both = patches[d, pl.ds(pl.multiple_of(16 * t, 16), 16), :].astype(jnp.float32)
-                cells = tile_cells(patches, d, t, groups) - (half * LANES).astype(jnp.float32)
-                inside = (cells >= 0.0) & (cells < LANES) & (iota((8, LANES), 0) < 4)
-                planes = [jnp.concatenate([both[4 * l : 4 * l + 4]] * 2, axis=0) for l in range(4)]
-                values.append([jnp.where(inside, plane, 0.0) for plane in planes])
+                part = patches[d, pl.ds(pl.multiple_of(16 * t, 16), 16), :].astype(jnp.float32)
+                values.append(jnp.where(lanes_inside(patches, d, t, groups, half), part, 0.0))
 
             def one(k, carry):
-                spot = quad == k
+                spot = owner == k
                 sums = []
                 for s in range(SLABS):
                     b = numbers[s] * blocks + t * GROUP + k
-                    amount = shift[b]
-                    at = (pl.ds(third[b], 4), pl.ds(second[b], 8))
-                    new = [
-                        pltpu.roll(jnp.where(spot, plane, 0.0), amount, 1) for plane in values[s]
-                    ]
-                    sums.append((at, slabs[s][at[0], at[1], :] + jnp.stack(new)))
-                for s, (at, new) in enumerate(sums):
-                    slabs[s][at[0], at[1], :] = new
+                    at = start[b]
+                    moved = pltpu.roll(jnp.where(spot, values[s], 0.0), shift[b], 1)
+                    here = plane < QUAD - (at & (QUAD - 1))
+                    near = slabs[s][pl.ds(at, 16), :] + jnp.where(here, moved, 0.0)
+                    at_next = at + (SLAB - QUAD)
+                    far = slabs[s][pl.ds(at_next, 16), :] + jnp.where(here, 0.0, moved)
+                    sums.append((at, near, at_next, far))
+                for s, (at, near, at_next, far) in enumerate(sums):
+                    slabs[s][pl.ds(at, 16), :] = near
+                    slabs[s][pl.ds(at_next, 16), :] = far
                 return carry
 
             lax.fori_loop(0, GROUP, one, 0, unroll=4)
 
         tile_loop(half, devices // cols, cols, groups, tile)
 
-    for z in range(0, ZC, 2):
-        pair = []
-        for plane in (z, z + 1):
-            at = chunk * ZC + plane
+    for z in range(0, ZC, QUAD):
+        base = pl.multiple_of((chunk * (ZC // QUAD) + z // QUAD) * SLAB, 8)
+        planes = []
+        for q in range(QUAD):
             parts = []
             for s in range(SLABS):
-                part = slabs[s][at, :PIECE, :]
+                part = slabs[s][pl.ds(base + (PAD + q), PIECE, stride=QUAD), :]
                 if s > 0:
-                    over = slabs[s - 1][at, PIECE:, :]
+                    at = base + (PAD + QUAD * PIECE + q)
+                    over = slabs[s - 1][pl.ds(at, 8, stride=QUAD), :]
                     part = jnp.concatenate([part[:8] + over, part[8:]], axis=0)
                 parts.append(part.astype(jnp.bfloat16))
-            pair.append(jnp.concatenate(parts, axis=0))
-        lines = dot(table[...], jnp.concatenate(pair, axis=1))
-        columns[pl.ds(z, freqs, stride=ZC), :] = lines[:, :LANES]
-        columns[pl.ds(z + 1, freqs, stride=ZC), :] = lines[:, LANES:]
+            planes.append(jnp.concatenate(parts, axis=0))
+        lines = dot(table[...], jnp.concatenate(planes, axis=1))
+        for q in range(QUAD):
+            columns[pl.ds(z + q, freqs, stride=ZC), :] = lines[:, LANES * q : LANES * q + LANES]
     out[...] = columns[...].reshape(freqs, ZC, LANES).astype(jnp.bfloat16)
 
 
@@ -250,33 +262,37 @@
     for g in range(count):
         line = jnp.concatenate([own[g], other[g]], axis=1)
         held[g * freqs : (g + 1) * freqs] = dot(third[...], line).astype(jnp.bfloat16)
-    s = dot(held[...], first[...]) * weights[...].reshape(count * freqs, P_SIZE)
-    held[...] = dot(s.astype(jnp.bfloat16), first_back[...]).astype(jnp.bfloat16)
+    step = max(1, G // freqs)
+    for g in range(0, count, step):
+        rows = slice(g * freqs, (g + step) * freqs)
+        s = dot(held[rows], first[...]) * weights[g : g + step].reshape(step * freqs, P_SIZE)
+        held[rows] = dot(s.astype(jnp.bfloat16), first_back[...]).astype(jnp.bfloat16)
     for g in range(count):
         line = dot(third_back[...], held[g * freqs : (g + 1) * freqs]).astype(jnp.bfloat16)
         own_out[g] = line[:, :LANES]
         other_out[g] = line[:, LANES:]
 
 
-def sample_kernel(
-    cols, place, shift, second, third, patches, own, other, table, out, columns, cells
-):
+def sample_kernel(cols, place, shift, start, patches, own, other, table, out, columns, cells):
     half = place[0]
     chunk = pl.program_id(0)
     devices, held, _ = out.shape
     groups = held // 16
     blocks = groups * GROUP
     freqs = table.shape[1]
-    quad = iota((8, LANES), 1) // 4
+    owner = iota((16, LANES), 1) // 4
+    plane = iota((16, LANES), 0) % QUAD
     both = own[...].astype(jnp.float32) + other[...].astype(jnp.float32)
     columns[...] = both.reshape(freqs * ZC, LANES)
-    for z in range(0, ZC, 2):
-        pair = [
-            columns[pl.ds(plane, freqs, stride=ZC), :].astype(jnp.bfloat16) for plane in (z, z + 1)
+    for z in range(0, ZC, QUAD):
+        planes = [
+            columns[pl.ds(z + q, freqs, stride=ZC), :].astype(jnp.bfloat16) for q in range(QUAD)
         ]
-        field = dot(table[...], jnp.concatenate(pair, axis=1))
-        cells[chunk * ZC + z, :G, :] = field[:, :LANES]
-        cells[chunk * ZC + z + 1, :G, :] = field[:, LANES:]
+        field = dot(table[...], jnp.concatenate(planes, axis=1))
+        base = pl.multiple_of((chunk * (ZC // QUAD) + z // QUAD) * CELLS, 8)
+        for q in range(QUAD):
+            part = field[:, LANES * q : LANES * q + LANES]
+            cells[pl.ds(base + (PAD + q), G, stride=QUAD), :] = part
 
     @pl.when(chunk == pl.num_programs(0) - 1)
     def _():
@@ -284,28 +300,25 @@
 
         def tile(numbers, t):
             def one(k, sums):
-                spot = quad == k
-                sums = list(sums)
+                spot = owner == k
+                new = []
                 for s in range(SLABS):
                     b = numbers[s] * blocks + t * GROUP + k
-                    amount = shift[b]
-                    here = cells[pl.ds(third[b], 4), pl.ds(second[b], 8), :]
-                    for l in range(4):
-                        moved = pltpu.roll(here[l], amount, 1)
-                        sums[4 * s + l] = jnp.where(spot, moved, sums[4 * s + l])
-                return tuple(sums)
-
-            zero = jnp.zeros((8, LANES), jnp.float32)
-            sums = lax.fori_loop(0, GROUP, one, (zero,) * (4 * SLABS), unroll=4)
-            at = pl.multiple_of(16 * t, 16)
-            for s in range(SLABS):
-                first = tile_cells(patches, numbers[s], t, groups)
-                first = first - (half * LANES).astype(jnp.float32)
-                inside = (first >= 0.0) & (first < LANES)
-                planes = [jnp.where(inside, sums[4 * s + l], 0.0)[:4] for l in range(4)]
-                out[numbers[s], pl.ds(at, 16), :] = jnp.concatenate(planes, axis=0).astype(
-                    jnp.bfloat16
-                )
+                    at = start[b]
+                    here = plane < QUAD - (at & (QUAD - 1))
+                    near = cells[pl.ds(at, 16), :]
+                    far = cells[pl.ds(at + (CELLS - QUAD), 16), :]
+                    moved = pltpu.roll(jnp.where(here, near, far), shift[b], 1)
+                    new.append(jnp.where(spot, moved, sums[s]))
+                return tuple(new)
+
+            zero = (jnp.zeros((16, LANES), jnp.float32),) * SLABS
+            sums = lax.fori_loop(0, GROUP, one, zero, unroll=4)
+            for s, d in enumerate(numbers):
+                inside = lanes_inside(patches, d, t, groups, half)
+                out[d, pl.ds(pl.multiple_of(16 * t, 16), 16), :] = jnp.where(
+                    inside, sums[s], 0.0
+                ).astype(jnp.bfloat16)
 
         tile_loop(half, devices // cols, cols, groups, tile)
 
@@ -350,16 +363,12 @@
     return pltpu.CompilerParams(vmem_limit_bytes=mib * MB)
 
 
-def neighbourhood(array):
-    array = array[None, None]
-    for axis, dim in (("row", 0), ("col", 1)):
-        count = lax.axis_size(axis)
-        up = [(i, i + 1) for i in range(count - 1)]
-        down = [(j, i) for i, j in up]
-        before = lax.ppermute(array, axis, up)
-        after = lax.ppermute(array, axis, down)
-        array = jnp.concatenate([before, array, after], axis=dim)
-    return array
+def beside(array, axis, dim):
+    count = lax.axis_size(axis)
+    up = [(i, i + 1) for i in range(count - 1)]
+    before = lax.ppermute(array, axis, up)
+    after = lax.ppermute(array, axis, [(j, i) for i, j in up])
+    return jnp.concatenate([before, array, after], axis=dim)
 
 
 def body(
@@ -387,19 +396,22 @@
     gs, fs, _ = kernel_spectrum.shape
     held = 16 * groups + 16
 
-    order = panel_order.reshape(blocks, BLK)
+    order = panel_order.reshape(strips, LANES)
     block_charges, sent = pl.pallas_call(
         project_kernel,
         out_shape=(
             struct((blocks, LANES), jnp.bfloat16),
             struct((held, LANES), jnp.bfloat16),
         ),
-        scratch_shapes=[pltpu.VMEM((strips, LANES), jnp.float32)],
+        scratch_shapes=[
+            pltpu.VMEM((strips, LANES), jnp.float32),
+            pltpu.VMEM((blocks, LANES), jnp.float32),
+        ],
         compiler_params=params(32),
         name="project",
     )(
         charges.reshape(strips, LANES),
-        jnp.concatenate([order, order], axis=1),
+        order,
         project,
         patch_anchor,
     )
@@ -410,16 +422,20 @@
         out_shape=struct((2 * strips, LANES), jnp.int32),
         compiler_params=params(32),
         name="inverse",
-    )(panel_order.reshape(strips, LANES))
-
+    )(order)
+
+    around = beside(block_charges[None, None], "row", 0)
+    gathered, around = lax.optimization_barrier((gathered, around))
+    around = beside(around, "col", 1).reshape(9, blocks, LANES)
     anchors = gathered[:, 17 * groups : 17 * groups + 3].astype(jnp.int32)
     lane = 4 * (jnp.arange(blocks, dtype=jnp.int32) % GROUP)
     forth = ((anchors[:, 0] - lane) & (LANES - 1)).reshape(devices * blocks)
     back = ((lane - anchors[:, 0]) & (LANES - 1)).reshape(devices * blocks)
-    second_at = anchors[:, 1].reshape(devices * blocks)
+    group = anchors[:, 2] // QUAD
+    inner = PAD + QUAD * anchors[:, 1] + anchors[:, 2] % QUAD
     piece = (jnp.arange(devices, dtype=jnp.int32) % cols * SLABS // cols * PIECE)[:, None]
-    slab_at = (anchors[:, 1] - piece).reshape(devices * blocks)
-    third_at = anchors[:, 2].reshape(devices * blocks)
+    slab_at = (group * SLAB + inner - QUAD * piece).reshape(devices * blocks)
+    cell_at = (group * CELLS + inner).reshape(devices * blocks)
     place = half.astype(jnp.int32).reshape(1)
 
     table = jnp.asarray(CAS)
@@ -435,15 +451,17 @@
     own = pl.pallas_call(
         functools.partial(scatter_kernel, cols),
         grid=(chunks,),
-        in_specs=[smem] * 4 + [whole(gathered.shape), whole(second.shape)],
+        in_specs=[smem] * 3 + [whole(gathered.shape), whole(second.shape)],
         out_specs=line_block,
         out_shape=lines_type,
         scratch_shapes=[pltpu.VMEM((gs * ZC, LANES), jnp.float32)]
-        + [pltpu.VMEM((G, SLAB, LANES), jnp.float32)] * SLABS,
+        + [pltpu.VMEM(((G // QUAD + 1) * SLAB, LANES), jnp.float32)] * SLABS,
         compiler_params=params(56),
         name="scatter",
-    )(place, forth, slab_at, third_at, gathered, second)
+    )(place, forth, slab_at, gathered, second)
     other = lax.ppermute(own, "col", mates)
+
+    other, around, inverse = lax.optimization_barrier((other, around, inverse))
 
     batch = 8
     part = lambda shape: pl.BlockSpec((batch,) + shape, lambda n: (n, 0, 0))
@@ -472,7 +490,6 @@
     code = (source_device // cols - row_at + 1) * 3 + (source_device % cols - col_at + 1)
     wanted = code * blocks + source % blocks
     target = near_pairs[0] - (row_at * cols + col_at) * blocks
-    around = neighbourhood(block_charges).reshape(9, blocks, LANES)
     pairs = near_blocks.shape[0]
     near = pl.pallas_call(
         near_kernel,
@@ -492,20 +509,20 @@
         compiler_params=params(48),
         name="near",
     )(wanted, near_blocks, target.reshape(1, pairs), around)
-
+    other, near = lax.optimization_barrier((other, near))
     values = pl.pallas_call(
         functools.partial(sample_kernel, cols),
         grid=(chunks,),
-        in_specs=[smem] * 4 + [whole(gathered.shape), line_block, line_block, whole((G, gs))],
+        in_specs=[smem] * 3 + [whole(gathered.shape), line_block, line_block, whole((G, gs))],
         out_specs=whole((devices, 16 * groups, LANES)),
         out_shape=struct((devices, 16 * groups, LANES), jnp.bfloat16),
         scratch_shapes=[
             pltpu.VMEM((gs * ZC, LANES), jnp.float32),
-            pltpu.VMEM((G, G + 8, LANES), jnp.float32),
+            pltpu.VMEM(((G // QUAD + 1) * CELLS, LANES), jnp.float32),
         ],
         compiler_params=params(56),
         name="sample",
-    )(place, back, second_at, third_at, gathered, own, other, second.T)
+    )(place, back, cell_at, gathered, own, other, second.T)
     values = lax.all_to_all(values, axes, split_axis=0, concat_axis=0, tiled=True)
 
     result = pl.pallas_call(

time: 186 us -> 158 us (0.85)
  the two profiles are of different devices: /device:TPU:11 before, /device:TPU:0 now
where the time goes in v4:
time: 158 us; the launch traced here: 157 us
  Pallas kernels  87.7 us (56%)
  blocking collectives  23.5 us (15%)
  starting transfers between devices  21.9 us (14%)
  local copies, waits for them, and re-layouts  11.9 us (8%)
  waiting for transfers between devices  9.99 us (6%)
  other arithmetic  1.7 us (1%)
    pallas_call x1, Pallas kernels, body(): pl.pallas_call(functools.partial(sample_kernel, cols), grid=(chunks,), in...  26.8 us
    pallas_call x1, Pallas kernels, body(): pl.pallas_call(functools.partial(scatter_kernel, cols), grid=(chunks,), i...  26.3 us
    all_to_all x1, blocking collectives, body(): lax.all_to_all(values, axes, split_axis=0, concat_axis=0, tiled=True)  23.5 us
    pallas_call x1, Pallas kernels, body(): pl.pallas_call(spectrum_kernel, grid=(gs // batch,), in_specs=[part((G, L...  16.8 us
    all_to_all x1, waiting for transfers between devices, body(): lax.all_to_all(copies, axes, split_axis=0, concat_axis=0, tiled=True)  9.97 us
    ppermute x2, starting transfers between devices, beside(): before = lax.ppermute(array, axis, up)  7.58 us
    all_to_all x1, starting transfers between devices, body(): lax.all_to_all(copies, axes, split_axis=0, concat_axis=0, tiled=True)  7.3 us
    unnamed x20, local copies, waits for them, and re-layouts  5.58 us
  transfers between devices with their start and end apart: 7, of which 1 were waited for; matrix products, arithmetic and copies ran while one was open for 4% of the time, Pallas kernels for 6%

profile of v4, /device:TPU:0, one launch (start us, length us, event | category | flops | bytes accessed | tf_op | source)
XLA Modules:
  0.0 156.8 jit_solution(18147188113455015994)
XLA Ops:
  0.0 1.2 copy-done.1
  1.2 0.8 copy-done.3
  3.4 3.8 %project.2 = (bf16[128,128]{1,0:T(8,128)(2,1)S(1)}, bf16[80,128]{1,0:T(8,128)(2,1)S(1)}) custom-call(bf16[64,128]{1,0:T(8,128)(2,1)S(1)} %bitcast.31, s32[64,128]{1,0:T(8,128)S(1)} %bitcast.26, bf16[128,4096]{1,0:T(8,128)(2,1)S(1)} %copy-done.1, s32[3,128]{1,0:T(4,128)S(1)} %copy-done.6), custom_call_target="tpu_custom_call" | custom-call | tf_op jit(solution)/shard_map/project/pallas_call | solution.py:400
  7.2 0.9 broadcast_in_dim.4
  8.1 7.3 %all-to-all-start = ((bf16[32,80,128]{2,1,0:T(8,128)(2,1)}), bf16[32,80,128]{2,1,0:T(8,128)(2,1)S(1)}, u32[]{:S(2)}, u32[]{:S(2)}) async-start(bf16[32,80,128]{2,1,0:T(8,128)(2,1)} %broadcast_in_dim.4), calls=%async_computation | async-start | bytes 1310720 | tf_op jit(solution)/shard_map/all_to_all | solution.py:419
  15.4 1.3 collective-permute-start.1
  16.7 4.5 %collective-permute-start = (bf16[1,1,128,128]{3,2,1,0:T(8,128)(2,1)S(1)}, bf16[1,1,128,128]{3,2,1,0:T(8,128)(2,1)S(1)}, u32[]{:S(2)}, u32[]{:S(2)}) collective-permute-start(bf16[1,1,128,128]{3,2,1,0:T(8,128)(2,1)S(1)} %bitcast.29), channel_id=1, source_target_pairs={{0,4},{4,8},{8,12},{12,16},{16,20},{20,24},{24,28},{1,5},{5,9},{9,... | collective-permute-start | bytes 98312 | tf_op jit(solution)/shard_map/ppermute | solution.py:369
  21.3 1.6 dynamic-slice_bitcast_fusion.1
  23.6 10.0 %all-to-all-done.patches = bf16[32,80,128]{2,1,0:T(8,128)(2,1)S(1)} async-done(((bf16[32,80,128]{2,1,0:T(8,128)(2,1)}), bf16[32,80,128]{2,1,0:T(8,128)(2,1)S(1)}, u32[]{:S(2)}, u32[]{:S(2)}) %all-to-all-start) | async-done | bytes 655392 | tf_op jit(solution)/shard_map/all_to_all | solution.py:419
  33.7 0.8 fusion.2
  34.5 26.3 %scatter.1.own = bf16[64,256,128]{2,1,0:T(8,128)(2,1)} custom-call(s32[1]{0:T(128)} %bitcast.place, s32[4096]{0:T(1024)} %get-tuple-element.40.shift, s32[4096]{0:T(1024)} %get-tuple-element.45.start, bf16[32,80,128]{2,1,0:T(8,128)(2,1)} %copy-done.7, bf16[64,256]{1,0:T(8,128)(2,1)} %copy.10.table), custom_call_target="tpu_custom_call" | custom-call | tf_op jit(solution)/shard_map/scatter/pallas_call | solution.py:451
  60.7 3.2 %collective-permute-start.2 = (bf16[64,256,128]{2,1,0:T(8,128)(2,1)}, bf16[64,256,128]{2,1,0:T(8,128)(2,1)}, u32[]{:S(2)}, u32[]{:S(2)}) collective-permute-start(bf16[64,256,128]{2,1,0:T(8,128)(2,1)} %scatter.1.own), channel_id=1, source_target_pairs={{0,1},{1,0},{2,3},{3,2},{4,5},{5,4},{6,7},{7,6},{8,9},{9,8},{10,11... | collective-permute-start | bytes 12582920 | tf_op jit(solution)/shard_map/ppermute | solution.py:462
  63.9 3.8 %inverse.1 = s32[128,128]{1,0:T(8,128)S(1)} custom-call(s32[64,128]{1,0:T(8,128)S(1)} %bitcast.27), custom_call_target="tpu_custom_call" | custom-call | tf_op jit(solution)/shard_map/inverse/pallas_call | solution.py:420
  67.7 1.5 dynamic-slice_bitcast_fusion
  70.0 1.3 collective-permute-start.4
  71.3 3.0 %collective-permute-start.3 = (bf16[3,1,128,128]{3,2,1,0:T(8,128)(2,1)S(1)}, bf16[3,1,128,128]{3,2,1,0:T(8,128)(2,1)S(1)}, u32[]{:S(2)}, u32[]{:S(2)}) collective-permute-start(bf16[3,1,128,128]{3,2,1,0:T(8,128)(2,1)S(1)} %pad_maximum_fusion.2), channel_id=1, source_target_pairs={{0,1},{1,2},{2,3},{4,5},{5,6},{6,7},{8,9},{9,10},{10,11},{12,13},{... | collective-permute-start | bytes 294920 | tf_op jit(solution)/shard_map/ppermute | solution.py:369
  75.1 0.8 copy.12.first
  76.0 16.8 %spectrum.1 = (bf16[64,256,128]{2,1,0:T(8,128)(2,1)}, bf16[64,256,128]{2,1,0:T(8,128)(2,1)}) custom-call(bf16[64,256,128]{2,1,0:T(8,128)(2,1)} %scatter.1.own, bf16[64,256,128]{2,1,0:T(8,128)(2,1)} %collective-permute-done.2.other, f32[64,128,512]{2,1,0:T(8,128)} %weights.1, bf16[128,256]{1,0:T(8,128)(2,1)} %copy.11.third, ...), custom_call_target="tpu_custom_call" | custom-call | tf_op jit(solution)/shard_map/spectrum/pallas_call | solution.py:468
  92.8 1.3 collective-permute-start.5
  94.1 2.2 %copy-done = bf16[512,4096]{1,0:T(8,128)(2,1)S(1)} copy-done((bf16[512,4096]{1,0:T(8,128)(2,1)S(1)}, bf16[512,4096]{1,0:T(8,128)(2,1)}, u32[]{:S(2)}) %copy-start) | copy-done | bytes 4194328
  96.3 5.4 %near.1 = f32[128,128]{1,0:T(8,128)S(1)} custom-call(s32[512]{0:T(512)S(1)} %fusion.11.source, bf16[512,4096]{1,0:T(8,128)(2,1)S(1)} %copy-done, s32[1,512]{1,0:T(1,128)S(1)} %get-tuple-element.42.target, bf16[9,128,128]{2,1,0:T(8,128)(2,1)S(1)} %bitcast.25), custom_call_target="tpu_custom_call" | custom-call | tf_op jit(solution)/shard_map/near/pallas_call | solution.py:494
  101.7 26.8 %sample.1 = bf16[32,64,128]{2,1,0:T(8,128)(2,1)} custom-call(s32[1]{0:T(128)} %bitcast.place, s32[4096]{0:T(1024)} %get-tuple-element.41.shift, s32[4096]{0:T(1024)} %get-tuple-element.44.start, bf16[32,80,128]{2,1,0:T(8,128)(2,1)} %copy-done.7, bf16[64,256,128]{2,1,0:T(8,128)(2,1)} %get-tuple-element.21.own, ...), custom_call_target="tpu_custom_call" | custom-call | tf_op jit(solution)/shard_map/sample/pallas_call | solution.py:513
  128.5 23.5 %all_to_all.10.values = bf16[32,64,128]{2,1,0:T(8,128)(2,1)S(1)} all-to-all(bf16[32,64,128]{2,1,0:T(8,128)(2,1)} %sample.1), channel_id=1, replica_groups=mesh['row'=8,'col'=4] {'row','col'}, dimensions={0} | all-to-all | bytes 1048576 | tf_op jit(solution)/shard_map/all_to_all | solution.py:526
  152.0 4.8 %finish.1 = f32[64,128]{1,0:T(8,128)} custom-call(bf16[32,64,128]{2,1,0:T(8,128)(2,1)S(1)} %all_to_all.10.values, bf16[128,4096]{1,0:T(8,128)(2,1)S(1)} %copy-done.2, f32[128,128]{1,0:T(8,128)S(1)} %near.1, s32[128,128]{1,0:T(8,128)S(1)} %inverse.1), custom_call_target="tpu_custom_call" | custom-call | tf_op jit(solution)/shard_map/finish/pallas_call | solution.py:528
  (35 shorter events, 3.8 us)
Async XLA Ops:
  0.0 1.2 copy-start.1
  1.2 0.8 copy-start.3
  2.0 0.7 copy-start.5
  2.7 0.7 copy-start.6
  3.4 60.5 %copy-start.4 = (s32[8192]{0:T(1024)S(1)}, s32[8192]{0:T(1024)}, u32[]{:S(2)}) copy-start(s32[8192]{0:T(1024)} %param.10) | copy-start | bytes 98308
  7.2 62.8 %copy-start.8 = (bf16[512,512]{0,1:T(8,128)(2,1)S(1)}, bf16[512,512]{0,1:T(8,128)(2,1)}, u32[]{:S(2)}) copy-start(bf16[512,512]{0,1:T(8,128)(2,1)} %constant.142.clone) | copy-start | bytes 1572868
  8.1 25.5 %all-to-all-start = ((bf16[32,80,128]{2,1,0:T(8,128)(2,1)}), bf16[32,80,128]{2,1,0:T(8,128)(2,1)S(1)}, u32[]{:S(2)}, u32[]{:S(2)}) async-start(bf16[32,80,128]{2,1,0:T(8,128)(2,1)} %broadcast_in_dim.4), calls=%async_computation | async-start | bytes 1310720 | tf_op jit(solution)/shard_map/all_to_all | solution.py:419
  15.4 8.2 %collective-permute-start.1 = (bf16[1,1,128,128]{3,2,1,0:T(8,128)(2,1)S(1)}, bf16[1,1,128,128]{3,2,1,0:T(8,128)(2,1)S(1)}, u32[]{:S(2)}, u32[]{:S(2)}) collective-permute-start(bf16[1,1,128,128]{3,2,1,0:T(8,128)(2,1)S(1)} %bitcast.28), channel_id=1, source_target_pairs={{4,0},{8,4},{12,8},{16,12},{20,16},{24,20},{28,24},{5,1},{9,5},{13... | collective-permute-start | bytes 98312 | tf_op jit(solution)/shard_map/ppermute | solution.py:370
  16.7 6.9 %collective-permute-start = (bf16[1,1,128,128]{3,2,1,0:T(8,128)(2,1)S(1)}, bf16[1,1,128,128]{3,2,1,0:T(8,128)(2,1)S(1)}, u32[]{:S(2)}, u32[]{:S(2)}) collective-permute-start(bf16[1,1,128,128]{3,2,1,0:T(8,128)(2,1)S(1)} %bitcast.29), channel_id=1, source_target_pairs={{0,4},{4,8},{8,12},{12,16},{16,20},{20,24},{24,28},{1,5},{5,9},{9,... | collective-permute-start | bytes 98312 | tf_op jit(solution)/shard_map/ppermute | solution.py:369
  33.6 0.9 copy-start.7
  60.7 15.2 %collective-permute-start.2 = (bf16[64,256,128]{2,1,0:T(8,128)(2,1)}, bf16[64,256,128]{2,1,0:T(8,128)(2,1)}, u32[]{:S(2)}, u32[]{:S(2)}) collective-permute-start(bf16[64,256,128]{2,1,0:T(8,128)(2,1)} %scatter.1.own), channel_id=1, source_target_pairs={{0,1},{1,0},{2,3},{3,2},{4,5},{5,4},{6,7},{7,6},{8,9},{9,8},{10,11... | collective-permute-start | bytes 12582920 | tf_op jit(solution)/shard_map/ppermute | solution.py:462
  70.0 5.9 %collective-permute-start.4 = (bf16[3,1,128,128]{3,2,1,0:T(8,128)(2,1)S(1)}, bf16[3,1,128,128]{3,2,1,0:T(8,128)(2,1)S(1)}, u32[]{:S(2)}, u32[]{:S(2)}) collective-permute-start(bf16[3,1,128,128]{3,2,1,0:T(8,128)(2,1)S(1)} %pad_maximum_fusion.2), channel_id=1, source_target_pairs={{1,0},{2,1},{3,2},{5,4},{6,5},{7,6},{9,8},{10,9},{11,10},{13,12},{... | collective-permute-start | bytes 294920 | tf_op jit(solution)/shard_map/ppermute | solution.py:370
  71.3 4.6 %collective-permute-start.3 = (bf16[3,1,128,128]{3,2,1,0:T(8,128)(2,1)S(1)}, bf16[3,1,128,128]{3,2,1,0:T(8,128)(2,1)S(1)}, u32[]{:S(2)}, u32[]{:S(2)}) collective-permute-start(bf16[3,1,128,128]{3,2,1,0:T(8,128)(2,1)S(1)} %pad_maximum_fusion.2), channel_id=1, source_target_pairs={{0,1},{1,2},{2,3},{4,5},{5,6},{6,7},{8,9},{9,10},{10,11},{12,13},{... | collective-permute-start | bytes 294920 | tf_op jit(solution)/shard_map/ppermute | solution.py:369
  76.0 18.1 %copy-start.9 = (s32[2,512]{1,0:T(2,128)S(1)}, s32[2,512]{1,0:T(2,128)}, u32[]{:S(2)}) copy-start(s32[2,512]{1,0:T(2,128)} %param.15) | copy-start | bytes 12292
  92.8 8.9 %collective-permute-start.5 = (bf16[64,256,128]{2,1,0:T(8,128)(2,1)}, bf16[64,256,128]{2,1,0:T(8,128)(2,1)}, u32[]{:S(2)}, u32[]{:S(2)}) collective-permute-start(bf16[64,256,128]{2,1,0:T(8,128)(2,1)} %get-tuple-element.22), channel_id=1, source_target_pairs={{0,1},{1,0},{2,3},{3,2},{4,5},{5,4},{6,7},{7,6},{8,9},{9,8},{10,11... | collective-permute-start | bytes 12582920 | tf_op jit(solution)/shard_map/ppermute | solution.py:486
  94.1 2.2 %copy-start = (bf16[512,4096]{1,0:T(8,128)(2,1)S(1)}, bf16[512,4096]{1,0:T(8,128)(2,1)}, u32[]{:S(2)}) copy-start(bf16[512,4096]{1,0:T(8,128)(2,1)} %near_blocks.1) | copy-start | bytes 12582916
  101.6 50.4 %copy-start.2 = (bf16[128,4096]{1,0:T(8,128)(2,1)S(1)}, bf16[128,4096]{1,0:T(8,128)(2,1)}, u32[]{:S(2)}) copy-start(bf16[128,4096]{1,0:T(8,128)(2,1)} %interpolate.1) | copy-start | bytes 3145732

commit v5 on v4

--- a/solution.py
+++ b/solution.py
@@ -23,6 +23,9 @@
 SLAB = PAD + QUAD * PIECE + 32
 CELLS = PAD + QUAD * G + 16
 ZC = 32
+STRIDE = G + 1
+BATCH = 8
+UNROLL = 16
 MB = 1 << 20
 NT = (((1,), (1,)), ((), ()))
 
@@ -84,9 +87,29 @@
     return rows, lanes
 
 
-def project_kernel(charges, order, project, anchors, charge_out, patch_out, table, doubled):
+def project_kernel(
+    charges_in,
+    order_in,
+    project_in,
+    anchors_in,
+    charge_out,
+    patch_out,
+    charges,
+    order,
+    project,
+    anchors,
+    table,
+    doubled,
+    sems,
+):
     blocks = charge_out.shape[0]
     groups = blocks // GROUP
+    pairs = ((charges_in, charges), (order_in, order), (project_in, project), (anchors_in, anchors))
+    copies = [pltpu.make_async_copy(a, b, sems.at[n]) for n, (a, b) in enumerate(pairs)]
+    for copy in copies:
+        copy.start()
+    copies[0].wait()
+    copies[1].wait()
     table[...] = charges[...].astype(jnp.float32)
     strips = table.shape[0]
     upper = order[...] // LANES
@@ -103,6 +126,8 @@
     doubled[pl.ds(1, strips, stride=2), :] = jnp.where(left, turned, slots)
     twice = doubled[...]
     charge_out[...] = twice.astype(jnp.bfloat16)
+    copies[2].wait()
+    copies[3].wait()
     patch = block_sums(project, twice)
     patch = jnp.where(iota(patch.shape, 1) < PTS, patch, 0.0).astype(jnp.bfloat16)
     rows, lanes = patch_places(blocks)
@@ -188,7 +213,9 @@
     return jnp.broadcast_to((cells >= 0.0) & (cells < LANES), (16, LANES))
 
 
-def scatter_kernel(cols, place, shift, start, patches, table, out, columns, *slabs):
+def scatter_kernel(
+    cols, place, shift, start, patches, table, third, own_out, other_out, lines, *slabs
+):
     half = place[0]
     chunk = pl.program_id(0)
     devices, held, _ = patches.shape
@@ -232,69 +259,96 @@
                     slabs[s][pl.ds(at_next, 16), :] = far
                 return carry
 
-            lax.fori_loop(0, GROUP, one, 0, unroll=4)
+            lax.fori_loop(0, GROUP, one, 0, unroll=UNROLL)
 
         tile_loop(half, devices // cols, cols, groups, tile)
 
-    for z in range(0, ZC, QUAD):
-        base = pl.multiple_of((chunk * (ZC // QUAD) + z // QUAD) * SLAB, 8)
-        planes = []
-        for q in range(QUAD):
-            parts = []
-            for s in range(SLABS):
-                part = slabs[s][pl.ds(base + (PAD + q), PIECE, stride=QUAD), :]
-                if s > 0:
-                    at = base + (PAD + QUAD * PIECE + q)
-                    over = slabs[s - 1][pl.ds(at, 8, stride=QUAD), :]
-                    part = jnp.concatenate([part[:8] + over, part[8:]], axis=0)
-                parts.append(part.astype(jnp.bfloat16))
-            planes.append(jnp.concatenate(parts, axis=0))
-        lines = dot(table[...], jnp.concatenate(planes, axis=1))
-        for q in range(QUAD):
-            columns[pl.ds(z + q, freqs, stride=ZC), :] = lines[:, LANES * q : LANES * q + LANES]
-    out[...] = columns[...].reshape(freqs, ZC, LANES).astype(jnp.bfloat16)
-
-
-def spectrum_kernel(
-    own, other, weights, third, third_back, first, first_back, own_out, other_out, held
+    @pl.when(chunk < G // ZC)
+    def _():
+        for z in range(0, ZC, QUAD):
+            base = pl.multiple_of((chunk * (ZC // QUAD) + z // QUAD) * SLAB, 8)
+            planes = []
+            for q in range(QUAD):
+                parts = []
+                for s in range(SLABS):
+                    part = slabs[s][pl.ds(base + (PAD + q), PIECE, stride=QUAD), :]
+                    if s > 0:
+                        at = base + (PAD + QUAD * PIECE + q)
+                        over = slabs[s - 1][pl.ds(at, 8, stride=QUAD), :]
+                        part = jnp.concatenate([part[:8] + over, part[8:]], axis=0)
+                    parts.append(part.astype(jnp.bfloat16))
+                planes.append(jnp.concatenate(parts, axis=0))
+            field = dot(table[...], jnp.concatenate(planes, axis=1))
+            for q in range(QUAD):
+                part = field[:, LANES * q : LANES * q + LANES]
+                lines[pl.ds(chunk * ZC + z + q, freqs, stride=STRIDE), :] = part
+
+    @pl.when(chunk >= G // ZC)
+    def _():
+        fs = third.shape[0] // 2
+        for g in range(0, BATCH, 2):
+            pair = []
+            for n in (g, g + 1):
+                at = ((chunk - G // ZC) * BATCH + n) * STRIDE
+                pair.append(lines[pl.ds(at, G), :].astype(jnp.bfloat16))
+            field = dot(third[...], jnp.concatenate(pair, axis=1)).astype(jnp.bfloat16)
+            for n in range(2):
+                own_out[g + n] = field[:fs, LANES * n : LANES * n + LANES]
+                other_out[g + n] = field[fs:, LANES * n : LANES * n + LANES]
+
+
+def spectrum_kernel(own, other, weights, first, first_back, own_out, other_out):
+    count, freqs, _ = weights.shape
+    step = max(1, G // freqs)
+    rows = step * freqs
+    for g in range(0, count, step):
+        part = slice(g, g + step)
+        line = jnp.concatenate(
+            [own[part].reshape(rows, LANES), other[part].reshape(rows, LANES)], axis=1
+        )
+        s = dot(line, first[...]) * weights[part].reshape(rows, P_SIZE)
+        line = dot(s.astype(jnp.bfloat16), first_back[...]).astype(jnp.bfloat16)
+        own_out[part] = line[:, :LANES].reshape(step, freqs, LANES)
+        other_out[part] = line[:, LANES:].reshape(step, freqs, LANES)
+
+
+def sample_kernel(
+    cols, place, shift, start, patches, own, other, table, third, out, lines, cells
 ):
-    count, freqs, _ = weights.shape
-    for g in range(count):
-        line = jnp.concatenate([own[g], other[g]], axis=1)
-        held[g * freqs : (g + 1) * freqs] = dot(third[...], line).astype(jnp.bfloat16)
-    step = max(1, G // freqs)
-    for g in range(0, count, step):
-        rows = slice(g * freqs, (g + step) * freqs)
-        s = dot(held[rows], first[...]) * weights[g : g + step].reshape(step * freqs, P_SIZE)
-        held[rows] = dot(s.astype(jnp.bfloat16), first_back[...]).astype(jnp.bfloat16)
-    for g in range(count):
-        line = dot(third_back[...], held[g * freqs : (g + 1) * freqs]).astype(jnp.bfloat16)
-        own_out[g] = line[:, :LANES]
-        other_out[g] = line[:, LANES:]
-
-
-def sample_kernel(cols, place, shift, start, patches, own, other, table, out, columns, cells):
     half = place[0]
-    chunk = pl.program_id(0)
+    step = pl.program_id(0)
     devices, held, _ = out.shape
     groups = held // 16
     blocks = groups * GROUP
     freqs = table.shape[1]
+    batches = freqs // BATCH
+    chunk = step - batches
     owner = iota((16, LANES), 1) // 4
     plane = iota((16, LANES), 0) % QUAD
-    both = own[...].astype(jnp.float32) + other[...].astype(jnp.float32)
-    columns[...] = both.reshape(freqs * ZC, LANES)
-    for z in range(0, ZC, QUAD):
-        planes = [
-            columns[pl.ds(z + q, freqs, stride=ZC), :].astype(jnp.bfloat16) for q in range(QUAD)
-        ]
-        field = dot(table[...], jnp.concatenate(planes, axis=1))
-        base = pl.multiple_of((chunk * (ZC // QUAD) + z // QUAD) * CELLS, 8)
-        for q in range(QUAD):
-            part = field[:, LANES * q : LANES * q + LANES]
-            cells[pl.ds(base + (PAD + q), G, stride=QUAD), :] = part
-
-    @pl.when(chunk == pl.num_programs(0) - 1)
+
+    @pl.when(step < batches)
+    def _():
+        for g in range(0, BATCH, 2):
+            pair = [jnp.concatenate([own[n], other[n]], axis=0) for n in (g, g + 1)]
+            field = dot(third[...], jnp.concatenate(pair, axis=1))
+            for n in range(2):
+                at = (step * BATCH + g + n) * STRIDE
+                lines[pl.ds(at, G), :] = field[:, LANES * n : LANES * n + LANES]
+
+    @pl.when(step >= batches)
+    def _():
+        for z in range(0, ZC, QUAD):
+            planes = [
+                lines[pl.ds(chunk * ZC + z + q, freqs, stride=STRIDE), :].astype(jnp.bfloat16)
+                for q in range(QUAD)
+            ]
+            field = dot(table[...], jnp.concatenate(planes, axis=1))
+            base = pl.multiple_of((chunk * (ZC // QUAD) + z // QUAD) * CELLS, 8)
+            for q in range(QUAD):
+                part = field[:, LANES * q : LANES * q + LANES]
+                cells[pl.ds(base + (PAD + q), G, stride=QUAD), :] = part
+
+    @pl.when(step == pl.num_programs(0) - 1)
     def _():
         out[...] = jnp.zeros_like(out)
 
@@ -313,7 +367,7 @@
                 return tuple(new)
 
             zero = (jnp.zeros((16, LANES), jnp.float32),) * SLABS
-            sums = lax.fori_loop(0, GROUP, one, zero, unroll=4)
+            sums = lax.fori_loop(0, GROUP, one, zero, unroll=UNROLL)
             for s, d in enumerate(numbers):
                 inside = lanes_inside(patches, d, t, groups, half)
                 out[d, pl.ds(pl.multiple_of(16 * t, 16), 16), :] = jnp.where(
@@ -403,9 +457,15 @@
             struct((blocks, LANES), jnp.bfloat16),
             struct((held, LANES), jnp.bfloat16),
         ),
+        in_specs=[pl.BlockSpec(memory_space=pltpu.HBM)] * 4,
         scratch_shapes=[
+            pltpu.VMEM((strips, LANES), jnp.bfloat16),
+            pltpu.VMEM((strips, LANES), jnp.int32),
+            pltpu.VMEM(project.shape, jnp.bfloat16),
+            pltpu.VMEM(patch_anchor.shape, jnp.int32),
             pltpu.VMEM((strips, LANES), jnp.float32),
             pltpu.VMEM((blocks, LANES), jnp.float32),
+            pltpu.SemaphoreType.DMA((4,)),
         ],
         compiler_params=params(32),
         name="project",
@@ -425,7 +485,21 @@
     )(order)
 
     around = beside(block_charges[None, None], "row", 0)
-    gathered, around = lax.optimization_barrier((gathered, around))
+    cas = jnp.asarray(CAS)
+    second = lax.dynamic_slice_in_dim(cas[:, :G], row_at * gs, gs, axis=0)
+    third = jnp.concatenate(
+        [lax.dynamic_slice_in_dim(cas[:, :G], c * fs, fs, axis=0) for c in (col_at, col_at ^ 1)],
+        axis=0,
+    )
+    first = jnp.concatenate(
+        [lax.dynamic_slice_in_dim(cas, h * LANES, LANES, axis=0) for h in (half, 1 - half)],
+        axis=0,
+    )
+    (gathered, around, inverse, second, second_back, third, third_back, first, first_back) = (
+        lax.optimization_barrier(
+            (gathered, around, inverse, second, second.T, third, third.T, first, first.T)
+        )
+    )
     around = beside(around, "col", 1).reshape(9, blocks, LANES)
     anchors = gathered[:, 17 * groups : 17 * groups + 3].astype(jnp.int32)
     lane = 4 * (jnp.arange(blocks, dtype=jnp.int32) % GROUP)
@@ -438,51 +512,41 @@
     cell_at = (group * CELLS + inner).reshape(devices * blocks)
     place = half.astype(jnp.int32).reshape(1)
 
-    table = jnp.asarray(CAS)
-    second = lax.dynamic_slice_in_dim(table[:, :G], row_at * gs, gs, axis=0)
-    third = lax.dynamic_slice_in_dim(table[:, :G], col_at * fs, fs, axis=0)
-    mine = lax.dynamic_slice_in_dim(table, half * LANES, LANES, axis=0)
-    yours = lax.dynamic_slice_in_dim(table, (1 - half) * LANES, LANES, axis=0)
-    first = jnp.concatenate([mine, yours], axis=0)
+    smem = pl.BlockSpec(memory_space=pltpu.SMEM)
     chunks = G // ZC
-    smem = pl.BlockSpec(memory_space=pltpu.SMEM)
-    line_block = pl.BlockSpec((gs, ZC, LANES), lambda z: (0, z, 0))
-    lines_type = struct((gs, G, LANES), jnp.bfloat16)
-    own = pl.pallas_call(
+    batches = gs // BATCH
+    lines_type = struct((gs, fs, LANES), jnp.bfloat16)
+    late = pl.BlockSpec((BATCH, fs, LANES), lambda n: (jnp.maximum(n - chunks, 0), 0, 0))
+    own, other = pl.pallas_call(
         functools.partial(scatter_kernel, cols),
-        grid=(chunks,),
-        in_specs=[smem] * 3 + [whole(gathered.shape), whole(second.shape)],
-        out_specs=line_block,
-        out_shape=lines_type,
-        scratch_shapes=[pltpu.VMEM((gs * ZC, LANES), jnp.float32)]
+        grid=(chunks + batches,),
+        in_specs=[smem] * 3 + [whole(gathered.shape), whole(second.shape), whole(third.shape)],
+        out_specs=(late, late),
+        out_shape=(lines_type, lines_type),
+        scratch_shapes=[pltpu.VMEM((gs * STRIDE, LANES), jnp.float32)]
         + [pltpu.VMEM(((G // QUAD + 1) * SLAB, LANES), jnp.float32)] * SLABS,
-        compiler_params=params(56),
+        compiler_params=params(58),
         name="scatter",
-    )(place, forth, slab_at, gathered, second)
-    other = lax.ppermute(own, "col", mates)
-
-    other, around, inverse = lax.optimization_barrier((other, around, inverse))
-
-    batch = 8
-    part = lambda shape: pl.BlockSpec((batch,) + shape, lambda n: (n, 0, 0))
+    )(place, forth, slab_at, gathered, second, third)
+    other = lax.ppermute(other, "col", mates)
+    other, around = lax.optimization_barrier((other, around))
+
+    part = lambda shape: pl.BlockSpec((BATCH,) + shape, lambda n: (n, 0, 0))
     own, other = pl.pallas_call(
         spectrum_kernel,
-        grid=(gs // batch,),
+        grid=(batches,),
         in_specs=[
-            part((G, LANES)),
-            part((G, LANES)),
+            part((fs, LANES)),
+            part((fs, LANES)),
             part((fs, P_SIZE)),
-            whole((fs, G)),
-            whole((G, fs)),
             whole((G, P_SIZE)),
             whole((P_SIZE, G)),
         ],
-        out_specs=(part((G, LANES)), part((G, LANES))),
+        out_specs=(part((fs, LANES)), part((fs, LANES))),
         out_shape=(lines_type, lines_type),
-        scratch_shapes=[pltpu.VMEM((batch * fs, G), jnp.bfloat16)],
         compiler_params=params(56),
         name="spectrum",
-    )(own, other, kernel_spectrum, third, third.T, first, first.T)
+    )(own, other, kernel_spectrum, first, first_back)
     other = lax.ppermute(other, "col", mates)
 
     source = near_pairs[1]
@@ -510,19 +574,21 @@
         name="near",
     )(wanted, near_blocks, target.reshape(1, pairs), around)
     other, near = lax.optimization_barrier((other, near))
+    early = pl.BlockSpec((BATCH, fs, LANES), lambda n: (jnp.minimum(n, batches - 1), 0, 0))
     values = pl.pallas_call(
         functools.partial(sample_kernel, cols),
-        grid=(chunks,),
-        in_specs=[smem] * 3 + [whole(gathered.shape), line_block, line_block, whole((G, gs))],
+        grid=(batches + chunks,),
+        in_specs=[smem] * 3
+        + [whole(gathered.shape), early, early, whole((G, gs)), whole((G, 2 * fs))],
         out_specs=whole((devices, 16 * groups, LANES)),
         out_shape=struct((devices, 16 * groups, LANES), jnp.bfloat16),
         scratch_shapes=[
-            pltpu.VMEM((gs * ZC, LANES), jnp.float32),
+            pltpu.VMEM((gs * STRIDE, LANES), jnp.float32),
             pltpu.VMEM(((G // QUAD + 1) * CELLS, LANES), jnp.float32),
         ],
-        compiler_params=params(56),
+        compiler_params=params(58),
         name="sample",
-    )(place, back, cell_at, gathered, own, other, second.T)
+    )(place, back, cell_at, gathered, own, other, second_back, third_back)
     values = lax.all_to_all(values, axes, split_axis=0, concat_axis=0, tiled=True)
 
     result = pl.pallas_call(

time: 158 us -> 136 us (0.86)
  Pallas kernels: 87.7 us -> 71.4 us
  waiting for transfers between devices: 9.99 us -> 6.32 us
  blocking collectives: 23.5 us -> 21.8 us
    pallas_call x3, Pallas kernels: 69.9 us -> 53.6 us  [the longest x1 20.4 us: body(): pl.pallas_call(functools.partial(sample_kernel, cols), grid=(batches + ch...]
    all_to_all x1, waiting for transfers between devices: 9.97 us -> 6.23 us  [body(): lax.all_to_all(copies, axes, split_axis=0, concat_axis=0, tiled=True)]
    ppermute x1 -> x0, starting transfers between devices: 3.19 us -> none  [body(): other = lax.ppermute(own, 'col', mates)]
    unnamed x20 -> x26, local copies, waits for them, and re-layouts: 5.58 us -> 8.26 us
    optimization_barrier x0 -> x3, local copies, waits for them, and re-layouts: none -> 2.34 us  [body(): lax.optimization_barrier((gathered, around, inverse, second, second.T, th...]
    transpose x2 -> x1, local copies, waits for them, and re-layouts: 3.04 us -> 0.72 us  [body(): gathered, around, inverse, second, second_back, third, third_back, first,...]
    ppermute x1 -> x2, starting transfers between devices: 1.26 us -> 3.4 us  [body(): other = lax.ppermute(other, 'col', mates)]
    all_to_all x1, blocking collectives: 23.5 us -> 21.8 us  [body(): lax.all_to_all(values, axes, split_axis=0, concat_axis=0, tiled=True)]
  transfers between devices with their start and end apart: 7 -> 7, of which waited for: 1 -> 2; matrix products, arithmetic and copies ran while one was open for 4% -> 2% of each run, Pallas kernels for 6% -> 7%
where the time goes in v5:
time: 136 us; the launch traced here: 135 us
  Pallas kernels  71.4 us (53%)
  blocking collectives  21.8 us (16%)
  starting transfers between devices  20.9 us (15%)
  local copies, waits for them, and re-layouts  12.3 us (9%)
  waiting for transfers between devices  6.32 us (5%)
  other arithmetic  2.23 us (2%)
    all_to_all x1, blocking collectives, body(): lax.all_to_all(values, axes, split_axis=0, concat_axis=0, tiled=True)  21.8 us
    pallas_call x1, Pallas kernels, body(): pl.pallas_call(functools.partial(sample_kernel, cols), grid=(batches + ch...  20.4 us
    pallas_call x1, Pallas kernels, body(): pl.pallas_call(functools.partial(scatter_kernel, cols), grid=(chunks + ba...  20 us
    pallas_call x1, Pallas kernels, body(): pl.pallas_call(spectrum_kernel, grid=(batches,), in_specs=[part((fs, LANE...  13.3 us
    unnamed x26, local copies, waits for them, and re-layouts  8.26 us
    ppermute x2, starting transfers between devices, beside(): before = lax.ppermute(array, axis, up)  7.58 us
    all_to_all x1, starting transfers between devices, body(): lax.all_to_all(copies, axes, split_axis=0, concat_axis=0, tiled=True)  7.3 us
    all_to_all x1, waiting for transfers between devices, body(): lax.all_to_all(copies, axes, split_axis=0, concat_axis=0, tiled=True)  6.23 us
  transfers between devices with their start and end apart: 7, of which 2 were waited for; matrix products, arithmetic and copies ran while one was open for 2% of the time, Pallas kernels for 7%

profile of v5, /device:TPU:0, one launch (start us, length us, event | category | flops | bytes accessed | tf_op | source)
XLA Modules:
  0.0 135.1 jit_solution(17864908659084703934)
XLA Ops:
  0.0 1.2 copy-done.1
  1.2 0.8 copy-done.3
  3.4 4.0 %project.1 = (bf16[128,128]{1,0:T(8,128)(2,1)S(1)}, bf16[80,128]{1,0:T(8,128)(2,1)S(1)}) custom-call(bf16[64,128]{1,0:T(8,128)(2,1)S(1)} %bitcast.31, s32[64,128]{1,0:T(8,128)S(1)} %bitcast.26, bf16[128,4096]{1,0:T(8,128)(2,1)S(1)} %copy-done.1, s32[3,128]{1,0:T(4,128)S(1)} %copy-done.6), custom_call_target="tpu_custom_call" | custom-call | tf_op jit(solution)/shard_map/project/pallas_call | solution.py:454
  7.4 0.9 broadcast_in_dim.4
  8.3 7.3 %all-to-all-start = ((bf16[32,80,128]{2,1,0:T(8,128)(2,1)}), bf16[32,80,128]{2,1,0:T(8,128)(2,1)S(1)}, u32[]{:S(2)}, u32[]{:S(2)}) async-start(bf16[32,80,128]{2,1,0:T(8,128)(2,1)} %broadcast_in_dim.4), calls=%async_computation | async-start | bytes 1310720 | tf_op jit(solution)/shard_map/all_to_all | solution.py:479
  15.6 1.3 collective-permute-start.1
  16.9 4.5 %collective-permute-start = (bf16[1,1,128,128]{3,2,1,0:T(8,128)(2,1)S(1)}, bf16[1,1,128,128]{3,2,1,0:T(8,128)(2,1)S(1)}, u32[]{:S(2)}, u32[]{:S(2)}) collective-permute-start(bf16[1,1,128,128]{3,2,1,0:T(8,128)(2,1)S(1)} %bitcast.29), channel_id=1, source_target_pairs={{0,4},{4,8},{8,12},{12,16},{16,20},{20,24},{24,28},{1,5},{5,9},{9,... | collective-permute-start | bytes 98312 | tf_op jit(solution)/shard_map/ppermute | solution.py:423
  23.7 3.8 %inverse.1 = s32[128,128]{1,0:T(8,128)S(1)} custom-call(s32[64,128]{1,0:T(8,128)S(1)} %bitcast.27), custom_call_target="tpu_custom_call" | custom-call | tf_op jit(solution)/shard_map/inverse/pallas_call | solution.py:480
  27.5 6.2 %all-to-all-done.patches = bf16[32,80,128]{2,1,0:T(8,128)(2,1)S(1)} async-done(((bf16[32,80,128]{2,1,0:T(8,128)(2,1)}), bf16[32,80,128]{2,1,0:T(8,128)(2,1)S(1)}, u32[]{:S(2)}, u32[]{:S(2)}) %all-to-all-start) | async-done | bytes 655392 | tf_op jit(solution)/shard_map/all_to_all | solution.py:479
  34.6 0.8 copy.11.third
  36.0 20.0 %scatter.1 = (bf16[64,128,128]{2,1,0:T(8,128)(2,1)}, bf16[64,128,128]{2,1,0:T(8,128)(2,1)}) custom-call(s32[1]{0:T(128)} %bitcast.place, s32[4096]{0:T(1024)} %get-tuple-element.58.shift, s32[4096]{0:T(1024)} %get-tuple-element.63.start, bf16[32,80,128]{2,1,0:T(8,128)(2,1)} %copy-done.7, bf16[64,256]{1,0:T(8,128)(2,1)} %copy.10.table, ...), custom_call_target="tpu_custom_call" | custom-call | tf_op jit(solution)/shard_map/scatter/pallas_call | solution.py:520
  56.0 1.5 %collective-permute-start.2 = (bf16[64,128,128]{2,1,0:T(8,128)(2,1)}, bf16[64,128,128]{2,1,0:T(8,128)(2,1)S(1)}, u32[]{:S(2)}, u32[]{:S(2)}) collective-permute-start(bf16[64,128,128]{2,1,0:T(8,128)(2,1)} %get-tuple-element.30), channel_id=1, source_target_pairs={{0,1},{1,0},{2,3},{3,2},{4,5},{5,4},{6,7},{7,6},{8,9},{9,8},{10,11... | collective-permute-start | bytes 6291464 | tf_op jit(solution)/shard_map/ppermute | solution.py:531
  57.4 1.3 collective-permute-start.4
  58.7 3.0 %collective-permute-start.3 = (bf16[3,1,128,128]{3,2,1,0:T(8,128)(2,1)S(1)}, bf16[3,1,128,128]{3,2,1,0:T(8,128)(2,1)S(1)}, u32[]{:S(2)}, u32[]{:S(2)}) collective-permute-start(bf16[3,1,128,128]{3,2,1,0:T(8,128)(2,1)S(1)} %pad_maximum_fusion.3), channel_id=1, source_target_pairs={{0,1},{1,2},{2,3},{4,5},{5,6},{6,7},{8,9},{9,10},{10,11},{12,13},{... | collective-permute-start | bytes 294920 | tf_op jit(solution)/shard_map/ppermute | solution.py:423
  61.8 0.8 copy.12.first
  62.8 1.4 %copy-done.9 = bf16[64,128,128]{2,1,0:T(8,128)(2,1)} copy-done((bf16[64,128,128]{2,1,0:T(8,128)(2,1)}, bf16[64,128,128]{2,1,0:T(8,128)(2,1)S(1)}, u32[]{:S(2)}) %copy-start.9) | copy-done | bytes 2097176
  64.1 13.3 %spectrum.1 = (bf16[64,128,128]{2,1,0:T(8,128)(2,1)}, bf16[64,128,128]{2,1,0:T(8,128)(2,1)}) custom-call(bf16[64,128,128]{2,1,0:T(8,128)(2,1)} %get-tuple-element.29.own, bf16[64,128,128]{2,1,0:T(8,128)(2,1)} %copy-done.9, f32[64,128,512]{2,1,0:T(8,128)} %weights.1, bf16[256,512]{1,0:T(8,128)(2,1)} %copy.12.first, bf16[512,256]{1,0:T(8,128)(2,1)} %get-tuple-element.34.first_back), custom_call_target="tpu_custom_call" | custom-call | tf_op jit(solution)/shard_map/spectrum/pallas_call | solution.py:535
  77.5 1.9 %collective-permute-start.5 = (bf16[64,128,128]{2,1,0:T(8,128)(2,1)}, bf16[64,128,128]{2,1,0:T(8,128)(2,1)S(1)}, u32[]{:S(2)}, u32[]{:S(2)}) collective-permute-start(bf16[64,128,128]{2,1,0:T(8,128)(2,1)} %get-tuple-element.36), channel_id=1, source_target_pairs={{0,1},{1,0},{2,3},{3,2},{4,5},{5,4},{6,7},{7,6},{8,9},{9,8},{10,11... | collective-permute-start | bytes 6291464 | tf_op jit(solution)/shard_map/ppermute | solution.py:550
  79.4 2.2 %copy-done = bf16[512,4096]{1,0:T(8,128)(2,1)S(1)} copy-done((bf16[512,4096]{1,0:T(8,128)(2,1)S(1)}, bf16[512,4096]{1,0:T(8,128)(2,1)}, u32[]{:S(2)}) %copy-start) | copy-done | bytes 4194328
  81.6 5.2 %near.1 = f32[128,128]{1,0:T(8,128)S(1)} custom-call(s32[512]{0:T(512)S(1)} %fusion.11.source, bf16[512,4096]{1,0:T(8,128)(2,1)S(1)} %copy-done, s32[1,512]{1,0:T(1,128)S(1)} %get-tuple-element.60.target, bf16[9,128,128]{2,1,0:T(8,128)(2,1)S(1)} %bitcast.25), custom_call_target="tpu_custom_call" | custom-call | tf_op jit(solution)/shard_map/near/pallas_call | solution.py:558
  86.9 1.3 copy-done.8
  88.2 20.4 %sample.1 = bf16[32,64,128]{2,1,0:T(8,128)(2,1)} custom-call(s32[1]{0:T(128)} %bitcast.place, s32[4096]{0:T(1024)} %get-tuple-element.59.shift, s32[4096]{0:T(1024)} %get-tuple-element.62.start, bf16[32,80,128]{2,1,0:T(8,128)(2,1)} %copy-done.7, bf16[64,128,128]{2,1,0:T(8,128)(2,1)} %get-tuple-element.35.own, bf16[64,128,128]{2,1,0:T(8,128)(2,1)} %copy-done.8, ...), custom_call_target="tpu_custom_call" | custom-call | tf_op jit(solution)/shard_map/sample/pallas_call | solution.py:578
  108.5 21.8 %all_to_all.10.values = bf16[32,64,128]{2,1,0:T(8,128)(2,1)S(1)} all-to-all(bf16[32,64,128]{2,1,0:T(8,128)(2,1)} %sample.1), channel_id=1, replica_groups=mesh['row'=8,'col'=4] {'row','col'}, dimensions={0} | all-to-all | bytes 1048576 | tf_op jit(solution)/shard_map/all_to_all | solution.py:592
  130.3 4.8 %finish.1 = f32[64,128]{1,0:T(8,128)} custom-call(bf16[32,64,128]{2,1,0:T(8,128)(2,1)S(1)} %all_to_all.10.values, bf16[128,4096]{1,0:T(8,128)(2,1)S(1)} %copy-done.2, f32[128,128]{1,0:T(8,128)S(1)} %near.1, s32[128,128]{1,0:T(8,128)S(1)} %inverse.1), custom_call_target="tpu_custom_call" | custom-call | tf_op jit(solution)/shard_map/finish/pallas_call | solution.py:594
  (42 shorter events, 5.3 us)
Async XLA Ops:
  0.0 1.2 copy-start.1
  1.2 0.8 copy-start.3
  2.0 0.7 copy-start.5
  2.7 0.7 copy-start.6
  3.4 18.1 %copy-start.10 = (bf16[512,256]{0,1:T(8,128)(2,1)S(1)}, bf16[512,256]{0,1:T(8,128)(2,1)}, u32[]{:S(2)}) copy-start(bf16[512,256]{0,1:T(8,128)(2,1)} %constant.143) | copy-start | bytes 786436
  3.4 19.5 %copy-start.11 = (bf16[512,512]{0,1:T(8,128)(2,1)S(1)}, bf16[512,512]{0,1:T(8,128)(2,1)}, u32[]{:S(2)}) copy-start(bf16[512,512]{0,1:T(8,128)(2,1)} %constant.142.clone) | copy-start | bytes 1572868
  7.4 16.3 %copy-start.4 = (s32[8192]{0:T(1024)S(1)}, s32[8192]{0:T(1024)}, u32[]{:S(2)}) copy-start(s32[8192]{0:T(1024)} %param.10) | copy-start | bytes 98308
  8.3 25.5 %all-to-all-start = ((bf16[32,80,128]{2,1,0:T(8,128)(2,1)}), bf16[32,80,128]{2,1,0:T(8,128)(2,1)S(1)}, u32[]{:S(2)}, u32[]{:S(2)}) async-start(bf16[32,80,128]{2,1,0:T(8,128)(2,1)} %broadcast_in_dim.4), calls=%async_computation | async-start | bytes 1310720 | tf_op jit(solution)/shard_map/all_to_all | solution.py:479
  15.6 11.9 %collective-permute-start.1 = (bf16[1,1,128,128]{3,2,1,0:T(8,128)(2,1)S(1)}, bf16[1,1,128,128]{3,2,1,0:T(8,128)(2,1)S(1)}, u32[]{:S(2)}, u32[]{:S(2)}) collective-permute-start(bf16[1,1,128,128]{3,2,1,0:T(8,128)(2,1)S(1)} %bitcast.28), channel_id=1, source_target_pairs={{4,0},{8,4},{12,8},{16,12},{20,16},{24,20},{28,24},{5,1},{9,5},{13... | collective-permute-start | bytes 98312 | tf_op jit(solution)/shard_map/ppermute | solution.py:424
  16.9 10.6 %collective-permute-start = (bf16[1,1,128,128]{3,2,1,0:T(8,128)(2,1)S(1)}, bf16[1,1,128,128]{3,2,1,0:T(8,128)(2,1)S(1)}, u32[]{:S(2)}, u32[]{:S(2)}) collective-permute-start(bf16[1,1,128,128]{3,2,1,0:T(8,128)(2,1)S(1)} %bitcast.29), channel_id=1, source_target_pairs={{0,4},{4,8},{8,12},{12,16},{16,20},{20,24},{24,28},{1,5},{5,9},{9,... | collective-permute-start | bytes 98312 | tf_op jit(solution)/shard_map/ppermute | solution.py:423
  33.8 2.3 %copy-start.7 = (bf16[32,80,128]{2,1,0:T(8,128)(2,1)}, bf16[32,80,128]{2,1,0:T(8,128)(2,1)S(1)}, u32[]{:S(2)}) copy-start(bf16[32,80,128]{2,1,0:T(8,128)(2,1)S(1)} %all-to-all-done.patches) | copy-start | bytes 1966084
  56.0 6.8 %collective-permute-start.2 = (bf16[64,128,128]{2,1,0:T(8,128)(2,1)}, bf16[64,128,128]{2,1,0:T(8,128)(2,1)S(1)}, u32[]{:S(2)}, u32[]{:S(2)}) collective-permute-start(bf16[64,128,128]{2,1,0:T(8,128)(2,1)} %get-tuple-element.30), channel_id=1, source_target_pairs={{0,1},{1,0},{2,3},{3,2},{4,5},{5,4},{6,7},{7,6},{8,9},{9,8},{10,11... | collective-permute-start | bytes 6291464 | tf_op jit(solution)/shard_map/ppermute | solution.py:531
  57.4 5.2 %collective-permute-start.4 = (bf16[3,1,128,128]{3,2,1,0:T(8,128)(2,1)S(1)}, bf16[3,1,128,128]{3,2,1,0:T(8,128)(2,1)S(1)}, u32[]{:S(2)}, u32[]{:S(2)}) collective-permute-start(bf16[3,1,128,128]{3,2,1,0:T(8,128)(2,1)S(1)} %pad_maximum_fusion.3), channel_id=1, source_target_pairs={{1,0},{2,1},{3,2},{5,4},{6,5},{7,6},{9,8},{10,9},{11,10},{13,12},{... | collective-permute-start | bytes 294920 | tf_op jit(solution)/shard_map/ppermute | solution.py:424
  58.7 4.0 %collective-permute-start.3 = (bf16[3,1,128,128]{3,2,1,0:T(8,128)(2,1)S(1)}, bf16[3,1,128,128]{3,2,1,0:T(8,128)(2,1)S(1)}, u32[]{:S(2)}, u32[]{:S(2)}) collective-permute-start(bf16[3,1,128,128]{3,2,1,0:T(8,128)(2,1)S(1)} %pad_maximum_fusion.3), channel_id=1, source_target_pairs={{0,1},{1,2},{2,3},{4,5},{5,6},{6,7},{8,9},{9,10},{10,11},{12,13},{... | collective-permute-start | bytes 294920 | tf_op jit(solution)/shard_map/ppermute | solution.py:423
  62.7 1.4 %copy-start.9 = (bf16[64,128,128]{2,1,0:T(8,128)(2,1)}, bf16[64,128,128]{2,1,0:T(8,128)(2,1)S(1)}, u32[]{:S(2)}) copy-start(bf16[64,128,128]{2,1,0:T(8,128)(2,1)S(1)} %collective-permute-done.2.other) | copy-start | bytes 6291460
  64.1 15.3 %copy-start.12 = (s32[2,512]{1,0:T(2,128)S(1)}, s32[2,512]{1,0:T(2,128)}, u32[]{:S(2)}) copy-start(s32[2,512]{1,0:T(2,128)} %param.15) | copy-start | bytes 12292
  77.5 9.4 %collective-permute-start.5 = (bf16[64,128,128]{2,1,0:T(8,128)(2,1)}, bf16[64,128,128]{2,1,0:T(8,128)(2,1)S(1)}, u32[]{:S(2)}, u32[]{:S(2)}) collective-permute-start(bf16[64,128,128]{2,1,0:T(8,128)(2,1)} %get-tuple-element.36), channel_id=1, source_target_pairs={{0,1},{1,0},{2,3},{3,2},{4,5},{5,4},{6,7},{7,6},{8,9},{9,8},{10,11... | collective-permute-start | bytes 6291464 | tf_op jit(solution)/shard_map/ppermute | solution.py:550
  79.4 2.2 %copy-start = (bf16[512,4096]{1,0:T(8,128)(2,1)S(1)}, bf16[512,4096]{1,0:T(8,128)(2,1)}, u32[]{:S(2)}) copy-start(bf16[512,4096]{1,0:T(8,128)(2,1)} %near_blocks.1) | copy-start | bytes 12582916
  86.9 1.3 copy-start.8
  88.2 42.1 %copy-start.2 = (bf16[128,4096]{1,0:T(8,128)(2,1)S(1)}, bf16[128,4096]{1,0:T(8,128)(2,1)}, u32[]{:S(2)}) copy-start(bf16[128,4096]{1,0:T(8,128)(2,1)} %interpolate.1) | copy-start | bytes 3145732

commit v6 on v5

--- a/solution.py
+++ b/solution.py
@@ -22,10 +22,11 @@
 PAD = 8
 SLAB = PAD + QUAD * PIECE + 32
 CELLS = PAD + QUAD * G + 16
-ZC = 32
 STRIDE = G + 1
 BATCH = 8
+LINES = 16
 UNROLL = 16
+UNROLL_PLANES = 8
 MB = 1 << 20
 NT = (((1,), (1,)), ((), ()))
 
@@ -120,10 +121,10 @@
         return jnp.where(upper == u, lane_gather(row, lower), acc)
 
     slots = lax.fori_loop(0, strips, step, jnp.zeros(lower.shape, jnp.float32), unroll=4)
-    turned = pltpu.roll(slots, BLK, 1)
+    swapped = pltpu.roll(slots, BLK, 1)
     left = iota(slots.shape, 1) < BLK
-    doubled[pl.ds(0, strips, stride=2), :] = jnp.where(left, slots, turned)
-    doubled[pl.ds(1, strips, stride=2), :] = jnp.where(left, turned, slots)
+    doubled[pl.ds(0, strips, stride=2), :] = jnp.where(left, slots, swapped)
+    doubled[pl.ds(1, strips, stride=2), :] = jnp.where(left, swapped, slots)
     twice = doubled[...]
     charge_out[...] = twice.astype(jnp.bfloat16)
     copies[2].wait()
@@ -191,6 +192,16 @@
     out[...] += dot(owner, high) + dot(owner, low)
 
 
+def table_rows(cas, numbers, count):
+    parts = [cas[pl.ds(pl.multiple_of(n * count, 16), count), :G] for n in numbers]
+    return jnp.concatenate(parts, axis=0) if len(parts) > 1 else parts[0]
+
+
+def turned(rows):
+    unit = (iota((G, G), 0) == iota((G, G), 1)).astype(jnp.float32).astype(jnp.bfloat16)
+    return dot_nt(unit, rows).astype(jnp.bfloat16)
+
+
 def tile_loop(half, rows, cols, groups, body):
     per_slab = cols // SLABS
     low = jnp.maximum(half * (rows // HALVES) - 1, 0)
@@ -214,18 +225,17 @@
 
 
 def scatter_kernel(
-    cols, place, shift, start, patches, table, third, own_out, other_out, lines, *slabs
+    cols, gs, fs, place, shift, start, patches, cas, own_out, other_out, lines, *slabs
 ):
     half = place[0]
-    chunk = pl.program_id(0)
+    step = pl.program_id(0)
     devices, held, _ = patches.shape
     groups = (held - 16) // 16
     blocks = groups * GROUP
-    freqs = table.shape[0]
     owner = iota((16, LANES), 1) // 4
     plane = iota((16, LANES), 0) % QUAD
 
-    @pl.when(chunk == 0)
+    @pl.when(step == 0)
     def _():
         def clear(n, carry):
             for slab in slabs:
@@ -263,11 +273,11 @@
 
         tile_loop(half, devices // cols, cols, groups, tile)
 
-    @pl.when(chunk < G // ZC)
-    def _():
-        for z in range(0, ZC, QUAD):
-            base = pl.multiple_of((chunk * (ZC // QUAD) + z // QUAD) * SLAB, 8)
-            planes = []
+        table = table_rows(cas, [place[1]], gs)
+
+        def planes(n, carry):
+            base = pl.multiple_of(n * SLAB, 8)
+            sheets = []
             for q in range(QUAD):
                 parts = []
                 for s in range(SLABS):
@@ -277,27 +287,33 @@
                         over = slabs[s - 1][pl.ds(at, 8, stride=QUAD), :]
                         part = jnp.concatenate([part[:8] + over, part[8:]], axis=0)
                     parts.append(part.astype(jnp.bfloat16))
-                planes.append(jnp.concatenate(parts, axis=0))
-            field = dot(table[...], jnp.concatenate(planes, axis=1))
+                sheets.append(jnp.concatenate(parts, axis=0))
+            field = dot(table, jnp.concatenate(sheets, axis=1))
             for q in range(QUAD):
                 part = field[:, LANES * q : LANES * q + LANES]
-                lines[pl.ds(chunk * ZC + z + q, freqs, stride=STRIDE), :] = part
-
-    @pl.when(chunk >= G // ZC)
+                lines[pl.ds(n * QUAD + q, gs, stride=STRIDE), :] = part
+            return carry
+
+        lax.fori_loop(0, G // QUAD, planes, 0, unroll=UNROLL_PLANES)
+
+    @pl.when(step > 0)
     def _():
-        fs = third.shape[0] // 2
-        for g in range(0, BATCH, 2):
+        third = table_rows(cas, [place[2], place[2] ^ 1], fs)
+        for g in range(0, LINES, 2):
             pair = []
             for n in (g, g + 1):
-                at = ((chunk - G // ZC) * BATCH + n) * STRIDE
+                at = ((step - 1) * LINES + n) * STRIDE
                 pair.append(lines[pl.ds(at, G), :].astype(jnp.bfloat16))
-            field = dot(third[...], jnp.concatenate(pair, axis=1)).astype(jnp.bfloat16)
+            field = dot(third, jnp.concatenate(pair, axis=1)).astype(jnp.bfloat16)
             for n in range(2):
                 own_out[g + n] = field[:fs, LANES * n : LANES * n + LANES]
                 other_out[g + n] = field[fs:, LANES * n : LANES * n + LANES]
 
 
-def spectrum_kernel(own, other, weights, first, first_back, own_out, other_out):
+def spectrum_kernel(place, own, other, weights, cas, own_out, other_out):
+    tiles = [pl.ds(pl.multiple_of(h * LANES, LANES), LANES) for h in (place[0], 1 - place[0])]
+    first = jnp.concatenate([cas[tile, :] for tile in tiles], axis=0)
+    first_back = jnp.concatenate([cas[:, tile] for tile in tiles], axis=1)
     count, freqs, _ = weights.shape
     step = max(1, G // freqs)
     rows = step * freqs
@@ -306,50 +322,51 @@
         line = jnp.concatenate(
             [own[part].reshape(rows, LANES), other[part].reshape(rows, LANES)], axis=1
         )
-        s = dot(line, first[...]) * weights[part].reshape(rows, P_SIZE)
-        line = dot(s.astype(jnp.bfloat16), first_back[...]).astype(jnp.bfloat16)
+        s = dot(line, first) * weights[part].reshape(rows, P_SIZE)
+        line = dot(s.astype(jnp.bfloat16), first_back).astype(jnp.bfloat16)
         own_out[part] = line[:, :LANES].reshape(step, freqs, LANES)
         other_out[part] = line[:, LANES:].reshape(step, freqs, LANES)
 
 
 def sample_kernel(
-    cols, place, shift, start, patches, own, other, table, third, out, lines, cells
+    cols, place, shift, start, patches, own, other, cas, out, second, third, lines, cells
 ):
     half = place[0]
     step = pl.program_id(0)
     devices, held, _ = out.shape
     groups = held // 16
     blocks = groups * GROUP
-    freqs = table.shape[1]
-    batches = freqs // BATCH
-    chunk = step - batches
+    gs = second.shape[1]
     owner = iota((16, LANES), 1) // 4
     plane = iota((16, LANES), 0) % QUAD
 
-    @pl.when(step < batches)
+    @pl.when(step == 0)
     def _():
-        for g in range(0, BATCH, 2):
-            pair = [jnp.concatenate([own[n], other[n]], axis=0) for n in (g, g + 1)]
-            field = dot(third[...], jnp.concatenate(pair, axis=1))
-            for n in range(2):
-                at = (step * BATCH + g + n) * STRIDE
-                lines[pl.ds(at, G), :] = field[:, LANES * n : LANES * n + LANES]
-
-    @pl.when(step >= batches)
+        second[...] = turned(table_rows(cas, [place[1]], gs))
+        third[...] = turned(table_rows(cas, [place[2], place[2] ^ 1], own.shape[1]))
+
+    for g in range(0, LINES, 2):
+        pair = [jnp.concatenate([own[n], other[n]], axis=0) for n in (g, g + 1)]
+        field = dot(third[...], jnp.concatenate(pair, axis=1))
+        for n in range(2):
+            at = (step * LINES + g + n) * STRIDE
+            lines[pl.ds(at, G), :] = field[:, LANES * n : LANES * n + LANES]
+
+    @pl.when(step == pl.num_programs(0) - 1)
     def _():
-        for z in range(0, ZC, QUAD):
-            planes = [
-                lines[pl.ds(chunk * ZC + z + q, freqs, stride=STRIDE), :].astype(jnp.bfloat16)
+        def planes(n, carry):
+            sheets = [
+                lines[pl.ds(n * QUAD + q, gs, stride=STRIDE), :].astype(jnp.bfloat16)
                 for q in range(QUAD)
             ]
-            field = dot(table[...], jnp.concatenate(planes, axis=1))
-            base = pl.multiple_of((chunk * (ZC // QUAD) + z // QUAD) * CELLS, 8)
+            field = dot(second[...], jnp.concatenate(sheets, axis=1))
+            base = pl.multiple_of(n * CELLS, 8)
             for q in range(QUAD):
                 part = field[:, LANES * q : LANES * q + LANES]
                 cells[pl.ds(base + (PAD + q), G, stride=QUAD), :] = part
-
-    @pl.when(step == pl.num_programs(0) - 1)
-    def _():
+            return carry
+
+        lax.fori_loop(0, G // QUAD, planes, 0, unroll=UNROLL_PLANES)
         out[...] = jnp.zeros_like(out)
 
         def tile(numbers, t):
@@ -388,8 +405,8 @@
     patch = jnp.zeros((blocks, LANES), jnp.float32)
     for part in split(spread):
         for i in range(4):
-            turned = dot_nt(lanes[i], part).astype(jnp.bfloat16)
-            patch = patch + dot(turned, rows[i])
+            column = dot_nt(lanes[i], part).astype(jnp.bfloat16)
+            patch = patch + dot(column, rows[i])
     total[...] = block_sums(interpolate, patch) + near[...]
     count = out.shape[0]
     even = total[pl.ds(0, count, stride=2), :]
@@ -467,7 +484,7 @@
             pltpu.VMEM((blocks, LANES), jnp.float32),
             pltpu.SemaphoreType.DMA((4,)),
         ],
-        compiler_params=params(32),
+        compiler_params=params(58),
         name="project",
     )(
         charges.reshape(strips, LANES),
@@ -485,22 +502,7 @@
     )(order)
 
     around = beside(block_charges[None, None], "row", 0)
-    cas = jnp.asarray(CAS)
-    second = lax.dynamic_slice_in_dim(cas[:, :G], row_at * gs, gs, axis=0)
-    third = jnp.concatenate(
-        [lax.dynamic_slice_in_dim(cas[:, :G], c * fs, fs, axis=0) for c in (col_at, col_at ^ 1)],
-        axis=0,
-    )
-    first = jnp.concatenate(
-        [lax.dynamic_slice_in_dim(cas, h * LANES, LANES, axis=0) for h in (half, 1 - half)],
-        axis=0,
-    )
-    (gathered, around, inverse, second, second_back, third, third_back, first, first_back) = (
-        lax.optimization_barrier(
-            (gathered, around, inverse, second, second.T, third, third.T, first, first.T)
-        )
-    )
-    around = beside(around, "col", 1).reshape(9, blocks, LANES)
+    gathered, around, inverse = lax.optimization_barrier((gathered, around, inverse))
     anchors = gathered[:, 17 * groups : 17 * groups + 3].astype(jnp.int32)
     lane = 4 * (jnp.arange(blocks, dtype=jnp.int32) % GROUP)
     forth = ((anchors[:, 0] - lane) & (LANES - 1)).reshape(devices * blocks)
@@ -510,45 +512,64 @@
     piece = (jnp.arange(devices, dtype=jnp.int32) % cols * SLABS // cols * PIECE)[:, None]
     slab_at = (group * SLAB + inner - QUAD * piece).reshape(devices * blocks)
     cell_at = (group * CELLS + inner).reshape(devices * blocks)
-    place = half.astype(jnp.int32).reshape(1)
+    place = jnp.stack([half, row_at, col_at]).astype(jnp.int32)
+    cas = jnp.asarray(CAS)
 
     smem = pl.BlockSpec(memory_space=pltpu.SMEM)
-    chunks = G // ZC
-    batches = gs // BATCH
+    steps = gs // LINES
     lines_type = struct((gs, fs, LANES), jnp.bfloat16)
-    late = pl.BlockSpec((BATCH, fs, LANES), lambda n: (jnp.maximum(n - chunks, 0), 0, 0))
+    late = pl.BlockSpec((LINES, fs, LANES), lambda n: (jnp.maximum(n - 1, 0), 0, 0))
     own, other = pl.pallas_call(
-        functools.partial(scatter_kernel, cols),
-        grid=(chunks + batches,),
-        in_specs=[smem] * 3 + [whole(gathered.shape), whole(second.shape), whole(third.shape)],
+        functools.partial(scatter_kernel, cols, gs, fs),
+        grid=(1 + steps,),
+        in_specs=[smem] * 3 + [whole(gathered.shape), whole(cas.shape)],
         out_specs=(late, late),
         out_shape=(lines_type, lines_type),
         scratch_shapes=[pltpu.VMEM((gs * STRIDE, LANES), jnp.float32)]
         + [pltpu.VMEM(((G // QUAD + 1) * SLAB, LANES), jnp.float32)] * SLABS,
-        compiler_params=params(58),
+        compiler_params=params(53),
         name="scatter",
-    )(place, forth, slab_at, gathered, second, third)
+    )(place, forth, slab_at, gathered, cas)
     other = lax.ppermute(other, "col", mates)
-    other, around = lax.optimization_barrier((other, around))
 
     part = lambda shape: pl.BlockSpec((BATCH,) + shape, lambda n: (n, 0, 0))
     own, other = pl.pallas_call(
         spectrum_kernel,
-        grid=(batches,),
+        grid=(gs // BATCH,),
         in_specs=[
+            smem,
             part((fs, LANES)),
             part((fs, LANES)),
             part((fs, P_SIZE)),
-            whole((G, P_SIZE)),
-            whole((P_SIZE, G)),
+            whole(cas.shape),
         ],
         out_specs=(part((fs, LANES)), part((fs, LANES))),
         out_shape=(lines_type, lines_type),
-        compiler_params=params(56),
+        compiler_params=params(40),
         name="spectrum",
-    )(own, other, kernel_spectrum, first, first_back)
+    )(place, own, other, kernel_spectrum, cas)
     other = lax.ppermute(other, "col", mates)
 
+    early = pl.BlockSpec((LINES, fs, LANES), lambda n: (n, 0, 0))
+    values = pl.pallas_call(
+        functools.partial(sample_kernel, cols),
+        grid=(steps,),
+        in_specs=[smem] * 3 + [whole(gathered.shape), early, early, whole(cas.shape)],
+        out_specs=whole((devices, 16 * groups, LANES)),
+        out_shape=struct((devices, 16 * groups, LANES), jnp.bfloat16),
+        scratch_shapes=[
+            pltpu.VMEM((G, gs), jnp.bfloat16),
+            pltpu.VMEM((G, 2 * fs), jnp.bfloat16),
+            pltpu.VMEM((gs * STRIDE, LANES), jnp.float32),
+            pltpu.VMEM(((G // QUAD + 1) * CELLS, LANES), jnp.float32),
+        ],
+        compiler_params=params(46),
+        name="sample",
+    )(place, back, cell_at, gathered, own, other, cas)
+    values, around = lax.optimization_barrier((values, around))
+    values = lax.all_to_all(values, axes, split_axis=0, concat_axis=0, tiled=True)
+
+    around = beside(around, "col", 1).reshape(9, blocks, LANES)
     source = near_pairs[1]
     source_device = source // blocks
     code = (source_device // cols - row_at + 1) * 3 + (source_device % cols - col_at + 1)
@@ -570,26 +591,9 @@
             pltpu.VMEM((9 * blocks, LANES), jnp.float32),
             pltpu.VMEM((blocks, LANES), jnp.float32),
         ],
-        compiler_params=params(48),
+        compiler_params=params(56),
         name="near",
     )(wanted, near_blocks, target.reshape(1, pairs), around)
-    other, near = lax.optimization_barrier((other, near))
-    early = pl.BlockSpec((BATCH, fs, LANES), lambda n: (jnp.minimum(n, batches - 1), 0, 0))
-    values = pl.pallas_call(
-        functools.partial(sample_kernel, cols),
-        grid=(batches + chunks,),
-        in_specs=[smem] * 3
-        + [whole(gathered.shape), early, early, whole((G, gs)), whole((G, 2 * fs))],
-        out_specs=whole((devices, 16 * groups, LANES)),
-        out_shape=struct((devices, 16 * groups, LANES), jnp.bfloat16),
-        scratch_shapes=[
-            pltpu.VMEM((gs * STRIDE, LANES), jnp.float32),
-            pltpu.VMEM(((G // QUAD + 1) * CELLS, LANES), jnp.float32),
-        ],
-        compiler_params=params(58),
-        name="sample",
-    )(place, back, cell_at, gathered, own, other, second_back, third_back)
-    values = lax.all_to_all(values, axes, split_axis=0, concat_axis=0, tiled=True)
 
     result = pl.pallas_call(
         finish_kernel,

time: 136 us -> 118 us (0.87)
  blocking collectives: 21.8 us -> 0 us
  waiting for transfers between devices: 6.32 us -> 18.6 us
  local copies, waits for them, and re-layouts: 12.3 us -> 4.83 us
  Pallas kernels: 71.4 us -> 66.2 us
  starting transfers between devices: 20.9 us -> 24.6 us
    all_to_all x1 -> x0, blocking collectives: 21.8 us -> none  [body(): lax.all_to_all(values, axes, split_axis=0, concat_axis=0, tiled=True)]
    pallas_call x3, Pallas kernels: 53.6 us -> 45.4 us  [the longest x1 17.7 us: body(): pl.pallas_call(functools.partial(scatter_kernel, cols, gs, fs), grid=(1 +...]
    ppermute x2, waiting for transfers between devices: 0.01 us -> 7.79 us  [body(): other = lax.ppermute(other, 'col', mates)]
    all_to_all x0 -> x1, starting transfers between devices: none -> 5.23 us  [body(): lax.all_to_all(values, axes, split_axis=0, concat_axis=0, tiled=True)]
    unnamed x26 -> x18, local copies, waits for them, and re-layouts: 8.26 us -> 3.15 us
    optimization_barrier x3 -> x0, local copies, waits for them, and re-layouts: 2.34 us -> none  [body(): lax.optimization_barrier((gathered, around, inverse, second, second.T, th...]
    all_to_all x0 -> x1, waiting for transfers between devices: none -> 2.14 us  [body(): lax.all_to_all(values, axes, split_axis=0, concat_axis=0, tiled=True)]
    all_to_all x1, waiting for transfers between devices: 6.23 us -> 8.35 us  [body(): lax.all_to_all(copies, axes, split_axis=0, concat_axis=0, tiled=True)]
  transfers between devices with their start and end apart: 7 -> 8, of which waited for: 2 -> 5; matrix products, arithmetic and copies ran while one was open for 2% -> 2% of each run, Pallas kernels for 7% -> 9%
where the time goes in v6:
time: 118 us; the launch traced here: 117 us
  Pallas kernels  66.2 us (56%)
  starting transfers between devices  24.6 us (21%)
  waiting for transfers between devices  18.6 us (16%)
  local copies, waits for them, and re-layouts  4.83 us (4%)
  other arithmetic  2.2 us (2%)
    pallas_call x1, Pallas kernels, body(): pl.pallas_call(functools.partial(scatter_kernel, cols, gs, fs), grid=(1 +...  17.7 us
    pallas_call x1, Pallas kernels, body(): pl.pallas_call(functools.partial(sample_kernel, cols), grid=(steps,), in_...  16.7 us
    pallas_call x1, Pallas kernels, body(): pl.pallas_call(spectrum_kernel, grid=(gs // BATCH,), in_specs=[smem, part...  11.1 us
    all_to_all x1, waiting for transfers between devices, body(): lax.all_to_all(copies, axes, split_axis=0, concat_axis=0, tiled=True)  8.35 us
    ppermute x2, waiting for transfers between devices, body(): other = lax.ppermute(other, 'col', mates)  7.79 us
    ppermute x2, starting transfers between devices, beside(): before = lax.ppermute(array, axis, up)  7.58 us
    all_to_all x1, starting transfers between devices, body(): lax.all_to_all(copies, axes, split_axis=0, concat_axis=0, tiled=True)  7.3 us
    pallas_call x1, Pallas kernels, body(): pl.pallas_call(near_kernel, grid=(pairs // blocks,), in_specs=[smem, pl.B...  6.81 us
  transfers between devices with their start and end apart: 8, of which 5 were waited for; matrix products, arithmetic and copies ran while one was open for 2% of the time, Pallas kernels for 9%

profile of v6, /device:TPU:0, one launch (start us, length us, event | category | flops | bytes accessed | tf_op | source)
XLA Modules:
  0.0 116.5 jit_solution(17729674012962650504)
XLA Ops:
  0.0 5.3 %project.1 = (bf16[128,128]{1,0:T(8,128)(2,1)}, bf16[80,128]{1,0:T(8,128)(2,1)}) custom-call(bf16[64,128]{1,0:T(8,128)(2,1)} %bitcast.30, s32[64,128]{1,0:T(8,128)} %bitcast.21, bf16[128,4096]{1,0:T(8,128)(2,1)} %project_in.1, s32[3,128]{1,0:T(4,128)} %anchors_in.1), custom_call_target="tpu_custom_call" | custom-call | tf_op jit(solution)/shard_map/project/pallas_call | solution.py:471
  5.3 1.7 %broadcast_in_dim.4 = bf16[32,80,128]{2,1,0:T(8,128)(2,1)} broadcast(bf16[80,128]{1,0:T(8,128)(2,1)} %get-tuple-element.16), dimensions={1,2} | broadcast | bytes 675840 | tf_op jit(solution)/shard_map/broadcast_in_dim | solution.py:495
  7.0 7.3 %all-to-all-start = ((bf16[32,80,128]{2,1,0:T(8,128)(2,1)}), bf16[32,80,128]{2,1,0:T(8,128)(2,1)S(1)}, u32[]{:S(2)}, u32[]{:S(2)}) async-start(bf16[32,80,128]{2,1,0:T(8,128)(2,1)} %broadcast_in_dim.4), calls=%async_computation | async-start | bytes 1310720 | tf_op jit(solution)/shard_map/all_to_all | solution.py:496
  14.3 1.3 %collective-permute-start.1 = (bf16[1,1,128,128]{3,2,1,0:T(8,128)(2,1)}, bf16[1,1,128,128]{3,2,1,0:T(8,128)(2,1)S(1)}, u32[]{:S(2)}, u32[]{:S(2)}) collective-permute-start(bf16[1,1,128,128]{3,2,1,0:T(8,128)(2,1)} %bitcast.27), channel_id=1, source_target_pairs={{4,0},{8,4},{12,8},{16,12},{20,16},{24,20},{28,24},{5,1},{9,5},{13... | collective-permute-start | bytes 98312 | tf_op jit(solution)/shard_map/ppermute | solution.py:441
  15.6 4.5 %collective-permute-start = (bf16[1,1,128,128]{3,2,1,0:T(8,128)(2,1)}, bf16[1,1,128,128]{3,2,1,0:T(8,128)(2,1)S(1)}, u32[]{:S(2)}, u32[]{:S(2)}) collective-permute-start(bf16[1,1,128,128]{3,2,1,0:T(8,128)(2,1)} %bitcast.28), channel_id=1, source_target_pairs={{0,4},{4,8},{8,12},{12,16},{16,20},{20,24},{24,28},{1,5},{5,9},{9,... | collective-permute-start | bytes 98312 | tf_op jit(solution)/shard_map/ppermute | solution.py:440
  20.3 3.8 %inverse.1 = s32[128,128]{1,0:T(8,128)S(1)} custom-call(s32[64,128]{1,0:T(8,128)S(1)} %bitcast.22), custom_call_target="tpu_custom_call" | custom-call | tf_op jit(solution)/shard_map/inverse/pallas_call | solution.py:497
  24.1 8.3 %all-to-all-done.patches = bf16[32,80,128]{2,1,0:T(8,128)(2,1)S(1)} async-done(((bf16[32,80,128]{2,1,0:T(8,128)(2,1)}), bf16[32,80,128]{2,1,0:T(8,128)(2,1)S(1)}, u32[]{:S(2)}, u32[]{:S(2)}) %all-to-all-start) | async-done | bytes 655392 | tf_op jit(solution)/shard_map/all_to_all | solution.py:496
  32.6 0.7 copy-done
  33.3 17.7 %scatter.1 = (bf16[64,128,128]{2,1,0:T(8,128)(2,1)}, bf16[64,128,128]{2,1,0:T(8,128)(2,1)}) custom-call(s32[3]{0:T(128)S(1)} %pad_add_fusion.place, s32[4096]{0:T(1024)S(1)} %get-tuple-element.32.shift, s32[4096]{0:T(1024)S(1)} %get-tuple-element.37.start, bf16[32,80,128]{2,1,0:T(8,128)(2,1)} %copy-done, bf16[512,512]{1,0:T(8,128)(2,1)S(1)} %copy-done.2), custom_call_target="tpu_custom_call" | custom-call | tf_op jit(solution)/shard_map/scatter/pallas_call | solution.py:522
  51.0 1.5 %collective-permute-start.2 = (bf16[64,128,128]{2,1,0:T(8,128)(2,1)}, bf16[64,128,128]{2,1,0:T(8,128)(2,1)S(1)}, u32[]{:S(2)}, u32[]{:S(2)}) collective-permute-start(bf16[64,128,128]{2,1,0:T(8,128)(2,1)} %get-tuple-element.20), channel_id=1, source_target_pairs={{0,1},{1,0},{2,3},{3,2},{4,5},{5,4},{6,7},{7,6},{8,9},{9,8},{10,11... | collective-permute-start | bytes 6291464 | tf_op jit(solution)/shard_map/ppermute | solution.py:533
  52.5 4.0 %collective-permute-done.2.other = bf16[64,128,128]{2,1,0:T(8,128)(2,1)S(1)} collective-permute-done((bf16[64,128,128]{2,1,0:T(8,128)(2,1)}, bf16[64,128,128]{2,1,0:T(8,128)(2,1)S(1)}, u32[]{:S(2)}, u32[]{:S(2)}) %collective-permute-start.2) | collective-permute-done | bytes 2097184 | tf_op jit(solution)/shard_map/ppermute | solution.py:533
  56.5 1.6 %copy-done.3 = bf16[64,128,128]{2,1,0:T(8,128)(2,1)S(1)} copy-done((bf16[64,128,128]{2,1,0:T(8,128)(2,1)S(1)}, bf16[64,128,128]{2,1,0:T(8,128)(2,1)}, u32[]{:S(2)}) %copy-start.3) | copy-done | bytes 2097176
  58.0 11.1 %spectrum.1 = (bf16[64,128,128]{2,1,0:T(8,128)(2,1)S(1)}, bf16[64,128,128]{2,1,0:T(8,128)(2,1)S(1)}) custom-call(s32[3]{0:T(128)S(1)} %pad_add_fusion.place, bf16[64,128,128]{2,1,0:T(8,128)(2,1)S(1)} %copy-done.3, bf16[64,128,128]{2,1,0:T(8,128)(2,1)S(1)} %collective-permute-done.2.other, f32[64,128,512]{2,1,0:T(8,128)} %weights.1, ...), custom_call_target="tpu_custom_call" | custom-call | tf_op jit(solution)/shard_map/spectrum/pallas_call | solution.py:536
  69.6 3.8 %collective-permute-done.3.other = bf16[64,128,128]{2,1,0:T(8,128)(2,1)S(1)} collective-permute-done((bf16[64,128,128]{2,1,0:T(8,128)(2,1)S(1)}, bf16[64,128,128]{2,1,0:T(8,128)(2,1)S(1)}, u32[]{:S(2)}, u32[]{:S(2)}) %collective-permute-start.3) | collective-permute-done | bytes 2097184 | tf_op jit(solution)/shard_map/ppermute | solution.py:551
  73.4 16.7 %sample.1 = bf16[32,64,128]{2,1,0:T(8,128)(2,1)} custom-call(s32[3]{0:T(128)S(1)} %pad_add_fusion.place, s32[4096]{0:T(1024)S(1)} %get-tuple-element.33.shift, s32[4096]{0:T(1024)S(1)} %get-tuple-element.36.start, bf16[32,80,128]{2,1,0:T(8,128)(2,1)S(1)} %copy-done.1, bf16[64,128,128]{2,1,0:T(8,128)(2,1)S(1)} %get-tuple-element.21.own, ...), custom_call_target="tpu_custom_call" | custom-call | tf_op jit(solution)/shard_map/sample/pallas_call | solution.py:554
  90.1 5.2 %all-to-all-start.1 = ((bf16[32,64,128]{2,1,0:T(8,128)(2,1)}), bf16[32,64,128]{2,1,0:T(8,128)(2,1)S(1)}, u32[]{:S(2)}, u32[]{:S(2)}) async-start(bf16[32,64,128]{2,1,0:T(8,128)(2,1)} %sample.1), calls=%async_computation.1 | async-start | bytes 1048576 | tf_op jit(solution)/shard_map/all_to_all | solution.py:570
  95.9 1.3 %collective-permute-start.5 = (bf16[3,1,128,128]{3,2,1,0:T(8,128)(2,1)S(1)}, bf16[3,1,128,128]{3,2,1,0:T(8,128)(2,1)S(1)}, u32[]{:S(2)}, u32[]{:S(2)}) collective-permute-start(bf16[3,1,128,128]{3,2,1,0:T(8,128)(2,1)S(1)} %pad_maximum_fusion.1), channel_id=1, source_target_pairs={{1,0},{2,1},{3,2},{5,4},{6,5},{7,6},{9,8},{10,9},{11,10},{13,12},{... | collective-permute-start | bytes 294920 | tf_op jit(solution)/shard_map/ppermute | solution.py:441
  97.2 3.0 %collective-permute-start.4 = (bf16[3,1,128,128]{3,2,1,0:T(8,128)(2,1)S(1)}, bf16[3,1,128,128]{3,2,1,0:T(8,128)(2,1)S(1)}, u32[]{:S(2)}, u32[]{:S(2)}) collective-permute-start(bf16[3,1,128,128]{3,2,1,0:T(8,128)(2,1)S(1)} %pad_maximum_fusion.1), channel_id=1, source_target_pairs={{0,1},{1,2},{2,3},{4,5},{5,6},{6,7},{8,9},{9,10},{10,11},{12,13},{... | collective-permute-start | bytes 294920 | tf_op jit(solution)/shard_map/ppermute | solution.py:440
  100.2 0.6 fusion.11.source
  101.2 0.7 pad_maximum_fusion
  101.9 6.8 %near.1 = f32[128,128]{1,0:T(8,128)} custom-call(s32[512]{0:T(512)} %fusion.11.source, bf16[512,4096]{1,0:T(8,128)(2,1)} %near_blocks.1, s32[1,512]{1,0:T(1,128)} %get-tuple-element.34.target, bf16[9,128,128]{2,1,0:T(8,128)(2,1)} %bitcast.23), custom_call_target="tpu_custom_call" | custom-call | tf_op jit(solution)/shard_map/near/pallas_call | solution.py:579
  108.7 2.1 %all-to-all-done.1.values = bf16[32,64,128]{2,1,0:T(8,128)(2,1)S(1)} async-done(((bf16[32,64,128]{2,1,0:T(8,128)(2,1)}), bf16[32,64,128]{2,1,0:T(8,128)(2,1)S(1)}, u32[]{:S(2)}, u32[]{:S(2)}) %all-to-all-start.1) | async-done | bytes 524320 | tf_op jit(solution)/shard_map/all_to_all | solution.py:570
  110.9 0.8 copy-done.5
  111.7 4.8 %finish.1 = f32[64,128]{1,0:T(8,128)} custom-call(bf16[32,64,128]{2,1,0:T(8,128)(2,1)S(1)} %all-to-all-done.1.values, bf16[128,4096]{1,0:T(8,128)(2,1)S(1)} %copy-done.4, f32[128,128]{1,0:T(8,128)S(1)} %copy-done.5, s32[128,128]{1,0:T(8,128)S(1)} %inverse.1), custom_call_target="tpu_custom_call" | custom-call | tf_op jit(solution)/shard_map/finish/pallas_call | solution.py:598
  (28 shorter events, 1.6 us)
Async XLA Ops:
  0.0 33.3 %copy-start.2 = (bf16[512,512]{1,0:T(8,128)(2,1)S(1)}, bf16[512,512]{1,0:T(8,128)(2,1)}, u32[]{:S(2)}) copy-start(bf16[512,512]{1,0:T(8,128)(2,1)} %constant.136.clone.cas) | copy-start | bytes 1572868
  0.0 20.3 %copy-start.6 = (s32[8192]{0:T(1024)S(1)}, s32[8192]{0:T(1024)}, u32[]{:S(2)}) copy-start(s32[8192]{0:T(1024)} %param.10) | copy-start | bytes 98308
  5.3 18.8 %copy-start.7 = (bf16[128,128]{1,0:T(8,128)(2,1)S(1)}, bf16[128,128]{1,0:T(8,128)(2,1)}, u32[]{:S(2)}) copy-start(bf16[128,128]{1,0:T(8,128)(2,1)} %get-tuple-element.17) | copy-start | bytes 98308
  7.0 25.5 %all-to-all-start = ((bf16[32,80,128]{2,1,0:T(8,128)(2,1)}), bf16[32,80,128]{2,1,0:T(8,128)(2,1)S(1)}, u32[]{:S(2)}, u32[]{:S(2)}) async-start(bf16[32,80,128]{2,1,0:T(8,128)(2,1)} %broadcast_in_dim.4), calls=%async_computation | async-start | bytes 1310720 | tf_op jit(solution)/shard_map/all_to_all | solution.py:496
  14.3 9.8 %collective-permute-start.1 = (bf16[1,1,128,128]{3,2,1,0:T(8,128)(2,1)}, bf16[1,1,128,128]{3,2,1,0:T(8,128)(2,1)S(1)}, u32[]{:S(2)}, u32[]{:S(2)}) collective-permute-start(bf16[1,1,128,128]{3,2,1,0:T(8,128)(2,1)} %bitcast.27), channel_id=1, source_target_pairs={{4,0},{8,4},{12,8},{16,12},{20,16},{24,20},{28,24},{5,1},{9,5},{13... | collective-permute-start | bytes 98312 | tf_op jit(solution)/shard_map/ppermute | solution.py:441
  15.6 8.5 %collective-permute-start = (bf16[1,1,128,128]{3,2,1,0:T(8,128)(2,1)}, bf16[1,1,128,128]{3,2,1,0:T(8,128)(2,1)S(1)}, u32[]{:S(2)}, u32[]{:S(2)}) collective-permute-start(bf16[1,1,128,128]{3,2,1,0:T(8,128)(2,1)} %bitcast.28), channel_id=1, source_target_pairs={{0,4},{4,8},{8,12},{12,16},{16,20},{20,24},{24,28},{1,5},{5,9},{9,... | collective-permute-start | bytes 98312 | tf_op jit(solution)/shard_map/ppermute | solution.py:440
  32.5 0.9 copy-start
  51.0 5.5 %collective-permute-start.2 = (bf16[64,128,128]{2,1,0:T(8,128)(2,1)}, bf16[64,128,128]{2,1,0:T(8,128)(2,1)S(1)}, u32[]{:S(2)}, u32[]{:S(2)}) collective-permute-start(bf16[64,128,128]{2,1,0:T(8,128)(2,1)} %get-tuple-element.20), channel_id=1, source_target_pairs={{0,1},{1,0},{2,3},{3,2},{4,5},{5,4},{6,7},{7,6},{8,9},{9,8},{10,11... | collective-permute-start | bytes 6291464 | tf_op jit(solution)/shard_map/ppermute | solution.py:533
  56.4 1.6 %copy-start.3 = (bf16[64,128,128]{2,1,0:T(8,128)(2,1)S(1)}, bf16[64,128,128]{2,1,0:T(8,128)(2,1)}, u32[]{:S(2)}) copy-start(bf16[64,128,128]{2,1,0:T(8,128)(2,1)} %get-tuple-element.19.own) | copy-start | bytes 6291460
  58.0 15.4 %copy-start.1 = (bf16[32,80,128]{2,1,0:T(8,128)(2,1)S(1)}, bf16[32,80,128]{2,1,0:T(8,128)(2,1)}, u32[]{:S(2)}) copy-start(bf16[32,80,128]{2,1,0:T(8,128)(2,1)} %copy-done) | copy-start | bytes 1966084
  69.2 4.2 %collective-permute-start.3 = (bf16[64,128,128]{2,1,0:T(8,128)(2,1)S(1)}, bf16[64,128,128]{2,1,0:T(8,128)(2,1)S(1)}, u32[]{:S(2)}, u32[]{:S(2)}) collective-permute-start(bf16[64,128,128]{2,1,0:T(8,128)(2,1)S(1)} %get-tuple-element.22), channel_id=1, source_target_pairs={{0,1},{1,0},{2,3},{3,2},{4,5},{5,4},{6,7},{7,6},{8,9},{9,8},{10,11... | collective-permute-start | bytes 6291464 | tf_op jit(solution)/shard_map/ppermute | solution.py:551
  73.4 21.9 %copy-start.8 = (s32[2,512]{1,0:T(2,128)S(1)}, s32[2,512]{1,0:T(2,128)}, u32[]{:S(2)}) copy-start(s32[2,512]{1,0:T(2,128)} %param.15) | copy-start | bytes 12292
  90.1 20.8 %all-to-all-start.1 = ((bf16[32,64,128]{2,1,0:T(8,128)(2,1)}), bf16[32,64,128]{2,1,0:T(8,128)(2,1)S(1)}, u32[]{:S(2)}, u32[]{:S(2)}) async-start(bf16[32,64,128]{2,1,0:T(8,128)(2,1)} %sample.1), calls=%async_computation.1 | async-start | bytes 1048576 | tf_op jit(solution)/shard_map/all_to_all | solution.py:570
  95.9 5.0 %collective-permute-start.5 = (bf16[3,1,128,128]{3,2,1,0:T(8,128)(2,1)S(1)}, bf16[3,1,128,128]{3,2,1,0:T(8,128)(2,1)S(1)}, u32[]{:S(2)}, u32[]{:S(2)}) collective-permute-start(bf16[3,1,128,128]{3,2,1,0:T(8,128)(2,1)S(1)} %pad_maximum_fusion.1), channel_id=1, source_target_pairs={{1,0},{2,1},{3,2},{5,4},{6,5},{7,6},{9,8},{10,9},{11,10},{13,12},{... | collective-permute-start | bytes 294920 | tf_op jit(solution)/shard_map/ppermute | solution.py:441
  97.2 4.0 %collective-permute-start.4 = (bf16[3,1,128,128]{3,2,1,0:T(8,128)(2,1)S(1)}, bf16[3,1,128,128]{3,2,1,0:T(8,128)(2,1)S(1)}, u32[]{:S(2)}, u32[]{:S(2)}) collective-permute-start(bf16[3,1,128,128]{3,2,1,0:T(8,128)(2,1)S(1)} %pad_maximum_fusion.1), channel_id=1, source_target_pairs={{0,1},{1,2},{2,3},{4,5},{5,6},{6,7},{8,9},{9,10},{10,11},{12,13},{... | collective-permute-start | bytes 294920 | tf_op jit(solution)/shard_map/ppermute | solution.py:440
  101.9 9.0 %copy-start.4 = (bf16[128,4096]{1,0:T(8,128)(2,1)S(1)}, bf16[128,4096]{1,0:T(8,128)(2,1)}, u32[]{:S(2)}) copy-start(bf16[128,4096]{1,0:T(8,128)(2,1)} %interpolate.1) | copy-start | bytes 3145732
  110.9 0.8 copy-start.5

commit v7 on v6

--- a/solution.py
+++ b/solution.py
@@ -208,29 +208,33 @@
     high = (half + 1) * (rows // HALVES)
     per_row = per_slab * groups
 
+    def place(row, col):
+        side = (col % HALVES) ^ half
+        return side * (rows * cols // HALVES) + row * (cols // HALVES) + col // HALVES
+
     def step(n, carry):
         row = low + n // per_row
         left = n % per_row
-        body([row * cols + s * per_slab + left // groups for s in range(SLABS)], left % groups)
+        body([place(row, s * per_slab + left // groups) for s in range(SLABS)], left % groups)
         return carry
 
     lax.fori_loop(0, (high - low) * per_row, step, 0)
 
 
-def lanes_inside(patches, d, t, groups, half):
-    extra = patches[d, 16 * groups :, :].astype(jnp.float32)
+def lanes_inside(extra, d, t, half):
+    extra = extra[d].astype(jnp.float32)
     picked = jnp.where(iota(extra.shape, 0) == t, extra, 0.0)
     cells = jnp.sum(picked, axis=0, keepdims=True) - (half * LANES).astype(jnp.float32)
     return jnp.broadcast_to((cells >= 0.0) & (cells < LANES), (16, LANES))
 
 
 def scatter_kernel(
-    cols, gs, fs, place, shift, start, patches, cas, own_out, other_out, lines, *slabs
+    cols, gs, fs, place, shift, start, mine, theirs, cas, own_out, other_out, patches, extra, lines, *slabs
 ):
     half = place[0]
     step = pl.program_id(0)
     devices, held, _ = patches.shape
-    groups = (held - 16) // 16
+    groups = held // 16
     blocks = groups * GROUP
     owner = iota((16, LANES), 1) // 4
     plane = iota((16, LANES), 0) % QUAD
@@ -245,12 +249,16 @@
             return carry
 
         lax.fori_loop(0, slabs[0].shape[0] // SLAB, clear, 0)
+        for side, part in enumerate((mine, theirs)):
+            at = slice(side * (devices // 2), (side + 1) * (devices // 2))
+            patches[at] = part[:, :held]
+            extra[at] = part[:, held:]
 
         def tile(numbers, t):
             values = []
             for d in numbers:
                 part = patches[d, pl.ds(pl.multiple_of(16 * t, 16), 16), :].astype(jnp.float32)
-                values.append(jnp.where(lanes_inside(patches, d, t, groups, half), part, 0.0))
+                values.append(jnp.where(lanes_inside(extra, d, t, half), part, 0.0))
 
             def one(k, carry):
                 spot = owner == k
@@ -329,7 +337,7 @@
 
 
 def sample_kernel(
-    cols, place, shift, start, patches, own, other, cas, out, second, third, lines, cells
+    cols, place, shift, start, mine, theirs, own, other, cas, out, extra, second, third, lines, cells
 ):
     half = place[0]
     step = pl.program_id(0)
@@ -342,6 +350,8 @@
 
     @pl.when(step == 0)
     def _():
+        for side, part in enumerate((mine, theirs)):
+            extra[side * (devices // 2) : (side + 1) * (devices // 2)] = part[:, held:]
         second[...] = turned(table_rows(cas, [place[1]], gs))
         third[...] = turned(table_rows(cas, [place[2], place[2] ^ 1], own.shape[1]))
 
@@ -386,7 +396,7 @@
             zero = (jnp.zeros((16, LANES), jnp.float32),) * SLABS
             sums = lax.fori_loop(0, GROUP, one, zero, unroll=UNROLL)
             for s, d in enumerate(numbers):
-                inside = lanes_inside(patches, d, t, groups, half)
+                inside = lanes_inside(extra, d, t, half)
                 out[d, pl.ds(pl.multiple_of(16 * t, 16), 16), :] = jnp.where(
                     inside, sums[s], 0.0
                 ).astype(jnp.bfloat16)
@@ -402,11 +412,11 @@
     for d in range(1, values.shape[0]):
         summed = summed + values[d].astype(jnp.float32)
     spread = jnp.concatenate([summed[16 * t : 16 * t + 16] for t in range(groups)], axis=1)
+    parts = jnp.concatenate(split(spread), axis=0)
     patch = jnp.zeros((blocks, LANES), jnp.float32)
-    for part in split(spread):
-        for i in range(4):
-            column = dot_nt(lanes[i], part).astype(jnp.bfloat16)
-            patch = patch + dot(column, rows[i])
+    for i in range(4):
+        column = dot_nt(lanes[i], parts).astype(jnp.bfloat16)
+        patch = patch + dot(column, jnp.concatenate([rows[i], rows[i]], axis=0))
     total[...] = block_sums(interpolate, patch) + near[...]
     count = out.shape[0]
     even = total[pl.ds(0, count, stride=2), :]
@@ -492,8 +502,19 @@
         project,
         patch_anchor,
     )
-    copies = jnp.broadcast_to(sent[None], (devices, held, LANES))
-    gathered = lax.all_to_all(copies, axes, split_axis=0, concat_axis=0, tiled=True)
+    members = devices // HALVES
+    cores = [
+        [r * cols + c for r in range(rows) for c in range(core, cols, HALVES)]
+        for core in range(HALVES)
+    ]
+
+    def swap_members(array):
+        return lax.all_to_all(
+            array, axes, split_axis=0, concat_axis=0, axis_index_groups=cores, tiled=True
+        )
+
+    mine = swap_members(jnp.broadcast_to(sent[None], (members, held, LANES)))
+    theirs = lax.ppermute(mine, "col", mates)
     inverse = pl.pallas_call(
         inverse_kernel,
         out_shape=struct((2 * strips, LANES), jnp.int32),
@@ -502,14 +523,17 @@
     )(order)
 
     around = beside(block_charges[None, None], "row", 0)
-    gathered, around, inverse = lax.optimization_barrier((gathered, around, inverse))
-    anchors = gathered[:, 17 * groups : 17 * groups + 3].astype(jnp.int32)
+    mine, around, inverse = lax.optimization_barrier((mine, around, inverse))
+    anchors = jnp.stack([part[:, 17 * groups : 17 * groups + 3] for part in (mine, theirs)])
+    anchors = anchors.astype(jnp.int32)
     lane = 4 * (jnp.arange(blocks, dtype=jnp.int32) % GROUP)
-    forth = ((anchors[:, 0] - lane) & (LANES - 1)).reshape(devices * blocks)
-    back = ((lane - anchors[:, 0]) & (LANES - 1)).reshape(devices * blocks)
-    group = anchors[:, 2] // QUAD
-    inner = PAD + QUAD * anchors[:, 1] + anchors[:, 2] % QUAD
-    piece = (jnp.arange(devices, dtype=jnp.int32) % cols * SLABS // cols * PIECE)[:, None]
+    forth = ((anchors[:, :, 0] - lane) & (LANES - 1)).reshape(devices * blocks)
+    back = ((lane - anchors[:, :, 0]) & (LANES - 1)).reshape(devices * blocks)
+    group = anchors[:, :, 2] // QUAD
+    inner = PAD + QUAD * anchors[:, :, 1] + anchors[:, :, 2] % QUAD
+    side = jnp.arange(HALVES, dtype=jnp.int32)[:, None] ^ half
+    col = jnp.arange(members, dtype=jnp.int32) % (cols // HALVES) * HALVES + side
+    piece = (col * SLABS // cols * PIECE)[:, :, None]
     slab_at = (group * SLAB + inner - QUAD * piece).reshape(devices * blocks)
     cell_at = (group * CELLS + inner).reshape(devices * blocks)
     place = jnp.stack([half, row_at, col_at]).astype(jnp.int32)
@@ -522,15 +546,21 @@
     own, other = pl.pallas_call(
         functools.partial(scatter_kernel, cols, gs, fs),
         grid=(1 + steps,),
-        in_specs=[smem] * 3 + [whole(gathered.shape), whole(cas.shape)],
+        in_specs=[smem] * 3 + [whole(mine.shape)] * 2 + [whole(cas.shape)],
         out_specs=(late, late),
         out_shape=(lines_type, lines_type),
-        scratch_shapes=[pltpu.VMEM((gs * STRIDE, LANES), jnp.float32)]
+        scratch_shapes=[
+            pltpu.VMEM((devices, 16 * groups, LANES), jnp.bfloat16),
+            pltpu.VMEM((devices, 16, LANES), jnp.bfloat16),
+            pltpu.VMEM((gs * STRIDE, LANES), jnp.float32),
+        ]
         + [pltpu.VMEM(((G // QUAD + 1) * SLAB, LANES), jnp.float32)] * SLABS,
         compiler_params=params(53),
         name="scatter",
-    )(place, forth, slab_at, gathered, cas)
+    )(place, forth, slab_at, mine, theirs, cas)
     other = lax.ppermute(other, "col", mates)
+    around = beside(around, "col", 1).reshape(9, blocks, LANES)
+    other, around = lax.optimization_barrier((other, around))
 
     part = lambda shape: pl.BlockSpec((BATCH,) + shape, lambda n: (n, 0, 0))
     own, other = pl.pallas_call(
@@ -554,10 +584,11 @@
     values = pl.pallas_call(
         functools.partial(sample_kernel, cols),
         grid=(steps,),
-        in_specs=[smem] * 3 + [whole(gathered.shape), early, early, whole(cas.shape)],
+        in_specs=[smem] * 3 + [whole(mine.shape)] * 2 + [early, early, whole(cas.shape)],
         out_specs=whole((devices, 16 * groups, LANES)),
         out_shape=struct((devices, 16 * groups, LANES), jnp.bfloat16),
         scratch_shapes=[
+            pltpu.VMEM((devices, 16, LANES), jnp.bfloat16),
             pltpu.VMEM((G, gs), jnp.bfloat16),
             pltpu.VMEM((G, 2 * fs), jnp.bfloat16),
             pltpu.VMEM((gs * STRIDE, LANES), jnp.float32),
@@ -565,11 +596,13 @@
         ],
         compiler_params=params(46),
         name="sample",
-    )(place, back, cell_at, gathered, own, other, cas)
+    )(place, back, cell_at, mine, theirs, own, other, cas)
+    values = values.reshape(HALVES, members, 16 * groups, LANES)
+    received = lax.ppermute(values[1], "col", mates).astype(jnp.float32)
+    values = (values[0].astype(jnp.float32) + received).astype(jnp.bfloat16)
     values, around = lax.optimization_barrier((values, around))
-    values = lax.all_to_all(values, axes, split_axis=0, concat_axis=0, tiled=True)
-
-    around = beside(around, "col", 1).reshape(9, blocks, LANES)
+    values = swap_members(values)
+
     source = near_pairs[1]
     source_device = source // blocks
     code = (source_device // cols - row_at + 1) * 3 + (source_device % cols - col_at + 1)

time: 118 us -> 120 us (1.017)
  starting transfers between devices: 24.6 us -> 30 us
  waiting for transfers between devices: 18.6 us -> 15.8 us
  other arithmetic: 2.2 us -> 3.76 us
    ppermute x2, waiting for transfers between devices: 7.79 us -> 3.79 us  [body(): other = lax.ppermute(other, 'col', mates)]
    ppermute x0 -> x2, starting transfers between devices: none -> 2.35 us  [the longest x1 2.34 us: body(): received = lax.ppermute(values[1], 'col', mates).astype(jnp.float32)]
    ppermute x0 -> x2, waiting for transfers between devices: none -> 1.98 us  [the longest x1 1.16 us: body(): received = lax.ppermute(values[1], 'col', mates).astype(jnp.float32)]
    ppermute x2, starting transfers between devices: 1.91 us -> 3.87 us  [body(): other = lax.ppermute(other, 'col', mates)]
    all_to_all x2, waiting for transfers between devices: 10.5 us -> 9.16 us  [swap_members(): lax.all_to_all(array, axes, split_axis=0, concat_axis=0, axis_index_group...]
    unnamed x18 -> x12, local copies, waits for them, and re-layouts: 3.15 us -> 2.45 us
  transfers between devices with their start and end apart: 8 -> 10, of which waited for: 5 -> 6; matrix products, arithmetic and copies ran while one was open for 2% -> 4% of each run, Pallas kernels for 9% -> 9%
where the time goes in v7:
time: 120 us
  Pallas kernels  65.8 us (55%)
  starting transfers between devices  30 us (25%)
  waiting for transfers between devices  15.8 us (13%)
  local copies, waits for them, and re-layouts  4.05 us (3%)
  other arithmetic  3.76 us (3%)
    pallas_call x1, Pallas kernels, body(): pl.pallas_call(functools.partial(scatter_kernel, cols, gs, fs), grid=(1 +...  18.1 us
    pallas_call x1, Pallas kernels, body(): pl.pallas_call(functools.partial(sample_kernel, cols), grid=(steps,), in_...  16.3 us
    all_to_all x2, starting transfers between devices, swap_members(): lax.all_to_all(array, axes, split_axis=0, concat_axis=0, axis_index_group...  12.6 us
    pallas_call x1, Pallas kernels, body(): pl.pallas_call(spectrum_kernel, grid=(gs // BATCH,), in_specs=[smem, part...  11 us
    all_to_all x2, waiting for transfers between devices, swap_members(): lax.all_to_all(array, axes, split_axis=0, concat_axis=0, axis_index_group...  9.16 us
    ppermute x2, starting transfers between devices, beside(): before = lax.ppermute(array, axis, up)  8.51 us
    pallas_call x1, Pallas kernels, body(): pl.pallas_call(near_kernel, grid=(pairs // blocks,), in_specs=[smem, pl.B...  6.8 us
    pallas_call x1, Pallas kernels, body(): pl.pallas_call(project_kernel, out_shape=(struct((blocks, LANES), jnp.bfl...  5.28 us
  transfers between devices with their start and end apart: 10, of which 6 were waited for; matrix products, arithmetic and copies ran while one was open for 4% of the time, Pallas kernels for 9%

profile of v7, /device:TPU:0, one launch (start us, length us, event | category | flops | bytes accessed | tf_op | source)
XLA Modules:
  0.0 119.6 jit_solution(6912785924455947481)
XLA Ops:
  0.0 5.3 %project.1 = (bf16[128,128]{1,0:T(8,128)(2,1)}, bf16[80,128]{1,0:T(8,128)(2,1)}) custom-call(bf16[64,128]{1,0:T(8,128)(2,1)} %bitcast.29, s32[64,128]{1,0:T(8,128)} %bitcast.18, bf16[128,4096]{1,0:T(8,128)(2,1)} %project_in.1, s32[3,128]{1,0:T(4,128)} %anchors_in.1), custom_call_target="tpu_custom_call" | custom-call | tf_op jit(solution)/shard_map/project/pallas_call | solution.py:481
  5.3 1.3 %collective-permute-start.1 = (bf16[1,1,128,128]{3,2,1,0:T(8,128)(2,1)}, bf16[1,1,128,128]{3,2,1,0:T(8,128)(2,1)S(1)}, u32[]{:S(2)}, u32[]{:S(2)}) collective-permute-start(bf16[1,1,128,128]{3,2,1,0:T(8,128)(2,1)} %bitcast.26), channel_id=1, source_target_pairs={{4,0},{8,4},{12,8},{16,12},{20,16},{24,20},{28,24},{5,1},{9,5},{13... | collective-permute-start | bytes 98312 | tf_op jit(solution)/shard_map/ppermute | solution.py:451
  6.6 5.5 %collective-permute-start = (bf16[1,1,128,128]{3,2,1,0:T(8,128)(2,1)}, bf16[1,1,128,128]{3,2,1,0:T(8,128)(2,1)S(1)}, u32[]{:S(2)}, u32[]{:S(2)}) collective-permute-start(bf16[1,1,128,128]{3,2,1,0:T(8,128)(2,1)} %bitcast.27), channel_id=1, source_target_pairs={{0,4},{4,8},{8,12},{12,16},{16,20},{20,24},{24,28},{1,5},{5,9},{9,... | collective-permute-start | bytes 98312 | tf_op jit(solution)/shard_map/ppermute | solution.py:450
  12.1 1.5 %broadcast_in_dim.4 = bf16[16,80,128]{2,1,0:T(8,128)(2,1)} broadcast(bf16[80,128]{1,0:T(8,128)(2,1)} %get-tuple-element.18), dimensions={1,2} | broadcast | bytes 348160 | tf_op jit(solution)/shard_map/broadcast_in_dim | solution.py:516
  13.6 7.3 %all-to-all-start = ((bf16[16,80,128]{2,1,0:T(8,128)(2,1)}), bf16[16,80,128]{2,1,0:T(8,128)(2,1)S(1)}, u32[]{:S(2)}, u32[]{:S(2)}) async-start(bf16[16,80,128]{2,1,0:T(8,128)(2,1)} %broadcast_in_dim.4), calls=%async_computation | async-start | bytes 655360 | tf_op jit(solution)/shard_map/all_to_all | solution.py:512
  21.0 3.8 %inverse.1 = s32[128,128]{1,0:T(8,128)S(1)} custom-call(s32[64,128]{1,0:T(8,128)S(1)} %bitcast.19), custom_call_target="tpu_custom_call" | custom-call | tf_op jit(solution)/shard_map/inverse/pallas_call | solution.py:518
  24.8 6.8 %all-to-all-done.mine = bf16[16,80,128]{2,1,0:T(8,128)(2,1)S(1)} async-done(((bf16[16,80,128]{2,1,0:T(8,128)(2,1)}), bf16[16,80,128]{2,1,0:T(8,128)(2,1)S(1)}, u32[]{:S(2)}, u32[]{:S(2)}) %all-to-all-start) | async-done | bytes 327712 | tf_op jit(solution)/shard_map/all_to_all | solution.py:512
  33.4 18.1 %scatter.1 = (bf16[64,128,128]{2,1,0:T(8,128)(2,1)}, bf16[64,128,128]{2,1,0:T(8,128)(2,1)}) custom-call(s32[3]{0:T(128)S(1)} %pad_add_fusion.place, s32[4096]{0:T(1024)S(1)} %get-tuple-element.40.shift, s32[4096]{0:T(1024)S(1)} %get-tuple-element.31.start, bf16[16,80,128]{2,1,0:T(8,128)(2,1)S(1)} %all-to-all-done.mine, ...), custom_call_target="tpu_custom_call" | custom-call | tf_op jit(solution)/shard_map/scatter/pallas_call | solution.py:546
  51.5 1.9 %collective-permute-start.3 = (bf16[64,128,128]{2,1,0:T(8,128)(2,1)}, bf16[64,128,128]{2,1,0:T(8,128)(2,1)S(1)}, u32[]{:S(2)}, u32[]{:S(2)}) collective-permute-start(bf16[64,128,128]{2,1,0:T(8,128)(2,1)} %get-tuple-element.22), channel_id=1, source_target_pairs={{0,1},{1,0},{2,3},{3,2},{4,5},{5,4},{6,7},{7,6},{8,9},{9,8},{10,11... | collective-permute-start | bytes 6291464 | tf_op jit(solution)/shard_map/ppermute | solution.py:561
  53.4 1.3 %collective-permute-start.5 = (bf16[3,1,128,128]{3,2,1,0:T(8,128)(2,1)S(1)}, bf16[3,1,128,128]{3,2,1,0:T(8,128)(2,1)S(1)}, u32[]{:S(2)}, u32[]{:S(2)}) collective-permute-start(bf16[3,1,128,128]{3,2,1,0:T(8,128)(2,1)S(1)} %pad_maximum_fusion.1), channel_id=1, source_target_pairs={{1,0},{2,1},{3,2},{5,4},{6,5},{7,6},{9,8},{10,9},{11,10},{13,12},{... | collective-permute-start | bytes 294920 | tf_op jit(solution)/shard_map/ppermute | solution.py:451
  54.7 3.0 %collective-permute-start.4 = (bf16[3,1,128,128]{3,2,1,0:T(8,128)(2,1)S(1)}, bf16[3,1,128,128]{3,2,1,0:T(8,128)(2,1)S(1)}, u32[]{:S(2)}, u32[]{:S(2)}) collective-permute-start(bf16[3,1,128,128]{3,2,1,0:T(8,128)(2,1)S(1)} %pad_maximum_fusion.1), channel_id=1, source_target_pairs={{0,1},{1,2},{2,3},{4,5},{5,6},{6,7},{8,9},{9,10},{10,11},{12,13},{... | collective-permute-start | bytes 294920 | tf_op jit(solution)/shard_map/ppermute | solution.py:450
  57.7 0.9 collective-permute-done.4
  59.4 1.6 %copy-done.1 = bf16[64,128,128]{2,1,0:T(8,128)(2,1)S(1)} copy-done((bf16[64,128,128]{2,1,0:T(8,128)(2,1)S(1)}, bf16[64,128,128]{2,1,0:T(8,128)(2,1)}, u32[]{:S(2)}) %copy-start.1) | copy-done | bytes 2097176
  61.0 11.0 %spectrum.1 = (bf16[64,128,128]{2,1,0:T(8,128)(2,1)S(1)}, bf16[64,128,128]{2,1,0:T(8,128)(2,1)S(1)}) custom-call(s32[3]{0:T(128)S(1)} %pad_add_fusion.place, bf16[64,128,128]{2,1,0:T(8,128)(2,1)S(1)} %copy-done.1, bf16[64,128,128]{2,1,0:T(8,128)(2,1)S(1)} %collective-permute-done.3.other, f32[64,128,512]{2,1,0:T(8,128)} %weights.1, bf16[512,512]{1,0:T(8,128)(2,1)S(1)} %copy-done), custom_call_target="tpu_custom_call" | custom-call | tf_op jit(solution)/shard_map/spectrum/pallas_call | solution.py:566
  72.0 2.0 %collective-permute-start.6 = (bf16[64,128,128]{2,1,0:T(8,128)(2,1)S(1)}, bf16[64,128,128]{2,1,0:T(8,128)(2,1)S(1)}, u32[]{:S(2)}, u32[]{:S(2)}) collective-permute-start(bf16[64,128,128]{2,1,0:T(8,128)(2,1)S(1)} %get-tuple-element.26), channel_id=1, source_target_pairs={{0,1},{1,0},{2,3},{3,2},{4,5},{5,4},{6,7},{7,6},{8,9},{9,8},{10,11... | collective-permute-start | bytes 6291464 | tf_op jit(solution)/shard_map/ppermute | solution.py:581
  74.0 3.8 %collective-permute-done.6.other = bf16[64,128,128]{2,1,0:T(8,128)(2,1)S(1)} collective-permute-done((bf16[64,128,128]{2,1,0:T(8,128)(2,1)S(1)}, bf16[64,128,128]{2,1,0:T(8,128)(2,1)S(1)}, u32[]{:S(2)}, u32[]{:S(2)}) %collective-permute-start.6) | collective-permute-done | bytes 2097184 | tf_op jit(solution)/shard_map/ppermute | solution.py:581
  77.8 16.3 %sample.1 = bf16[32,64,128]{2,1,0:T(8,128)(2,1)S(1)} custom-call(s32[3]{0:T(128)S(1)} %pad_add_fusion.place, s32[4096]{0:T(1024)S(1)} %get-tuple-element.39.shift, s32[4096]{0:T(1024)S(1)} %get-tuple-element.32.start, bf16[16,80,128]{2,1,0:T(8,128)(2,1)S(1)} %all-to-all-done.mine, bf16[16,80,128]{2,1,0:T(8,128)(2,1)S(1)} %collective-permute-done.2.theirs, ...), custom_call_target="tpu_custom_call" | custom-call | tf_op jit(solution)/shard_map/sample/pallas_call | solution.py:584
  94.1 2.3 %collective-permute-start.7 = (bf16[16,64,128]{2,1,0:T(8,128)(2,1)S(1)}, bf16[16,64,128]{2,1,0:T(8,128)(2,1)S(1)}, u32[]{:S(2)}, u32[]{:S(2)}) collective-permute-start(bf16[16,64,128]{2,1,0:T(8,128)(2,1)S(1)} %slice.42), channel_id=1, source_target_pairs={{0,1},{1,0},{2,3},{3,2},{4,5},{5,4},{6,7},{7,6},{8,9},{9,8},{10,11... | collective-permute-start | bytes 786440 | tf_op jit(solution)/shard_map/ppermute | solution.py:601
  96.5 1.2 collective-permute-done.7
  98.4 5.4 %all-to-all-start.1 = ((bf16[16,64,128]{2,1,0:T(8,128)(2,1)}), bf16[16,64,128]{2,1,0:T(8,128)(2,1)S(1)}, u32[]{:S(2)}, u32[]{:S(2)}) async-start(bf16[16,64,128]{2,1,0:T(8,128)(2,1)} %add_convert_fusion), calls=%async_computation.1 | async-start | bytes 524288 | tf_op jit(solution)/shard_map/all_to_all | solution.py:512
  105.0 6.8 %near.1 = f32[128,128]{1,0:T(8,128)} custom-call(s32[512]{0:T(512)} %fusion.11.source, bf16[512,4096]{1,0:T(8,128)(2,1)} %near_blocks.1, s32[1,512]{1,0:T(1,128)} %get-tuple-element.37.target, bf16[9,128,128]{2,1,0:T(8,128)(2,1)} %bitcast.20), custom_call_target="tpu_custom_call" | custom-call | tf_op jit(solution)/shard_map/near/pallas_call | solution.py:612
  111.8 2.4 %all-to-all-done.1.values = bf16[16,64,128]{2,1,0:T(8,128)(2,1)S(1)} async-done(((bf16[16,64,128]{2,1,0:T(8,128)(2,1)}), bf16[16,64,128]{2,1,0:T(8,128)(2,1)S(1)}, u32[]{:S(2)}, u32[]{:S(2)}) %all-to-all-start.1) | async-done | bytes 262176 | tf_op jit(solution)/shard_map/all_to_all | solution.py:512
  114.2 0.8 copy-done.3
  115.0 4.6 %finish.1 = f32[64,128]{1,0:T(8,128)} custom-call(bf16[16,64,128]{2,1,0:T(8,128)(2,1)S(1)} %all-to-all-done.1.values, bf16[128,4096]{1,0:T(8,128)(2,1)S(1)} %copy-done.2, f32[128,128]{1,0:T(8,128)S(1)} %copy-done.3, s32[128,128]{1,0:T(8,128)S(1)} %inverse.1), custom_call_target="tpu_custom_call" | custom-call | tf_op jit(solution)/shard_map/finish/pallas_call | solution.py:631
  (34 shorter events, 4.7 us)
Async XLA Ops:
  0.0 21.0 %copy-start.4 = (s32[8192]{0:T(1024)S(1)}, s32[8192]{0:T(1024)}, u32[]{:S(2)}) copy-start(s32[8192]{0:T(1024)} %param.10) | copy-start | bytes 98308
  0.0 59.4 %copy-start = (bf16[512,512]{1,0:T(8,128)(2,1)S(1)}, bf16[512,512]{1,0:T(8,128)(2,1)}, u32[]{:S(2)}) copy-start(bf16[512,512]{1,0:T(8,128)(2,1)} %constant.137.clone.cas) | copy-start | bytes 1572868
  5.3 26.3 %collective-permute-start.1 = (bf16[1,1,128,128]{3,2,1,0:T(8,128)(2,1)}, bf16[1,1,128,128]{3,2,1,0:T(8,128)(2,1)S(1)}, u32[]{:S(2)}, u32[]{:S(2)}) collective-permute-start(bf16[1,1,128,128]{3,2,1,0:T(8,128)(2,1)} %bitcast.26), channel_id=1, source_target_pairs={{4,0},{8,4},{12,8},{16,12},{20,16},{24,20},{28,24},{5,1},{9,5},{13... | collective-permute-start | bytes 98312 | tf_op jit(solution)/shard_map/ppermute | solution.py:451
  6.6 25.0 %collective-permute-start = (bf16[1,1,128,128]{3,2,1,0:T(8,128)(2,1)}, bf16[1,1,128,128]{3,2,1,0:T(8,128)(2,1)S(1)}, u32[]{:S(2)}, u32[]{:S(2)}) collective-permute-start(bf16[1,1,128,128]{3,2,1,0:T(8,128)(2,1)} %bitcast.27), channel_id=1, source_target_pairs={{0,4},{4,8},{8,12},{12,16},{16,20},{20,24},{24,28},{1,5},{5,9},{9,... | collective-permute-start | bytes 98312 | tf_op jit(solution)/shard_map/ppermute | solution.py:450
  13.6 18.0 %all-to-all-start = ((bf16[16,80,128]{2,1,0:T(8,128)(2,1)}), bf16[16,80,128]{2,1,0:T(8,128)(2,1)S(1)}, u32[]{:S(2)}, u32[]{:S(2)}) async-start(bf16[16,80,128]{2,1,0:T(8,128)(2,1)} %broadcast_in_dim.4), calls=%async_computation | async-start | bytes 655360 | tf_op jit(solution)/shard_map/all_to_all | solution.py:512
  31.6 1.6 %collective-permute-start.2 = (bf16[16,80,128]{2,1,0:T(8,128)(2,1)S(1)}, bf16[16,80,128]{2,1,0:T(8,128)(2,1)S(1)}, u32[]{:S(2)}, u32[]{:S(2)}) collective-permute-start(bf16[16,80,128]{2,1,0:T(8,128)(2,1)S(1)} %all-to-all-done.mine), channel_id=1, source_target_pairs={{0,1},{1,0},{2,3},{3,2},{4,5},{5,4},{6,7},{7,6},{8,9},{9,8},{10,11... | collective-permute-start | bytes 983048 | tf_op jit(solution)/shard_map/ppermute | solution.py:517
  51.5 7.9 %collective-permute-start.3 = (bf16[64,128,128]{2,1,0:T(8,128)(2,1)}, bf16[64,128,128]{2,1,0:T(8,128)(2,1)S(1)}, u32[]{:S(2)}, u32[]{:S(2)}) collective-permute-start(bf16[64,128,128]{2,1,0:T(8,128)(2,1)} %get-tuple-element.22), channel_id=1, source_target_pairs={{0,1},{1,0},{2,3},{3,2},{4,5},{5,4},{6,7},{7,6},{8,9},{9,8},{10,11... | collective-permute-start | bytes 6291464 | tf_op jit(solution)/shard_map/ppermute | solution.py:561
  53.4 4.3 %collective-permute-start.5 = (bf16[3,1,128,128]{3,2,1,0:T(8,128)(2,1)S(1)}, bf16[3,1,128,128]{3,2,1,0:T(8,128)(2,1)S(1)}, u32[]{:S(2)}, u32[]{:S(2)}) collective-permute-start(bf16[3,1,128,128]{3,2,1,0:T(8,128)(2,1)S(1)} %pad_maximum_fusion.1), channel_id=1, source_target_pairs={{1,0},{2,1},{3,2},{5,4},{6,5},{7,6},{9,8},{10,9},{11,10},{13,12},{... | collective-permute-start | bytes 294920 | tf_op jit(solution)/shard_map/ppermute | solution.py:451
  54.7 4.0 %collective-permute-start.4 = (bf16[3,1,128,128]{3,2,1,0:T(8,128)(2,1)S(1)}, bf16[3,1,128,128]{3,2,1,0:T(8,128)(2,1)S(1)}, u32[]{:S(2)}, u32[]{:S(2)}) collective-permute-start(bf16[3,1,128,128]{3,2,1,0:T(8,128)(2,1)S(1)} %pad_maximum_fusion.1), channel_id=1, source_target_pairs={{0,1},{1,2},{2,3},{4,5},{5,6},{6,7},{8,9},{9,10},{10,11},{12,13},{... | collective-permute-start | bytes 294920 | tf_op jit(solution)/shard_map/ppermute | solution.py:450
  59.4 1.6 %copy-start.1 = (bf16[64,128,128]{2,1,0:T(8,128)(2,1)S(1)}, bf16[64,128,128]{2,1,0:T(8,128)(2,1)}, u32[]{:S(2)}) copy-start(bf16[64,128,128]{2,1,0:T(8,128)(2,1)} %get-tuple-element.21.own) | copy-start | bytes 6291460
  72.0 5.8 %collective-permute-start.6 = (bf16[64,128,128]{2,1,0:T(8,128)(2,1)S(1)}, bf16[64,128,128]{2,1,0:T(8,128)(2,1)S(1)}, u32[]{:S(2)}, u32[]{:S(2)}) collective-permute-start(bf16[64,128,128]{2,1,0:T(8,128)(2,1)S(1)} %get-tuple-element.26), channel_id=1, source_target_pairs={{0,1},{1,0},{2,3},{3,2},{4,5},{5,4},{6,7},{7,6},{8,9},{9,8},{10,11... | collective-permute-start | bytes 6291464 | tf_op jit(solution)/shard_map/ppermute | solution.py:581
  77.8 26.0 %copy-start.5 = (s32[2,512]{1,0:T(2,128)S(1)}, s32[2,512]{1,0:T(2,128)}, u32[]{:S(2)}) copy-start(s32[2,512]{1,0:T(2,128)} %param.15) | copy-start | bytes 12292
  94.1 3.5 %collective-permute-start.7 = (bf16[16,64,128]{2,1,0:T(8,128)(2,1)S(1)}, bf16[16,64,128]{2,1,0:T(8,128)(2,1)S(1)}, u32[]{:S(2)}, u32[]{:S(2)}) collective-permute-start(bf16[16,64,128]{2,1,0:T(8,128)(2,1)S(1)} %slice.42), channel_id=1, source_target_pairs={{0,1},{1,0},{2,3},{3,2},{4,5},{5,4},{6,7},{7,6},{8,9},{9,8},{10,11... | collective-permute-start | bytes 786440 | tf_op jit(solution)/shard_map/ppermute | solution.py:601
  98.4 15.8 %all-to-all-start.1 = ((bf16[16,64,128]{2,1,0:T(8,128)(2,1)}), bf16[16,64,128]{2,1,0:T(8,128)(2,1)S(1)}, u32[]{:S(2)}, u32[]{:S(2)}) async-start(bf16[16,64,128]{2,1,0:T(8,128)(2,1)} %add_convert_fusion), calls=%async_computation.1 | async-start | bytes 524288 | tf_op jit(solution)/shard_map/all_to_all | solution.py:512
  105.0 9.2 %copy-start.2 = (bf16[128,4096]{1,0:T(8,128)(2,1)S(1)}, bf16[128,4096]{1,0:T(8,128)(2,1)}, u32[]{:S(2)}) copy-start(bf16[128,4096]{1,0:T(8,128)(2,1)} %interpolate.1) | copy-start | bytes 3145732
  114.2 0.8 copy-start.3

commit v8 on v7

--- a/solution.py
+++ b/solution.py
@@ -25,8 +25,8 @@
 STRIDE = G + 1
 BATCH = 8
 LINES = 16
-UNROLL = 16
-UNROLL_PLANES = 8
+UNROLL = 32
+UNROLL_PLANES = 16
 MB = 1 << 20
 NT = (((1,), (1,)), ((), ()))
 
@@ -73,19 +73,32 @@
     return total[:rows] + total[rows:]
 
 
-def patch_places(blocks):
-    lanes = [
-        (iota((blocks, 4 * blocks), 1) == 4 * iota((blocks, 4 * blocks), 0) + i).astype(
-            jnp.bfloat16
-        )
-        for i in range(4)
-    ]
+def patch_places(spots):
+    blocks = spots.shape[0]
+    spots = jnp.concatenate([spots] * (4 * blocks // LANES), axis=1)
+    lane = iota(spots.shape, 1)
+    lanes = [(lane == 4 * spots + i).astype(jnp.float32).astype(jnp.bfloat16) for i in range(4)]
     row = iota((16, LANES), 0)
     rows = [
-        (iota((16, LANES), 1) % PTS == 16 * i + row).astype(jnp.bfloat16)
+        (iota((16, LANES), 1) % PTS == 16 * i + row).astype(jnp.float32).astype(jnp.bfloat16)
         for i in range(4)
     ]
     return rows, lanes
+
+
+def block_spots(first):
+    blocks = first.shape[1]
+    shape = (blocks, blocks)
+    crossing = ((first & (LANES - 1)) > LANES - 4).astype(jnp.float32)
+    crossing = jnp.broadcast_to(crossing, (8, blocks))
+    earlier = (iota(shape, 0) < iota(shape, 1)).astype(jnp.float32).astype(jnp.bfloat16)
+    ahead = dot(crossing.astype(jnp.bfloat16), earlier)
+    total = jnp.sum(crossing, axis=1, keepdims=True)
+    block = iota((8, blocks), 1).astype(jnp.float32)
+    spot = jnp.where(crossing > 0.0, ahead, total + block - ahead)
+    spread = jnp.broadcast_to(spot[:1], (LANES, blocks)).astype(jnp.bfloat16)
+    unit = (iota(shape, 0) == iota(shape, 1)).astype(jnp.float32).astype(jnp.bfloat16)
+    return dot_nt(unit, spread).astype(jnp.int32)
 
 
 def project_kernel(
@@ -95,6 +108,7 @@
     anchors_in,
     charge_out,
     patch_out,
+    spot_out,
     charges,
     order,
     project,
@@ -131,20 +145,26 @@
     copies[3].wait()
     patch = block_sums(project, twice)
     patch = jnp.where(iota(patch.shape, 1) < PTS, patch, 0.0).astype(jnp.bfloat16)
-    rows, lanes = patch_places(blocks)
-    corner = anchors[...].astype(jnp.float32)
+    spots = block_spots(anchors[:1, :])
+    spot_out[...] = spots
+    rows, lanes = patch_places(spots)
+    moved = (iota(spots.shape, 1) == spots).astype(jnp.float32).astype(jnp.bfloat16)
+    corner = anchors[...].astype(jnp.float32).astype(jnp.bfloat16)
+    corner = dot(jnp.concatenate([corner] * 3, axis=0)[:8], moved)
     spread = jnp.zeros((16, 4 * blocks), jnp.float32)
     cells = (iota((8, 4 * blocks), 1) % 4).astype(jnp.float32)
-    start = jnp.broadcast_to(corner[:1], (8, blocks)).astype(jnp.bfloat16)
+    start = jnp.broadcast_to(anchors[:1, :].astype(jnp.float32), (8, blocks)).astype(jnp.bfloat16)
     for i in range(4):
         spread = spread + dot(dot_nt(rows[i], patch).astype(jnp.bfloat16), lanes[i])
         cells = cells + dot(start, lanes[i])
     tiles = [slice(LANES * t, LANES * t + LANES) for t in range(groups)]
-    for t in range(groups):
-        patch_out[16 * t : 16 * t + 16] = spread[:, tiles[t]].astype(jnp.bfloat16)
-    extra = [cells[:1, tile] for tile in tiles] + [corner]
-    extra.append(jnp.zeros((16 - groups - corner.shape[0], LANES), jnp.float32))
-    patch_out[16 * groups :] = jnp.concatenate(extra, axis=0).astype(jnp.bfloat16)
+    sent = [spread[:, tile].astype(jnp.bfloat16) for tile in tiles]
+    extra = [cells[:1, tile] for tile in tiles] + [corner[:3]]
+    extra.append(jnp.zeros((13 - groups, LANES), jnp.float32))
+    sent.append(jnp.concatenate(extra, axis=0).astype(jnp.bfloat16))
+    for n in range(patch_out.shape[0]):
+        for t, part in enumerate(sent):
+            patch_out[n, 16 * t : 16 * t + 16] = part
 
 
 def inverse_kernel(order, out):
@@ -202,7 +222,7 @@
     return dot_nt(unit, rows).astype(jnp.bfloat16)
 
 
-def tile_loop(half, rows, cols, groups, body):
+def tile_loop(half, rows, cols, groups, crosses, body):
     per_slab = cols // SLABS
     low = jnp.maximum(half * (rows // HALVES) - 1, 0)
     high = (half + 1) * (rows // HALVES)
@@ -215,7 +235,11 @@
     def step(n, carry):
         row = low + n // per_row
         left = n % per_row
-        body([place(row, s * per_slab + left // groups) for s in range(SLABS)], left % groups)
+        t = left % groups
+        devices = [place(row, s * per_slab + left // groups) for s in range(SLABS)]
+        found = [crosses((d * groups + t) * GROUP) for d in devices]
+        inside = row >= half * (rows // HALVES)
+        pl.when(functools.reduce(jnp.logical_or, found, inside))(lambda: body(devices, t))
         return carry
 
     lax.fori_loop(0, (high - low) * per_row, step, 0)
@@ -279,7 +303,10 @@
 
             lax.fori_loop(0, GROUP, one, 0, unroll=UNROLL)
 
-        tile_loop(half, devices // cols, cols, groups, tile)
+        def crosses(b):
+            return shift[b] > LANES - 4
+
+        tile_loop(half, devices // cols, cols, groups, crosses, tile)
 
         table = table_rows(cas, [place[1]], gs)
 
@@ -401,13 +428,16 @@
                     inside, sums[s], 0.0
                 ).astype(jnp.bfloat16)
 
-        tile_loop(half, devices // cols, cols, groups, tile)
-
-
-def finish_kernel(values, interpolate, near, inverse, out, total):
+        def crosses(b):
+            return (shift[b] > 0) & (shift[b] < 4)
+
+        tile_loop(half, devices // cols, cols, groups, crosses, tile)
+
+
+def finish_kernel(values, interpolate, near, inverse, spots, out, total):
     blocks = near.shape[0]
     groups = values.shape[1] // 16
-    rows, lanes = patch_places(blocks)
+    rows, lanes = patch_places(spots[...])
     summed = values[0].astype(jnp.float32)
     for d in range(1, values.shape[0]):
         summed = summed + values[d].astype(jnp.float32)
@@ -478,11 +508,13 @@
     held = 16 * groups + 16
 
     order = panel_order.reshape(strips, LANES)
-    block_charges, sent = pl.pallas_call(
+    members = devices // HALVES
+    block_charges, sent, spots = pl.pallas_call(
         project_kernel,
         out_shape=(
             struct((blocks, LANES), jnp.bfloat16),
-            struct((held, LANES), jnp.bfloat16),
+            struct((members, held, LANES), jnp.bfloat16),
+            struct((blocks, LANES), jnp.int32),
         ),
         in_specs=[pl.BlockSpec(memory_space=pltpu.HBM)] * 4,
         scratch_shapes=[
@@ -502,7 +534,6 @@
         project,
         patch_anchor,
     )
-    members = devices // HALVES
     cores = [
         [r * cols + c for r in range(rows) for c in range(core, cols, HALVES)]
         for core in range(HALVES)
@@ -513,8 +544,9 @@
             array, axes, split_axis=0, concat_axis=0, axis_index_groups=cores, tiled=True
         )
 
-    mine = swap_members(jnp.broadcast_to(sent[None], (members, held, LANES)))
+    mine = swap_members(sent)
     theirs = lax.ppermute(mine, "col", mates)
+    order, block_charges = lax.optimization_barrier((order, block_charges))
     inverse = pl.pallas_call(
         inverse_kernel,
         out_shape=struct((2 * strips, LANES), jnp.int32),
@@ -522,6 +554,7 @@
         name="inverse",
     )(order)
 
+    block_charges, inverse = lax.optimization_barrier((block_charges, inverse))
     around = beside(block_charges[None, None], "row", 0)
     mine, around, inverse = lax.optimization_barrier((mine, around, inverse))
     anchors = jnp.stack([part[:, 17 * groups : 17 * groups + 3] for part in (mine, theirs)])
@@ -559,8 +592,6 @@
         name="scatter",
     )(place, forth, slab_at, mine, theirs, cas)
     other = lax.ppermute(other, "col", mates)
-    around = beside(around, "col", 1).reshape(9, blocks, LANES)
-    other, around = lax.optimization_barrier((other, around))
 
     part = lambda shape: pl.BlockSpec((BATCH,) + shape, lambda n: (n, 0, 0))
     own, other = pl.pallas_call(
@@ -579,6 +610,9 @@
         name="spectrum",
     )(place, own, other, kernel_spectrum, cas)
     other = lax.ppermute(other, "col", mates)
+    own, around = lax.optimization_barrier((own, around))
+    around = beside(around, "col", 1).reshape(9, blocks, LANES)
+    other, around = lax.optimization_barrier((other, around))
 
     early = pl.BlockSpec((LINES, fs, LANES), lambda n: (n, 0, 0))
     values = pl.pallas_call(
@@ -634,7 +668,7 @@
         scratch_shapes=[pltpu.VMEM((blocks, LANES), jnp.float32)],
         compiler_params=params(32),
         name="finish",
-    )(values, interpolate, near, inverse)
+    )(values, interpolate, near, inverse, spots)
     return result.reshape(panels)
 
 

time: 120 us -> 118 us (0.983)
  waiting for transfers between devices: 15.8 us -> 19.6 us
  Pallas kernels: 65.8 us -> 62.7 us
  starting transfers between devices: 30 us -> 27.2 us
    all_to_all x2, waiting for transfers between devices: 9.16 us -> 12.7 us  [swap_members(): lax.all_to_all(array, axes, split_axis=0, concat_axis=0, axis_index_group...]
    ppermute x2, starting transfers between devices: 3.87 us -> 1.12 us  [body(): other = lax.ppermute(other, 'col', mates)]
    pallas_call x1, Pallas kernels: 16.3 us -> 14.2 us  [body(): pl.pallas_call(functools.partial(sample_kernel, cols), grid=(steps,), in_...]
    broadcast_in_dim x1 -> x0, local copies, waits for them, and re-layouts: 1.49 us -> none  [body(): mine = swap_members(jnp.broadcast_to(sent[None], (members, held, LANES)))]
    pallas_call x1, Pallas kernels: 18.1 us -> 16.7 us  [body(): pl.pallas_call(functools.partial(scatter_kernel, cols, gs, fs), grid=(1 +...]
    unnamed x12 -> x14, local copies, waits for them, and re-layouts: 2.45 us -> 3.2 us
  transfers between devices with their start and end apart: 10 -> 10, of which waited for: 6 -> 6; matrix products, arithmetic and copies ran while one was open for 4% -> 2% of each run, Pallas kernels for 9% -> 6%
where the time goes in v8:
time: 118 us; the launch traced here: 117 us
  Pallas kernels  62.7 us (53%)
  starting transfers between devices  27.2 us (23%)
  waiting for transfers between devices  19.6 us (17%)
  other arithmetic  3.76 us (3%)
  local copies, waits for them, and re-layouts  3.32 us (3%)
    pallas_call x1, Pallas kernels, body(): pl.pallas_call(functools.partial(scatter_kernel, cols, gs, fs), grid=(1 +...  16.7 us
    pallas_call x1, Pallas kernels, body(): pl.pallas_call(functools.partial(sample_kernel, cols), grid=(steps,), in_...  14.2 us
    all_to_all x2, waiting for transfers between devices, swap_members(): lax.all_to_all(array, axes, split_axis=0, concat_axis=0, axis_index_group...  12.7 us
    all_to_all x2, starting transfers between devices, swap_members(): lax.all_to_all(array, axes, split_axis=0, concat_axis=0, axis_index_group...  12.3 us
    pallas_call x1, Pallas kernels, body(): pl.pallas_call(spectrum_kernel, grid=(gs // BATCH,), in_specs=[smem, part...  11 us
    ppermute x2, starting transfers between devices, beside(): before = lax.ppermute(array, axis, up)  8.51 us
    pallas_call x1, Pallas kernels, body(): pl.pallas_call(near_kernel, grid=(pairs // blocks,), in_specs=[smem, pl.B...  6.82 us
    pallas_call x1, Pallas kernels, body(): pl.pallas_call(project_kernel, out_shape=(struct((blocks, LANES), jnp.bfl...  5.56 us
  transfers between devices with their start and end apart: 10, of which 6 were waited for; matrix products, arithmetic and copies ran while one was open for 2% of the time, Pallas kernels for 6%

profile of v8, /device:TPU:0, one launch (start us, length us, event | category | flops | bytes accessed | tf_op | source)
XLA Modules:
  0.0 116.8 jit_solution(6334271841687953982)
XLA Ops:
  0.0 5.6 %project.1 = (bf16[128,128]{1,0:T(8,128)(2,1)}, bf16[16,80,128]{2,1,0:T(8,128)(2,1)}, s32[128,128]{1,0:T(8,128)}) custom-call(bf16[64,128]{1,0:T(8,128)(2,1)} %bitcast.29, s32[64,128]{1,0:T(8,128)} %bitcast.18, bf16[128,4096]{1,0:T(8,128)(2,1)} %project_in.1, s32[3,128]{1,0:T(4,128)} %anchors_in.1), custom_call_target="tpu_custom_call" | custom-call | tf_op jit(solution)/shard_map/project/pallas_call | solution.py:512
  6.3 3.8 %inverse.1 = s32[128,128]{1,0:T(8,128)S(1)} custom-call(s32[64,128]{1,0:T(8,128)S(1)} %bitcast.19), custom_call_target="tpu_custom_call" | custom-call | tf_op jit(solution)/shard_map/inverse/pallas_call | solution.py:550
  10.1 1.3 %collective-permute-start.1 = (bf16[1,1,128,128]{3,2,1,0:T(8,128)(2,1)}, bf16[1,1,128,128]{3,2,1,0:T(8,128)(2,1)S(1)}, u32[]{:S(2)}, u32[]{:S(2)}) collective-permute-start(bf16[1,1,128,128]{3,2,1,0:T(8,128)(2,1)} %bitcast.26), channel_id=1, source_target_pairs={{4,0},{8,4},{12,8},{16,12},{20,16},{24,20},{28,24},{5,1},{9,5},{13... | collective-permute-start | bytes 98312 | tf_op jit(solution)/shard_map/ppermute | solution.py:481
  11.4 5.5 %collective-permute-start = (bf16[1,1,128,128]{3,2,1,0:T(8,128)(2,1)}, bf16[1,1,128,128]{3,2,1,0:T(8,128)(2,1)S(1)}, u32[]{:S(2)}, u32[]{:S(2)}) collective-permute-start(bf16[1,1,128,128]{3,2,1,0:T(8,128)(2,1)} %bitcast.27), channel_id=1, source_target_pairs={{0,4},{4,8},{8,12},{12,16},{16,20},{20,24},{24,28},{1,5},{5,9},{9,... | collective-permute-start | bytes 98312 | tf_op jit(solution)/shard_map/ppermute | solution.py:480
  16.9 7.3 %all-to-all-start = ((bf16[16,80,128]{2,1,0:T(8,128)(2,1)}), bf16[16,80,128]{2,1,0:T(8,128)(2,1)S(1)}, u32[]{:S(2)}, u32[]{:S(2)}) async-start(bf16[16,80,128]{2,1,0:T(8,128)(2,1)} %get-tuple-element.25), calls=%async_computation | async-start | bytes 655360 | tf_op jit(solution)/shard_map/all_to_all | solution.py:543
  24.4 10.6 %all-to-all-done.mine = bf16[16,80,128]{2,1,0:T(8,128)(2,1)S(1)} async-done(((bf16[16,80,128]{2,1,0:T(8,128)(2,1)}), bf16[16,80,128]{2,1,0:T(8,128)(2,1)S(1)}, u32[]{:S(2)}, u32[]{:S(2)}) %all-to-all-start) | async-done | bytes 327712 | tf_op jit(solution)/shard_map/all_to_all | solution.py:543
  35.0 0.8 pad_maximum_fusion.1
  35.8 0.8 collective-permute-done.2.theirs
  36.8 16.7 %scatter.1 = (bf16[64,128,128]{2,1,0:T(8,128)(2,1)}, bf16[64,128,128]{2,1,0:T(8,128)(2,1)}) custom-call(s32[3]{0:T(128)S(1)} %pad_add_fusion.place, s32[4096]{0:T(1024)S(1)} %get-tuple-element.54.shift, s32[4096]{0:T(1024)S(1)} %get-tuple-element.45.start, bf16[16,80,128]{2,1,0:T(8,128)(2,1)S(1)} %all-to-all-done.mine, ...), custom_call_target="tpu_custom_call" | custom-call | tf_op jit(solution)/shard_map/scatter/pallas_call | solution.py:579
  54.2 4.0 %collective-permute-done.3.other = bf16[64,128,128]{2,1,0:T(8,128)(2,1)S(1)} collective-permute-done((bf16[64,128,128]{2,1,0:T(8,128)(2,1)}, bf16[64,128,128]{2,1,0:T(8,128)(2,1)S(1)}, u32[]{:S(2)}, u32[]{:S(2)}) %collective-permute-start.3) | collective-permute-done | bytes 2097184 | tf_op jit(solution)/shard_map/ppermute | solution.py:594
  58.2 1.6 %copy-done.1 = bf16[64,128,128]{2,1,0:T(8,128)(2,1)S(1)} copy-done((bf16[64,128,128]{2,1,0:T(8,128)(2,1)S(1)}, bf16[64,128,128]{2,1,0:T(8,128)(2,1)}, u32[]{:S(2)}) %copy-start.1) | copy-done | bytes 2097176
  59.8 11.0 %spectrum.1 = (bf16[64,128,128]{2,1,0:T(8,128)(2,1)S(1)}, bf16[64,128,128]{2,1,0:T(8,128)(2,1)S(1)}) custom-call(s32[3]{0:T(128)S(1)} %pad_add_fusion.place, bf16[64,128,128]{2,1,0:T(8,128)(2,1)S(1)} %copy-done.1, bf16[64,128,128]{2,1,0:T(8,128)(2,1)S(1)} %collective-permute-done.3.other, f32[64,128,512]{2,1,0:T(8,128)} %weights.1, bf16[512,512]{1,0:T(8,128)(2,1)S(1)} %copy-done), custom_call_target="tpu_custom_call" | custom-call | tf_op jit(solution)/shard_map/spectrum/pallas_call | solution.py:597
  71.3 1.3 %collective-permute-start.6 = (bf16[3,1,128,128]{3,2,1,0:T(8,128)(2,1)S(1)}, bf16[3,1,128,128]{3,2,1,0:T(8,128)(2,1)S(1)}, u32[]{:S(2)}, u32[]{:S(2)}) collective-permute-start(bf16[3,1,128,128]{3,2,1,0:T(8,128)(2,1)S(1)} %pad_maximum_fusion.1), channel_id=1, source_target_pairs={{1,0},{2,1},{3,2},{5,4},{6,5},{7,6},{9,8},{10,9},{11,10},{13,12},{... | collective-permute-start | bytes 294920 | tf_op jit(solution)/shard_map/ppermute | solution.py:481
  72.6 3.0 %collective-permute-start.5 = (bf16[3,1,128,128]{3,2,1,0:T(8,128)(2,1)S(1)}, bf16[3,1,128,128]{3,2,1,0:T(8,128)(2,1)S(1)}, u32[]{:S(2)}, u32[]{:S(2)}) collective-permute-start(bf16[3,1,128,128]{3,2,1,0:T(8,128)(2,1)S(1)} %pad_maximum_fusion.1), channel_id=1, source_target_pairs={{0,1},{1,2},{2,3},{4,5},{5,6},{6,7},{8,9},{9,10},{10,11},{12,13},{... | collective-permute-start | bytes 294920 | tf_op jit(solution)/shard_map/ppermute | solution.py:480
  75.6 0.9 collective-permute-done.5
  77.3 14.2 %sample.1 = bf16[32,64,128]{2,1,0:T(8,128)(2,1)S(1)} custom-call(s32[3]{0:T(128)S(1)} %pad_add_fusion.place, s32[4096]{0:T(1024)S(1)} %get-tuple-element.53.shift, s32[4096]{0:T(1024)S(1)} %get-tuple-element.46.start, bf16[16,80,128]{2,1,0:T(8,128)(2,1)S(1)} %all-to-all-done.mine, bf16[16,80,128]{2,1,0:T(8,128)(2,1)S(1)} %collective-permute-done.2.theirs, ...), custom_call_target="tpu_custom_call" | custom-call | tf_op jit(solution)/shard_map/sample/pallas_call | solution.py:618
  91.5 2.7 %collective-permute-start.7 = (bf16[16,64,128]{2,1,0:T(8,128)(2,1)S(1)}, bf16[16,64,128]{2,1,0:T(8,128)(2,1)S(1)}, u32[]{:S(2)}, u32[]{:S(2)}) collective-permute-start(bf16[16,64,128]{2,1,0:T(8,128)(2,1)S(1)} %slice.42), channel_id=1, source_target_pairs={{0,1},{1,0},{2,3},{3,2},{4,5},{5,4},{6,7},{7,6},{8,9},{9,8},{10,11... | collective-permute-start | bytes 786440 | tf_op jit(solution)/shard_map/ppermute | solution.py:635
  94.2 1.2 collective-permute-done.7
  95.3 0.8 add_convert_fusion
  96.1 5.0 %all-to-all-start.1 = ((bf16[16,64,128]{2,1,0:T(8,128)(2,1)}), bf16[16,64,128]{2,1,0:T(8,128)(2,1)S(1)}, u32[]{:S(2)}, u32[]{:S(2)}) async-start(bf16[16,64,128]{2,1,0:T(8,128)(2,1)} %add_convert_fusion), calls=%async_computation.1 | async-start | bytes 524288 | tf_op jit(solution)/shard_map/all_to_all | solution.py:543
  102.4 6.8 %near.1 = f32[128,128]{1,0:T(8,128)} custom-call(s32[512]{0:T(512)} %fusion.11.source, bf16[512,4096]{1,0:T(8,128)(2,1)} %near_blocks.1, s32[1,512]{1,0:T(1,128)} %get-tuple-element.51.target, bf16[9,128,128]{2,1,0:T(8,128)(2,1)} %bitcast.20), custom_call_target="tpu_custom_call" | custom-call | tf_op jit(solution)/shard_map/near/pallas_call | solution.py:646
  109.2 2.1 %all-to-all-done.1.values = bf16[16,64,128]{2,1,0:T(8,128)(2,1)S(1)} async-done(((bf16[16,64,128]{2,1,0:T(8,128)(2,1)}), bf16[16,64,128]{2,1,0:T(8,128)(2,1)S(1)}, u32[]{:S(2)}, u32[]{:S(2)}) %all-to-all-start.1) | async-done | bytes 262176 | tf_op jit(solution)/shard_map/all_to_all | solution.py:543
  111.3 0.8 copy-done.3
  112.2 4.6 %finish.1 = f32[64,128]{1,0:T(8,128)} custom-call(bf16[16,64,128]{2,1,0:T(8,128)(2,1)S(1)} %all-to-all-done.1.values, bf16[128,4096]{1,0:T(8,128)(2,1)S(1)} %copy-done.2, f32[128,128]{1,0:T(8,128)S(1)} %copy-done.3, s32[128,128]{1,0:T(8,128)S(1)} %inverse.1, s32[128,128]{1,0:T(8,128)S(1)} %copy-done.5), custom_call_target="tpu_custom_call" | custom-call | tf_op jit(solution)/shard_map/finish/pallas_call | solution.py:665
  (35 shorter events, 4.2 us)
Async XLA Ops:
  0.0 58.2 %copy-start = (bf16[512,512]{1,0:T(8,128)(2,1)S(1)}, bf16[512,512]{1,0:T(8,128)(2,1)}, u32[]{:S(2)}) copy-start(bf16[512,512]{1,0:T(8,128)(2,1)} %constant.137.clone.cas) | copy-start | bytes 1572868
  5.6 0.8 copy-start.4
  10.1 24.8 %collective-permute-start.1 = (bf16[1,1,128,128]{3,2,1,0:T(8,128)(2,1)}, bf16[1,1,128,128]{3,2,1,0:T(8,128)(2,1)S(1)}, u32[]{:S(2)}, u32[]{:S(2)}) collective-permute-start(bf16[1,1,128,128]{3,2,1,0:T(8,128)(2,1)} %bitcast.26), channel_id=1, source_target_pairs={{4,0},{8,4},{12,8},{16,12},{20,16},{24,20},{28,24},{5,1},{9,5},{13... | collective-permute-start | bytes 98312 | tf_op jit(solution)/shard_map/ppermute | solution.py:481
  11.4 23.5 %collective-permute-start = (bf16[1,1,128,128]{3,2,1,0:T(8,128)(2,1)}, bf16[1,1,128,128]{3,2,1,0:T(8,128)(2,1)S(1)}, u32[]{:S(2)}, u32[]{:S(2)}) collective-permute-start(bf16[1,1,128,128]{3,2,1,0:T(8,128)(2,1)} %bitcast.27), channel_id=1, source_target_pairs={{0,4},{4,8},{8,12},{12,16},{16,20},{20,24},{24,28},{1,5},{5,9},{9,... | collective-permute-start | bytes 98312 | tf_op jit(solution)/shard_map/ppermute | solution.py:480
  16.9 18.1 %all-to-all-start = ((bf16[16,80,128]{2,1,0:T(8,128)(2,1)}), bf16[16,80,128]{2,1,0:T(8,128)(2,1)S(1)}, u32[]{:S(2)}, u32[]{:S(2)}) async-start(bf16[16,80,128]{2,1,0:T(8,128)(2,1)} %get-tuple-element.25), calls=%async_computation | async-start | bytes 655360 | tf_op jit(solution)/shard_map/all_to_all | solution.py:543
  34.9 1.6 %collective-permute-start.2 = (bf16[16,80,128]{2,1,0:T(8,128)(2,1)S(1)}, bf16[16,80,128]{2,1,0:T(8,128)(2,1)S(1)}, u32[]{:S(2)}, u32[]{:S(2)}) collective-permute-start(bf16[16,80,128]{2,1,0:T(8,128)(2,1)S(1)} %all-to-all-done.mine), channel_id=1, source_target_pairs={{0,1},{1,0},{2,3},{3,2},{4,5},{5,4},{6,7},{7,6},{8,9},{9,8},{10,11... | collective-permute-start | bytes 983048 | tf_op jit(solution)/shard_map/ppermute | solution.py:548
  53.5 4.7 %collective-permute-start.3 = (bf16[64,128,128]{2,1,0:T(8,128)(2,1)}, bf16[64,128,128]{2,1,0:T(8,128)(2,1)S(1)}, u32[]{:S(2)}, u32[]{:S(2)}) collective-permute-start(bf16[64,128,128]{2,1,0:T(8,128)(2,1)} %get-tuple-element.33), channel_id=1, source_target_pairs={{0,1},{1,0},{2,3},{3,2},{4,5},{5,4},{6,7},{7,6},{8,9},{9,8},{10,11... | collective-permute-start | bytes 6291464 | tf_op jit(solution)/shard_map/ppermute | solution.py:594
  58.2 1.6 %copy-start.1 = (bf16[64,128,128]{2,1,0:T(8,128)(2,1)S(1)}, bf16[64,128,128]{2,1,0:T(8,128)(2,1)}, u32[]{:S(2)}) copy-start(bf16[64,128,128]{2,1,0:T(8,128)(2,1)} %get-tuple-element.32.own) | copy-start | bytes 6291460
  70.8 6.4 %collective-permute-start.4 = (bf16[64,128,128]{2,1,0:T(8,128)(2,1)S(1)}, bf16[64,128,128]{2,1,0:T(8,128)(2,1)S(1)}, u32[]{:S(2)}, u32[]{:S(2)}) collective-permute-start(bf16[64,128,128]{2,1,0:T(8,128)(2,1)S(1)} %get-tuple-element.37), channel_id=1, source_target_pairs={{0,1},{1,0},{2,3},{3,2},{4,5},{5,4},{6,7},{7,6},{8,9},{9,8},{10,11... | collective-permute-start | bytes 6291464 | tf_op jit(solution)/shard_map/ppermute | solution.py:612
  71.3 4.3 %collective-permute-start.6 = (bf16[3,1,128,128]{3,2,1,0:T(8,128)(2,1)S(1)}, bf16[3,1,128,128]{3,2,1,0:T(8,128)(2,1)S(1)}, u32[]{:S(2)}, u32[]{:S(2)}) collective-permute-start(bf16[3,1,128,128]{3,2,1,0:T(8,128)(2,1)S(1)} %pad_maximum_fusion.1), channel_id=1, source_target_pairs={{1,0},{2,1},{3,2},{5,4},{6,5},{7,6},{9,8},{10,9},{11,10},{13,12},{... | collective-permute-start | bytes 294920 | tf_op jit(solution)/shard_map/ppermute | solution.py:481
  72.6 4.0 %collective-permute-start.5 = (bf16[3,1,128,128]{3,2,1,0:T(8,128)(2,1)S(1)}, bf16[3,1,128,128]{3,2,1,0:T(8,128)(2,1)S(1)}, u32[]{:S(2)}, u32[]{:S(2)}) collective-permute-start(bf16[3,1,128,128]{3,2,1,0:T(8,128)(2,1)S(1)} %pad_maximum_fusion.1), channel_id=1, source_target_pairs={{0,1},{1,2},{2,3},{4,5},{5,6},{6,7},{8,9},{9,10},{10,11},{12,13},{... | collective-permute-start | bytes 294920 | tf_op jit(solution)/shard_map/ppermute | solution.py:480
  77.3 23.9 %copy-start.6 = (s32[2,512]{1,0:T(2,128)S(1)}, s32[2,512]{1,0:T(2,128)}, u32[]{:S(2)}) copy-start(s32[2,512]{1,0:T(2,128)} %param.15) | copy-start | bytes 12292
  91.5 3.9 %collective-permute-start.7 = (bf16[16,64,128]{2,1,0:T(8,128)(2,1)S(1)}, bf16[16,64,128]{2,1,0:T(8,128)(2,1)S(1)}, u32[]{:S(2)}, u32[]{:S(2)}) collective-permute-start(bf16[16,64,128]{2,1,0:T(8,128)(2,1)S(1)} %slice.42), channel_id=1, source_target_pairs={{0,1},{1,0},{2,3},{3,2},{4,5},{5,4},{6,7},{7,6},{8,9},{9,8},{10,11... | collective-permute-start | bytes 786440 | tf_op jit(solution)/shard_map/ppermute | solution.py:635
  96.1 15.2 %all-to-all-start.1 = ((bf16[16,64,128]{2,1,0:T(8,128)(2,1)}), bf16[16,64,128]{2,1,0:T(8,128)(2,1)S(1)}, u32[]{:S(2)}, u32[]{:S(2)}) async-start(bf16[16,64,128]{2,1,0:T(8,128)(2,1)} %add_convert_fusion), calls=%async_computation.1 | async-start | bytes 524288 | tf_op jit(solution)/shard_map/all_to_all | solution.py:543
  102.4 9.0 %copy-start.2 = (bf16[128,4096]{1,0:T(8,128)(2,1)S(1)}, bf16[128,4096]{1,0:T(8,128)(2,1)}, u32[]{:S(2)}) copy-start(bf16[128,4096]{1,0:T(8,128)(2,1)} %interpolate.1) | copy-start | bytes 3145732
  102.4 9.0 %copy-start.5 = (s32[128,128]{1,0:T(8,128)S(1)}, s32[128,128]{1,0:T(8,128)}, u32[]{:S(2)}) copy-start(s32[128,128]{1,0:T(8,128)} %get-tuple-element.44.spots) | copy-start | bytes 196612
  111.3 0.8 copy-start.3

commit v9 on v8

--- a/solution.py
+++ b/solution.py
@@ -123,6 +123,17 @@
     copies = [pltpu.make_async_copy(a, b, sems.at[n]) for n, (a, b) in enumerate(pairs)]
     for copy in copies:
         copy.start()
+    copies[3].wait()
+    spots = block_spots(anchors[:1, :])
+    spot_out[...] = spots
+    rows, lanes = patch_places(spots)
+    moved = (iota(spots.shape, 1) == spots).astype(jnp.float32).astype(jnp.bfloat16)
+    corner = anchors[...].astype(jnp.float32).astype(jnp.bfloat16)
+    corner = dot(jnp.concatenate([corner] * 3, axis=0)[:8], moved)
+    cells = (iota((8, 4 * blocks), 1) % 4).astype(jnp.float32)
+    start = jnp.broadcast_to(anchors[:1, :].astype(jnp.float32), (8, blocks)).astype(jnp.bfloat16)
+    for i in range(4):
+        cells = cells + dot(start, lanes[i])
     copies[0].wait()
     copies[1].wait()
     table[...] = charges[...].astype(jnp.float32)
@@ -142,21 +153,11 @@
     twice = doubled[...]
     charge_out[...] = twice.astype(jnp.bfloat16)
     copies[2].wait()
-    copies[3].wait()
     patch = block_sums(project, twice)
     patch = jnp.where(iota(patch.shape, 1) < PTS, patch, 0.0).astype(jnp.bfloat16)
-    spots = block_spots(anchors[:1, :])
-    spot_out[...] = spots
-    rows, lanes = patch_places(spots)
-    moved = (iota(spots.shape, 1) == spots).astype(jnp.float32).astype(jnp.bfloat16)
-    corner = anchors[...].astype(jnp.float32).astype(jnp.bfloat16)
-    corner = dot(jnp.concatenate([corner] * 3, axis=0)[:8], moved)
     spread = jnp.zeros((16, 4 * blocks), jnp.float32)
-    cells = (iota((8, 4 * blocks), 1) % 4).astype(jnp.float32)
-    start = jnp.broadcast_to(anchors[:1, :].astype(jnp.float32), (8, blocks)).astype(jnp.bfloat16)
     for i in range(4):
         spread = spread + dot(dot_nt(rows[i], patch).astype(jnp.bfloat16), lanes[i])
-        cells = cells + dot(start, lanes[i])
     tiles = [slice(LANES * t, LANES * t + LANES) for t in range(groups)]
     sent = [spread[:, tile].astype(jnp.bfloat16) for tile in tiles]
     extra = [cells[:1, tile] for tile in tiles] + [corner[:3]]
@@ -546,7 +547,6 @@
 
     mine = swap_members(sent)
     theirs = lax.ppermute(mine, "col", mates)
-    order, block_charges = lax.optimization_barrier((order, block_charges))
     inverse = pl.pallas_call(
         inverse_kernel,
         out_shape=struct((2 * strips, LANES), jnp.int32),
@@ -554,9 +554,7 @@
         name="inverse",
     )(order)
 
-    block_charges, inverse = lax.optimization_barrier((block_charges, inverse))
-    around = beside(block_charges[None, None], "row", 0)
-    mine, around, inverse = lax.optimization_barrier((mine, around, inverse))
+    mine, inverse = lax.optimization_barrier((mine, inverse))
     anchors = jnp.stack([part[:, 17 * groups : 17 * groups + 3] for part in (mine, theirs)])
     anchors = anchors.astype(jnp.int32)
     lane = 4 * (jnp.arange(blocks, dtype=jnp.int32) % GROUP)
@@ -592,6 +590,9 @@
         name="scatter",
     )(place, forth, slab_at, mine, theirs, cas)
     other = lax.ppermute(other, "col", mates)
+    own, block_charges = lax.optimization_barrier((own, block_charges))
+    around = beside(block_charges[None, None], "row", 0)
+    other, around = lax.optimization_barrier((other, around))
 
     part = lambda shape: pl.BlockSpec((BATCH,) + shape, lambda n: (n, 0, 0))
     own, other = pl.pallas_call(

time: 118 us -> 114 us (0.966)
  waiting for transfers between devices: 19.6 us -> 13.9 us
  starting transfers between devices: 27.2 us -> 29.3 us
    ppermute x2, waiting for transfers between devices: 4 us -> 0.01 us  [body(): other = lax.ppermute(other, 'col', mates)]
    all_to_all x2, waiting for transfers between devices: 12.7 us -> 8.76 us  [swap_members(): lax.all_to_all(array, axes, split_axis=0, concat_axis=0, axis_index_group...]
    all_to_all x2, starting transfers between devices: 12.3 us -> 15.3 us  [swap_members(): lax.all_to_all(array, axes, split_axis=0, concat_axis=0, axis_index_group...]
    ppermute x2, waiting for transfers between devices: 0.91 us -> 2.48 us  [beside(): before = lax.ppermute(array, axis, up)]
    unnamed x14 -> x16, local copies, waits for them, and re-layouts: 3.2 us -> 3.2 us
  transfers between devices with their start and end apart: 10 -> 10, of which waited for: 6 -> 6; matrix products, arithmetic and copies ran while one was open for 2% -> 2% of each run, Pallas kernels for 6% -> 9%
where the time goes in v9:
time: 114 us; the launch traced here: 113 us
  Pallas kernels  63.5 us (56%)
  starting transfers between devices  29.3 us (26%)
  waiting for transfers between devices  13.9 us (12%)
  local copies, waits for them, and re-layouts  3.31 us (3%)
  other arithmetic  3 us (3%)
    pallas_call x1, Pallas kernels, body(): pl.pallas_call(functools.partial(scatter_kernel, cols, gs, fs), grid=(1 +...  16.7 us
    all_to_all x2, starting transfers between devices, swap_members(): lax.all_to_all(array, axes, split_axis=0, concat_axis=0, axis_index_group...  15.3 us
    pallas_call x1, Pallas kernels, body(): pl.pallas_call(functools.partial(sample_kernel, cols), grid=(steps,), in_...  14.2 us
    pallas_call x1, Pallas kernels, body(): pl.pallas_call(spectrum_kernel, grid=(gs // BATCH,), in_specs=[smem, part...  11 us
    all_to_all x2, waiting for transfers between devices, swap_members(): lax.all_to_all(array, axes, split_axis=0, concat_axis=0, axis_index_group...  8.76 us
    ppermute x2, starting transfers between devices, beside(): before = lax.ppermute(array, axis, up)  7.58 us
    pallas_call x1, Pallas kernels, body(): pl.pallas_call(near_kernel, grid=(pairs // blocks,), in_specs=[smem, pl.B...  6.82 us
    pallas_call x1, Pallas kernels, body(): pl.pallas_call(project_kernel, out_shape=(struct((blocks, LANES), jnp.bfl...  6.4 us
  transfers between devices with their start and end apart: 10, of which 6 were waited for; matrix products, arithmetic and copies ran while one was open for 2% of the time, Pallas kernels for 9%

profile of v9, /device:TPU:0, one launch (start us, length us, event | category | flops | bytes accessed | tf_op | source)
XLA Modules:
  0.0 113.3 jit_solution(5157332676321607939)
XLA Ops:
  0.0 6.4 %project.1 = (bf16[128,128]{1,0:T(8,128)(2,1)}, bf16[16,80,128]{2,1,0:T(8,128)(2,1)}, s32[128,128]{1,0:T(8,128)}) custom-call(bf16[64,128]{1,0:T(8,128)(2,1)} %bitcast.29, s32[64,128]{1,0:T(8,128)} %bitcast.18, bf16[128,4096]{1,0:T(8,128)(2,1)} %project_in.1, s32[3,128]{1,0:T(4,128)} %anchors_in.1), custom_call_target="tpu_custom_call" | custom-call | tf_op jit(solution)/shard_map/project/pallas_call | solution.py:513
  6.4 8.3 %all-to-all-start = ((bf16[16,80,128]{2,1,0:T(8,128)(2,1)}), bf16[16,80,128]{2,1,0:T(8,128)(2,1)S(1)}, u32[]{:S(2)}, u32[]{:S(2)}) async-start(bf16[16,80,128]{2,1,0:T(8,128)(2,1)} %get-tuple-element.24), calls=%async_computation | async-start | bytes 655360 | tf_op jit(solution)/shard_map/all_to_all | solution.py:544
  14.8 0.7 copy-done.4
  15.5 3.8 %inverse.1 = s32[128,128]{1,0:T(8,128)S(1)} custom-call(s32[64,128]{1,0:T(8,128)S(1)} %bitcast.19), custom_call_target="tpu_custom_call" | custom-call | tf_op jit(solution)/shard_map/inverse/pallas_call | solution.py:550
  19.4 6.6 %all-to-all-done.mine = bf16[16,80,128]{2,1,0:T(8,128)(2,1)S(1)} async-done(((bf16[16,80,128]{2,1,0:T(8,128)(2,1)}), bf16[16,80,128]{2,1,0:T(8,128)(2,1)S(1)}, u32[]{:S(2)}, u32[]{:S(2)}) %all-to-all-start) | async-done | bytes 327712 | tf_op jit(solution)/shard_map/all_to_all | solution.py:544
  26.2 1.5 %collective-permute-done.theirs = bf16[16,80,128]{2,1,0:T(8,128)(2,1)S(1)} collective-permute-done((bf16[16,80,128]{2,1,0:T(8,128)(2,1)S(1)}, bf16[16,80,128]{2,1,0:T(8,128)(2,1)S(1)}, u32[]{:S(2)}, u32[]{:S(2)}) %collective-permute-start) | collective-permute-done | bytes 327712 | tf_op jit(solution)/shard_map/ppermute | solution.py:549
  27.9 16.7 %scatter.1 = (bf16[64,128,128]{2,1,0:T(8,128)(2,1)}, bf16[64,128,128]{2,1,0:T(8,128)(2,1)}) custom-call(s32[3]{0:T(128)S(1)} %pad_add_fusion.place, s32[4096]{0:T(1024)S(1)} %get-tuple-element.52.shift, s32[4096]{0:T(1024)S(1)} %get-tuple-element.43.start, bf16[16,80,128]{2,1,0:T(8,128)(2,1)S(1)} %all-to-all-done.mine, ...), custom_call_target="tpu_custom_call" | custom-call | tf_op jit(solution)/shard_map/scatter/pallas_call | solution.py:577
  45.3 1.3 %collective-permute-start.3 = (bf16[1,1,128,128]{3,2,1,0:T(8,128)(2,1)S(1)}, bf16[1,1,128,128]{3,2,1,0:T(8,128)(2,1)S(1)}, u32[]{:S(2)}, u32[]{:S(2)}) collective-permute-start(bf16[1,1,128,128]{3,2,1,0:T(8,128)(2,1)S(1)} %bitcast.26), channel_id=1, source_target_pairs={{4,0},{8,4},{12,8},{16,12},{20,16},{24,20},{28,24},{5,1},{9,5},{13... | collective-permute-start | bytes 98312 | tf_op jit(solution)/shard_map/ppermute | solution.py:482
  46.6 4.5 %collective-permute-start.2 = (bf16[1,1,128,128]{3,2,1,0:T(8,128)(2,1)S(1)}, bf16[1,1,128,128]{3,2,1,0:T(8,128)(2,1)S(1)}, u32[]{:S(2)}, u32[]{:S(2)}) collective-permute-start(bf16[1,1,128,128]{3,2,1,0:T(8,128)(2,1)S(1)} %bitcast.27), channel_id=1, source_target_pairs={{0,4},{4,8},{8,12},{12,16},{16,20},{20,24},{24,28},{1,5},{5,9},{9,... | collective-permute-start | bytes 98312 | tf_op jit(solution)/shard_map/ppermute | solution.py:481
  51.2 1.6 %collective-permute-done.2 = bf16[1,1,128,128]{3,2,1,0:T(8,128)(2,1)S(1)} collective-permute-done((bf16[1,1,128,128]{3,2,1,0:T(8,128)(2,1)S(1)}, bf16[1,1,128,128]{3,2,1,0:T(8,128)(2,1)S(1)}, u32[]{:S(2)}, u32[]{:S(2)}) %collective-permute-start.2) | collective-permute-done | bytes 32800 | tf_op jit(solution)/shard_map/ppermute | solution.py:481
  52.8 1.6 %copy-done.1 = bf16[64,128,128]{2,1,0:T(8,128)(2,1)S(1)} copy-done((bf16[64,128,128]{2,1,0:T(8,128)(2,1)S(1)}, bf16[64,128,128]{2,1,0:T(8,128)(2,1)}, u32[]{:S(2)}) %copy-start.1) | copy-done | bytes 2097176
  54.4 11.0 %spectrum.1 = (bf16[64,128,128]{2,1,0:T(8,128)(2,1)S(1)}, bf16[64,128,128]{2,1,0:T(8,128)(2,1)S(1)}) custom-call(s32[3]{0:T(128)S(1)} %pad_add_fusion.place, bf16[64,128,128]{2,1,0:T(8,128)(2,1)S(1)} %copy-done.1, bf16[64,128,128]{2,1,0:T(8,128)(2,1)S(1)} %collective-permute-done.1.other, f32[64,128,512]{2,1,0:T(8,128)} %weights.1, bf16[512,512]{1,0:T(8,128)(2,1)S(1)} %copy-done), custom_call_target="tpu_custom_call" | custom-call | tf_op jit(solution)/shard_map/spectrum/pallas_call | solution.py:598
  65.5 1.3 %collective-permute-start.6 = (bf16[3,1,128,128]{3,2,1,0:T(8,128)(2,1)S(1)}, bf16[3,1,128,128]{3,2,1,0:T(8,128)(2,1)S(1)}, u32[]{:S(2)}, u32[]{:S(2)}) collective-permute-start(bf16[3,1,128,128]{3,2,1,0:T(8,128)(2,1)S(1)} %pad_maximum_fusion.1), channel_id=1, source_target_pairs={{1,0},{2,1},{3,2},{5,4},{6,5},{7,6},{9,8},{10,9},{11,10},{13,12},{... | collective-permute-start | bytes 294920 | tf_op jit(solution)/shard_map/ppermute | solution.py:482
  66.8 3.0 %collective-permute-start.5 = (bf16[3,1,128,128]{3,2,1,0:T(8,128)(2,1)S(1)}, bf16[3,1,128,128]{3,2,1,0:T(8,128)(2,1)S(1)}, u32[]{:S(2)}, u32[]{:S(2)}) collective-permute-start(bf16[3,1,128,128]{3,2,1,0:T(8,128)(2,1)S(1)} %pad_maximum_fusion.1), channel_id=1, source_target_pairs={{0,1},{1,2},{2,3},{4,5},{5,6},{6,7},{8,9},{9,10},{10,11},{12,13},{... | collective-permute-start | bytes 294920 | tf_op jit(solution)/shard_map/ppermute | solution.py:481
  69.8 0.9 collective-permute-done.5
  71.5 14.2 %sample.1 = bf16[32,64,128]{2,1,0:T(8,128)(2,1)S(1)} custom-call(s32[3]{0:T(128)S(1)} %pad_add_fusion.place, s32[4096]{0:T(1024)S(1)} %get-tuple-element.51.shift, s32[4096]{0:T(1024)S(1)} %get-tuple-element.44.start, bf16[16,80,128]{2,1,0:T(8,128)(2,1)S(1)} %all-to-all-done.mine, bf16[16,80,128]{2,1,0:T(8,128)(2,1)S(1)} %collective-permute-done.theirs, ...), custom_call_target="tpu_custom_call" | custom-call | tf_op jit(solution)/shard_map/sample/pallas_call | solution.py:619
  85.7 3.0 %collective-permute-start.7 = (bf16[16,64,128]{2,1,0:T(8,128)(2,1)S(1)}, bf16[16,64,128]{2,1,0:T(8,128)(2,1)S(1)}, u32[]{:S(2)}, u32[]{:S(2)}) collective-permute-start(bf16[16,64,128]{2,1,0:T(8,128)(2,1)S(1)} %slice.42), channel_id=1, source_target_pairs={{0,1},{1,0},{2,3},{3,2},{4,5},{5,4},{6,7},{7,6},{8,9},{9,8},{10,11... | collective-permute-start | bytes 786440 | tf_op jit(solution)/shard_map/ppermute | solution.py:636
  88.7 1.2 %collective-permute-done.7 = bf16[16,64,128]{2,1,0:T(8,128)(2,1)S(1)} collective-permute-done((bf16[16,64,128]{2,1,0:T(8,128)(2,1)S(1)}, bf16[16,64,128]{2,1,0:T(8,128)(2,1)S(1)}, u32[]{:S(2)}, u32[]{:S(2)}) %collective-permute-start.7) | collective-permute-done | bytes 262176 | tf_op jit(solution)/shard_map/ppermute | solution.py:636
  89.9 0.8 add_convert_fusion
  90.7 7.0 %all-to-all-start.1 = ((bf16[16,64,128]{2,1,0:T(8,128)(2,1)}), bf16[16,64,128]{2,1,0:T(8,128)(2,1)S(1)}, u32[]{:S(2)}, u32[]{:S(2)}) async-start(bf16[16,64,128]{2,1,0:T(8,128)(2,1)} %add_convert_fusion), calls=%async_computation.1 | async-start | bytes 524288 | tf_op jit(solution)/shard_map/all_to_all | solution.py:544
  98.9 6.8 %near.1 = f32[128,128]{1,0:T(8,128)} custom-call(s32[512]{0:T(512)} %fusion.11.source, bf16[512,4096]{1,0:T(8,128)(2,1)} %near_blocks.1, s32[1,512]{1,0:T(1,128)} %get-tuple-element.49.target, bf16[9,128,128]{2,1,0:T(8,128)(2,1)} %bitcast.20), custom_call_target="tpu_custom_call" | custom-call | tf_op jit(solution)/shard_map/near/pallas_call | solution.py:647
  105.7 2.1 %all-to-all-done.1.values = bf16[16,64,128]{2,1,0:T(8,128)(2,1)S(1)} async-done(((bf16[16,64,128]{2,1,0:T(8,128)(2,1)}), bf16[16,64,128]{2,1,0:T(8,128)(2,1)S(1)}, u32[]{:S(2)}, u32[]{:S(2)}) %all-to-all-start.1) | async-done | bytes 262176 | tf_op jit(solution)/shard_map/all_to_all | solution.py:544
  107.9 0.8 copy-done.3
  108.7 4.6 %finish.1 = f32[64,128]{1,0:T(8,128)} custom-call(bf16[16,64,128]{2,1,0:T(8,128)(2,1)S(1)} %all-to-all-done.1.values, bf16[128,4096]{1,0:T(8,128)(2,1)S(1)} %copy-done.2, f32[128,128]{1,0:T(8,128)S(1)} %copy-done.3, s32[128,128]{1,0:T(8,128)S(1)} %inverse.1, s32[128,128]{1,0:T(8,128)S(1)} %copy-done.5), custom_call_target="tpu_custom_call" | custom-call | tf_op jit(solution)/shard_map/finish/pallas_call | solution.py:666
  (37 shorter events, 3.1 us)
Async XLA Ops:
  0.0 52.8 %copy-start = (bf16[512,512]{1,0:T(8,128)(2,1)S(1)}, bf16[512,512]{1,0:T(8,128)(2,1)}, u32[]{:S(2)}) copy-start(bf16[512,512]{1,0:T(8,128)(2,1)} %constant.137.clone.cas) | copy-start | bytes 1572868
  6.4 38.9 %copy-start.6 = (bf16[128,128]{1,0:T(8,128)(2,1)S(1)}, bf16[128,128]{1,0:T(8,128)(2,1)}, u32[]{:S(2)}) copy-start(bf16[128,128]{1,0:T(8,128)(2,1)} %get-tuple-element.30) | copy-start | bytes 98308
  6.4 19.6 %all-to-all-start = ((bf16[16,80,128]{2,1,0:T(8,128)(2,1)}), bf16[16,80,128]{2,1,0:T(8,128)(2,1)S(1)}, u32[]{:S(2)}, u32[]{:S(2)}) async-start(bf16[16,80,128]{2,1,0:T(8,128)(2,1)} %get-tuple-element.24), calls=%async_computation | async-start | bytes 655360 | tf_op jit(solution)/shard_map/all_to_all | solution.py:544
  14.8 0.8 copy-start.4
  26.1 1.6 %collective-permute-start = (bf16[16,80,128]{2,1,0:T(8,128)(2,1)S(1)}, bf16[16,80,128]{2,1,0:T(8,128)(2,1)S(1)}, u32[]{:S(2)}, u32[]{:S(2)}) collective-permute-start(bf16[16,80,128]{2,1,0:T(8,128)(2,1)S(1)} %all-to-all-done.mine), channel_id=1, source_target_pairs={{0,1},{1,0},{2,3},{3,2},{4,5},{5,4},{6,7},{7,6},{8,9},{9,8},{10,11... | collective-permute-start | bytes 983048 | tf_op jit(solution)/shard_map/ppermute | solution.py:549
  44.6 8.1 %collective-permute-start.1 = (bf16[64,128,128]{2,1,0:T(8,128)(2,1)}, bf16[64,128,128]{2,1,0:T(8,128)(2,1)S(1)}, u32[]{:S(2)}, u32[]{:S(2)}) collective-permute-start(bf16[64,128,128]{2,1,0:T(8,128)(2,1)} %get-tuple-element.29), channel_id=1, source_target_pairs={{0,1},{1,0},{2,3},{3,2},{4,5},{5,4},{6,7},{7,6},{8,9},{9,8},{10,11... | collective-permute-start | bytes 6291464 | tf_op jit(solution)/shard_map/ppermute | solution.py:592
  45.3 5.8 %collective-permute-start.3 = (bf16[1,1,128,128]{3,2,1,0:T(8,128)(2,1)S(1)}, bf16[1,1,128,128]{3,2,1,0:T(8,128)(2,1)S(1)}, u32[]{:S(2)}, u32[]{:S(2)}) collective-permute-start(bf16[1,1,128,128]{3,2,1,0:T(8,128)(2,1)S(1)} %bitcast.26), channel_id=1, source_target_pairs={{4,0},{8,4},{12,8},{16,12},{20,16},{24,20},{28,24},{5,1},{9,5},{13... | collective-permute-start | bytes 98312 | tf_op jit(solution)/shard_map/ppermute | solution.py:482
  46.6 6.1 %collective-permute-start.2 = (bf16[1,1,128,128]{3,2,1,0:T(8,128)(2,1)S(1)}, bf16[1,1,128,128]{3,2,1,0:T(8,128)(2,1)S(1)}, u32[]{:S(2)}, u32[]{:S(2)}) collective-permute-start(bf16[1,1,128,128]{3,2,1,0:T(8,128)(2,1)S(1)} %bitcast.27), channel_id=1, source_target_pairs={{0,4},{4,8},{8,12},{12,16},{16,20},{20,24},{24,28},{1,5},{5,9},{9,... | collective-permute-start | bytes 98312 | tf_op jit(solution)/shard_map/ppermute | solution.py:481
  52.8 1.6 %copy-start.1 = (bf16[64,128,128]{2,1,0:T(8,128)(2,1)S(1)}, bf16[64,128,128]{2,1,0:T(8,128)(2,1)}, u32[]{:S(2)}) copy-start(bf16[64,128,128]{2,1,0:T(8,128)(2,1)} %get-tuple-element.28.own) | copy-start | bytes 6291460
  65.4 6.1 %collective-permute-start.4 = (bf16[64,128,128]{2,1,0:T(8,128)(2,1)S(1)}, bf16[64,128,128]{2,1,0:T(8,128)(2,1)S(1)}, u32[]{:S(2)}, u32[]{:S(2)}) collective-permute-start(bf16[64,128,128]{2,1,0:T(8,128)(2,1)S(1)} %get-tuple-element.35), channel_id=1, source_target_pairs={{0,1},{1,0},{2,3},{3,2},{4,5},{5,4},{6,7},{7,6},{8,9},{9,8},{10,11... | collective-permute-start | bytes 6291464 | tf_op jit(solution)/shard_map/ppermute | solution.py:613
  65.5 4.3 %collective-permute-start.6 = (bf16[3,1,128,128]{3,2,1,0:T(8,128)(2,1)S(1)}, bf16[3,1,128,128]{3,2,1,0:T(8,128)(2,1)S(1)}, u32[]{:S(2)}, u32[]{:S(2)}) collective-permute-start(bf16[3,1,128,128]{3,2,1,0:T(8,128)(2,1)S(1)} %pad_maximum_fusion.1), channel_id=1, source_target_pairs={{1,0},{2,1},{3,2},{5,4},{6,5},{7,6},{9,8},{10,9},{11,10},{13,12},{... | collective-permute-start | bytes 294920 | tf_op jit(solution)/shard_map/ppermute | solution.py:482
  66.8 4.0 %collective-permute-start.5 = (bf16[3,1,128,128]{3,2,1,0:T(8,128)(2,1)S(1)}, bf16[3,1,128,128]{3,2,1,0:T(8,128)(2,1)S(1)}, u32[]{:S(2)}, u32[]{:S(2)}) collective-permute-start(bf16[3,1,128,128]{3,2,1,0:T(8,128)(2,1)S(1)} %pad_maximum_fusion.1), channel_id=1, source_target_pairs={{0,1},{1,2},{2,3},{4,5},{5,6},{6,7},{8,9},{9,10},{10,11},{12,13},{... | collective-permute-start | bytes 294920 | tf_op jit(solution)/shard_map/ppermute | solution.py:481
  71.5 26.2 %copy-start.7 = (s32[2,512]{1,0:T(2,128)S(1)}, s32[2,512]{1,0:T(2,128)}, u32[]{:S(2)}) copy-start(s32[2,512]{1,0:T(2,128)} %param.15) | copy-start | bytes 12292
  85.7 4.2 %collective-permute-start.7 = (bf16[16,64,128]{2,1,0:T(8,128)(2,1)S(1)}, bf16[16,64,128]{2,1,0:T(8,128)(2,1)S(1)}, u32[]{:S(2)}, u32[]{:S(2)}) collective-permute-start(bf16[16,64,128]{2,1,0:T(8,128)(2,1)S(1)} %slice.42), channel_id=1, source_target_pairs={{0,1},{1,0},{2,3},{3,2},{4,5},{5,4},{6,7},{7,6},{8,9},{9,8},{10,11... | collective-permute-start | bytes 786440 | tf_op jit(solution)/shard_map/ppermute | solution.py:636
  90.7 17.2 %all-to-all-start.1 = ((bf16[16,64,128]{2,1,0:T(8,128)(2,1)}), bf16[16,64,128]{2,1,0:T(8,128)(2,1)S(1)}, u32[]{:S(2)}, u32[]{:S(2)}) async-start(bf16[16,64,128]{2,1,0:T(8,128)(2,1)} %add_convert_fusion), calls=%async_computation.1 | async-start | bytes 524288 | tf_op jit(solution)/shard_map/all_to_all | solution.py:544
  98.9 9.0 %copy-start.2 = (bf16[128,4096]{1,0:T(8,128)(2,1)S(1)}, bf16[128,4096]{1,0:T(8,128)(2,1)}, u32[]{:S(2)}) copy-start(bf16[128,4096]{1,0:T(8,128)(2,1)} %interpolate.1) | copy-start | bytes 3145732
  98.9 9.0 %copy-start.5 = (s32[128,128]{1,0:T(8,128)S(1)}, s32[128,128]{1,0:T(8,128)}, u32[]{:S(2)}) copy-start(s32[128,128]{1,0:T(8,128)} %get-tuple-element.42.spots) | copy-start | bytes 196612
  107.9 0.8 copy-start.3

commit v10 on v8

--- a/solution.py
+++ b/solution.py
@@ -106,8 +106,7 @@
     order_in,
     project_in,
     anchors_in,
-    charge_out,
-    patch_out,
+    sent_out,
     spot_out,
     charges,
     order,
@@ -117,7 +116,7 @@
     doubled,
     sems,
 ):
-    blocks = charge_out.shape[0]
+    blocks = spot_out.shape[0]
     groups = blocks // GROUP
     pairs = ((charges_in, charges), (order_in, order), (project_in, project), (anchors_in, anchors))
     copies = [pltpu.make_async_copy(a, b, sems.at[n]) for n, (a, b) in enumerate(pairs)]
@@ -140,7 +139,6 @@
     doubled[pl.ds(0, strips, stride=2), :] = jnp.where(left, slots, swapped)
     doubled[pl.ds(1, strips, stride=2), :] = jnp.where(left, swapped, slots)
     twice = doubled[...]
-    charge_out[...] = twice.astype(jnp.bfloat16)
     copies[2].wait()
     copies[3].wait()
     patch = block_sums(project, twice)
@@ -151,20 +149,22 @@
     moved = (iota(spots.shape, 1) == spots).astype(jnp.float32).astype(jnp.bfloat16)
     corner = anchors[...].astype(jnp.float32).astype(jnp.bfloat16)
     corner = dot(jnp.concatenate([corner] * 3, axis=0)[:8], moved)
-    spread = jnp.zeros((16, 4 * blocks), jnp.float32)
     cells = (iota((8, 4 * blocks), 1) % 4).astype(jnp.float32)
     start = jnp.broadcast_to(anchors[:1, :].astype(jnp.float32), (8, blocks)).astype(jnp.bfloat16)
     for i in range(4):
+        cells = cells + dot(start, lanes[i])
+    spread = jnp.zeros((16, 4 * blocks), jnp.float32)
+    for i in range(4):
         spread = spread + dot(dot_nt(rows[i], patch).astype(jnp.bfloat16), lanes[i])
-        cells = cells + dot(start, lanes[i])
     tiles = [slice(LANES * t, LANES * t + LANES) for t in range(groups)]
     sent = [spread[:, tile].astype(jnp.bfloat16) for tile in tiles]
+    sent.append(slots.astype(jnp.bfloat16))
     extra = [cells[:1, tile] for tile in tiles] + [corner[:3]]
     extra.append(jnp.zeros((13 - groups, LANES), jnp.float32))
     sent.append(jnp.concatenate(extra, axis=0).astype(jnp.bfloat16))
-    for n in range(patch_out.shape[0]):
-        for t, part in enumerate(sent):
-            patch_out[n, 16 * t : 16 * t + 16] = part
+    sent = jnp.concatenate(sent, axis=0)
+    for n in range(sent_out.shape[0]):
+        sent_out[n] = sent
 
 
 def inverse_kernel(order, out):
@@ -190,15 +190,22 @@
     ).astype(jnp.int32)
 
 
-def near_kernel(source, near_blocks, target, charges, out, table, picked):
+def near_kernel(source, near_blocks, target, mine, theirs, out, table, picked):
     step = pl.program_id(0)
     pairs = picked.shape[0]
     blocks = out.shape[0]
 
     @pl.when(step == 0)
     def _():
-        for d in range(charges.shape[0]):
-            table[d * blocks : (d + 1) * blocks] = charges[d].astype(jnp.float32)
+        members, strips, _ = mine.shape
+        left = iota((strips, LANES), 1) < BLK
+        for side, part in enumerate((mine, theirs)):
+            for n in range(members):
+                at = (side * members + n) * blocks
+                slots = part[n].astype(jnp.float32)
+                swapped = pltpu.roll(slots, BLK, 1)
+                table[pl.ds(at, strips, stride=2), :] = jnp.where(left, slots, swapped)
+                table[pl.ds(at + 1, strips, stride=2), :] = jnp.where(left, swapped, slots)
         out[...] = jnp.zeros_like(out)
 
     def pick(p, carry):
@@ -253,7 +260,23 @@
 
 
 def scatter_kernel(
-    cols, gs, fs, place, shift, start, mine, theirs, cas, own_out, other_out, patches, extra, lines, *slabs
+    cols,
+    gs,
+    fs,
+    place,
+    shift,
+    start,
+    mine,
+    theirs,
+    my_extra,
+    their_extra,
+    cas,
+    own_out,
+    other_out,
+    patches,
+    extra,
+    lines,
+    *slabs,
 ):
     half = place[0]
     step = pl.program_id(0)
@@ -273,10 +296,10 @@
             return carry
 
         lax.fori_loop(0, slabs[0].shape[0] // SLAB, clear, 0)
-        for side, part in enumerate((mine, theirs)):
+        for side, part in enumerate(((mine, my_extra), (theirs, their_extra))):
             at = slice(side * (devices // 2), (side + 1) * (devices // 2))
-            patches[at] = part[:, :held]
-            extra[at] = part[:, held:]
+            patches[at] = part[0][...]
+            extra[at] = part[1][...]
 
         def tile(numbers, t):
             values = []
@@ -364,7 +387,21 @@
 
 
 def sample_kernel(
-    cols, place, shift, start, mine, theirs, own, other, cas, out, extra, second, third, lines, cells
+    cols,
+    place,
+    shift,
+    start,
+    my_extra,
+    their_extra,
+    own,
+    other,
+    cas,
+    out,
+    extra,
+    second,
+    third,
+    lines,
+    cells,
 ):
     half = place[0]
     step = pl.program_id(0)
@@ -377,8 +414,8 @@
 
     @pl.when(step == 0)
     def _():
-        for side, part in enumerate((mine, theirs)):
-            extra[side * (devices // 2) : (side + 1) * (devices // 2)] = part[:, held:]
+        for side, part in enumerate((my_extra, their_extra)):
+            extra[side * (devices // 2) : (side + 1) * (devices // 2)] = part[...]
         second[...] = turned(table_rows(cas, [place[1]], gs))
         third[...] = turned(table_rows(cas, [place[2], place[2] ^ 1], own.shape[1]))
 
@@ -472,14 +509,6 @@
 
 def params(mib):
     return pltpu.CompilerParams(vmem_limit_bytes=mib * MB)
-
-
-def beside(array, axis, dim):
-    count = lax.axis_size(axis)
-    up = [(i, i + 1) for i in range(count - 1)]
-    before = lax.ppermute(array, axis, up)
-    after = lax.ppermute(array, axis, [(j, i) for i, j in up])
-    return jnp.concatenate([before, array, after], axis=dim)
 
 
 def body(
@@ -505,14 +534,13 @@
     panels = charges.shape[0]
     strips = panels // LANES
     gs, fs, _ = kernel_spectrum.shape
-    held = 16 * groups + 16
+    held = 16 * groups + strips + 16
 
     order = panel_order.reshape(strips, LANES)
     members = devices // HALVES
-    block_charges, sent, spots = pl.pallas_call(
+    sent, spots = pl.pallas_call(
         project_kernel,
         out_shape=(
-            struct((blocks, LANES), jnp.bfloat16),
             struct((members, held, LANES), jnp.bfloat16),
             struct((blocks, LANES), jnp.int32),
         ),
@@ -546,7 +574,6 @@
 
     mine = swap_members(sent)
     theirs = lax.ppermute(mine, "col", mates)
-    order, block_charges = lax.optimization_barrier((order, block_charges))
     inverse = pl.pallas_call(
         inverse_kernel,
         out_shape=struct((2 * strips, LANES), jnp.int32),
@@ -554,10 +581,9 @@
         name="inverse",
     )(order)
 
-    block_charges, inverse = lax.optimization_barrier((block_charges, inverse))
-    around = beside(block_charges[None, None], "row", 0)
-    mine, around, inverse = lax.optimization_barrier((mine, around, inverse))
-    anchors = jnp.stack([part[:, 17 * groups : 17 * groups + 3] for part in (mine, theirs)])
+    mine, inverse = lax.optimization_barrier((mine, inverse))
+    at = held - 16 + groups
+    anchors = jnp.stack([part[:, at : at + 3] for part in (mine, theirs)])
     anchors = anchors.astype(jnp.int32)
     lane = 4 * (jnp.arange(blocks, dtype=jnp.int32) % GROUP)
     forth = ((anchors[:, :, 0] - lane) & (LANES - 1)).reshape(devices * blocks)
@@ -573,13 +599,20 @@
     cas = jnp.asarray(CAS)
 
     smem = pl.BlockSpec(memory_space=pltpu.SMEM)
+
+    def rows_at(start, count):
+        return pl.BlockSpec((members, count, LANES), lambda *_: (0, start // count, 0))
+
+    patch_rows = rows_at(0, 16 * groups)
+    charge_rows = rows_at(16 * groups, strips)
+    extra_rows = rows_at(16 * groups + strips, 16)
     steps = gs // LINES
     lines_type = struct((gs, fs, LANES), jnp.bfloat16)
     late = pl.BlockSpec((LINES, fs, LANES), lambda n: (jnp.maximum(n - 1, 0), 0, 0))
     own, other = pl.pallas_call(
         functools.partial(scatter_kernel, cols, gs, fs),
         grid=(1 + steps,),
-        in_specs=[smem] * 3 + [whole(mine.shape)] * 2 + [whole(cas.shape)],
+        in_specs=[smem] * 3 + [patch_rows] * 2 + [extra_rows] * 2 + [whole(cas.shape)],
         out_specs=(late, late),
         out_shape=(lines_type, lines_type),
         scratch_shapes=[
@@ -590,7 +623,7 @@
         + [pltpu.VMEM(((G // QUAD + 1) * SLAB, LANES), jnp.float32)] * SLABS,
         compiler_params=params(53),
         name="scatter",
-    )(place, forth, slab_at, mine, theirs, cas)
+    )(place, forth, slab_at, mine, theirs, mine, theirs, cas)
     other = lax.ppermute(other, "col", mates)
 
     part = lambda shape: pl.BlockSpec((BATCH,) + shape, lambda n: (n, 0, 0))
@@ -610,15 +643,12 @@
         name="spectrum",
     )(place, own, other, kernel_spectrum, cas)
     other = lax.ppermute(other, "col", mates)
-    own, around = lax.optimization_barrier((own, around))
-    around = beside(around, "col", 1).reshape(9, blocks, LANES)
-    other, around = lax.optimization_barrier((other, around))
 
     early = pl.BlockSpec((LINES, fs, LANES), lambda n: (n, 0, 0))
     values = pl.pallas_call(
         functools.partial(sample_kernel, cols),
         grid=(steps,),
-        in_specs=[smem] * 3 + [whole(mine.shape)] * 2 + [early, early, whole(cas.shape)],
+        in_specs=[smem] * 3 + [extra_rows] * 2 + [early, early, whole(cas.shape)],
         out_specs=whole((devices, 16 * groups, LANES)),
         out_shape=struct((devices, 16 * groups, LANES), jnp.bfloat16),
         scratch_shapes=[
@@ -634,13 +664,14 @@
     values = values.reshape(HALVES, members, 16 * groups, LANES)
     received = lax.ppermute(values[1], "col", mates).astype(jnp.float32)
     values = (values[0].astype(jnp.float32) + received).astype(jnp.bfloat16)
-    values, around = lax.optimization_barrier((values, around))
+    values, my_charges, their_charges = lax.optimization_barrier((values, mine, theirs))
     values = swap_members(values)
 
     source = near_pairs[1]
-    source_device = source // blocks
-    code = (source_device // cols - row_at + 1) * 3 + (source_device % cols - col_at + 1)
-    wanted = code * blocks + source % blocks
+    source_row = source // blocks // cols
+    source_col = source // blocks % cols
+    wanted = (source_col % HALVES ^ half) * members + source_row * (cols // HALVES)
+    wanted = (wanted + source_col // HALVES) * blocks + source % blocks
     target = near_pairs[0] - (row_at * cols + col_at) * blocks
     pairs = near_blocks.shape[0]
     near = pl.pallas_call(
@@ -650,17 +681,18 @@
             smem,
             pl.BlockSpec((blocks, BLK * BLK), lambda n: (n, 0)),
             pl.BlockSpec((1, blocks), lambda n: (0, n)),
-            whole((9, blocks, LANES)),
+            charge_rows,
+            charge_rows,
         ],
         out_specs=whole((blocks, LANES)),
         out_shape=struct((blocks, LANES), jnp.float32),
         scratch_shapes=[
-            pltpu.VMEM((9 * blocks, LANES), jnp.float32),
+            pltpu.VMEM((devices * blocks, LANES), jnp.float32),
             pltpu.VMEM((blocks, LANES), jnp.float32),
         ],
         compiler_params=params(56),
         name="near",
-    )(wanted, near_blocks, target.reshape(1, pairs), around)
+    )(wanted, near_blocks, target.reshape(1, pairs), my_charges, their_charges)
 
     result = pl.pallas_call(
         finish_kernel,

time: 118 us -> 112 us (0.949)
  starting transfers between devices: 27.2 us -> 15 us
  waiting for transfers between devices: 19.6 us -> 27.3 us
  other arithmetic: 3.76 us -> 2.26 us
    ppermute x4 -> x0, starting transfers between devices: 11.1 us -> none  [the longest x2 8.51 us: beside(): before = lax.ppermute(array, axis, up)]
    all_to_all x2, waiting for transfers between devices: 12.7 us -> 18.3 us  [swap_members(): lax.all_to_all(array, axes, split_axis=0, concat_axis=0, axis_index_group...]
    ppermute x2, waiting for transfers between devices: 4 us -> 7.78 us  [body(): other = lax.ppermute(other, 'col', mates)]
    ppermute x1, starting transfers between devices: 2.7 us -> 0.99 us  [body(): received = lax.ppermute(values[1], 'col', mates).astype(jnp.float32)]
    concatenate x2 -> x0, other arithmetic: 1.52 us -> none  [beside(): return jnp.concatenate([before, array, after], axis=dim)]
    unnamed x14 -> x22, local copies, waits for them, and re-layouts: 3.2 us -> 3.06 us
  transfers between devices with their start and end apart: 10 -> 6, of which waited for: 6 -> 5; matrix products, arithmetic and copies ran while one was open for 2% -> 1% of each run, Pallas kernels for 6% -> 10%
where the time goes in v10:
time: 112 us; the launch traced here: 111 us
  Pallas kernels  63.5 us (57%)
  waiting for transfers between devices  27.3 us (24%)
  starting transfers between devices  15 us (13%)
  local copies, waits for them, and re-layouts  3.17 us (3%)
  other arithmetic  2.26 us (2%)
    all_to_all x2, waiting for transfers between devices, swap_members(): lax.all_to_all(array, axes, split_axis=0, concat_axis=0, axis_index_group...  18.3 us
    pallas_call x1, Pallas kernels, body(): pl.pallas_call(functools.partial(scatter_kernel, cols, gs, fs), grid=(1 +...  16.8 us
    pallas_call x1, Pallas kernels, body(): pl.pallas_call(functools.partial(sample_kernel, cols), grid=(steps,), in_...  14.2 us
    all_to_all x2, starting transfers between devices, swap_members(): lax.all_to_all(array, axes, split_axis=0, concat_axis=0, axis_index_group...  12.5 us
    pallas_call x1, Pallas kernels, body(): pl.pallas_call(spectrum_kernel, grid=(gs // BATCH,), in_specs=[smem, part...  11.1 us
    ppermute x2, waiting for transfers between devices, body(): other = lax.ppermute(other, 'col', mates)  7.78 us
    pallas_call x1, Pallas kernels, body(): pl.pallas_call(near_kernel, grid=(pairs // blocks,), in_specs=[smem, pl.B...  7.08 us
    pallas_call x1, Pallas kernels, body(): pl.pallas_call(project_kernel, out_shape=(struct((members, held, LANES),...  6.01 us
  transfers between devices with their start and end apart: 6, of which 5 were waited for; matrix products, arithmetic and copies ran while one was open for 1% of the time, Pallas kernels for 10%

profile of v10, /device:TPU:0, one launch (start us, length us, event | category | flops | bytes accessed | tf_op | source)
XLA Modules:
  0.0 111.4 jit_solution(2951538942708332664)
XLA Ops:
  0.0 6.0 %project.1 = (bf16[16,144,128]{2,1,0:T(8,128)(2,1)}, s32[128,128]{1,0:T(8,128)}) custom-call(bf16[64,128]{1,0:T(8,128)(2,1)} %bitcast.23, s32[64,128]{1,0:T(8,128)} %bitcast.16, bf16[128,4096]{1,0:T(8,128)(2,1)} %project_in.1, s32[3,128]{1,0:T(4,128)} %anchors_in.1), custom_call_target="tpu_custom_call" | custom-call | tf_op jit(solution)/shard_map/project/pallas_call | solution.py:541
  6.0 8.3 %all-to-all-start = ((bf16[16,144,128]{2,1,0:T(8,128)(2,1)}), bf16[16,144,128]{2,1,0:T(8,128)(2,1)S(1)}, u32[]{:S(2)}, u32[]{:S(2)}) async-start(bf16[16,144,128]{2,1,0:T(8,128)(2,1)} %get-tuple-element.16), calls=%async_computation | async-start | bytes 1179648 | tf_op jit(solution)/shard_map/all_to_all | solution.py:571
  14.4 16.2 %all-to-all-done.mine.my_extra = bf16[16,144,128]{2,1,0:T(8,128)(2,1)S(1)} async-done(((bf16[16,144,128]{2,1,0:T(8,128)(2,1)}), bf16[16,144,128]{2,1,0:T(8,128)(2,1)S(1)}, u32[]{:S(2)}, u32[]{:S(2)}) %all-to-all-start) | async-done | bytes 589856 | tf_op jit(solution)/shard_map/all_to_all | solution.py:571
  30.7 3.8 %inverse.1 = s32[128,128]{1,0:T(8,128)S(1)} custom-call(s32[64,128]{1,0:T(8,128)S(1)} %bitcast.17), custom_call_target="tpu_custom_call" | custom-call | tf_op jit(solution)/shard_map/inverse/pallas_call | solution.py:577
  34.5 0.1 fusion.18
  34.9 0.6 copy-done.2
  35.5 16.8 %scatter.1 = (bf16[64,128,128]{2,1,0:T(8,128)(2,1)}, bf16[64,128,128]{2,1,0:T(8,128)(2,1)}) custom-call(s32[3]{0:T(128)S(1)} %pad_add_fusion.place, s32[4096]{0:T(1024)S(1)} %get-tuple-element.36.shift, s32[4096]{0:T(1024)S(1)} %get-tuple-element.27.start, bf16[16,144,128]{2,1,0:T(8,128)(2,1)} %copy-done, bf16[16,144,128]{2,1,0:T(8,128)(2,1)} %copy-done.2, ...), custom_call_target="tpu_custom_call" | custom-call | tf_op jit(solution)/shard_map/scatter/pallas_call | solution.py:612
  52.2 1.0 collective-permute-start.1
  53.3 4.0 %collective-permute-done.1.other = bf16[64,128,128]{2,1,0:T(8,128)(2,1)S(1)} collective-permute-done((bf16[64,128,128]{2,1,0:T(8,128)(2,1)}, bf16[64,128,128]{2,1,0:T(8,128)(2,1)S(1)}, u32[]{:S(2)}, u32[]{:S(2)}) %collective-permute-start.1) | collective-permute-done | bytes 2097184 | tf_op jit(solution)/shard_map/ppermute | solution.py:627
  57.3 1.6 %copy-done.5 = bf16[64,128,128]{2,1,0:T(8,128)(2,1)S(1)} copy-done((bf16[64,128,128]{2,1,0:T(8,128)(2,1)S(1)}, bf16[64,128,128]{2,1,0:T(8,128)(2,1)}, u32[]{:S(2)}) %copy-start.5) | copy-done | bytes 2097176
  58.9 11.1 %spectrum.1 = (bf16[64,128,128]{2,1,0:T(8,128)(2,1)S(1)}, bf16[64,128,128]{2,1,0:T(8,128)(2,1)S(1)}) custom-call(s32[3]{0:T(128)S(1)} %pad_add_fusion.place, bf16[64,128,128]{2,1,0:T(8,128)(2,1)S(1)} %copy-done.5, bf16[64,128,128]{2,1,0:T(8,128)(2,1)S(1)} %collective-permute-done.1.other, f32[64,128,512]{2,1,0:T(8,128)} %weights.1, ...), custom_call_target="tpu_custom_call" | custom-call | tf_op jit(solution)/shard_map/spectrum/pallas_call | solution.py:630
  70.0 0.4 collective-permute-start.2
  70.4 3.8 %collective-permute-done.2.other = bf16[64,128,128]{2,1,0:T(8,128)(2,1)S(1)} collective-permute-done((bf16[64,128,128]{2,1,0:T(8,128)(2,1)S(1)}, bf16[64,128,128]{2,1,0:T(8,128)(2,1)S(1)}, u32[]{:S(2)}, u32[]{:S(2)}) %collective-permute-start.2) | collective-permute-done | bytes 2097184 | tf_op jit(solution)/shard_map/ppermute | solution.py:645
  74.2 14.2 %sample.1 = bf16[32,64,128]{2,1,0:T(8,128)(2,1)S(1)} custom-call(s32[3]{0:T(128)S(1)} %pad_add_fusion.place, s32[4096]{0:T(1024)S(1)} %get-tuple-element.35.shift, s32[4096]{0:T(1024)S(1)} %get-tuple-element.28.start, bf16[16,144,128]{2,1,0:T(8,128)(2,1)S(1)} %copy-done.1, bf16[16,144,128]{2,1,0:T(8,128)(2,1)S(1)} %copy-done.3, ...), custom_call_target="tpu_custom_call" | custom-call | tf_op jit(solution)/shard_map/sample/pallas_call | solution.py:648
  88.4 1.0 collective-permute-start.3
  89.4 1.2 %collective-permute-done.3 = bf16[16,64,128]{2,1,0:T(8,128)(2,1)S(1)} collective-permute-done((bf16[16,64,128]{2,1,0:T(8,128)(2,1)S(1)}, bf16[16,64,128]{2,1,0:T(8,128)(2,1)S(1)}, u32[]{:S(2)}, u32[]{:S(2)}) %collective-permute-start.3) | collective-permute-done | bytes 262176 | tf_op jit(solution)/shard_map/ppermute | solution.py:665
  90.6 0.8 add_convert_fusion
  91.4 4.2 %all-to-all-start.1 = ((bf16[16,64,128]{2,1,0:T(8,128)(2,1)}), bf16[16,64,128]{2,1,0:T(8,128)(2,1)S(1)}, u32[]{:S(2)}, u32[]{:S(2)}) async-start(bf16[16,64,128]{2,1,0:T(8,128)(2,1)} %add_convert_fusion), calls=%async_computation.1 | async-start | bytes 524288 | tf_op jit(solution)/shard_map/all_to_all | solution.py:571
  95.6 0.6 slice_subtract_fusion
  96.2 0.6 fusion.11.source
  96.8 7.1 %near.1 = f32[128,128]{1,0:T(8,128)} custom-call(s32[512]{0:T(512)} %fusion.11.source, bf16[512,4096]{1,0:T(8,128)(2,1)} %near_blocks.1, s32[1,512]{1,0:T(1,128)} %get-tuple-element.33.target, bf16[16,144,128]{2,1,0:T(8,128)(2,1)} %copy-done, bf16[16,144,128]{2,1,0:T(8,128)(2,1)} %copy-done.2), custom_call_target="tpu_custom_call" | custom-call | tf_op jit(solution)/shard_map/near/pallas_call | solution.py:677
  103.9 2.1 %all-to-all-done.1.values = bf16[16,64,128]{2,1,0:T(8,128)(2,1)S(1)} async-done(((bf16[16,64,128]{2,1,0:T(8,128)(2,1)}), bf16[16,64,128]{2,1,0:T(8,128)(2,1)S(1)}, u32[]{:S(2)}, u32[]{:S(2)}) %all-to-all-start.1) | async-done | bytes 262176 | tf_op jit(solution)/shard_map/all_to_all | solution.py:571
  106.0 0.8 copy-done.7
  106.8 4.6 %finish.1 = f32[64,128]{1,0:T(8,128)} custom-call(bf16[16,64,128]{2,1,0:T(8,128)(2,1)S(1)} %all-to-all-done.1.values, bf16[128,4096]{1,0:T(8,128)(2,1)S(1)} %copy-done.6, f32[128,128]{1,0:T(8,128)S(1)} %copy-done.7, s32[128,128]{1,0:T(8,128)S(1)} %inverse.1, s32[128,128]{1,0:T(8,128)S(1)} %copy-done.9), custom_call_target="tpu_custom_call" | custom-call | tf_op jit(solution)/shard_map/finish/pallas_call | solution.py:697
  (33 shorter events, 0.4 us)
Async XLA Ops:
  0.0 35.5 %copy-start.4 = (bf16[512,512]{1,0:T(8,128)(2,1)S(1)}, bf16[512,512]{1,0:T(8,128)(2,1)}, u32[]{:S(2)}) copy-start(bf16[512,512]{1,0:T(8,128)(2,1)} %constant.153.clone.cas) | copy-start | bytes 1572868
  0.0 30.6 %copy-start.8 = (s32[8192]{0:T(1024)S(1)}, s32[8192]{0:T(1024)}, u32[]{:S(2)}) copy-start(s32[8192]{0:T(1024)} %param.10) | copy-start | bytes 98308
  6.0 24.6 %all-to-all-start = ((bf16[16,144,128]{2,1,0:T(8,128)(2,1)}), bf16[16,144,128]{2,1,0:T(8,128)(2,1)S(1)}, u32[]{:S(2)}, u32[]{:S(2)}) async-start(bf16[16,144,128]{2,1,0:T(8,128)(2,1)} %get-tuple-element.16), calls=%async_computation | async-start | bytes 1179648 | tf_op jit(solution)/shard_map/all_to_all | solution.py:571
  30.6 4.2 %copy-start = (bf16[16,144,128]{2,1,0:T(8,128)(2,1)}, bf16[16,144,128]{2,1,0:T(8,128)(2,1)S(1)}, u32[]{:S(2)}) copy-start(bf16[16,144,128]{2,1,0:T(8,128)(2,1)S(1)} %all-to-all-done.mine.my_extra) | copy-start | bytes 1769476
  30.6 4.0 %collective-permute-start = (bf16[16,144,128]{2,1,0:T(8,128)(2,1)S(1)}, bf16[16,144,128]{2,1,0:T(8,128)(2,1)S(1)}, u32[]{:S(2)}, u32[]{:S(2)}) collective-permute-start(bf16[16,144,128]{2,1,0:T(8,128)(2,1)S(1)} %all-to-all-done.mine.my_extra), channel_id=1, source_target_pairs={{0,1},{1,0},{2,3},{3,2},{4,5},{5,4},{6,7},{7,6},{8,9},{9,8},{10,11... | collective-permute-start | bytes 1769480 | tf_op jit(solution)/shard_map/ppermute | solution.py:576
  34.6 0.8 copy-start.2
  52.2 5.0 %collective-permute-start.1 = (bf16[64,128,128]{2,1,0:T(8,128)(2,1)}, bf16[64,128,128]{2,1,0:T(8,128)(2,1)S(1)}, u32[]{:S(2)}, u32[]{:S(2)}) collective-permute-start(bf16[64,128,128]{2,1,0:T(8,128)(2,1)} %get-tuple-element.19), channel_id=1, source_target_pairs={{0,1},{1,0},{2,3},{3,2},{4,5},{5,4},{6,7},{7,6},{8,9},{9,8},{10,11... | collective-permute-start | bytes 6291464 | tf_op jit(solution)/shard_map/ppermute | solution.py:627
  57.3 1.6 %copy-start.5 = (bf16[64,128,128]{2,1,0:T(8,128)(2,1)S(1)}, bf16[64,128,128]{2,1,0:T(8,128)(2,1)}, u32[]{:S(2)}) copy-start(bf16[64,128,128]{2,1,0:T(8,128)(2,1)} %get-tuple-element.18.own) | copy-start | bytes 6291460
  58.8 15.3 %copy-start.1 = (bf16[16,144,128]{2,1,0:T(8,128)(2,1)S(1)}, bf16[16,144,128]{2,1,0:T(8,128)(2,1)}, u32[]{:S(2)}) copy-start(bf16[16,144,128]{2,1,0:T(8,128)(2,1)} %copy-done) | copy-start | bytes 1769476
  58.9 15.3 %copy-start.3 = (bf16[16,144,128]{2,1,0:T(8,128)(2,1)S(1)}, bf16[16,144,128]{2,1,0:T(8,128)(2,1)}, u32[]{:S(2)}) copy-start(bf16[16,144,128]{2,1,0:T(8,128)(2,1)} %copy-done.2) | copy-start | bytes 1769476
  70.0 4.2 %collective-permute-start.2 = (bf16[64,128,128]{2,1,0:T(8,128)(2,1)S(1)}, bf16[64,128,128]{2,1,0:T(8,128)(2,1)S(1)}, u32[]{:S(2)}, u32[]{:S(2)}) collective-permute-start(bf16[64,128,128]{2,1,0:T(8,128)(2,1)S(1)} %get-tuple-element.21), channel_id=1, source_target_pairs={{0,1},{1,0},{2,3},{3,2},{4,5},{5,4},{6,7},{7,6},{8,9},{9,8},{10,11... | collective-permute-start | bytes 6291464 | tf_op jit(solution)/shard_map/ppermute | solution.py:645
  74.2 21.4 %copy-start.10 = (s32[2,512]{1,0:T(2,128)S(1)}, s32[2,512]{1,0:T(2,128)}, u32[]{:S(2)}) copy-start(s32[2,512]{1,0:T(2,128)} %param.15) | copy-start | bytes 12292
  88.4 2.2 %collective-permute-start.3 = (bf16[16,64,128]{2,1,0:T(8,128)(2,1)S(1)}, bf16[16,64,128]{2,1,0:T(8,128)(2,1)S(1)}, u32[]{:S(2)}, u32[]{:S(2)}) collective-permute-start(bf16[16,64,128]{2,1,0:T(8,128)(2,1)S(1)} %slice.42), channel_id=1, source_target_pairs={{0,1},{1,0},{2,3},{3,2},{4,5},{5,4},{6,7},{7,6},{8,9},{9,8},{10,11... | collective-permute-start | bytes 786440 | tf_op jit(solution)/shard_map/ppermute | solution.py:665
  91.4 14.6 %all-to-all-start.1 = ((bf16[16,64,128]{2,1,0:T(8,128)(2,1)}), bf16[16,64,128]{2,1,0:T(8,128)(2,1)S(1)}, u32[]{:S(2)}, u32[]{:S(2)}) async-start(bf16[16,64,128]{2,1,0:T(8,128)(2,1)} %add_convert_fusion), calls=%async_computation.1 | async-start | bytes 524288 | tf_op jit(solution)/shard_map/all_to_all | solution.py:571
  96.8 9.2 %copy-start.6 = (bf16[128,4096]{1,0:T(8,128)(2,1)S(1)}, bf16[128,4096]{1,0:T(8,128)(2,1)}, u32[]{:S(2)}) copy-start(bf16[128,4096]{1,0:T(8,128)(2,1)} %interpolate.1) | copy-start | bytes 3145732
  96.8 9.2 %copy-start.9 = (s32[128,128]{1,0:T(8,128)S(1)}, s32[128,128]{1,0:T(8,128)}, u32[]{:S(2)}) copy-start(s32[128,128]{1,0:T(8,128)} %get-tuple-element.26.spots) | copy-start | bytes 196612
  106.0 0.8 copy-start.7

commit v11 on v10

--- a/solution.py
+++ b/solution.py
@@ -20,7 +20,7 @@
 PIECE = G // SLABS
 QUAD = 4
 PAD = 8
-SLAB = PAD + QUAD * PIECE + 32
+SLAB = PAD + QUAD * PIECE + 16
 CELLS = PAD + QUAD * G + 16
 STRIDE = G + 1
 BATCH = 8
@@ -133,7 +133,7 @@
         row = jnp.broadcast_to(table[pl.ds(u, 1), :], lower.shape)
         return jnp.where(upper == u, lane_gather(row, lower), acc)
 
-    slots = lax.fori_loop(0, strips, step, jnp.zeros(lower.shape, jnp.float32), unroll=4)
+    slots = lax.fori_loop(0, strips, step, jnp.zeros(lower.shape, jnp.float32), unroll=16)
     swapped = pltpu.roll(slots, BLK, 1)
     left = iota(slots.shape, 1) < BLK
     doubled[pl.ds(0, strips, stride=2), :] = jnp.where(left, slots, swapped)
@@ -290,12 +290,11 @@
     def _():
         def clear(n, carry):
             for slab in slabs:
-                slab[pl.ds(pl.multiple_of(n * SLAB, 8), SLAB), :] = jnp.zeros(
-                    (SLAB, LANES), jnp.float32
-                )
+                at = pl.multiple_of(n * SLAB + PAD, 8)
+                slab[pl.ds(at, SLAB - PAD), :] = jnp.zeros((SLAB - PAD, LANES), jnp.float32)
             return carry
 
-        lax.fori_loop(0, slabs[0].shape[0] // SLAB, clear, 0)
+        lax.fori_loop(0, G // QUAD, clear, 0)
         for side, part in enumerate(((mine, my_extra), (theirs, their_extra))):
             at = slice(side * (devices // 2), (side + 1) * (devices // 2))
             patches[at] = part[0][...]
@@ -342,7 +341,8 @@
                     part = slabs[s][pl.ds(base + (PAD + q), PIECE, stride=QUAD), :]
                     if s > 0:
                         at = base + (PAD + QUAD * PIECE + q)
-                        over = slabs[s - 1][pl.ds(at, 8, stride=QUAD), :]
+                        over = slabs[s - 1][pl.ds(at, 4, stride=QUAD), :]
+                        over = jnp.concatenate([over, jnp.zeros_like(over)], axis=0)
                         part = jnp.concatenate([part[:8] + over, part[8:]], axis=0)
                     parts.append(part.astype(jnp.bfloat16))
                 sheets.append(jnp.concatenate(parts, axis=0))
@@ -373,7 +373,7 @@
     first = jnp.concatenate([cas[tile, :] for tile in tiles], axis=0)
     first_back = jnp.concatenate([cas[:, tile] for tile in tiles], axis=1)
     count, freqs, _ = weights.shape
-    step = max(1, G // freqs)
+    step = min(count, max(1, 2 * G // freqs))
     rows = step * freqs
     for g in range(0, count, step):
         part = slice(g, g + step)
@@ -408,7 +408,7 @@
     devices, held, _ = out.shape
     groups = held // 16
     blocks = groups * GROUP
-    gs = second.shape[1]
+    gs = second.shape[1] // QUAD
     owner = iota((16, LANES), 1) // 4
     plane = iota((16, LANES), 0) % QUAD
 
@@ -416,7 +416,13 @@
     def _():
         for side, part in enumerate((my_extra, their_extra)):
             extra[side * (devices // 2) : (side + 1) * (devices // 2)] = part[...]
-        second[...] = turned(table_rows(cas, [place[1]], gs))
+        wide = (iota((gs, QUAD * gs), 1) % gs == iota((gs, QUAD * gs), 0)).astype(jnp.float32)
+        back = turned(table_rows(cas, [place[1]], gs))
+        back = dot(back, wide.astype(jnp.bfloat16)).astype(jnp.bfloat16)
+        tall = (iota((QUAD * G, G), 0) // QUAD == iota((QUAD * G, G), 1)).astype(jnp.float32)
+        back = dot(tall.astype(jnp.bfloat16), back)
+        same = iota(back.shape, 0) % QUAD == iota(back.shape, 1) // gs
+        second[...] = jnp.where(same, back, 0.0).astype(jnp.bfloat16)
         third[...] = turned(table_rows(cas, [place[2], place[2] ^ 1], own.shape[1]))
 
     for g in range(0, LINES, 2):
@@ -429,18 +435,20 @@
     @pl.when(step == pl.num_programs(0) - 1)
     def _():
         def planes(n, carry):
-            sheets = [
-                lines[pl.ds(n * QUAD + q, gs, stride=STRIDE), :].astype(jnp.bfloat16)
-                for q in range(QUAD)
-            ]
+            sheets = []
+            for group in (2 * n, 2 * n + 1):
+                rows = [
+                    lines[pl.ds(group * QUAD + q, gs, stride=STRIDE), :].astype(jnp.bfloat16)
+                    for q in range(QUAD)
+                ]
+                sheets.append(jnp.concatenate(rows, axis=0))
             field = dot(second[...], jnp.concatenate(sheets, axis=1))
-            base = pl.multiple_of(n * CELLS, 8)
-            for q in range(QUAD):
-                part = field[:, LANES * q : LANES * q + LANES]
-                cells[pl.ds(base + (PAD + q), G, stride=QUAD), :] = part
+            for m in range(2):
+                at = pl.multiple_of((2 * n + m) * CELLS + PAD, 8)
+                cells[pl.ds(at, QUAD * G), :] = field[:, LANES * m : LANES * m + LANES]
             return carry
 
-        lax.fori_loop(0, G // QUAD, planes, 0, unroll=UNROLL_PLANES)
+        lax.fori_loop(0, G // QUAD // 2, planes, 0, unroll=4)
         out[...] = jnp.zeros_like(out)
 
         def tile(numbers, t):
@@ -496,7 +504,7 @@
         row = jnp.broadcast_to(total[pl.ds(u, 1), :], lower.shape)
         return jnp.where(upper == u, lane_gather(row, lower), acc)
 
-    out[...] = lax.fori_loop(0, count, step, jnp.zeros(out.shape, jnp.float32), unroll=4)
+    out[...] = lax.fori_loop(0, count, step, jnp.zeros(out.shape, jnp.float32), unroll=16)
 
 
 def struct(shape, dtype):
@@ -574,14 +582,6 @@
 
     mine = swap_members(sent)
     theirs = lax.ppermute(mine, "col", mates)
-    inverse = pl.pallas_call(
-        inverse_kernel,
-        out_shape=struct((2 * strips, LANES), jnp.int32),
-        compiler_params=params(32),
-        name="inverse",
-    )(order)
-
-    mine, inverse = lax.optimization_barrier((mine, inverse))
     at = held - 16 + groups
     anchors = jnp.stack([part[:, at : at + 3] for part in (mine, theirs)])
     anchors = anchors.astype(jnp.int32)
@@ -625,6 +625,15 @@
         name="scatter",
     )(place, forth, slab_at, mine, theirs, mine, theirs, cas)
     other = lax.ppermute(other, "col", mates)
+    own, order = lax.optimization_barrier((own, order))
+    inverse = pl.pallas_call(
+        inverse_kernel,
+        out_shape=struct((2 * strips, LANES), jnp.int32),
+        compiler_params=params(32),
+        name="inverse",
+    )(order)
+
+    other, inverse = lax.optimization_barrier((other, inverse))
 
     part = lambda shape: pl.BlockSpec((BATCH,) + shape, lambda n: (n, 0, 0))
     own, other = pl.pallas_call(
@@ -653,7 +662,7 @@
         out_shape=struct((devices, 16 * groups, LANES), jnp.bfloat16),
         scratch_shapes=[
             pltpu.VMEM((devices, 16, LANES), jnp.bfloat16),
-            pltpu.VMEM((G, gs), jnp.bfloat16),
+            pltpu.VMEM((QUAD * G, QUAD * gs), jnp.bfloat16),
             pltpu.VMEM((G, 2 * fs), jnp.bfloat16),
             pltpu.VMEM((gs * STRIDE, LANES), jnp.float32),
             pltpu.VMEM(((G // QUAD + 1) * CELLS, LANES), jnp.float32),

time: 112 us -> 109 us (0.973)
  waiting for transfers between devices: 27.3 us -> 25.4 us
    ppermute x2, waiting for transfers between devices: 7.78 us -> 4.08 us  [body(): other = lax.ppermute(other, 'col', mates)]
    ppermute x1, waiting for transfers between devices: 0.01 us -> 1.81 us  [body(): theirs = lax.ppermute(mine, 'col', mates)]
    pallas_call x1, Pallas kernels: 14.2 us -> 15.4 us  [body(): pl.pallas_call(functools.partial(sample_kernel, cols), grid=(steps,), in_...]
  transfers between devices with their start and end apart: 6 -> 6, of which waited for: 5 -> 6; matrix products, arithmetic and copies ran while one was open for 1% -> 1% of each run, Pallas kernels for 10% -> 10%
where the time goes in v11:
time: 109 us; the launch traced here: 108 us
  Pallas kernels  62.8 us (58%)
  waiting for transfers between devices  25.4 us (23%)
  starting transfers between devices  14.4 us (13%)
  local copies, waits for them, and re-layouts  3.3 us (3%)
  other arithmetic  2.26 us (2%)
    all_to_all x2, waiting for transfers between devices, swap_members(): lax.all_to_all(array, axes, split_axis=0, concat_axis=0, axis_index_group...  18.3 us
    pallas_call x1, Pallas kernels, body(): pl.pallas_call(functools.partial(scatter_kernel, cols, gs, fs), grid=(1 +...  16.5 us
    pallas_call x1, Pallas kernels, body(): pl.pallas_call(functools.partial(sample_kernel, cols), grid=(steps,), in_...  15.4 us
    all_to_all x2, starting transfers between devices, swap_members(): lax.all_to_all(array, axes, split_axis=0, concat_axis=0, axis_index_group...  12.5 us
    pallas_call x1, Pallas kernels, body(): pl.pallas_call(spectrum_kernel, grid=(gs // BATCH,), in_specs=[smem, part...  11 us
    pallas_call x1, Pallas kernels, body(): pl.pallas_call(near_kernel, grid=(pairs // blocks,), in_specs=[smem, pl.B...  7.08 us
    pallas_call x1, Pallas kernels, body(): pl.pallas_call(project_kernel, out_shape=(struct((members, held, LANES),...  5.19 us
    ppermute x2, waiting for transfers between devices, body(): other = lax.ppermute(other, 'col', mates)  4.08 us
  transfers between devices with their start and end apart: 6, of which 6 were waited for; matrix products, arithmetic and copies ran while one was open for 1% of the time, Pallas kernels for 10%

profile of v11, /device:TPU:0, one launch (start us, length us, event | category | flops | bytes accessed | tf_op | source)
XLA Modules:
  0.0 108.3 jit_solution(12030889691965740896)
XLA Ops:
  0.0 5.2 %project.1 = (bf16[16,144,128]{2,1,0:T(8,128)(2,1)}, s32[128,128]{1,0:T(8,128)}) custom-call(bf16[64,128]{1,0:T(8,128)(2,1)} %bitcast.23, s32[64,128]{1,0:T(8,128)} %bitcast.16, bf16[128,4096]{1,0:T(8,128)(2,1)} %project_in.1, s32[3,128]{1,0:T(4,128)} %anchors_in.1), custom_call_target="tpu_custom_call" | custom-call | tf_op jit(solution)/shard_map/project/pallas_call | solution.py:549
  5.2 8.3 %all-to-all-start = ((bf16[16,144,128]{2,1,0:T(8,128)(2,1)}), bf16[16,144,128]{2,1,0:T(8,128)(2,1)S(1)}, u32[]{:S(2)}, u32[]{:S(2)}) async-start(bf16[16,144,128]{2,1,0:T(8,128)(2,1)} %get-tuple-element.18), calls=%async_computation | async-start | bytes 1179648 | tf_op jit(solution)/shard_map/all_to_all | solution.py:579
  13.6 16.2 %all-to-all-done.mine.my_extra = bf16[16,144,128]{2,1,0:T(8,128)(2,1)S(1)} async-done(((bf16[16,144,128]{2,1,0:T(8,128)(2,1)}), bf16[16,144,128]{2,1,0:T(8,128)(2,1)S(1)}, u32[]{:S(2)}, u32[]{:S(2)}) %all-to-all-start) | async-done | bytes 589856 | tf_op jit(solution)/shard_map/all_to_all | solution.py:579
  30.0 1.8 %collective-permute-done.theirs.their_extra = bf16[16,144,128]{2,1,0:T(8,128)(2,1)S(1)} collective-permute-done((bf16[16,144,128]{2,1,0:T(8,128)(2,1)S(1)}, bf16[16,144,128]{2,1,0:T(8,128)(2,1)S(1)}, u32[]{:S(2)}, u32[]{:S(2)}) %collective-permute-start) | collective-permute-done | bytes 589856 | tf_op jit(solution)/shard_map/ppermute | solution.py:584
  32.1 0.6 copy-done.2
  32.7 16.5 %scatter.1 = (bf16[64,128,128]{2,1,0:T(8,128)(2,1)}, bf16[64,128,128]{2,1,0:T(8,128)(2,1)}) custom-call(s32[3]{0:T(128)S(1)} %pad_add_fusion.place, s32[4096]{0:T(1024)S(1)} %get-tuple-element.40.shift, s32[4096]{0:T(1024)S(1)} %get-tuple-element.31.start, bf16[16,144,128]{2,1,0:T(8,128)(2,1)} %copy-done, bf16[16,144,128]{2,1,0:T(8,128)(2,1)} %copy-done.2, ...), custom_call_target="tpu_custom_call" | custom-call | tf_op jit(solution)/shard_map/scatter/pallas_call | solution.py:612
  49.2 0.7 collective-permute-start.1
  49.9 3.8 %inverse.1 = s32[128,128]{1,0:T(8,128)S(1)} custom-call(s32[64,128]{1,0:T(8,128)S(1)} %bitcast.17), custom_call_target="tpu_custom_call" | custom-call | tf_op jit(solution)/shard_map/inverse/pallas_call | solution.py:629
  53.7 0.2 collective-permute-done.1.other
  53.9 1.7 %copy-done.5 = bf16[64,128,128]{2,1,0:T(8,128)(2,1)S(1)} copy-done((bf16[64,128,128]{2,1,0:T(8,128)(2,1)S(1)}, bf16[64,128,128]{2,1,0:T(8,128)(2,1)}, u32[]{:S(2)}) %copy-start.5) | copy-done | bytes 2097176
  55.6 11.0 %spectrum.1 = (bf16[64,128,128]{2,1,0:T(8,128)(2,1)S(1)}, bf16[64,128,128]{2,1,0:T(8,128)(2,1)S(1)}) custom-call(s32[3]{0:T(128)S(1)} %pad_add_fusion.place, bf16[64,128,128]{2,1,0:T(8,128)(2,1)S(1)} %copy-done.5, bf16[64,128,128]{2,1,0:T(8,128)(2,1)S(1)} %collective-permute-done.1.other, f32[64,128,512]{2,1,0:T(8,128)} %weights.1, ...), custom_call_target="tpu_custom_call" | custom-call | tf_op jit(solution)/shard_map/spectrum/pallas_call | solution.py:639
  66.6 0.3 collective-permute-start.2
  66.9 3.9 %collective-permute-done.2.other = bf16[64,128,128]{2,1,0:T(8,128)(2,1)S(1)} collective-permute-done((bf16[64,128,128]{2,1,0:T(8,128)(2,1)S(1)}, bf16[64,128,128]{2,1,0:T(8,128)(2,1)S(1)}, u32[]{:S(2)}, u32[]{:S(2)}) %collective-permute-start.2) | collective-permute-done | bytes 2097184 | tf_op jit(solution)/shard_map/ppermute | solution.py:654
  70.8 15.4 %sample.1 = bf16[32,64,128]{2,1,0:T(8,128)(2,1)S(1)} custom-call(s32[3]{0:T(128)S(1)} %pad_add_fusion.place, s32[4096]{0:T(1024)S(1)} %get-tuple-element.39.shift, s32[4096]{0:T(1024)S(1)} %get-tuple-element.32.start, bf16[16,144,128]{2,1,0:T(8,128)(2,1)S(1)} %copy-done.1, bf16[16,144,128]{2,1,0:T(8,128)(2,1)S(1)} %copy-done.3, ...), custom_call_target="tpu_custom_call" | custom-call | tf_op jit(solution)/shard_map/sample/pallas_call | solution.py:657
  86.3 0.9 collective-permute-start.3
  87.2 1.2 %collective-permute-done.3 = bf16[16,64,128]{2,1,0:T(8,128)(2,1)S(1)} collective-permute-done((bf16[16,64,128]{2,1,0:T(8,128)(2,1)S(1)}, bf16[16,64,128]{2,1,0:T(8,128)(2,1)S(1)}, u32[]{:S(2)}, u32[]{:S(2)}) %collective-permute-start.3) | collective-permute-done | bytes 262176 | tf_op jit(solution)/shard_map/ppermute | solution.py:674
  88.3 0.8 add_convert_fusion
  89.1 4.2 %all-to-all-start.1 = ((bf16[16,64,128]{2,1,0:T(8,128)(2,1)}), bf16[16,64,128]{2,1,0:T(8,128)(2,1)S(1)}, u32[]{:S(2)}, u32[]{:S(2)}) async-start(bf16[16,64,128]{2,1,0:T(8,128)(2,1)} %add_convert_fusion), calls=%async_computation.1 | async-start | bytes 524288 | tf_op jit(solution)/shard_map/all_to_all | solution.py:579
  93.3 0.6 slice_subtract_fusion
  93.9 0.6 fusion.11.source
  94.5 7.1 %near.1 = f32[128,128]{1,0:T(8,128)} custom-call(s32[512]{0:T(512)} %fusion.11.source, bf16[512,4096]{1,0:T(8,128)(2,1)} %near_blocks.1, s32[1,512]{1,0:T(1,128)} %get-tuple-element.37.target, bf16[16,144,128]{2,1,0:T(8,128)(2,1)} %copy-done, bf16[16,144,128]{2,1,0:T(8,128)(2,1)} %copy-done.2), custom_call_target="tpu_custom_call" | custom-call | tf_op jit(solution)/shard_map/near/pallas_call | solution.py:686
  101.6 2.1 %all-to-all-done.1.values = bf16[16,64,128]{2,1,0:T(8,128)(2,1)S(1)} async-done(((bf16[16,64,128]{2,1,0:T(8,128)(2,1)}), bf16[16,64,128]{2,1,0:T(8,128)(2,1)S(1)}, u32[]{:S(2)}, u32[]{:S(2)}) %all-to-all-start.1) | async-done | bytes 262176 | tf_op jit(solution)/shard_map/all_to_all | solution.py:579
  103.7 0.8 copy-done.7
  104.5 3.8 %finish.1 = f32[64,128]{1,0:T(8,128)} custom-call(bf16[16,64,128]{2,1,0:T(8,128)(2,1)S(1)} %all-to-all-done.1.values, bf16[128,4096]{1,0:T(8,128)(2,1)S(1)} %copy-done.6, f32[128,128]{1,0:T(8,128)S(1)} %copy-done.7, s32[128,128]{1,0:T(8,128)S(1)} %inverse.1, s32[128,128]{1,0:T(8,128)S(1)} %copy-done.9), custom_call_target="tpu_custom_call" | custom-call | tf_op jit(solution)/shard_map/finish/pallas_call | solution.py:706
  (33 shorter events, 0.4 us)
Async XLA Ops:
  0.0 32.7 %copy-start.4 = (bf16[512,512]{1,0:T(8,128)(2,1)S(1)}, bf16[512,512]{1,0:T(8,128)(2,1)}, u32[]{:S(2)}) copy-start(bf16[512,512]{1,0:T(8,128)(2,1)} %constant.153.clone.cas) | copy-start | bytes 1572868
  5.2 44.7 %copy-start.8 = (s32[8192]{0:T(1024)S(1)}, s32[8192]{0:T(1024)}, u32[]{:S(2)}) copy-start(s32[8192]{0:T(1024)} %param.10) | copy-start | bytes 98308
  5.2 24.6 %all-to-all-start = ((bf16[16,144,128]{2,1,0:T(8,128)(2,1)}), bf16[16,144,128]{2,1,0:T(8,128)(2,1)S(1)}, u32[]{:S(2)}, u32[]{:S(2)}) async-start(bf16[16,144,128]{2,1,0:T(8,128)(2,1)} %get-tuple-element.18), calls=%async_computation | async-start | bytes 1179648 | tf_op jit(solution)/shard_map/all_to_all | solution.py:579
  29.8 2.2 %copy-start = (bf16[16,144,128]{2,1,0:T(8,128)(2,1)}, bf16[16,144,128]{2,1,0:T(8,128)(2,1)S(1)}, u32[]{:S(2)}) copy-start(bf16[16,144,128]{2,1,0:T(8,128)(2,1)S(1)} %all-to-all-done.mine.my_extra) | copy-start | bytes 1769476
  29.8 2.0 %collective-permute-start = (bf16[16,144,128]{2,1,0:T(8,128)(2,1)S(1)}, bf16[16,144,128]{2,1,0:T(8,128)(2,1)S(1)}, u32[]{:S(2)}, u32[]{:S(2)}) collective-permute-start(bf16[16,144,128]{2,1,0:T(8,128)(2,1)S(1)} %all-to-all-done.mine.my_extra), channel_id=1, source_target_pairs={{0,1},{1,0},{2,3},{3,2},{4,5},{5,4},{6,7},{7,6},{8,9},{9,8},{10,11... | collective-permute-start | bytes 1769480 | tf_op jit(solution)/shard_map/ppermute | solution.py:584
  31.8 0.8 copy-start.2
  49.2 4.7 %collective-permute-start.1 = (bf16[64,128,128]{2,1,0:T(8,128)(2,1)}, bf16[64,128,128]{2,1,0:T(8,128)(2,1)S(1)}, u32[]{:S(2)}, u32[]{:S(2)}) collective-permute-start(bf16[64,128,128]{2,1,0:T(8,128)(2,1)} %get-tuple-element.21), channel_id=1, source_target_pairs={{0,1},{1,0},{2,3},{3,2},{4,5},{5,4},{6,7},{7,6},{8,9},{9,8},{10,11... | collective-permute-start | bytes 6291464 | tf_op jit(solution)/shard_map/ppermute | solution.py:627
  53.7 17.2 %copy-start.1 = (bf16[16,144,128]{2,1,0:T(8,128)(2,1)S(1)}, bf16[16,144,128]{2,1,0:T(8,128)(2,1)}, u32[]{:S(2)}) copy-start(bf16[16,144,128]{2,1,0:T(8,128)(2,1)} %copy-done) | copy-start | bytes 1769476
  53.7 17.1 %copy-start.3 = (bf16[16,144,128]{2,1,0:T(8,128)(2,1)S(1)}, bf16[16,144,128]{2,1,0:T(8,128)(2,1)}, u32[]{:S(2)}) copy-start(bf16[16,144,128]{2,1,0:T(8,128)(2,1)} %copy-done.2) | copy-start | bytes 1769476
  53.9 1.7 %copy-start.5 = (bf16[64,128,128]{2,1,0:T(8,128)(2,1)S(1)}, bf16[64,128,128]{2,1,0:T(8,128)(2,1)}, u32[]{:S(2)}) copy-start(bf16[64,128,128]{2,1,0:T(8,128)(2,1)} %get-tuple-element.20.own) | copy-start | bytes 6291460
  66.6 4.2 %collective-permute-start.2 = (bf16[64,128,128]{2,1,0:T(8,128)(2,1)S(1)}, bf16[64,128,128]{2,1,0:T(8,128)(2,1)S(1)}, u32[]{:S(2)}, u32[]{:S(2)}) collective-permute-start(bf16[64,128,128]{2,1,0:T(8,128)(2,1)S(1)} %get-tuple-element.25), channel_id=1, source_target_pairs={{0,1},{1,0},{2,3},{3,2},{4,5},{5,4},{6,7},{7,6},{8,9},{9,8},{10,11... | collective-permute-start | bytes 6291464 | tf_op jit(solution)/shard_map/ppermute | solution.py:654
  70.8 22.5 %copy-start.10 = (s32[2,512]{1,0:T(2,128)S(1)}, s32[2,512]{1,0:T(2,128)}, u32[]{:S(2)}) copy-start(s32[2,512]{1,0:T(2,128)} %param.15) | copy-start | bytes 12292
  86.3 2.1 %collective-permute-start.3 = (bf16[16,64,128]{2,1,0:T(8,128)(2,1)S(1)}, bf16[16,64,128]{2,1,0:T(8,128)(2,1)S(1)}, u32[]{:S(2)}, u32[]{:S(2)}) collective-permute-start(bf16[16,64,128]{2,1,0:T(8,128)(2,1)S(1)} %slice.43), channel_id=1, source_target_pairs={{0,1},{1,0},{2,3},{3,2},{4,5},{5,4},{6,7},{7,6},{8,9},{9,8},{10,11... | collective-permute-start | bytes 786440 | tf_op jit(solution)/shard_map/ppermute | solution.py:674
  89.1 14.6 %all-to-all-start.1 = ((bf16[16,64,128]{2,1,0:T(8,128)(2,1)}), bf16[16,64,128]{2,1,0:T(8,128)(2,1)S(1)}, u32[]{:S(2)}, u32[]{:S(2)}) async-start(bf16[16,64,128]{2,1,0:T(8,128)(2,1)} %add_convert_fusion), calls=%async_computation.1 | async-start | bytes 524288 | tf_op jit(solution)/shard_map/all_to_all | solution.py:579
  94.5 9.2 %copy-start.6 = (bf16[128,4096]{1,0:T(8,128)(2,1)S(1)}, bf16[128,4096]{1,0:T(8,128)(2,1)}, u32[]{:S(2)}) copy-start(bf16[128,4096]{1,0:T(8,128)(2,1)} %interpolate.1) | copy-start | bytes 3145732
  94.5 9.2 %copy-start.9 = (s32[128,128]{1,0:T(8,128)S(1)}, s32[128,128]{1,0:T(8,128)}, u32[]{:S(2)}) copy-start(s32[128,128]{1,0:T(8,128)} %get-tuple-element.30.spots) | copy-start | bytes 196612
  103.7 0.8 copy-start.7

commit v12 on v10

--- a/solution.py
+++ b/solution.py
@@ -20,10 +20,11 @@
 PIECE = G // SLABS
 QUAD = 4
 PAD = 8
-SLAB = PAD + QUAD * PIECE + 32
+SLAB = PAD + QUAD * PIECE + 16
 CELLS = PAD + QUAD * G + 16
 STRIDE = G + 1
 BATCH = 8
+WAYS = 4
 LINES = 16
 UNROLL = 32
 UNROLL_PLANES = 16
@@ -133,7 +134,7 @@
         row = jnp.broadcast_to(table[pl.ds(u, 1), :], lower.shape)
         return jnp.where(upper == u, lane_gather(row, lower), acc)
 
-    slots = lax.fori_loop(0, strips, step, jnp.zeros(lower.shape, jnp.float32), unroll=4)
+    slots = lax.fori_loop(0, strips, step, jnp.zeros(lower.shape, jnp.float32), unroll=True)
     swapped = pltpu.roll(slots, BLK, 1)
     left = iota(slots.shape, 1) < BLK
     doubled[pl.ds(0, strips, stride=2), :] = jnp.where(left, slots, swapped)
@@ -290,12 +291,11 @@
     def _():
         def clear(n, carry):
             for slab in slabs:
-                slab[pl.ds(pl.multiple_of(n * SLAB, 8), SLAB), :] = jnp.zeros(
-                    (SLAB, LANES), jnp.float32
-                )
+                at = pl.multiple_of(n * SLAB + PAD, 8)
+                slab[pl.ds(at, SLAB - PAD), :] = jnp.zeros((SLAB - PAD, LANES), jnp.float32)
             return carry
 
-        lax.fori_loop(0, slabs[0].shape[0] // SLAB, clear, 0)
+        lax.fori_loop(0, G // QUAD, clear, 0)
         for side, part in enumerate(((mine, my_extra), (theirs, their_extra))):
             at = slice(side * (devices // 2), (side + 1) * (devices // 2))
             patches[at] = part[0][...]
@@ -342,7 +342,8 @@
                     part = slabs[s][pl.ds(base + (PAD + q), PIECE, stride=QUAD), :]
                     if s > 0:
                         at = base + (PAD + QUAD * PIECE + q)
-                        over = slabs[s - 1][pl.ds(at, 8, stride=QUAD), :]
+                        over = slabs[s - 1][pl.ds(at, 4, stride=QUAD), :]
+                        over = jnp.concatenate([over, jnp.zeros_like(over)], axis=0)
                         part = jnp.concatenate([part[:8] + over, part[8:]], axis=0)
                     parts.append(part.astype(jnp.bfloat16))
                 sheets.append(jnp.concatenate(parts, axis=0))
@@ -368,19 +369,19 @@
                 other_out[g + n] = field[fs:, LANES * n : LANES * n + LANES]
 
 
-def spectrum_kernel(place, own, other, weights, cas, own_out, other_out):
+def spectrum_kernel(place, own, other, *refs):
+    weights, (cas, own_out, other_out) = refs[:WAYS], refs[WAYS:]
     tiles = [pl.ds(pl.multiple_of(h * LANES, LANES), LANES) for h in (place[0], 1 - place[0])]
     first = jnp.concatenate([cas[tile, :] for tile in tiles], axis=0)
     first_back = jnp.concatenate([cas[:, tile] for tile in tiles], axis=1)
-    count, freqs, _ = weights.shape
-    step = max(1, G // freqs)
+    step, freqs, _ = weights[0].shape
     rows = step * freqs
-    for g in range(0, count, step):
-        part = slice(g, g + step)
+    for n in range(WAYS):
+        part = slice(n * step, (n + 1) * step)
         line = jnp.concatenate(
             [own[part].reshape(rows, LANES), other[part].reshape(rows, LANES)], axis=1
         )
-        s = dot(line, first) * weights[part].reshape(rows, P_SIZE)
+        s = dot(line, first) * weights[n][...].reshape(rows, P_SIZE)
         line = dot(s.astype(jnp.bfloat16), first_back).astype(jnp.bfloat16)
         own_out[part] = line[:, :LANES].reshape(step, freqs, LANES)
         other_out[part] = line[:, LANES:].reshape(step, freqs, LANES)
@@ -496,7 +497,7 @@
         row = jnp.broadcast_to(total[pl.ds(u, 1), :], lower.shape)
         return jnp.where(upper == u, lane_gather(row, lower), acc)
 
-    out[...] = lax.fori_loop(0, count, step, jnp.zeros(out.shape, jnp.float32), unroll=4)
+    out[...] = lax.fori_loop(0, count, step, jnp.zeros(out.shape, jnp.float32), unroll=True)
 
 
 def struct(shape, dtype):
@@ -574,14 +575,6 @@
 
     mine = swap_members(sent)
     theirs = lax.ppermute(mine, "col", mates)
-    inverse = pl.pallas_call(
-        inverse_kernel,
-        out_shape=struct((2 * strips, LANES), jnp.int32),
-        compiler_params=params(32),
-        name="inverse",
-    )(order)
-
-    mine, inverse = lax.optimization_barrier((mine, inverse))
     at = held - 16 + groups
     anchors = jnp.stack([part[:, at : at + 3] for part in (mine, theirs)])
     anchors = anchors.astype(jnp.int32)
@@ -625,8 +618,21 @@
         name="scatter",
     )(place, forth, slab_at, mine, theirs, mine, theirs, cas)
     other = lax.ppermute(other, "col", mates)
+    own, order = lax.optimization_barrier((own, order))
+    inverse = pl.pallas_call(
+        inverse_kernel,
+        out_shape=struct((2 * strips, LANES), jnp.int32),
+        compiler_params=params(32),
+        name="inverse",
+    )(order)
+
+    other, inverse = lax.optimization_barrier((other, inverse))
 
     part = lambda shape: pl.BlockSpec((BATCH,) + shape, lambda n: (n, 0, 0))
+
+    def weight_part(way):
+        return pl.BlockSpec((BATCH // WAYS, fs, P_SIZE), lambda n: (n * WAYS + way, 0, 0))
+
     own, other = pl.pallas_call(
         spectrum_kernel,
         grid=(gs // BATCH,),
@@ -634,14 +640,14 @@
             smem,
             part((fs, LANES)),
             part((fs, LANES)),
-            part((fs, P_SIZE)),
+            *[weight_part(n) for n in range(WAYS)],
             whole(cas.shape),
         ],
         out_specs=(part((fs, LANES)), part((fs, LANES))),
         out_shape=(lines_type, lines_type),
         compiler_params=params(40),
         name="spectrum",
-    )(place, own, other, kernel_spectrum, cas)
+    )(place, own, other, *[kernel_spectrum] * WAYS, cas)
     other = lax.ppermute(other, "col", mates)
 
     early = pl.BlockSpec((LINES, fs, LANES), lambda n: (n, 0, 0))

time: 112 us -> 107 us (0.955)
  Pallas kernels: 63.5 us -> 60.9 us
  waiting for transfers between devices: 27.3 us -> 25.4 us
    ppermute x2, waiting for transfers between devices: 7.78 us -> 4.09 us  [body(): other = lax.ppermute(other, 'col', mates)]
    ppermute x1, waiting for transfers between devices: 0.01 us -> 1.81 us  [body(): theirs = lax.ppermute(mine, 'col', mates)]
  transfers between devices with their start and end apart: 6 -> 6, of which waited for: 5 -> 6; matrix products, arithmetic and copies ran while one was open for 1% -> 1% of each run, Pallas kernels for 10% -> 10%
where the time goes in v12:
time: 107 us; the launch traced here: 106 us
  Pallas kernels  60.9 us (57%)
  waiting for transfers between devices  25.4 us (24%)
  starting transfers between devices  14.4 us (13%)
  local copies, waits for them, and re-layouts  3.3 us (3%)
  other arithmetic  2.26 us (2%)
    all_to_all x2, waiting for transfers between devices, swap_members(): lax.all_to_all(array, axes, split_axis=0, concat_axis=0, axis_index_group...  18.3 us
    pallas_call x1, Pallas kernels, body(): pl.pallas_call(functools.partial(scatter_kernel, cols, gs, fs), grid=(1 +...  16.5 us
    pallas_call x1, Pallas kernels, body(): pl.pallas_call(functools.partial(sample_kernel, cols), grid=(steps,), in_...  14.2 us
    all_to_all x2, starting transfers between devices, swap_members(): lax.all_to_all(array, axes, split_axis=0, concat_axis=0, axis_index_group...  12.5 us
    pallas_call x1, Pallas kernels, body(): pl.pallas_call(spectrum_kernel, grid=(gs // BATCH,), in_specs=[smem, part...  10.7 us
    pallas_call x1, Pallas kernels, body(): pl.pallas_call(near_kernel, grid=(pairs // blocks,), in_specs=[smem, pl.B...  7.08 us
    pallas_call x1, Pallas kernels, body(): pl.pallas_call(project_kernel, out_shape=(struct((members, held, LANES),...  4.98 us
    ppermute x2, waiting for transfers between devices, body(): other = lax.ppermute(other, 'col', mates)  4.09 us
  transfers between devices with their start and end apart: 6, of which 6 were waited for; matrix products, arithmetic and copies ran while one was open for 1% of the time, Pallas kernels for 10%

profile of v12, /device:TPU:0, one launch (start us, length us, event | category | flops | bytes accessed | tf_op | source)
XLA Modules:
  0.0 106.4 jit_solution(4857502747668318639)
XLA Ops:
  0.0 5.0 %project.1 = (bf16[16,144,128]{2,1,0:T(8,128)(2,1)}, s32[128,128]{1,0:T(8,128)}) custom-call(bf16[64,128]{1,0:T(8,128)(2,1)} %bitcast.23, s32[64,128]{1,0:T(8,128)} %bitcast.16, bf16[128,4096]{1,0:T(8,128)(2,1)} %project_in.1, s32[3,128]{1,0:T(4,128)} %anchors_in.1), custom_call_target="tpu_custom_call" | custom-call | tf_op jit(solution)/shard_map/project/pallas_call | solution.py:542
  5.0 8.3 %all-to-all-start = ((bf16[16,144,128]{2,1,0:T(8,128)(2,1)}), bf16[16,144,128]{2,1,0:T(8,128)(2,1)S(1)}, u32[]{:S(2)}, u32[]{:S(2)}) async-start(bf16[16,144,128]{2,1,0:T(8,128)(2,1)} %get-tuple-element.18), calls=%async_computation | async-start | bytes 1179648 | tf_op jit(solution)/shard_map/all_to_all | solution.py:572
  13.4 16.2 %all-to-all-done.mine.my_extra = bf16[16,144,128]{2,1,0:T(8,128)(2,1)S(1)} async-done(((bf16[16,144,128]{2,1,0:T(8,128)(2,1)}), bf16[16,144,128]{2,1,0:T(8,128)(2,1)S(1)}, u32[]{:S(2)}, u32[]{:S(2)}) %all-to-all-start) | async-done | bytes 589856 | tf_op jit(solution)/shard_map/all_to_all | solution.py:572
  29.8 1.8 %collective-permute-done.theirs.their_extra = bf16[16,144,128]{2,1,0:T(8,128)(2,1)S(1)} collective-permute-done((bf16[16,144,128]{2,1,0:T(8,128)(2,1)S(1)}, bf16[16,144,128]{2,1,0:T(8,128)(2,1)S(1)}, u32[]{:S(2)}, u32[]{:S(2)}) %collective-permute-start) | collective-permute-done | bytes 589856 | tf_op jit(solution)/shard_map/ppermute | solution.py:577
  31.8 0.6 copy-done.2
  32.5 16.5 %scatter.1 = (bf16[64,128,128]{2,1,0:T(8,128)(2,1)}, bf16[64,128,128]{2,1,0:T(8,128)(2,1)}) custom-call(s32[3]{0:T(128)S(1)} %pad_add_fusion.place, s32[4096]{0:T(1024)S(1)} %get-tuple-element.40.shift, s32[4096]{0:T(1024)S(1)} %get-tuple-element.31.start, bf16[16,144,128]{2,1,0:T(8,128)(2,1)} %copy-done, bf16[16,144,128]{2,1,0:T(8,128)(2,1)} %copy-done.2, ...), custom_call_target="tpu_custom_call" | custom-call | tf_op jit(solution)/shard_map/scatter/pallas_call | solution.py:605
  49.0 0.7 collective-permute-start.1
  49.7 3.8 %inverse.1 = s32[128,128]{1,0:T(8,128)S(1)} custom-call(s32[64,128]{1,0:T(8,128)S(1)} %bitcast.17), custom_call_target="tpu_custom_call" | custom-call | tf_op jit(solution)/shard_map/inverse/pallas_call | solution.py:622
  53.5 0.2 collective-permute-done.1.other
  53.7 1.7 %copy-done.5 = bf16[64,128,128]{2,1,0:T(8,128)(2,1)S(1)} copy-done((bf16[64,128,128]{2,1,0:T(8,128)(2,1)S(1)}, bf16[64,128,128]{2,1,0:T(8,128)(2,1)}, u32[]{:S(2)}) %copy-start.5) | copy-done | bytes 2097176
  55.4 10.7 %spectrum.1 = (bf16[64,128,128]{2,1,0:T(8,128)(2,1)S(1)}, bf16[64,128,128]{2,1,0:T(8,128)(2,1)S(1)}) custom-call(s32[3]{0:T(128)S(1)} %pad_add_fusion.place, bf16[64,128,128]{2,1,0:T(8,128)(2,1)S(1)} %copy-done.5, bf16[64,128,128]{2,1,0:T(8,128)(2,1)S(1)} %collective-permute-done.1.other, f32[64,128,512]{2,1,0:T(8,128)} %refs_3_.1, f32[64,128,512]{2,1,0:T(8,128)} %refs_3_.1, ...), custom_call_target="tpu_custom_call" | custom-call | tf_op jit(solution)/shard_map/spectrum/pallas_call | solution.py:636
  66.1 0.3 collective-permute-start.2
  66.4 3.9 %collective-permute-done.2.other = bf16[64,128,128]{2,1,0:T(8,128)(2,1)S(1)} collective-permute-done((bf16[64,128,128]{2,1,0:T(8,128)(2,1)S(1)}, bf16[64,128,128]{2,1,0:T(8,128)(2,1)S(1)}, u32[]{:S(2)}, u32[]{:S(2)}) %collective-permute-start.2) | collective-permute-done | bytes 2097184 | tf_op jit(solution)/shard_map/ppermute | solution.py:651
  70.3 14.2 %sample.1 = bf16[32,64,128]{2,1,0:T(8,128)(2,1)S(1)} custom-call(s32[3]{0:T(128)S(1)} %pad_add_fusion.place, s32[4096]{0:T(1024)S(1)} %get-tuple-element.39.shift, s32[4096]{0:T(1024)S(1)} %get-tuple-element.32.start, bf16[16,144,128]{2,1,0:T(8,128)(2,1)S(1)} %copy-done.1, bf16[16,144,128]{2,1,0:T(8,128)(2,1)S(1)} %copy-done.3, ...), custom_call_target="tpu_custom_call" | custom-call | tf_op jit(solution)/shard_map/sample/pallas_call | solution.py:654
  84.6 0.9 collective-permute-start.3
  85.4 1.2 %collective-permute-done.3 = bf16[16,64,128]{2,1,0:T(8,128)(2,1)S(1)} collective-permute-done((bf16[16,64,128]{2,1,0:T(8,128)(2,1)S(1)}, bf16[16,64,128]{2,1,0:T(8,128)(2,1)S(1)}, u32[]{:S(2)}, u32[]{:S(2)}) %collective-permute-start.3) | collective-permute-done | bytes 262176 | tf_op jit(solution)/shard_map/ppermute | solution.py:671
  86.6 0.8 add_convert_fusion
  87.4 4.2 %all-to-all-start.1 = ((bf16[16,64,128]{2,1,0:T(8,128)(2,1)}), bf16[16,64,128]{2,1,0:T(8,128)(2,1)S(1)}, u32[]{:S(2)}, u32[]{:S(2)}) async-start(bf16[16,64,128]{2,1,0:T(8,128)(2,1)} %add_convert_fusion), calls=%async_computation.1 | async-start | bytes 524288 | tf_op jit(solution)/shard_map/all_to_all | solution.py:572
  91.6 0.6 slice_subtract_fusion
  92.2 0.6 fusion.11.source
  92.8 7.1 %near.1 = f32[128,128]{1,0:T(8,128)} custom-call(s32[512]{0:T(512)} %fusion.11.source, bf16[512,4096]{1,0:T(8,128)(2,1)} %near_blocks.1, s32[1,512]{1,0:T(1,128)} %get-tuple-element.37.target, bf16[16,144,128]{2,1,0:T(8,128)(2,1)} %copy-done, bf16[16,144,128]{2,1,0:T(8,128)(2,1)} %copy-done.2), custom_call_target="tpu_custom_call" | custom-call | tf_op jit(solution)/shard_map/near/pallas_call | solution.py:683
  99.9 2.1 %all-to-all-done.1.values = bf16[16,64,128]{2,1,0:T(8,128)(2,1)S(1)} async-done(((bf16[16,64,128]{2,1,0:T(8,128)(2,1)}), bf16[16,64,128]{2,1,0:T(8,128)(2,1)S(1)}, u32[]{:S(2)}, u32[]{:S(2)}) %all-to-all-start.1) | async-done | bytes 262176 | tf_op jit(solution)/shard_map/all_to_all | solution.py:572
  102.0 0.8 copy-done.7
  102.8 3.6 %finish.1 = f32[64,128]{1,0:T(8,128)} custom-call(bf16[16,64,128]{2,1,0:T(8,128)(2,1)S(1)} %all-to-all-done.1.values, bf16[128,4096]{1,0:T(8,128)(2,1)S(1)} %copy-done.6, f32[128,128]{1,0:T(8,128)S(1)} %copy-done.7, s32[128,128]{1,0:T(8,128)S(1)} %inverse.1, s32[128,128]{1,0:T(8,128)S(1)} %copy-done.9), custom_call_target="tpu_custom_call" | custom-call | tf_op jit(solution)/shard_map/finish/pallas_call | solution.py:703
  (33 shorter events, 0.4 us)
Async XLA Ops:
  0.0 32.5 %copy-start.4 = (bf16[512,512]{1,0:T(8,128)(2,1)S(1)}, bf16[512,512]{1,0:T(8,128)(2,1)}, u32[]{:S(2)}) copy-start(bf16[512,512]{1,0:T(8,128)(2,1)} %constant.153.clone.cas.refs_4_) | copy-start | bytes 1572868
  5.0 44.7 %copy-start.8 = (s32[8192]{0:T(1024)S(1)}, s32[8192]{0:T(1024)}, u32[]{:S(2)}) copy-start(s32[8192]{0:T(1024)} %param.10) | copy-start | bytes 98308
  5.0 24.6 %all-to-all-start = ((bf16[16,144,128]{2,1,0:T(8,128)(2,1)}), bf16[16,144,128]{2,1,0:T(8,128)(2,1)S(1)}, u32[]{:S(2)}, u32[]{:S(2)}) async-start(bf16[16,144,128]{2,1,0:T(8,128)(2,1)} %get-tuple-element.18), calls=%async_computation | async-start | bytes 1179648 | tf_op jit(solution)/shard_map/all_to_all | solution.py:572
  29.6 2.2 %copy-start = (bf16[16,144,128]{2,1,0:T(8,128)(2,1)}, bf16[16,144,128]{2,1,0:T(8,128)(2,1)S(1)}, u32[]{:S(2)}) copy-start(bf16[16,144,128]{2,1,0:T(8,128)(2,1)S(1)} %all-to-all-done.mine.my_extra) | copy-start | bytes 1769476
  29.6 2.0 %collective-permute-start = (bf16[16,144,128]{2,1,0:T(8,128)(2,1)S(1)}, bf16[16,144,128]{2,1,0:T(8,128)(2,1)S(1)}, u32[]{:S(2)}, u32[]{:S(2)}) collective-permute-start(bf16[16,144,128]{2,1,0:T(8,128)(2,1)S(1)} %all-to-all-done.mine.my_extra), channel_id=1, source_target_pairs={{0,1},{1,0},{2,3},{3,2},{4,5},{5,4},{6,7},{7,6},{8,9},{9,8},{10,11... | collective-permute-start | bytes 1769480 | tf_op jit(solution)/shard_map/ppermute | solution.py:577
  31.6 0.8 copy-start.2
  49.0 4.7 %collective-permute-start.1 = (bf16[64,128,128]{2,1,0:T(8,128)(2,1)}, bf16[64,128,128]{2,1,0:T(8,128)(2,1)S(1)}, u32[]{:S(2)}, u32[]{:S(2)}) collective-permute-start(bf16[64,128,128]{2,1,0:T(8,128)(2,1)} %get-tuple-element.21), channel_id=1, source_target_pairs={{0,1},{1,0},{2,3},{3,2},{4,5},{5,4},{6,7},{7,6},{8,9},{9,8},{10,11... | collective-permute-start | bytes 6291464 | tf_op jit(solution)/shard_map/ppermute | solution.py:620
  53.4 16.9 %copy-start.1 = (bf16[16,144,128]{2,1,0:T(8,128)(2,1)S(1)}, bf16[16,144,128]{2,1,0:T(8,128)(2,1)}, u32[]{:S(2)}) copy-start(bf16[16,144,128]{2,1,0:T(8,128)(2,1)} %copy-done) | copy-start | bytes 1769476
  53.4 16.9 %copy-start.3 = (bf16[16,144,128]{2,1,0:T(8,128)(2,1)S(1)}, bf16[16,144,128]{2,1,0:T(8,128)(2,1)}, u32[]{:S(2)}) copy-start(bf16[16,144,128]{2,1,0:T(8,128)(2,1)} %copy-done.2) | copy-start | bytes 1769476
  53.7 1.7 %copy-start.5 = (bf16[64,128,128]{2,1,0:T(8,128)(2,1)S(1)}, bf16[64,128,128]{2,1,0:T(8,128)(2,1)}, u32[]{:S(2)}) copy-start(bf16[64,128,128]{2,1,0:T(8,128)(2,1)} %get-tuple-element.20.own) | copy-start | bytes 6291460
  66.1 4.2 %collective-permute-start.2 = (bf16[64,128,128]{2,1,0:T(8,128)(2,1)S(1)}, bf16[64,128,128]{2,1,0:T(8,128)(2,1)S(1)}, u32[]{:S(2)}, u32[]{:S(2)}) collective-permute-start(bf16[64,128,128]{2,1,0:T(8,128)(2,1)S(1)} %get-tuple-element.25), channel_id=1, source_target_pairs={{0,1},{1,0},{2,3},{3,2},{4,5},{5,4},{6,7},{7,6},{8,9},{9,8},{10,11... | collective-permute-start | bytes 6291464 | tf_op jit(solution)/shard_map/ppermute | solution.py:651
  70.3 21.3 %copy-start.10 = (s32[2,512]{1,0:T(2,128)S(1)}, s32[2,512]{1,0:T(2,128)}, u32[]{:S(2)}) copy-start(s32[2,512]{1,0:T(2,128)} %param.15) | copy-start | bytes 12292
  84.6 2.0 %collective-permute-start.3 = (bf16[16,64,128]{2,1,0:T(8,128)(2,1)S(1)}, bf16[16,64,128]{2,1,0:T(8,128)(2,1)S(1)}, u32[]{:S(2)}, u32[]{:S(2)}) collective-permute-start(bf16[16,64,128]{2,1,0:T(8,128)(2,1)S(1)} %slice.43), channel_id=1, source_target_pairs={{0,1},{1,0},{2,3},{3,2},{4,5},{5,4},{6,7},{7,6},{8,9},{9,8},{10,11... | collective-permute-start | bytes 786440 | tf_op jit(solution)/shard_map/ppermute | solution.py:671
  87.4 14.6 %all-to-all-start.1 = ((bf16[16,64,128]{2,1,0:T(8,128)(2,1)}), bf16[16,64,128]{2,1,0:T(8,128)(2,1)S(1)}, u32[]{:S(2)}, u32[]{:S(2)}) async-start(bf16[16,64,128]{2,1,0:T(8,128)(2,1)} %add_convert_fusion), calls=%async_computation.1 | async-start | bytes 524288 | tf_op jit(solution)/shard_map/all_to_all | solution.py:572
  92.8 9.2 %copy-start.6 = (bf16[128,4096]{1,0:T(8,128)(2,1)S(1)}, bf16[128,4096]{1,0:T(8,128)(2,1)}, u32[]{:S(2)}) copy-start(bf16[128,4096]{1,0:T(8,128)(2,1)} %interpolate.1) | copy-start | bytes 3145732
  92.8 9.2 %copy-start.9 = (s32[128,128]{1,0:T(8,128)S(1)}, s32[128,128]{1,0:T(8,128)}, u32[]{:S(2)}) copy-start(s32[128,128]{1,0:T(8,128)} %get-tuple-element.30.spots) | copy-start | bytes 196612
  102.0 0.8 copy-start.7

commit v13 on v12

--- a/solution.py
+++ b/solution.py
@@ -26,7 +26,6 @@
 BATCH = 8
 WAYS = 4
 LINES = 16
-UNROLL = 32
 UNROLL_PLANES = 16
 MB = 1 << 20
 NT = (((1,), (1,)), ((), ()))
@@ -284,7 +283,7 @@
     devices, held, _ = patches.shape
     groups = held // 16
     blocks = groups * GROUP
-    owner = iota((16, LANES), 1) // 4
+    owner = (iota((16, LANES), 1) // 4).astype(jnp.float32).astype(jnp.bfloat16)
     plane = iota((16, LANES), 0) % QUAD
 
     @pl.when(step == 0)
@@ -305,15 +304,16 @@
             values = []
             for d in numbers:
                 part = patches[d, pl.ds(pl.multiple_of(16 * t, 16), 16), :].astype(jnp.float32)
-                values.append(jnp.where(lanes_inside(extra, d, t, half), part, 0.0))
-
-            def one(k, carry):
-                spot = owner == k
+                part = jnp.where(lanes_inside(extra, d, t, half), part, 0.0)
+                values.append(part.astype(jnp.bfloat16))
+
+            for k in range(GROUP):
                 sums = []
                 for s in range(SLABS):
                     b = numbers[s] * blocks + t * GROUP + k
                     at = start[b]
-                    moved = pltpu.roll(jnp.where(spot, values[s], 0.0), shift[b], 1)
+                    moved = jnp.where(owner == k, values[s], jnp.zeros_like(values[s]))
+                    moved = pltpu.roll(moved, shift[b], 1).astype(jnp.float32)
                     here = plane < QUAD - (at & (QUAD - 1))
                     near = slabs[s][pl.ds(at, 16), :] + jnp.where(here, moved, 0.0)
                     at_next = at + (SLAB - QUAD)
@@ -322,9 +322,6 @@
                 for s, (at, near, at_next, far) in enumerate(sums):
                     slabs[s][pl.ds(at, 16), :] = near
                     slabs[s][pl.ds(at_next, 16), :] = far
-                return carry
-
-            lax.fori_loop(0, GROUP, one, 0, unroll=UNROLL)
 
         def crosses(b):
             return shift[b] > LANES - 4
@@ -410,7 +407,7 @@
     groups = held // 16
     blocks = groups * GROUP
     gs = second.shape[1]
-    owner = iota((16, LANES), 1) // 4
+    owner = (iota((16, LANES), 1) // 4).astype(jnp.float32).astype(jnp.bfloat16)
     plane = iota((16, LANES), 0) % QUAD
 
     @pl.when(step == 0)
@@ -445,25 +442,20 @@
         out[...] = jnp.zeros_like(out)
 
         def tile(numbers, t):
-            def one(k, sums):
-                spot = owner == k
-                new = []
+            sums = [jnp.zeros((16, LANES), jnp.bfloat16)] * SLABS
+            for k in range(GROUP):
                 for s in range(SLABS):
                     b = numbers[s] * blocks + t * GROUP + k
                     at = start[b]
                     here = plane < QUAD - (at & (QUAD - 1))
                     near = cells[pl.ds(at, 16), :]
                     far = cells[pl.ds(at + (CELLS - QUAD), 16), :]
-                    moved = pltpu.roll(jnp.where(here, near, far), shift[b], 1)
-                    new.append(jnp.where(spot, moved, sums[s]))
-                return tuple(new)
-
-            zero = (jnp.zeros((16, LANES), jnp.float32),) * SLABS
-            sums = lax.fori_loop(0, GROUP, one, zero, unroll=UNROLL)
+                    moved = jnp.where(here, near, far).astype(jnp.bfloat16)
+                    sums[s] = jnp.where(owner == k, pltpu.roll(moved, shift[b], 1), sums[s])
             for s, d in enumerate(numbers):
                 inside = lanes_inside(extra, d, t, half)
                 out[d, pl.ds(pl.multiple_of(16 * t, 16), 16), :] = jnp.where(
-                    inside, sums[s], 0.0
+                    inside, sums[s].astype(jnp.float32), 0.0
                 ).astype(jnp.bfloat16)
 
         def crosses(b):

time: 107 us -> 107 us (level)
  no operation moved by 1% of the time
where the time goes in v13:
time: 107 us; the launch traced here: 106 us
  Pallas kernels  60.8 us (57%)
  waiting for transfers between devices  25.4 us (24%)
  starting transfers between devices  14.4 us (13%)
  local copies, waits for them, and re-layouts  3.3 us (3%)
  other arithmetic  2.26 us (2%)
    all_to_all x2, waiting for transfers between devices, swap_members(): lax.all_to_all(array, axes, split_axis=0, concat_axis=0, axis_index_group...  18.3 us
    pallas_call x1, Pallas kernels, body(): pl.pallas_call(functools.partial(scatter_kernel, cols, gs, fs), grid=(1 +...  16.5 us
    pallas_call x1, Pallas kernels, body(): pl.pallas_call(functools.partial(sample_kernel, cols), grid=(steps,), in_...  14.2 us
    all_to_all x2, starting transfers between devices, swap_members(): lax.all_to_all(array, axes, split_axis=0, concat_axis=0, axis_index_group...  12.5 us
    pallas_call x1, Pallas kernels, body(): pl.pallas_call(spectrum_kernel, grid=(gs // BATCH,), in_specs=[smem, part...  10.7 us
    pallas_call x1, Pallas kernels, body(): pl.pallas_call(near_kernel, grid=(pairs // blocks,), in_specs=[smem, pl.B...  7.07 us
    pallas_call x1, Pallas kernels, body(): pl.pallas_call(project_kernel, out_shape=(struct((members, held, LANES),...  4.98 us
    ppermute x2, waiting for transfers between devices, body(): other = lax.ppermute(other, 'col', mates)  4.09 us
  transfers between devices with their start and end apart: 6, of which 6 were waited for; matrix products, arithmetic and copies ran while one was open for 1% of the time, Pallas kernels for 10%

profile of v13, /device:TPU:0, one launch (start us, length us, event | category | flops | bytes accessed | tf_op | source)
XLA Modules:
  0.0 106.3 jit_solution(17328781341674505795)
XLA Ops:
  0.0 5.0 %project.1 = (bf16[16,144,128]{2,1,0:T(8,128)(2,1)}, s32[128,128]{1,0:T(8,128)}) custom-call(bf16[64,128]{1,0:T(8,128)(2,1)} %bitcast.23, s32[64,128]{1,0:T(8,128)} %bitcast.16, bf16[128,4096]{1,0:T(8,128)(2,1)} %project_in.1, s32[3,128]{1,0:T(4,128)} %anchors_in.1), custom_call_target="tpu_custom_call" | custom-call | tf_op jit(solution)/shard_map/project/pallas_call | solution.py:534
  5.0 8.3 %all-to-all-start = ((bf16[16,144,128]{2,1,0:T(8,128)(2,1)}), bf16[16,144,128]{2,1,0:T(8,128)(2,1)S(1)}, u32[]{:S(2)}, u32[]{:S(2)}) async-start(bf16[16,144,128]{2,1,0:T(8,128)(2,1)} %get-tuple-element.18), calls=%async_computation | async-start | bytes 1179648 | tf_op jit(solution)/shard_map/all_to_all | solution.py:564
  13.4 16.2 %all-to-all-done.mine.my_extra = bf16[16,144,128]{2,1,0:T(8,128)(2,1)S(1)} async-done(((bf16[16,144,128]{2,1,0:T(8,128)(2,1)}), bf16[16,144,128]{2,1,0:T(8,128)(2,1)S(1)}, u32[]{:S(2)}, u32[]{:S(2)}) %all-to-all-start) | async-done | bytes 589856 | tf_op jit(solution)/shard_map/all_to_all | solution.py:564
  29.8 1.8 %collective-permute-done.theirs.their_extra = bf16[16,144,128]{2,1,0:T(8,128)(2,1)S(1)} collective-permute-done((bf16[16,144,128]{2,1,0:T(8,128)(2,1)S(1)}, bf16[16,144,128]{2,1,0:T(8,128)(2,1)S(1)}, u32[]{:S(2)}, u32[]{:S(2)}) %collective-permute-start) | collective-permute-done | bytes 589856 | tf_op jit(solution)/shard_map/ppermute | solution.py:569
  31.8 0.6 copy-done.2
  32.5 16.5 %scatter.1 = (bf16[64,128,128]{2,1,0:T(8,128)(2,1)}, bf16[64,128,128]{2,1,0:T(8,128)(2,1)}) custom-call(s32[3]{0:T(128)S(1)} %pad_add_fusion.place, s32[4096]{0:T(1024)S(1)} %get-tuple-element.40.shift, s32[4096]{0:T(1024)S(1)} %get-tuple-element.31.start, bf16[16,144,128]{2,1,0:T(8,128)(2,1)} %copy-done, bf16[16,144,128]{2,1,0:T(8,128)(2,1)} %copy-done.2, ...), custom_call_target="tpu_custom_call" | custom-call | tf_op jit(solution)/shard_map/scatter/pallas_call | solution.py:597
  48.9 0.7 collective-permute-start.1
  49.6 3.8 %inverse.1 = s32[128,128]{1,0:T(8,128)S(1)} custom-call(s32[64,128]{1,0:T(8,128)S(1)} %bitcast.17), custom_call_target="tpu_custom_call" | custom-call | tf_op jit(solution)/shard_map/inverse/pallas_call | solution.py:614
  53.4 0.2 collective-permute-done.1.other
  53.6 1.7 %copy-done.5 = bf16[64,128,128]{2,1,0:T(8,128)(2,1)S(1)} copy-done((bf16[64,128,128]{2,1,0:T(8,128)(2,1)S(1)}, bf16[64,128,128]{2,1,0:T(8,128)(2,1)}, u32[]{:S(2)}) %copy-start.5) | copy-done | bytes 2097176
  55.3 10.7 %spectrum.1 = (bf16[64,128,128]{2,1,0:T(8,128)(2,1)S(1)}, bf16[64,128,128]{2,1,0:T(8,128)(2,1)S(1)}) custom-call(s32[3]{0:T(128)S(1)} %pad_add_fusion.place, bf16[64,128,128]{2,1,0:T(8,128)(2,1)S(1)} %copy-done.5, bf16[64,128,128]{2,1,0:T(8,128)(2,1)S(1)} %collective-permute-done.1.other, f32[64,128,512]{2,1,0:T(8,128)} %refs_3_.1, f32[64,128,512]{2,1,0:T(8,128)} %refs_3_.1, ...), custom_call_target="tpu_custom_call" | custom-call | tf_op jit(solution)/shard_map/spectrum/pallas_call | solution.py:628
  66.0 0.3 collective-permute-start.2
  66.4 3.9 %collective-permute-done.2.other = bf16[64,128,128]{2,1,0:T(8,128)(2,1)S(1)} collective-permute-done((bf16[64,128,128]{2,1,0:T(8,128)(2,1)S(1)}, bf16[64,128,128]{2,1,0:T(8,128)(2,1)S(1)}, u32[]{:S(2)}, u32[]{:S(2)}) %collective-permute-start.2) | collective-permute-done | bytes 2097184 | tf_op jit(solution)/shard_map/ppermute | solution.py:643
  70.3 14.2 %sample.1 = bf16[32,64,128]{2,1,0:T(8,128)(2,1)S(1)} custom-call(s32[3]{0:T(128)S(1)} %pad_add_fusion.place, s32[4096]{0:T(1024)S(1)} %get-tuple-element.39.shift, s32[4096]{0:T(1024)S(1)} %get-tuple-element.32.start, bf16[16,144,128]{2,1,0:T(8,128)(2,1)S(1)} %copy-done.1, bf16[16,144,128]{2,1,0:T(8,128)(2,1)S(1)} %copy-done.3, ...), custom_call_target="tpu_custom_call" | custom-call | tf_op jit(solution)/shard_map/sample/pallas_call | solution.py:646
  84.5 0.9 collective-permute-start.3
  85.4 1.2 %collective-permute-done.3 = bf16[16,64,128]{2,1,0:T(8,128)(2,1)S(1)} collective-permute-done((bf16[16,64,128]{2,1,0:T(8,128)(2,1)S(1)}, bf16[16,64,128]{2,1,0:T(8,128)(2,1)S(1)}, u32[]{:S(2)}, u32[]{:S(2)}) %collective-permute-start.3) | collective-permute-done | bytes 262176 | tf_op jit(solution)/shard_map/ppermute | solution.py:663
  86.6 0.8 add_convert_fusion
  87.3 4.2 %all-to-all-start.1 = ((bf16[16,64,128]{2,1,0:T(8,128)(2,1)}), bf16[16,64,128]{2,1,0:T(8,128)(2,1)S(1)}, u32[]{:S(2)}, u32[]{:S(2)}) async-start(bf16[16,64,128]{2,1,0:T(8,128)(2,1)} %add_convert_fusion), calls=%async_computation.1 | async-start | bytes 524288 | tf_op jit(solution)/shard_map/all_to_all | solution.py:564
  91.5 0.6 slice_subtract_fusion
  92.1 0.6 fusion.11.source
  92.7 7.1 %near.1 = f32[128,128]{1,0:T(8,128)} custom-call(s32[512]{0:T(512)} %fusion.11.source, bf16[512,4096]{1,0:T(8,128)(2,1)} %near_blocks.1, s32[1,512]{1,0:T(1,128)} %get-tuple-element.37.target, bf16[16,144,128]{2,1,0:T(8,128)(2,1)} %copy-done, bf16[16,144,128]{2,1,0:T(8,128)(2,1)} %copy-done.2), custom_call_target="tpu_custom_call" | custom-call | tf_op jit(solution)/shard_map/near/pallas_call | solution.py:675
  99.8 2.1 %all-to-all-done.1.values = bf16[16,64,128]{2,1,0:T(8,128)(2,1)S(1)} async-done(((bf16[16,64,128]{2,1,0:T(8,128)(2,1)}), bf16[16,64,128]{2,1,0:T(8,128)(2,1)S(1)}, u32[]{:S(2)}, u32[]{:S(2)}) %all-to-all-start.1) | async-done | bytes 262176 | tf_op jit(solution)/shard_map/all_to_all | solution.py:564
  101.9 0.8 copy-done.7
  102.8 3.6 %finish.1 = f32[64,128]{1,0:T(8,128)} custom-call(bf16[16,64,128]{2,1,0:T(8,128)(2,1)S(1)} %all-to-all-done.1.values, bf16[128,4096]{1,0:T(8,128)(2,1)S(1)} %copy-done.6, f32[128,128]{1,0:T(8,128)S(1)} %copy-done.7, s32[128,128]{1,0:T(8,128)S(1)} %inverse.1, s32[128,128]{1,0:T(8,128)S(1)} %copy-done.9), custom_call_target="tpu_custom_call" | custom-call | tf_op jit(solution)/shard_map/finish/pallas_call | solution.py:695
  (33 shorter events, 0.4 us)
Async XLA Ops:
  0.0 32.5 %copy-start.4 = (bf16[512,512]{1,0:T(8,128)(2,1)S(1)}, bf16[512,512]{1,0:T(8,128)(2,1)}, u32[]{:S(2)}) copy-start(bf16[512,512]{1,0:T(8,128)(2,1)} %constant.153.clone.cas.refs_4_) | copy-start | bytes 1572868
  5.0 44.6 %copy-start.8 = (s32[8192]{0:T(1024)S(1)}, s32[8192]{0:T(1024)}, u32[]{:S(2)}) copy-start(s32[8192]{0:T(1024)} %param.10) | copy-start | bytes 98308
  5.0 24.6 %all-to-all-start = ((bf16[16,144,128]{2,1,0:T(8,128)(2,1)}), bf16[16,144,128]{2,1,0:T(8,128)(2,1)S(1)}, u32[]{:S(2)}, u32[]{:S(2)}) async-start(bf16[16,144,128]{2,1,0:T(8,128)(2,1)} %get-tuple-element.18), calls=%async_computation | async-start | bytes 1179648 | tf_op jit(solution)/shard_map/all_to_all | solution.py:564
  29.6 2.2 %copy-start = (bf16[16,144,128]{2,1,0:T(8,128)(2,1)}, bf16[16,144,128]{2,1,0:T(8,128)(2,1)S(1)}, u32[]{:S(2)}) copy-start(bf16[16,144,128]{2,1,0:T(8,128)(2,1)S(1)} %all-to-all-done.mine.my_extra) | copy-start | bytes 1769476
  29.6 2.0 %collective-permute-start = (bf16[16,144,128]{2,1,0:T(8,128)(2,1)S(1)}, bf16[16,144,128]{2,1,0:T(8,128)(2,1)S(1)}, u32[]{:S(2)}, u32[]{:S(2)}) collective-permute-start(bf16[16,144,128]{2,1,0:T(8,128)(2,1)S(1)} %all-to-all-done.mine.my_extra), channel_id=1, source_target_pairs={{0,1},{1,0},{2,3},{3,2},{4,5},{5,4},{6,7},{7,6},{8,9},{9,8},{10,11... | collective-permute-start | bytes 1769480 | tf_op jit(solution)/shard_map/ppermute | solution.py:569
  31.6 0.8 copy-start.2
  48.9 4.7 %collective-permute-start.1 = (bf16[64,128,128]{2,1,0:T(8,128)(2,1)}, bf16[64,128,128]{2,1,0:T(8,128)(2,1)S(1)}, u32[]{:S(2)}, u32[]{:S(2)}) collective-permute-start(bf16[64,128,128]{2,1,0:T(8,128)(2,1)} %get-tuple-element.21), channel_id=1, source_target_pairs={{0,1},{1,0},{2,3},{3,2},{4,5},{5,4},{6,7},{7,6},{8,9},{9,8},{10,11... | collective-permute-start | bytes 6291464 | tf_op jit(solution)/shard_map/ppermute | solution.py:612
  53.4 16.9 %copy-start.1 = (bf16[16,144,128]{2,1,0:T(8,128)(2,1)S(1)}, bf16[16,144,128]{2,1,0:T(8,128)(2,1)}, u32[]{:S(2)}) copy-start(bf16[16,144,128]{2,1,0:T(8,128)(2,1)} %copy-done) | copy-start | bytes 1769476
  53.4 16.9 %copy-start.3 = (bf16[16,144,128]{2,1,0:T(8,128)(2,1)S(1)}, bf16[16,144,128]{2,1,0:T(8,128)(2,1)}, u32[]{:S(2)}) copy-start(bf16[16,144,128]{2,1,0:T(8,128)(2,1)} %copy-done.2) | copy-start | bytes 1769476
  53.6 1.7 %copy-start.5 = (bf16[64,128,128]{2,1,0:T(8,128)(2,1)S(1)}, bf16[64,128,128]{2,1,0:T(8,128)(2,1)}, u32[]{:S(2)}) copy-start(bf16[64,128,128]{2,1,0:T(8,128)(2,1)} %get-tuple-element.20.own) | copy-start | bytes 6291460
  66.0 4.2 %collective-permute-start.2 = (bf16[64,128,128]{2,1,0:T(8,128)(2,1)S(1)}, bf16[64,128,128]{2,1,0:T(8,128)(2,1)S(1)}, u32[]{:S(2)}, u32[]{:S(2)}) collective-permute-start(bf16[64,128,128]{2,1,0:T(8,128)(2,1)S(1)} %get-tuple-element.25), channel_id=1, source_target_pairs={{0,1},{1,0},{2,3},{3,2},{4,5},{5,4},{6,7},{7,6},{8,9},{9,8},{10,11... | collective-permute-start | bytes 6291464 | tf_op jit(solution)/shard_map/ppermute | solution.py:643
  70.3 21.3 %copy-start.10 = (s32[2,512]{1,0:T(2,128)S(1)}, s32[2,512]{1,0:T(2,128)}, u32[]{:S(2)}) copy-start(s32[2,512]{1,0:T(2,128)} %param.15) | copy-start | bytes 12292
  84.5 2.0 %collective-permute-start.3 = (bf16[16,64,128]{2,1,0:T(8,128)(2,1)S(1)}, bf16[16,64,128]{2,1,0:T(8,128)(2,1)S(1)}, u32[]{:S(2)}, u32[]{:S(2)}) collective-permute-start(bf16[16,64,128]{2,1,0:T(8,128)(2,1)S(1)} %slice.43), channel_id=1, source_target_pairs={{0,1},{1,0},{2,3},{3,2},{4,5},{5,4},{6,7},{7,6},{8,9},{9,8},{10,11... | collective-permute-start | bytes 786440 | tf_op jit(solution)/shard_map/ppermute | solution.py:663
  87.3 14.6 %all-to-all-start.1 = ((bf16[16,64,128]{2,1,0:T(8,128)(2,1)}), bf16[16,64,128]{2,1,0:T(8,128)(2,1)S(1)}, u32[]{:S(2)}, u32[]{:S(2)}) async-start(bf16[16,64,128]{2,1,0:T(8,128)(2,1)} %add_convert_fusion), calls=%async_computation.1 | async-start | bytes 524288 | tf_op jit(solution)/shard_map/all_to_all | solution.py:564
  92.7 9.2 %copy-start.6 = (bf16[128,4096]{1,0:T(8,128)(2,1)S(1)}, bf16[128,4096]{1,0:T(8,128)(2,1)}, u32[]{:S(2)}) copy-start(bf16[128,4096]{1,0:T(8,128)(2,1)} %interpolate.1) | copy-start | bytes 3145732
  92.7 9.2 %copy-start.9 = (s32[128,128]{1,0:T(8,128)S(1)}, s32[128,128]{1,0:T(8,128)}, u32[]{:S(2)}) copy-start(s32[128,128]{1,0:T(8,128)} %get-tuple-element.30.spots) | copy-start | bytes 196612
  101.9 0.8 copy-start.7

commit v14 on v13

--- a/solution.py
+++ b/solution.py
@@ -378,8 +378,11 @@
         line = jnp.concatenate(
             [own[part].reshape(rows, LANES), other[part].reshape(rows, LANES)], axis=1
         )
-        s = dot(line, first) * weights[n][...].reshape(rows, P_SIZE)
-        line = dot(s.astype(jnp.bfloat16), first_back).astype(jnp.bfloat16)
+        total = jnp.zeros((rows, G), jnp.float32)
+        for f in (slice(0, G), slice(G, P_SIZE)):
+            s = dot(line, first[:, f]) * weights[n][:, :, f].reshape(rows, G)
+            total = total + dot(s.astype(jnp.bfloat16), first_back[f])
+        line = total.astype(jnp.bfloat16)
         own_out[part] = line[:, :LANES].reshape(step, freqs, LANES)
         other_out[part] = line[:, LANES:].reshape(step, freqs, LANES)
 
@@ -606,7 +609,7 @@
             pltpu.VMEM((gs * STRIDE, LANES), jnp.float32),
         ]
         + [pltpu.VMEM(((G // QUAD + 1) * SLAB, LANES), jnp.float32)] * SLABS,
-        compiler_params=params(53),
+        compiler_params=params(50),
         name="scatter",
     )(place, forth, slab_at, mine, theirs, mine, theirs, cas)
     other = lax.ppermute(other, "col", mates)
@@ -688,7 +691,7 @@
             pltpu.VMEM((devices * blocks, LANES), jnp.float32),
             pltpu.VMEM((blocks, LANES), jnp.float32),
         ],
-        compiler_params=params(56),
+        compiler_params=params(40),
         name="near",
     )(wanted, near_blocks, target.reshape(1, pairs), my_charges, their_charges)
 

time: 107 us -> 104 us (0.972)
  Pallas kernels: 60.8 us -> 59.1 us
  other arithmetic: 2.26 us -> 1.08 us
    pallas_call x1, Pallas kernels: 7.07 us -> 5.43 us  [body(): pl.pallas_call(near_kernel, grid=(pairs // blocks,), in_specs=[smem, pl.B...]
    unnamed x22 -> x12, local copies, waits for them, and re-layouts: 3.18 us -> 2.2 us
  transfers between devices with their start and end apart: 6 -> 6, of which waited for: 6 -> 6; matrix products, arithmetic and copies ran while one was open for 1% -> 0% of each run, Pallas kernels for 10% -> 9%
where the time goes in v14:
time: 104 us; the launch traced here: 103 us
  Pallas kernels  59.1 us (57%)
  waiting for transfers between devices  25.9 us (25%)
  starting transfers between devices  14.6 us (14%)
  local copies, waits for them, and re-layouts  2.32 us (2%)
  other arithmetic  1.08 us (1%)
    all_to_all x2, waiting for transfers between devices, swap_members(): lax.all_to_all(array, axes, split_axis=0, concat_axis=0, axis_index_group...  18.9 us
    pallas_call x1, Pallas kernels, body(): pl.pallas_call(functools.partial(scatter_kernel, cols, gs, fs), grid=(1 +...  16.2 us
    pallas_call x1, Pallas kernels, body(): pl.pallas_call(functools.partial(sample_kernel, cols), grid=(steps,), in_...  14.2 us
    all_to_all x2, starting transfers between devices, swap_members(): lax.all_to_all(array, axes, split_axis=0, concat_axis=0, axis_index_group...  12.5 us
    pallas_call x1, Pallas kernels, body(): pl.pallas_call(spectrum_kernel, grid=(gs // BATCH,), in_specs=[smem, part...  11 us
    pallas_call x1, Pallas kernels, body(): pl.pallas_call(near_kernel, grid=(pairs // blocks,), in_specs=[smem, pl.B...  5.43 us
    pallas_call x1, Pallas kernels, body(): pl.pallas_call(project_kernel, out_shape=(struct((members, held, LANES),...  4.97 us
    ppermute x2, waiting for transfers between devices, body(): other = lax.ppermute(other, 'col', mates)  4 us
  transfers between devices with their start and end apart: 6, of which 6 were waited for; matrix products, arithmetic and copies ran while one was open for 0% of the time, Pallas kernels for 9%

profile of v14, /device:TPU:0, one launch (start us, length us, event | category | flops | bytes accessed | tf_op | source)
XLA Modules:
  0.0 103.2 jit_solution(6071188844768977026)
XLA Ops:
  0.0 5.0 %project.1 = (bf16[16,144,128]{2,1,0:T(8,128)(2,1)}, s32[128,128]{1,0:T(8,128)}) custom-call(bf16[64,128]{1,0:T(8,128)(2,1)} %bitcast.23, s32[64,128]{1,0:T(8,128)} %bitcast.16, bf16[128,4096]{1,0:T(8,128)(2,1)} %project_in.1, s32[3,128]{1,0:T(4,128)} %anchors_in.1), custom_call_target="tpu_custom_call" | custom-call | tf_op jit(solution)/shard_map/project/pallas_call | solution.py:537
  5.0 0.0 copy-start.3
  5.0 8.3 %all-to-all-start = ((bf16[16,144,128]{2,1,0:T(8,128)(2,1)}), bf16[16,144,128]{2,1,0:T(8,128)(2,1)S(1)}, u32[]{:S(2)}, u32[]{:S(2)}) async-start(bf16[16,144,128]{2,1,0:T(8,128)(2,1)} %get-tuple-element.18), calls=%async_computation | async-start | bytes 1179648 | tf_op jit(solution)/shard_map/all_to_all | solution.py:567
  13.4 16.2 %all-to-all-done.mine.my_extra = bf16[16,144,128]{2,1,0:T(8,128)(2,1)S(1)} async-done(((bf16[16,144,128]{2,1,0:T(8,128)(2,1)}), bf16[16,144,128]{2,1,0:T(8,128)(2,1)S(1)}, u32[]{:S(2)}, u32[]{:S(2)}) %all-to-all-start) | async-done | bytes 589856 | tf_op jit(solution)/shard_map/all_to_all | solution.py:567
  29.6 0.1 pad_add_fusion.place
  29.7 0.1 fusion.18
  29.8 1.8 %collective-permute-done.theirs.their_extra = bf16[16,144,128]{2,1,0:T(8,128)(2,1)S(1)} collective-permute-done((bf16[16,144,128]{2,1,0:T(8,128)(2,1)S(1)}, bf16[16,144,128]{2,1,0:T(8,128)(2,1)S(1)}, u32[]{:S(2)}, u32[]{:S(2)}) %collective-permute-start) | collective-permute-done | bytes 589856 | tf_op jit(solution)/shard_map/ppermute | solution.py:572
  31.7 0.1 sub.74
  31.8 16.2 %scatter.1 = (bf16[64,128,128]{2,1,0:T(8,128)(2,1)S(1)}, bf16[64,128,128]{2,1,0:T(8,128)(2,1)}) custom-call(s32[3]{0:T(128)S(1)} %pad_add_fusion.place, s32[4096]{0:T(1024)S(1)} %get-tuple-element.40.shift, s32[4096]{0:T(1024)S(1)} %get-tuple-element.31.start, bf16[16,144,128]{2,1,0:T(8,128)(2,1)S(1)} %all-to-all-done.mine.my_extra, ...), custom_call_target="tpu_custom_call" | custom-call | tf_op jit(solution)/shard_map/scatter/pallas_call | solution.py:600
  48.0 0.7 collective-permute-start.1
  48.7 3.8 %inverse.1 = s32[128,128]{1,0:T(8,128)S(1)} custom-call(s32[64,128]{1,0:T(8,128)S(1)} %bitcast.17), custom_call_target="tpu_custom_call" | custom-call | tf_op jit(solution)/shard_map/inverse/pallas_call | solution.py:617
  52.5 0.2 collective-permute-done.1.other
  52.7 11.0 %spectrum.1 = (bf16[64,128,128]{2,1,0:T(8,128)(2,1)S(1)}, bf16[64,128,128]{2,1,0:T(8,128)(2,1)S(1)}) custom-call(s32[3]{0:T(128)S(1)} %pad_add_fusion.place, bf16[64,128,128]{2,1,0:T(8,128)(2,1)S(1)} %get-tuple-element.20.own, bf16[64,128,128]{2,1,0:T(8,128)(2,1)S(1)} %collective-permute-done.1.other, f32[64,128,512]{2,1,0:T(8,128)} %refs_3_.1, ...), custom_call_target="tpu_custom_call" | custom-call | tf_op jit(solution)/shard_map/spectrum/pallas_call | solution.py:631
  63.7 0.4 collective-permute-start.2
  64.2 3.8 %collective-permute-done.2.other = bf16[64,128,128]{2,1,0:T(8,128)(2,1)S(1)} collective-permute-done((bf16[64,128,128]{2,1,0:T(8,128)(2,1)S(1)}, bf16[64,128,128]{2,1,0:T(8,128)(2,1)S(1)}, u32[]{:S(2)}, u32[]{:S(2)}) %collective-permute-start.2) | collective-permute-done | bytes 2097184 | tf_op jit(solution)/shard_map/ppermute | solution.py:646
  68.0 14.2 %sample.1 = bf16[32,64,128]{2,1,0:T(8,128)(2,1)S(1)} custom-call(s32[3]{0:T(128)S(1)} %pad_add_fusion.place, s32[4096]{0:T(1024)S(1)} %get-tuple-element.39.shift, s32[4096]{0:T(1024)S(1)} %get-tuple-element.32.start, bf16[16,144,128]{2,1,0:T(8,128)(2,1)S(1)} %all-to-all-done.mine.my_extra, ...), custom_call_target="tpu_custom_call" | custom-call | tf_op jit(solution)/shard_map/sample/pallas_call | solution.py:649
  82.2 1.0 collective-permute-start.3
  83.2 1.2 %collective-permute-done.3 = bf16[16,64,128]{2,1,0:T(8,128)(2,1)S(1)} collective-permute-done((bf16[16,64,128]{2,1,0:T(8,128)(2,1)S(1)}, bf16[16,64,128]{2,1,0:T(8,128)(2,1)S(1)}, u32[]{:S(2)}, u32[]{:S(2)}) %collective-permute-start.3) | collective-permute-done | bytes 262176 | tf_op jit(solution)/shard_map/ppermute | solution.py:666
  84.3 0.8 add_convert_fusion
  85.1 4.2 %all-to-all-start.1 = ((bf16[16,64,128]{2,1,0:T(8,128)(2,1)}), bf16[16,64,128]{2,1,0:T(8,128)(2,1)S(1)}, u32[]{:S(2)}, u32[]{:S(2)}) async-start(bf16[16,64,128]{2,1,0:T(8,128)(2,1)} %add_convert_fusion), calls=%async_computation.1 | async-start | bytes 524288 | tf_op jit(solution)/shard_map/all_to_all | solution.py:567
  89.3 2.2 %copy-done.1 = bf16[512,4096]{1,0:T(8,128)(2,1)S(1)} copy-done((bf16[512,4096]{1,0:T(8,128)(2,1)S(1)}, bf16[512,4096]{1,0:T(8,128)(2,1)}, u32[]{:S(2)}) %copy-start.1) | copy-done | bytes 4194328
  91.5 5.4 %near.1 = f32[128,128]{1,0:T(8,128)S(1)} custom-call(s32[512]{0:T(512)S(1)} %fusion.11.source, bf16[512,4096]{1,0:T(8,128)(2,1)S(1)} %copy-done.1, s32[1,512]{1,0:T(1,128)S(1)} %get-tuple-element.37.target, bf16[16,144,128]{2,1,0:T(8,128)(2,1)S(1)} %all-to-all-done.mine.my_extra, bf16[16,144,128]{2,1,0:T(8,128)(2,1)S(1)} %collective-permute-done.theirs.their_extra), custom_call_target="tpu_custom_call" | custom-call | tf_op jit(solution)/shard_map/near/pallas_call | solution.py:678
  97.0 2.7 %all-to-all-done.1.values = bf16[16,64,128]{2,1,0:T(8,128)(2,1)S(1)} async-done(((bf16[16,64,128]{2,1,0:T(8,128)(2,1)}), bf16[16,64,128]{2,1,0:T(8,128)(2,1)S(1)}, u32[]{:S(2)}, u32[]{:S(2)}) %all-to-all-start.1) | async-done | bytes 262176 | tf_op jit(solution)/shard_map/all_to_all | solution.py:567
  99.7 3.6 %finish.1 = f32[64,128]{1,0:T(8,128)} custom-call(bf16[16,64,128]{2,1,0:T(8,128)(2,1)S(1)} %all-to-all-done.1.values, bf16[128,4096]{1,0:T(8,128)(2,1)S(1)} %copy-done.2, f32[128,128]{1,0:T(8,128)S(1)} %near.1, s32[128,128]{1,0:T(8,128)S(1)} %inverse.1, s32[128,128]{1,0:T(8,128)S(1)} %copy-done.4), custom_call_target="tpu_custom_call" | custom-call | tf_op jit(solution)/shard_map/finish/pallas_call | solution.py:698
  (23 shorter events, 0.2 us)
Async XLA Ops:
  0.0 31.8 %copy-start = (bf16[512,512]{1,0:T(8,128)(2,1)S(1)}, bf16[512,512]{1,0:T(8,128)(2,1)}, u32[]{:S(2)}) copy-start(bf16[512,512]{1,0:T(8,128)(2,1)} %constant.153.clone.cas.refs_4_) | copy-start | bytes 1572868
  5.0 43.7 %copy-start.3 = (s32[8192]{0:T(1024)S(1)}, s32[8192]{0:T(1024)}, u32[]{:S(2)}) copy-start(s32[8192]{0:T(1024)} %param.10) | copy-start | bytes 98308
  5.0 24.6 %all-to-all-start = ((bf16[16,144,128]{2,1,0:T(8,128)(2,1)}), bf16[16,144,128]{2,1,0:T(8,128)(2,1)S(1)}, u32[]{:S(2)}, u32[]{:S(2)}) async-start(bf16[16,144,128]{2,1,0:T(8,128)(2,1)} %get-tuple-element.18), calls=%async_computation | async-start | bytes 1179648 | tf_op jit(solution)/shard_map/all_to_all | solution.py:567
  29.6 2.0 %collective-permute-start = (bf16[16,144,128]{2,1,0:T(8,128)(2,1)S(1)}, bf16[16,144,128]{2,1,0:T(8,128)(2,1)S(1)}, u32[]{:S(2)}, u32[]{:S(2)}) collective-permute-start(bf16[16,144,128]{2,1,0:T(8,128)(2,1)S(1)} %all-to-all-done.mine.my_extra), channel_id=1, source_target_pairs={{0,1},{1,0},{2,3},{3,2},{4,5},{5,4},{6,7},{7,6},{8,9},{9,8},{10,11... | collective-permute-start | bytes 1769480 | tf_op jit(solution)/shard_map/ppermute | solution.py:572
  48.0 4.7 %collective-permute-start.1 = (bf16[64,128,128]{2,1,0:T(8,128)(2,1)}, bf16[64,128,128]{2,1,0:T(8,128)(2,1)S(1)}, u32[]{:S(2)}, u32[]{:S(2)}) collective-permute-start(bf16[64,128,128]{2,1,0:T(8,128)(2,1)} %get-tuple-element.21), channel_id=1, source_target_pairs={{0,1},{1,0},{2,3},{3,2},{4,5},{5,4},{6,7},{7,6},{8,9},{9,8},{10,11... | collective-permute-start | bytes 6291464 | tf_op jit(solution)/shard_map/ppermute | solution.py:615
  63.7 4.2 %collective-permute-start.2 = (bf16[64,128,128]{2,1,0:T(8,128)(2,1)S(1)}, bf16[64,128,128]{2,1,0:T(8,128)(2,1)S(1)}, u32[]{:S(2)}, u32[]{:S(2)}) collective-permute-start(bf16[64,128,128]{2,1,0:T(8,128)(2,1)S(1)} %get-tuple-element.25), channel_id=1, source_target_pairs={{0,1},{1,0},{2,3},{3,2},{4,5},{5,4},{6,7},{7,6},{8,9},{9,8},{10,11... | collective-permute-start | bytes 6291464 | tf_op jit(solution)/shard_map/ppermute | solution.py:646
  68.0 21.3 %copy-start.5 = (s32[2,512]{1,0:T(2,128)S(1)}, s32[2,512]{1,0:T(2,128)}, u32[]{:S(2)}) copy-start(s32[2,512]{1,0:T(2,128)} %param.15) | copy-start | bytes 12292
  82.2 2.2 %collective-permute-start.3 = (bf16[16,64,128]{2,1,0:T(8,128)(2,1)S(1)}, bf16[16,64,128]{2,1,0:T(8,128)(2,1)S(1)}, u32[]{:S(2)}, u32[]{:S(2)}) collective-permute-start(bf16[16,64,128]{2,1,0:T(8,128)(2,1)S(1)} %slice.43), channel_id=1, source_target_pairs={{0,1},{1,0},{2,3},{3,2},{4,5},{5,4},{6,7},{7,6},{8,9},{9,8},{10,11... | collective-permute-start | bytes 786440 | tf_op jit(solution)/shard_map/ppermute | solution.py:666
  85.1 14.6 %all-to-all-start.1 = ((bf16[16,64,128]{2,1,0:T(8,128)(2,1)}), bf16[16,64,128]{2,1,0:T(8,128)(2,1)S(1)}, u32[]{:S(2)}, u32[]{:S(2)}) async-start(bf16[16,64,128]{2,1,0:T(8,128)(2,1)} %add_convert_fusion), calls=%async_computation.1 | async-start | bytes 524288 | tf_op jit(solution)/shard_map/all_to_all | solution.py:567
  89.3 2.2 %copy-start.1 = (bf16[512,4096]{1,0:T(8,128)(2,1)S(1)}, bf16[512,4096]{1,0:T(8,128)(2,1)}, u32[]{:S(2)}) copy-start(bf16[512,4096]{1,0:T(8,128)(2,1)} %near_blocks.1) | copy-start | bytes 12582916
  91.5 8.1 %copy-start.2 = (bf16[128,4096]{1,0:T(8,128)(2,1)S(1)}, bf16[128,4096]{1,0:T(8,128)(2,1)}, u32[]{:S(2)}) copy-start(bf16[128,4096]{1,0:T(8,128)(2,1)} %interpolate.1) | copy-start | bytes 3145732
  91.5 8.1 %copy-start.4 = (s32[128,128]{1,0:T(8,128)S(1)}, s32[128,128]{1,0:T(8,128)}, u32[]{:S(2)}) copy-start(s32[128,128]{1,0:T(8,128)} %get-tuple-element.30.spots) | copy-start | bytes 196612

commit v15 on v13

--- a/solution.py
+++ b/solution.py
@@ -23,10 +23,10 @@
 SLAB = PAD + QUAD * PIECE + 16
 CELLS = PAD + QUAD * G + 16
 STRIDE = G + 1
-BATCH = 8
+BATCH = 16
 WAYS = 4
 LINES = 16
-UNROLL_PLANES = 16
+UNROLL_PLANES = 8
 MB = 1 << 20
 NT = (((1,), (1,)), ((), ()))
 
@@ -73,17 +73,20 @@
     return total[:rows] + total[rows:]
 
 
+def patch_rows():
+    row = iota((16, LANES), 0)
+    return [
+        (iota((16, LANES), 1) % PTS == 16 * i + row).astype(jnp.float32).astype(jnp.bfloat16)
+        for i in range(4)
+    ]
+
+
 def patch_places(spots):
     blocks = spots.shape[0]
     spots = jnp.concatenate([spots] * (4 * blocks // LANES), axis=1)
     lane = iota(spots.shape, 1)
     lanes = [(lane == 4 * spots + i).astype(jnp.float32).astype(jnp.bfloat16) for i in range(4)]
-    row = iota((16, LANES), 0)
-    rows = [
-        (iota((16, LANES), 1) % PTS == 16 * i + row).astype(jnp.float32).astype(jnp.bfloat16)
-        for i in range(4)
-    ]
-    return rows, lanes
+    return patch_rows(), lanes
 
 
 def block_spots(first):
@@ -190,7 +193,7 @@
     ).astype(jnp.int32)
 
 
-def near_kernel(source, near_blocks, target, mine, theirs, out, table, picked):
+def near_kernel(source, near_blocks, target, mine, theirs, spots, out, lanes_out, table, picked):
     step = pl.program_id(0)
     pairs = picked.shape[0]
     blocks = out.shape[0]
@@ -207,6 +210,8 @@
                 table[pl.ds(at, strips, stride=2), :] = jnp.where(left, slots, swapped)
                 table[pl.ds(at + 1, strips, stride=2), :] = jnp.where(left, swapped, slots)
         out[...] = jnp.zeros_like(out)
+        for i, lanes in enumerate(patch_places(spots[...])[1]):
+            lanes_out[i] = lanes
 
     def pick(p, carry):
         picked[pl.ds(p, 1), :] = table[pl.ds(source[step * pairs + p], 1), :]
@@ -464,10 +469,10 @@
         tile_loop(half, devices // cols, cols, groups, crosses, tile)
 
 
-def finish_kernel(values, interpolate, near, inverse, spots, out, total):
+def finish_kernel(values, interpolate, near, inverse, lanes, out, total):
     blocks = near.shape[0]
     groups = values.shape[1] // 16
-    rows, lanes = patch_places(spots[...])
+    rows = patch_rows()
     summed = values[0].astype(jnp.float32)
     for d in range(1, values.shape[0]):
         summed = summed + values[d].astype(jnp.float32)
@@ -606,7 +611,7 @@
             pltpu.VMEM((gs * STRIDE, LANES), jnp.float32),
         ]
         + [pltpu.VMEM(((G // QUAD + 1) * SLAB, LANES), jnp.float32)] * SLABS,
-        compiler_params=params(53),
+        compiler_params=params(50),
         name="scatter",
     )(place, forth, slab_at, mine, theirs, mine, theirs, cas)
     other = lax.ppermute(other, "col", mates)
@@ -672,7 +677,7 @@
     wanted = (wanted + source_col // HALVES) * blocks + source % blocks
     target = near_pairs[0] - (row_at * cols + col_at) * blocks
     pairs = near_blocks.shape[0]
-    near = pl.pallas_call(
+    near, lanes = pl.pallas_call(
         near_kernel,
         grid=(pairs // blocks,),
         in_specs=[
@@ -681,16 +686,20 @@
             pl.BlockSpec((1, blocks), lambda n: (0, n)),
             charge_rows,
             charge_rows,
+            whole((blocks, LANES)),
         ],
-        out_specs=whole((blocks, LANES)),
-        out_shape=struct((blocks, LANES), jnp.float32),
+        out_specs=(whole((blocks, LANES)), whole((4, blocks, 4 * blocks))),
+        out_shape=(
+            struct((blocks, LANES), jnp.float32),
+            struct((4, blocks, 4 * blocks), jnp.bfloat16),
+        ),
         scratch_shapes=[
             pltpu.VMEM((devices * blocks, LANES), jnp.float32),
             pltpu.VMEM((blocks, LANES), jnp.float32),
         ],
-        compiler_params=params(56),
+        compiler_params=params(40),
         name="near",
-    )(wanted, near_blocks, target.reshape(1, pairs), my_charges, their_charges)
+    )(wanted, near_blocks, target.reshape(1, pairs), my_charges, their_charges, spots)
 
     result = pl.pallas_call(
         finish_kernel,
@@ -698,7 +707,7 @@
         scratch_shapes=[pltpu.VMEM((blocks, LANES), jnp.float32)],
         compiler_params=params(32),
         name="finish",
-    )(values, interpolate, near, inverse, spots)
+    )(values, interpolate, near, inverse, lanes)
     return result.reshape(panels)
 
 

time: 107 us -> 102 us (0.953)
  Pallas kernels: 60.8 us -> 58.1 us
  other arithmetic: 2.26 us -> 1.09 us
    pallas_call x1, Pallas kernels: 10.7 us -> 8.81 us  [body(): pl.pallas_call(spectrum_kernel, grid=(gs // BATCH,), in_specs=[smem, part...]
    pallas_call x1, Pallas kernels: 7.07 us -> 5.66 us  [body(): pl.pallas_call(near_kernel, grid=(pairs // blocks,), in_specs=[smem, pl.B...]
    unnamed x22 -> x12, local copies, waits for them, and re-layouts: 3.18 us -> 2.2 us
  transfers between devices with their start and end apart: 6 -> 6, of which waited for: 6 -> 6; matrix products, arithmetic and copies ran while one was open for 1% -> 0% of each run, Pallas kernels for 10% -> 9%
where the time goes in v15:
time: 102 us
  Pallas kernels  58.1 us (57%)
  waiting for transfers between devices  25.7 us (25%)
  starting transfers between devices  14.6 us (14%)
  local copies, waits for them, and re-layouts  2.32 us (2%)
  other arithmetic  1.09 us (1%)
    all_to_all x2, waiting for transfers between devices, swap_members(): lax.all_to_all(array, axes, split_axis=0, concat_axis=0, axis_index_group...  18.7 us
    pallas_call x1, Pallas kernels, body(): pl.pallas_call(functools.partial(scatter_kernel, cols, gs, fs), grid=(1 +...  16.6 us
    pallas_call x1, Pallas kernels, body(): pl.pallas_call(functools.partial(sample_kernel, cols), grid=(steps,), in_...  14.7 us
    all_to_all x2, starting transfers between devices, swap_members(): lax.all_to_all(array, axes, split_axis=0, concat_axis=0, axis_index_group...  12.5 us
    pallas_call x1, Pallas kernels, body(): pl.pallas_call(spectrum_kernel, grid=(gs // BATCH,), in_specs=[smem, part...  8.81 us
    pallas_call x1, Pallas kernels, body(): pl.pallas_call(near_kernel, grid=(pairs // blocks,), in_specs=[smem, pl.B...  5.66 us
    pallas_call x1, Pallas kernels, body(): pl.pallas_call(project_kernel, out_shape=(struct((members, held, LANES),...  4.98 us
    ppermute x2, waiting for transfers between devices, body(): other = lax.ppermute(other, 'col', mates)  4 us
  transfers between devices with their start and end apart: 6, of which 6 were waited for; matrix products, arithmetic and copies ran while one was open for 0% of the time, Pallas kernels for 9%

profile of v15, /device:TPU:0, one launch (start us, length us, event | category | flops | bytes accessed | tf_op | source)
XLA Modules:
  0.0 102.0 jit_solution(17899834897614229559)
XLA Ops:
  0.0 5.0 %project.1 = (bf16[16,144,128]{2,1,0:T(8,128)(2,1)}, s32[128,128]{1,0:T(8,128)}) custom-call(bf16[64,128]{1,0:T(8,128)(2,1)} %bitcast.23, s32[64,128]{1,0:T(8,128)} %bitcast.16, bf16[128,4096]{1,0:T(8,128)(2,1)} %project_in.1, s32[3,128]{1,0:T(4,128)} %anchors_in.1), custom_call_target="tpu_custom_call" | custom-call | tf_op jit(solution)/shard_map/project/pallas_call | solution.py:539
  5.0 0.0 copy-start.3
  5.0 8.3 %all-to-all-start = ((bf16[16,144,128]{2,1,0:T(8,128)(2,1)}), bf16[16,144,128]{2,1,0:T(8,128)(2,1)S(1)}, u32[]{:S(2)}, u32[]{:S(2)}) async-start(bf16[16,144,128]{2,1,0:T(8,128)(2,1)} %get-tuple-element.20), calls=%async_computation | async-start | bytes 1179648 | tf_op jit(solution)/shard_map/all_to_all | solution.py:569
  13.4 16.2 %all-to-all-done.mine.my_extra = bf16[16,144,128]{2,1,0:T(8,128)(2,1)S(1)} async-done(((bf16[16,144,128]{2,1,0:T(8,128)(2,1)}), bf16[16,144,128]{2,1,0:T(8,128)(2,1)S(1)}, u32[]{:S(2)}, u32[]{:S(2)}) %all-to-all-start) | async-done | bytes 589856 | tf_op jit(solution)/shard_map/all_to_all | solution.py:569
  29.6 0.1 pad_add_fusion.place
  29.7 0.1 fusion.18
  29.8 1.8 %collective-permute-done.theirs.their_extra = bf16[16,144,128]{2,1,0:T(8,128)(2,1)S(1)} collective-permute-done((bf16[16,144,128]{2,1,0:T(8,128)(2,1)S(1)}, bf16[16,144,128]{2,1,0:T(8,128)(2,1)S(1)}, u32[]{:S(2)}, u32[]{:S(2)}) %collective-permute-start) | collective-permute-done | bytes 589856 | tf_op jit(solution)/shard_map/ppermute | solution.py:574
  31.7 0.1 sub.74
  31.8 16.6 %scatter.1 = (bf16[64,128,128]{2,1,0:T(8,128)(2,1)S(1)}, bf16[64,128,128]{2,1,0:T(8,128)(2,1)}) custom-call(s32[3]{0:T(128)S(1)} %pad_add_fusion.place, s32[4096]{0:T(1024)S(1)} %get-tuple-element.44.shift, s32[4096]{0:T(1024)S(1)} %get-tuple-element.35.start, bf16[16,144,128]{2,1,0:T(8,128)(2,1)S(1)} %all-to-all-done.mine.my_extra, ...), custom_call_target="tpu_custom_call" | custom-call | tf_op jit(solution)/shard_map/scatter/pallas_call | solution.py:602
  48.5 0.7 collective-permute-start.1
  49.1 3.8 %inverse.1 = s32[128,128]{1,0:T(8,128)S(1)} custom-call(s32[64,128]{1,0:T(8,128)S(1)} %bitcast.17), custom_call_target="tpu_custom_call" | custom-call | tf_op jit(solution)/shard_map/inverse/pallas_call | solution.py:619
  52.9 0.2 collective-permute-done.1.other
  53.1 8.8 %spectrum.1 = (bf16[64,128,128]{2,1,0:T(8,128)(2,1)S(1)}, bf16[64,128,128]{2,1,0:T(8,128)(2,1)S(1)}) custom-call(s32[3]{0:T(128)S(1)} %pad_add_fusion.place, bf16[64,128,128]{2,1,0:T(8,128)(2,1)S(1)} %get-tuple-element.22.own, bf16[64,128,128]{2,1,0:T(8,128)(2,1)S(1)} %collective-permute-done.1.other, f32[64,128,512]{2,1,0:T(8,128)} %refs_3_.1, ...), custom_call_target="tpu_custom_call" | custom-call | tf_op jit(solution)/shard_map/spectrum/pallas_call | solution.py:633
  62.0 0.4 collective-permute-start.2
  62.4 3.8 %collective-permute-done.2.other = bf16[64,128,128]{2,1,0:T(8,128)(2,1)S(1)} collective-permute-done((bf16[64,128,128]{2,1,0:T(8,128)(2,1)S(1)}, bf16[64,128,128]{2,1,0:T(8,128)(2,1)S(1)}, u32[]{:S(2)}, u32[]{:S(2)}) %collective-permute-start.2) | collective-permute-done | bytes 2097184 | tf_op jit(solution)/shard_map/ppermute | solution.py:648
  66.2 14.7 %sample.1 = bf16[32,64,128]{2,1,0:T(8,128)(2,1)S(1)} custom-call(s32[3]{0:T(128)S(1)} %pad_add_fusion.place, s32[4096]{0:T(1024)S(1)} %get-tuple-element.43.shift, s32[4096]{0:T(1024)S(1)} %get-tuple-element.36.start, bf16[16,144,128]{2,1,0:T(8,128)(2,1)S(1)} %all-to-all-done.mine.my_extra, ...), custom_call_target="tpu_custom_call" | custom-call | tf_op jit(solution)/shard_map/sample/pallas_call | solution.py:651
  80.9 1.0 collective-permute-start.3
  81.9 1.2 %collective-permute-done.3 = bf16[16,64,128]{2,1,0:T(8,128)(2,1)S(1)} collective-permute-done((bf16[16,64,128]{2,1,0:T(8,128)(2,1)S(1)}, bf16[16,64,128]{2,1,0:T(8,128)(2,1)S(1)}, u32[]{:S(2)}, u32[]{:S(2)}) %collective-permute-start.3) | collective-permute-done | bytes 262176 | tf_op jit(solution)/shard_map/ppermute | solution.py:668
  83.1 0.8 add_convert_fusion
  83.9 4.2 %all-to-all-start.1 = ((bf16[16,64,128]{2,1,0:T(8,128)(2,1)}), bf16[16,64,128]{2,1,0:T(8,128)(2,1)S(1)}, u32[]{:S(2)}, u32[]{:S(2)}) async-start(bf16[16,64,128]{2,1,0:T(8,128)(2,1)} %add_convert_fusion), calls=%async_computation.1 | async-start | bytes 524288 | tf_op jit(solution)/shard_map/all_to_all | solution.py:569
  88.1 2.2 %copy-done.1 = bf16[512,4096]{1,0:T(8,128)(2,1)S(1)} copy-done((bf16[512,4096]{1,0:T(8,128)(2,1)S(1)}, bf16[512,4096]{1,0:T(8,128)(2,1)}, u32[]{:S(2)}) %copy-start.1) | copy-done | bytes 4194328
  90.3 5.7 %near.1 = (f32[128,128]{1,0:T(8,128)S(1)}, bf16[4,128,512]{2,1,0:T(8,128)(2,1)S(1)}) custom-call(s32[512]{0:T(512)S(1)} %fusion.11.source, bf16[512,4096]{1,0:T(8,128)(2,1)S(1)} %copy-done.1, s32[1,512]{1,0:T(1,128)S(1)} %get-tuple-element.41.target, bf16[16,144,128]{2,1,0:T(8,128)(2,1)S(1)} %all-to-all-done.mine.my_extra, ...), custom_call_target="tpu_custom_call" | custom-call | tf_op jit(solution)/shard_map/near/pallas_call | solution.py:680
  96.0 2.5 %all-to-all-done.1.values = bf16[16,64,128]{2,1,0:T(8,128)(2,1)S(1)} async-done(((bf16[16,64,128]{2,1,0:T(8,128)(2,1)}), bf16[16,64,128]{2,1,0:T(8,128)(2,1)S(1)}, u32[]{:S(2)}, u32[]{:S(2)}) %all-to-all-start.1) | async-done | bytes 262176 | tf_op jit(solution)/shard_map/all_to_all | solution.py:569
  98.4 3.6 %finish.1 = f32[64,128]{1,0:T(8,128)} custom-call(bf16[16,64,128]{2,1,0:T(8,128)(2,1)S(1)} %all-to-all-done.1.values, bf16[128,4096]{1,0:T(8,128)(2,1)S(1)} %copy-done.2, f32[128,128]{1,0:T(8,128)S(1)} %get-tuple-element.32.near, s32[128,128]{1,0:T(8,128)S(1)} %inverse.1, bf16[4,128,512]{2,1,0:T(8,128)(2,1)S(1)} %get-tuple-element.34.lanes), custom_call_target="tpu_custom_call" | custom-call | tf_op jit(solution)/shard_map/finish/pallas_call | solution.py:704
  (23 shorter events, 0.2 us)
Async XLA Ops:
  0.0 31.8 %copy-start = (bf16[512,512]{1,0:T(8,128)(2,1)S(1)}, bf16[512,512]{1,0:T(8,128)(2,1)}, u32[]{:S(2)}) copy-start(bf16[512,512]{1,0:T(8,128)(2,1)} %constant.153.clone.cas.refs_4_) | copy-start | bytes 1572868
  5.0 44.1 %copy-start.3 = (s32[8192]{0:T(1024)S(1)}, s32[8192]{0:T(1024)}, u32[]{:S(2)}) copy-start(s32[8192]{0:T(1024)} %param.10) | copy-start | bytes 98308
  5.0 24.6 %all-to-all-start = ((bf16[16,144,128]{2,1,0:T(8,128)(2,1)}), bf16[16,144,128]{2,1,0:T(8,128)(2,1)S(1)}, u32[]{:S(2)}, u32[]{:S(2)}) async-start(bf16[16,144,128]{2,1,0:T(8,128)(2,1)} %get-tuple-element.20), calls=%async_computation | async-start | bytes 1179648 | tf_op jit(solution)/shard_map/all_to_all | solution.py:569
  29.6 2.0 %collective-permute-start = (bf16[16,144,128]{2,1,0:T(8,128)(2,1)S(1)}, bf16[16,144,128]{2,1,0:T(8,128)(2,1)S(1)}, u32[]{:S(2)}, u32[]{:S(2)}) collective-permute-start(bf16[16,144,128]{2,1,0:T(8,128)(2,1)S(1)} %all-to-all-done.mine.my_extra), channel_id=1, source_target_pairs={{0,1},{1,0},{2,3},{3,2},{4,5},{5,4},{6,7},{7,6},{8,9},{9,8},{10,11... | collective-permute-start | bytes 1769480 | tf_op jit(solution)/shard_map/ppermute | solution.py:574
  48.5 4.7 %collective-permute-start.1 = (bf16[64,128,128]{2,1,0:T(8,128)(2,1)}, bf16[64,128,128]{2,1,0:T(8,128)(2,1)S(1)}, u32[]{:S(2)}, u32[]{:S(2)}) collective-permute-start(bf16[64,128,128]{2,1,0:T(8,128)(2,1)} %get-tuple-element.23), channel_id=1, source_target_pairs={{0,1},{1,0},{2,3},{3,2},{4,5},{5,4},{6,7},{7,6},{8,9},{9,8},{10,11... | collective-permute-start | bytes 6291464 | tf_op jit(solution)/shard_map/ppermute | solution.py:617
  62.0 4.2 %collective-permute-start.2 = (bf16[64,128,128]{2,1,0:T(8,128)(2,1)S(1)}, bf16[64,128,128]{2,1,0:T(8,128)(2,1)S(1)}, u32[]{:S(2)}, u32[]{:S(2)}) collective-permute-start(bf16[64,128,128]{2,1,0:T(8,128)(2,1)S(1)} %get-tuple-element.27), channel_id=1, source_target_pairs={{0,1},{1,0},{2,3},{3,2},{4,5},{5,4},{6,7},{7,6},{8,9},{9,8},{10,11... | collective-permute-start | bytes 6291464 | tf_op jit(solution)/shard_map/ppermute | solution.py:648
  66.2 21.9 %copy-start.5 = (s32[2,512]{1,0:T(2,128)S(1)}, s32[2,512]{1,0:T(2,128)}, u32[]{:S(2)}) copy-start(s32[2,512]{1,0:T(2,128)} %param.15) | copy-start | bytes 12292
  66.2 21.9 %copy-start.4 = (s32[128,128]{1,0:T(8,128)S(1)}, s32[128,128]{1,0:T(8,128)}, u32[]{:S(2)}) copy-start(s32[128,128]{1,0:T(8,128)} %get-tuple-element.31.spots) | copy-start | bytes 196612
  80.9 2.1 %collective-permute-start.3 = (bf16[16,64,128]{2,1,0:T(8,128)(2,1)S(1)}, bf16[16,64,128]{2,1,0:T(8,128)(2,1)S(1)}, u32[]{:S(2)}, u32[]{:S(2)}) collective-permute-start(bf16[16,64,128]{2,1,0:T(8,128)(2,1)S(1)} %slice.43), channel_id=1, source_target_pairs={{0,1},{1,0},{2,3},{3,2},{4,5},{5,4},{6,7},{7,6},{8,9},{9,8},{10,11... | collective-permute-start | bytes 786440 | tf_op jit(solution)/shard_map/ppermute | solution.py:668
  83.9 14.6 %all-to-all-start.1 = ((bf16[16,64,128]{2,1,0:T(8,128)(2,1)}), bf16[16,64,128]{2,1,0:T(8,128)(2,1)S(1)}, u32[]{:S(2)}, u32[]{:S(2)}) async-start(bf16[16,64,128]{2,1,0:T(8,128)(2,1)} %add_convert_fusion), calls=%async_computation.1 | async-start | bytes 524288 | tf_op jit(solution)/shard_map/all_to_all | solution.py:569
  88.1 2.2 %copy-start.1 = (bf16[512,4096]{1,0:T(8,128)(2,1)S(1)}, bf16[512,4096]{1,0:T(8,128)(2,1)}, u32[]{:S(2)}) copy-start(bf16[512,4096]{1,0:T(8,128)(2,1)} %near_blocks.1) | copy-start | bytes 12582916
  90.3 8.1 %copy-start.2 = (bf16[128,4096]{1,0:T(8,128)(2,1)S(1)}, bf16[128,4096]{1,0:T(8,128)(2,1)}, u32[]{:S(2)}) copy-start(bf16[128,4096]{1,0:T(8,128)(2,1)} %interpolate.1) | copy-start | bytes 3145732

commit v16 on v15

--- a/solution.py
+++ b/solution.py
@@ -25,8 +25,8 @@
 STRIDE = G + 1
 BATCH = 16
 WAYS = 4
-LINES = 16
-UNROLL_PLANES = 8
+LINES = 32
+UNROLL_PLANES = 32
 MB = 1 << 20
 NT = (((1,), (1,)), ((), ()))
 

time: 102 us -> 100 us (0.980)
  Pallas kernels: 58.1 us -> 55.7 us
    pallas_call x1, Pallas kernels: 16.6 us -> 15.4 us  [body(): pl.pallas_call(functools.partial(scatter_kernel, cols, gs, fs), grid=(1 +...]
    pallas_call x1, Pallas kernels: 14.7 us -> 13.5 us  [body(): pl.pallas_call(functools.partial(sample_kernel, cols), grid=(steps,), in_...]
where the time goes in v16:
time: 100 us; the launch traced here: 99.6 us
  Pallas kernels  55.7 us (56%)
  waiting for transfers between devices  25.7 us (26%)
  starting transfers between devices  14.6 us (15%)
  local copies, waits for them, and re-layouts  2.32 us (2%)
  other arithmetic  1.09 us (1%)
    all_to_all x2, waiting for transfers between devices, swap_members(): lax.all_to_all(array, axes, split_axis=0, concat_axis=0, axis_index_group...  18.7 us
    pallas_call x1, Pallas kernels, body(): pl.pallas_call(functools.partial(scatter_kernel, cols, gs, fs), grid=(1 +...  15.4 us
    pallas_call x1, Pallas kernels, body(): pl.pallas_call(functools.partial(sample_kernel, cols), grid=(steps,), in_...  13.5 us
    all_to_all x2, starting transfers between devices, swap_members(): lax.all_to_all(array, axes, split_axis=0, concat_axis=0, axis_index_group...  12.5 us
    pallas_call x1, Pallas kernels, body(): pl.pallas_call(spectrum_kernel, grid=(gs // BATCH,), in_specs=[smem, part...  8.81 us
    pallas_call x1, Pallas kernels, body(): pl.pallas_call(near_kernel, grid=(pairs // blocks,), in_specs=[smem, pl.B...  5.66 us
    pallas_call x1, Pallas kernels, body(): pl.pallas_call(project_kernel, out_shape=(struct((members, held, LANES),...  4.98 us
    ppermute x2, waiting for transfers between devices, body(): other = lax.ppermute(other, 'col', mates)  4 us
  transfers between devices with their start and end apart: 6, of which 6 were waited for; matrix products, arithmetic and copies ran while one was open for 0% of the time, Pallas kernels for 9%

profile of v16, /device:TPU:0, one launch (start us, length us, event | category | flops | bytes accessed | tf_op | source)
XLA Modules:
  0.0 99.6 jit_solution(4229692612961594831)
XLA Ops:
  0.0 5.0 %project.1 = (bf16[16,144,128]{2,1,0:T(8,128)(2,1)}, s32[128,128]{1,0:T(8,128)}) custom-call(bf16[64,128]{1,0:T(8,128)(2,1)} %bitcast.23, s32[64,128]{1,0:T(8,128)} %bitcast.16, bf16[128,4096]{1,0:T(8,128)(2,1)} %project_in.1, s32[3,128]{1,0:T(4,128)} %anchors_in.1), custom_call_target="tpu_custom_call" | custom-call | tf_op jit(solution)/shard_map/project/pallas_call | solution.py:539
  5.0 0.0 copy-start.3
  5.0 8.3 %all-to-all-start = ((bf16[16,144,128]{2,1,0:T(8,128)(2,1)}), bf16[16,144,128]{2,1,0:T(8,128)(2,1)S(1)}, u32[]{:S(2)}, u32[]{:S(2)}) async-start(bf16[16,144,128]{2,1,0:T(8,128)(2,1)} %get-tuple-element.20), calls=%async_computation | async-start | bytes 1179648 | tf_op jit(solution)/shard_map/all_to_all | solution.py:569
  13.4 16.2 %all-to-all-done.mine.my_extra = bf16[16,144,128]{2,1,0:T(8,128)(2,1)S(1)} async-done(((bf16[16,144,128]{2,1,0:T(8,128)(2,1)}), bf16[16,144,128]{2,1,0:T(8,128)(2,1)S(1)}, u32[]{:S(2)}, u32[]{:S(2)}) %all-to-all-start) | async-done | bytes 589856 | tf_op jit(solution)/shard_map/all_to_all | solution.py:569
  29.6 0.1 pad_add_fusion.place
  29.7 0.1 fusion.18
  29.8 1.8 %collective-permute-done.theirs.their_extra = bf16[16,144,128]{2,1,0:T(8,128)(2,1)S(1)} collective-permute-done((bf16[16,144,128]{2,1,0:T(8,128)(2,1)S(1)}, bf16[16,144,128]{2,1,0:T(8,128)(2,1)S(1)}, u32[]{:S(2)}, u32[]{:S(2)}) %collective-permute-start) | collective-permute-done | bytes 589856 | tf_op jit(solution)/shard_map/ppermute | solution.py:574
  31.7 0.1 sub.74
  31.8 15.4 %scatter.1 = (bf16[64,128,128]{2,1,0:T(8,128)(2,1)S(1)}, bf16[64,128,128]{2,1,0:T(8,128)(2,1)}) custom-call(s32[3]{0:T(128)S(1)} %pad_add_fusion.place, s32[4096]{0:T(1024)S(1)} %get-tuple-element.44.shift, s32[4096]{0:T(1024)S(1)} %get-tuple-element.35.start, bf16[16,144,128]{2,1,0:T(8,128)(2,1)S(1)} %all-to-all-done.mine.my_extra, ...), custom_call_target="tpu_custom_call" | custom-call | tf_op jit(solution)/shard_map/scatter/pallas_call | solution.py:602
  47.2 0.7 collective-permute-start.1
  47.9 3.8 %inverse.1 = s32[128,128]{1,0:T(8,128)S(1)} custom-call(s32[64,128]{1,0:T(8,128)S(1)} %bitcast.17), custom_call_target="tpu_custom_call" | custom-call | tf_op jit(solution)/shard_map/inverse/pallas_call | solution.py:619
  51.7 0.2 collective-permute-done.1.other
  51.9 8.8 %spectrum.1 = (bf16[64,128,128]{2,1,0:T(8,128)(2,1)S(1)}, bf16[64,128,128]{2,1,0:T(8,128)(2,1)S(1)}) custom-call(s32[3]{0:T(128)S(1)} %pad_add_fusion.place, bf16[64,128,128]{2,1,0:T(8,128)(2,1)S(1)} %get-tuple-element.22.own, bf16[64,128,128]{2,1,0:T(8,128)(2,1)S(1)} %collective-permute-done.1.other, f32[64,128,512]{2,1,0:T(8,128)} %refs_3_.1, ...), custom_call_target="tpu_custom_call" | custom-call | tf_op jit(solution)/shard_map/spectrum/pallas_call | solution.py:633
  60.7 0.4 collective-permute-start.2
  61.1 3.8 %collective-permute-done.2.other = bf16[64,128,128]{2,1,0:T(8,128)(2,1)S(1)} collective-permute-done((bf16[64,128,128]{2,1,0:T(8,128)(2,1)S(1)}, bf16[64,128,128]{2,1,0:T(8,128)(2,1)S(1)}, u32[]{:S(2)}, u32[]{:S(2)}) %collective-permute-start.2) | collective-permute-done | bytes 2097184 | tf_op jit(solution)/shard_map/ppermute | solution.py:648
  64.9 13.5 %sample.1 = bf16[32,64,128]{2,1,0:T(8,128)(2,1)S(1)} custom-call(s32[3]{0:T(128)S(1)} %pad_add_fusion.place, s32[4096]{0:T(1024)S(1)} %get-tuple-element.43.shift, s32[4096]{0:T(1024)S(1)} %get-tuple-element.36.start, bf16[16,144,128]{2,1,0:T(8,128)(2,1)S(1)} %all-to-all-done.mine.my_extra, ...), custom_call_target="tpu_custom_call" | custom-call | tf_op jit(solution)/shard_map/sample/pallas_call | solution.py:651
  78.5 1.0 collective-permute-start.3
  79.5 1.2 %collective-permute-done.3 = bf16[16,64,128]{2,1,0:T(8,128)(2,1)S(1)} collective-permute-done((bf16[16,64,128]{2,1,0:T(8,128)(2,1)S(1)}, bf16[16,64,128]{2,1,0:T(8,128)(2,1)S(1)}, u32[]{:S(2)}, u32[]{:S(2)}) %collective-permute-start.3) | collective-permute-done | bytes 262176 | tf_op jit(solution)/shard_map/ppermute | solution.py:668
  80.6 0.8 add_convert_fusion
  81.4 4.2 %all-to-all-start.1 = ((bf16[16,64,128]{2,1,0:T(8,128)(2,1)}), bf16[16,64,128]{2,1,0:T(8,128)(2,1)S(1)}, u32[]{:S(2)}, u32[]{:S(2)}) async-start(bf16[16,64,128]{2,1,0:T(8,128)(2,1)} %add_convert_fusion), calls=%async_computation.1 | async-start | bytes 524288 | tf_op jit(solution)/shard_map/all_to_all | solution.py:569
  85.7 2.2 %copy-done.1 = bf16[512,4096]{1,0:T(8,128)(2,1)S(1)} copy-done((bf16[512,4096]{1,0:T(8,128)(2,1)S(1)}, bf16[512,4096]{1,0:T(8,128)(2,1)}, u32[]{:S(2)}) %copy-start.1) | copy-done | bytes 4194328
  87.9 5.7 %near.1 = (f32[128,128]{1,0:T(8,128)S(1)}, bf16[4,128,512]{2,1,0:T(8,128)(2,1)S(1)}) custom-call(s32[512]{0:T(512)S(1)} %fusion.11.source, bf16[512,4096]{1,0:T(8,128)(2,1)S(1)} %copy-done.1, s32[1,512]{1,0:T(1,128)S(1)} %get-tuple-element.41.target, bf16[16,144,128]{2,1,0:T(8,128)(2,1)S(1)} %all-to-all-done.mine.my_extra, ...), custom_call_target="tpu_custom_call" | custom-call | tf_op jit(solution)/shard_map/near/pallas_call | solution.py:680
  93.5 2.5 %all-to-all-done.1.values = bf16[16,64,128]{2,1,0:T(8,128)(2,1)S(1)} async-done(((bf16[16,64,128]{2,1,0:T(8,128)(2,1)}), bf16[16,64,128]{2,1,0:T(8,128)(2,1)S(1)}, u32[]{:S(2)}, u32[]{:S(2)}) %all-to-all-start.1) | async-done | bytes 262176 | tf_op jit(solution)/shard_map/all_to_all | solution.py:569
  96.0 3.6 %finish.1 = f32[64,128]{1,0:T(8,128)} custom-call(bf16[16,64,128]{2,1,0:T(8,128)(2,1)S(1)} %all-to-all-done.1.values, bf16[128,4096]{1,0:T(8,128)(2,1)S(1)} %copy-done.2, f32[128,128]{1,0:T(8,128)S(1)} %get-tuple-element.32.near, s32[128,128]{1,0:T(8,128)S(1)} %inverse.1, bf16[4,128,512]{2,1,0:T(8,128)(2,1)S(1)} %get-tuple-element.34.lanes), custom_call_target="tpu_custom_call" | custom-call | tf_op jit(solution)/shard_map/finish/pallas_call | solution.py:704
  (23 shorter events, 0.2 us)
Async XLA Ops:
  0.0 31.8 %copy-start = (bf16[512,512]{1,0:T(8,128)(2,1)S(1)}, bf16[512,512]{1,0:T(8,128)(2,1)}, u32[]{:S(2)}) copy-start(bf16[512,512]{1,0:T(8,128)(2,1)} %constant.153.clone.cas.refs_4_) | copy-start | bytes 1572868
  5.0 42.9 %copy-start.3 = (s32[8192]{0:T(1024)S(1)}, s32[8192]{0:T(1024)}, u32[]{:S(2)}) copy-start(s32[8192]{0:T(1024)} %param.10) | copy-start | bytes 98308
  5.0 24.6 %all-to-all-start = ((bf16[16,144,128]{2,1,0:T(8,128)(2,1)}), bf16[16,144,128]{2,1,0:T(8,128)(2,1)S(1)}, u32[]{:S(2)}, u32[]{:S(2)}) async-start(bf16[16,144,128]{2,1,0:T(8,128)(2,1)} %get-tuple-element.20), calls=%async_computation | async-start | bytes 1179648 | tf_op jit(solution)/shard_map/all_to_all | solution.py:569
  29.6 2.0 %collective-permute-start = (bf16[16,144,128]{2,1,0:T(8,128)(2,1)S(1)}, bf16[16,144,128]{2,1,0:T(8,128)(2,1)S(1)}, u32[]{:S(2)}, u32[]{:S(2)}) collective-permute-start(bf16[16,144,128]{2,1,0:T(8,128)(2,1)S(1)} %all-to-all-done.mine.my_extra), channel_id=1, source_target_pairs={{0,1},{1,0},{2,3},{3,2},{4,5},{5,4},{6,7},{7,6},{8,9},{9,8},{10,11... | collective-permute-start | bytes 1769480 | tf_op jit(solution)/shard_map/ppermute | solution.py:574
  47.2 4.7 %collective-permute-start.1 = (bf16[64,128,128]{2,1,0:T(8,128)(2,1)}, bf16[64,128,128]{2,1,0:T(8,128)(2,1)S(1)}, u32[]{:S(2)}, u32[]{:S(2)}) collective-permute-start(bf16[64,128,128]{2,1,0:T(8,128)(2,1)} %get-tuple-element.23), channel_id=1, source_target_pairs={{0,1},{1,0},{2,3},{3,2},{4,5},{5,4},{6,7},{7,6},{8,9},{9,8},{10,11... | collective-permute-start | bytes 6291464 | tf_op jit(solution)/shard_map/ppermute | solution.py:617
  60.7 4.2 %collective-permute-start.2 = (bf16[64,128,128]{2,1,0:T(8,128)(2,1)S(1)}, bf16[64,128,128]{2,1,0:T(8,128)(2,1)S(1)}, u32[]{:S(2)}, u32[]{:S(2)}) collective-permute-start(bf16[64,128,128]{2,1,0:T(8,128)(2,1)S(1)} %get-tuple-element.27), channel_id=1, source_target_pairs={{0,1},{1,0},{2,3},{3,2},{4,5},{5,4},{6,7},{7,6},{8,9},{9,8},{10,11... | collective-permute-start | bytes 6291464 | tf_op jit(solution)/shard_map/ppermute | solution.py:648
  64.9 20.7 %copy-start.5 = (s32[2,512]{1,0:T(2,128)S(1)}, s32[2,512]{1,0:T(2,128)}, u32[]{:S(2)}) copy-start(s32[2,512]{1,0:T(2,128)} %param.15) | copy-start | bytes 12292
  64.9 20.7 %copy-start.4 = (s32[128,128]{1,0:T(8,128)S(1)}, s32[128,128]{1,0:T(8,128)}, u32[]{:S(2)}) copy-start(s32[128,128]{1,0:T(8,128)} %get-tuple-element.31.spots) | copy-start | bytes 196612
  78.5 2.1 %collective-permute-start.3 = (bf16[16,64,128]{2,1,0:T(8,128)(2,1)S(1)}, bf16[16,64,128]{2,1,0:T(8,128)(2,1)S(1)}, u32[]{:S(2)}, u32[]{:S(2)}) collective-permute-start(bf16[16,64,128]{2,1,0:T(8,128)(2,1)S(1)} %slice.43), channel_id=1, source_target_pairs={{0,1},{1,0},{2,3},{3,2},{4,5},{5,4},{6,7},{7,6},{8,9},{9,8},{10,11... | collective-permute-start | bytes 786440 | tf_op jit(solution)/shard_map/ppermute | solution.py:668
  81.4 14.6 %all-to-all-start.1 = ((bf16[16,64,128]{2,1,0:T(8,128)(2,1)}), bf16[16,64,128]{2,1,0:T(8,128)(2,1)S(1)}, u32[]{:S(2)}, u32[]{:S(2)}) async-start(bf16[16,64,128]{2,1,0:T(8,128)(2,1)} %add_convert_fusion), calls=%async_computation.1 | async-start | bytes 524288 | tf_op jit(solution)/shard_map/all_to_all | solution.py:569
  85.7 2.2 %copy-start.1 = (bf16[512,4096]{1,0:T(8,128)(2,1)S(1)}, bf16[512,4096]{1,0:T(8,128)(2,1)}, u32[]{:S(2)}) copy-start(bf16[512,4096]{1,0:T(8,128)(2,1)} %near_blocks.1) | copy-start | bytes 12582916
  87.9 8.1 %copy-start.2 = (bf16[128,4096]{1,0:T(8,128)(2,1)S(1)}, bf16[128,4096]{1,0:T(8,128)(2,1)}, u32[]{:S(2)}) copy-start(bf16[128,4096]{1,0:T(8,128)(2,1)} %interpolate.1) | copy-start | bytes 3145732

commit v17 on v16

--- a/solution.py
+++ b/solution.py
@@ -24,9 +24,9 @@
 CELLS = PAD + QUAD * G + 16
 STRIDE = G + 1
 BATCH = 16
-WAYS = 4
+WAYS = 8
 LINES = 32
-UNROLL_PLANES = 32
+UNROLL_PLANES = 64
 MB = 1 << 20
 NT = (((1,), (1,)), ((), ()))
 

time: 100 us -> 99.7 us (level)
  transfers between devices with their start and end apart: 6 -> 6, of which waited for: 6 -> 6; matrix products, arithmetic and copies ran while one was open for 0% -> 0% of each run, Pallas kernels for 9% -> 10%
where the time goes in v17:
time: 99.7 us; the launch traced here: 99.3 us
  Pallas kernels  55.4 us (56%)
  waiting for transfers between devices  25.7 us (26%)
  starting transfers between devices  14.6 us (15%)
  local copies, waits for them, and re-layouts  2.32 us (2%)
  other arithmetic  1.09 us (1%)
    all_to_all x2, waiting for transfers between devices, swap_members(): lax.all_to_all(array, axes, split_axis=0, concat_axis=0, axis_index_group...  18.7 us
    pallas_call x1, Pallas kernels, body(): pl.pallas_call(functools.partial(scatter_kernel, cols, gs, fs), grid=(1 +...  15.3 us
    pallas_call x1, Pallas kernels, body(): pl.pallas_call(functools.partial(sample_kernel, cols), grid=(steps,), in_...  13.3 us
    all_to_all x2, starting transfers between devices, swap_members(): lax.all_to_all(array, axes, split_axis=0, concat_axis=0, axis_index_group...  12.5 us
    pallas_call x1, Pallas kernels, body(): pl.pallas_call(spectrum_kernel, grid=(gs // BATCH,), in_specs=[smem, part...  8.82 us
    pallas_call x1, Pallas kernels, body(): pl.pallas_call(near_kernel, grid=(pairs // blocks,), in_specs=[smem, pl.B...  5.67 us
    pallas_call x1, Pallas kernels, body(): pl.pallas_call(project_kernel, out_shape=(struct((members, held, LANES),...  4.98 us
    ppermute x2, waiting for transfers between devices, body(): other = lax.ppermute(other, 'col', mates)  4 us
  transfers between devices with their start and end apart: 6, of which 6 were waited for; matrix products, arithmetic and copies ran while one was open for 0% of the time, Pallas kernels for 10%

profile of v17, /device:TPU:0, one launch (start us, length us, event | category | flops | bytes accessed | tf_op | source)
XLA Modules:
  0.0 99.3 jit_solution(4309817020934494678)
XLA Ops:
  0.0 5.0 %project.1 = (bf16[16,144,128]{2,1,0:T(8,128)(2,1)}, s32[128,128]{1,0:T(8,128)}) custom-call(bf16[64,128]{1,0:T(8,128)(2,1)} %bitcast.23, s32[64,128]{1,0:T(8,128)} %bitcast.16, bf16[128,4096]{1,0:T(8,128)(2,1)} %project_in.1, s32[3,128]{1,0:T(4,128)} %anchors_in.1), custom_call_target="tpu_custom_call" | custom-call | tf_op jit(solution)/shard_map/project/pallas_call | solution.py:539
  5.0 8.3 %all-to-all-start = ((bf16[16,144,128]{2,1,0:T(8,128)(2,1)}), bf16[16,144,128]{2,1,0:T(8,128)(2,1)S(1)}, u32[]{:S(2)}, u32[]{:S(2)}) async-start(bf16[16,144,128]{2,1,0:T(8,128)(2,1)} %get-tuple-element.20), calls=%async_computation | async-start | bytes 1179648 | tf_op jit(solution)/shard_map/all_to_all | solution.py:569
  13.4 16.2 %all-to-all-done.mine.my_extra = bf16[16,144,128]{2,1,0:T(8,128)(2,1)S(1)} async-done(((bf16[16,144,128]{2,1,0:T(8,128)(2,1)}), bf16[16,144,128]{2,1,0:T(8,128)(2,1)S(1)}, u32[]{:S(2)}, u32[]{:S(2)}) %all-to-all-start) | async-done | bytes 589856 | tf_op jit(solution)/shard_map/all_to_all | solution.py:569
  29.6 0.1 pad_add_fusion.place
  29.7 0.1 fusion.18
  29.8 1.8 %collective-permute-done.theirs.their_extra = bf16[16,144,128]{2,1,0:T(8,128)(2,1)S(1)} collective-permute-done((bf16[16,144,128]{2,1,0:T(8,128)(2,1)S(1)}, bf16[16,144,128]{2,1,0:T(8,128)(2,1)S(1)}, u32[]{:S(2)}, u32[]{:S(2)}) %collective-permute-start) | collective-permute-done | bytes 589856 | tf_op jit(solution)/shard_map/ppermute | solution.py:574
  31.7 0.1 sub.74
  31.8 15.3 %scatter.1 = (bf16[64,128,128]{2,1,0:T(8,128)(2,1)S(1)}, bf16[64,128,128]{2,1,0:T(8,128)(2,1)}) custom-call(s32[3]{0:T(128)S(1)} %pad_add_fusion.place, s32[4096]{0:T(1024)S(1)} %get-tuple-element.44.shift, s32[4096]{0:T(1024)S(1)} %get-tuple-element.35.start, bf16[16,144,128]{2,1,0:T(8,128)(2,1)S(1)} %all-to-all-done.mine.my_extra, ...), custom_call_target="tpu_custom_call" | custom-call | tf_op jit(solution)/shard_map/scatter/pallas_call | solution.py:602
  47.1 0.7 collective-permute-start.1
  47.8 3.8 %inverse.1 = s32[128,128]{1,0:T(8,128)S(1)} custom-call(s32[64,128]{1,0:T(8,128)S(1)} %bitcast.17), custom_call_target="tpu_custom_call" | custom-call | tf_op jit(solution)/shard_map/inverse/pallas_call | solution.py:619
  51.6 0.2 collective-permute-done.1.other
  51.8 8.8 %spectrum.1 = (bf16[64,128,128]{2,1,0:T(8,128)(2,1)S(1)}, bf16[64,128,128]{2,1,0:T(8,128)(2,1)S(1)}) custom-call(s32[3]{0:T(128)S(1)} %pad_add_fusion.place, bf16[64,128,128]{2,1,0:T(8,128)(2,1)S(1)} %get-tuple-element.22.own, bf16[64,128,128]{2,1,0:T(8,128)(2,1)S(1)} %collective-permute-done.1.other, f32[64,128,512]{2,1,0:T(8,128)} %refs_7_.1, ...), custom_call_target="tpu_custom_call" | custom-call | tf_op jit(solution)/shard_map/spectrum/pallas_call | solution.py:633
  60.6 0.4 collective-permute-start.2
  61.0 3.8 %collective-permute-done.2.other = bf16[64,128,128]{2,1,0:T(8,128)(2,1)S(1)} collective-permute-done((bf16[64,128,128]{2,1,0:T(8,128)(2,1)S(1)}, bf16[64,128,128]{2,1,0:T(8,128)(2,1)S(1)}, u32[]{:S(2)}, u32[]{:S(2)}) %collective-permute-start.2) | collective-permute-done | bytes 2097184 | tf_op jit(solution)/shard_map/ppermute | solution.py:648
  64.8 13.3 %sample.1 = bf16[32,64,128]{2,1,0:T(8,128)(2,1)S(1)} custom-call(s32[3]{0:T(128)S(1)} %pad_add_fusion.place, s32[4096]{0:T(1024)S(1)} %get-tuple-element.43.shift, s32[4096]{0:T(1024)S(1)} %get-tuple-element.36.start, bf16[16,144,128]{2,1,0:T(8,128)(2,1)S(1)} %all-to-all-done.mine.my_extra, ...), custom_call_target="tpu_custom_call" | custom-call | tf_op jit(solution)/shard_map/sample/pallas_call | solution.py:651
  78.2 1.0 collective-permute-start.3
  79.2 1.2 %collective-permute-done.3 = bf16[16,64,128]{2,1,0:T(8,128)(2,1)S(1)} collective-permute-done((bf16[16,64,128]{2,1,0:T(8,128)(2,1)S(1)}, bf16[16,64,128]{2,1,0:T(8,128)(2,1)S(1)}, u32[]{:S(2)}, u32[]{:S(2)}) %collective-permute-start.3) | collective-permute-done | bytes 262176 | tf_op jit(solution)/shard_map/ppermute | solution.py:668
  80.4 0.8 add_convert_fusion
  81.1 4.2 %all-to-all-start.1 = ((bf16[16,64,128]{2,1,0:T(8,128)(2,1)}), bf16[16,64,128]{2,1,0:T(8,128)(2,1)S(1)}, u32[]{:S(2)}, u32[]{:S(2)}) async-start(bf16[16,64,128]{2,1,0:T(8,128)(2,1)} %add_convert_fusion), calls=%async_computation.1 | async-start | bytes 524288 | tf_op jit(solution)/shard_map/all_to_all | solution.py:569
  85.4 0.0 copy-start.1
  85.4 2.2 %copy-done.1 = bf16[512,4096]{1,0:T(8,128)(2,1)S(1)} copy-done((bf16[512,4096]{1,0:T(8,128)(2,1)S(1)}, bf16[512,4096]{1,0:T(8,128)(2,1)}, u32[]{:S(2)}) %copy-start.1) | copy-done | bytes 4194328
  87.6 5.7 %near.1 = (f32[128,128]{1,0:T(8,128)S(1)}, bf16[4,128,512]{2,1,0:T(8,128)(2,1)S(1)}) custom-call(s32[512]{0:T(512)S(1)} %fusion.11.source, bf16[512,4096]{1,0:T(8,128)(2,1)S(1)} %copy-done.1, s32[1,512]{1,0:T(1,128)S(1)} %get-tuple-element.41.target, bf16[16,144,128]{2,1,0:T(8,128)(2,1)S(1)} %all-to-all-done.mine.my_extra, ...), custom_call_target="tpu_custom_call" | custom-call | tf_op jit(solution)/shard_map/near/pallas_call | solution.py:680
  93.3 2.5 %all-to-all-done.1.values = bf16[16,64,128]{2,1,0:T(8,128)(2,1)S(1)} async-done(((bf16[16,64,128]{2,1,0:T(8,128)(2,1)}), bf16[16,64,128]{2,1,0:T(8,128)(2,1)S(1)}, u32[]{:S(2)}, u32[]{:S(2)}) %all-to-all-start.1) | async-done | bytes 262176 | tf_op jit(solution)/shard_map/all_to_all | solution.py:569
  95.7 3.6 %finish.1 = f32[64,128]{1,0:T(8,128)} custom-call(bf16[16,64,128]{2,1,0:T(8,128)(2,1)S(1)} %all-to-all-done.1.values, bf16[128,4096]{1,0:T(8,128)(2,1)S(1)} %copy-done.2, f32[128,128]{1,0:T(8,128)S(1)} %get-tuple-element.32.near, s32[128,128]{1,0:T(8,128)S(1)} %inverse.1, bf16[4,128,512]{2,1,0:T(8,128)(2,1)S(1)} %get-tuple-element.34.lanes), custom_call_target="tpu_custom_call" | custom-call | tf_op jit(solution)/shard_map/finish/pallas_call | solution.py:704
  (23 shorter events, 0.2 us)
Async XLA Ops:
  0.0 31.8 %copy-start = (bf16[512,512]{1,0:T(8,128)(2,1)S(1)}, bf16[512,512]{1,0:T(8,128)(2,1)}, u32[]{:S(2)}) copy-start(bf16[512,512]{1,0:T(8,128)(2,1)} %constant.153.clone.cas.refs_8_) | copy-start | bytes 1572868
  5.0 42.8 %copy-start.3 = (s32[8192]{0:T(1024)S(1)}, s32[8192]{0:T(1024)}, u32[]{:S(2)}) copy-start(s32[8192]{0:T(1024)} %param.10) | copy-start | bytes 98308
  5.0 24.6 %all-to-all-start = ((bf16[16,144,128]{2,1,0:T(8,128)(2,1)}), bf16[16,144,128]{2,1,0:T(8,128)(2,1)S(1)}, u32[]{:S(2)}, u32[]{:S(2)}) async-start(bf16[16,144,128]{2,1,0:T(8,128)(2,1)} %get-tuple-element.20), calls=%async_computation | async-start | bytes 1179648 | tf_op jit(solution)/shard_map/all_to_all | solution.py:569
  29.6 2.0 %collective-permute-start = (bf16[16,144,128]{2,1,0:T(8,128)(2,1)S(1)}, bf16[16,144,128]{2,1,0:T(8,128)(2,1)S(1)}, u32[]{:S(2)}, u32[]{:S(2)}) collective-permute-start(bf16[16,144,128]{2,1,0:T(8,128)(2,1)S(1)} %all-to-all-done.mine.my_extra), channel_id=1, source_target_pairs={{0,1},{1,0},{2,3},{3,2},{4,5},{5,4},{6,7},{7,6},{8,9},{9,8},{10,11... | collective-permute-start | bytes 1769480 | tf_op jit(solution)/shard_map/ppermute | solution.py:574
  47.1 4.7 %collective-permute-start.1 = (bf16[64,128,128]{2,1,0:T(8,128)(2,1)}, bf16[64,128,128]{2,1,0:T(8,128)(2,1)S(1)}, u32[]{:S(2)}, u32[]{:S(2)}) collective-permute-start(bf16[64,128,128]{2,1,0:T(8,128)(2,1)} %get-tuple-element.23), channel_id=1, source_target_pairs={{0,1},{1,0},{2,3},{3,2},{4,5},{5,4},{6,7},{7,6},{8,9},{9,8},{10,11... | collective-permute-start | bytes 6291464 | tf_op jit(solution)/shard_map/ppermute | solution.py:617
  60.6 4.2 %collective-permute-start.2 = (bf16[64,128,128]{2,1,0:T(8,128)(2,1)S(1)}, bf16[64,128,128]{2,1,0:T(8,128)(2,1)S(1)}, u32[]{:S(2)}, u32[]{:S(2)}) collective-permute-start(bf16[64,128,128]{2,1,0:T(8,128)(2,1)S(1)} %get-tuple-element.27), channel_id=1, source_target_pairs={{0,1},{1,0},{2,3},{3,2},{4,5},{5,4},{6,7},{7,6},{8,9},{9,8},{10,11... | collective-permute-start | bytes 6291464 | tf_op jit(solution)/shard_map/ppermute | solution.py:648
  64.8 20.5 %copy-start.5 = (s32[2,512]{1,0:T(2,128)S(1)}, s32[2,512]{1,0:T(2,128)}, u32[]{:S(2)}) copy-start(s32[2,512]{1,0:T(2,128)} %param.15) | copy-start | bytes 12292
  64.8 20.5 %copy-start.4 = (s32[128,128]{1,0:T(8,128)S(1)}, s32[128,128]{1,0:T(8,128)}, u32[]{:S(2)}) copy-start(s32[128,128]{1,0:T(8,128)} %get-tuple-element.31.spots) | copy-start | bytes 196612
  78.2 2.2 %collective-permute-start.3 = (bf16[16,64,128]{2,1,0:T(8,128)(2,1)S(1)}, bf16[16,64,128]{2,1,0:T(8,128)(2,1)S(1)}, u32[]{:S(2)}, u32[]{:S(2)}) collective-permute-start(bf16[16,64,128]{2,1,0:T(8,128)(2,1)S(1)} %slice.43), channel_id=1, source_target_pairs={{0,1},{1,0},{2,3},{3,2},{4,5},{5,4},{6,7},{7,6},{8,9},{9,8},{10,11... | collective-permute-start | bytes 786440 | tf_op jit(solution)/shard_map/ppermute | solution.py:668
  81.1 14.6 %all-to-all-start.1 = ((bf16[16,64,128]{2,1,0:T(8,128)(2,1)}), bf16[16,64,128]{2,1,0:T(8,128)(2,1)S(1)}, u32[]{:S(2)}, u32[]{:S(2)}) async-start(bf16[16,64,128]{2,1,0:T(8,128)(2,1)} %add_convert_fusion), calls=%async_computation.1 | async-start | bytes 524288 | tf_op jit(solution)/shard_map/all_to_all | solution.py:569
  85.4 2.2 %copy-start.1 = (bf16[512,4096]{1,0:T(8,128)(2,1)S(1)}, bf16[512,4096]{1,0:T(8,128)(2,1)}, u32[]{:S(2)}) copy-start(bf16[512,4096]{1,0:T(8,128)(2,1)} %near_blocks.1) | copy-start | bytes 12582916
  87.6 8.1 %copy-start.2 = (bf16[128,4096]{1,0:T(8,128)(2,1)S(1)}, bf16[128,4096]{1,0:T(8,128)(2,1)}, u32[]{:S(2)}) copy-start(bf16[128,4096]{1,0:T(8,128)(2,1)} %interpolate.1) | copy-start | bytes 3145732
